TPU v7x, 32 devices: a whole 2x2x4 slice. The times are simulated.
32 devices in a mesh: seq: 8 (over y, x, core), batch: 4 (over z).
Axes of the slice: x: 2, y: 2, z: 4, core: 2. Of those that a mesh axis runs over, the one named last changes fastest.
Arguments:
- tokens: bfloat16 [4, 1024, 2048], P('batch', 'seq'), may hold values from -6 to 6
- segments: int32 [4, 1024], P('batch'), may hold values from 0 to 3, as said below
- expert_ids: int32 [4, 1024, 8], P('batch', 'seq'), may hold values from 0 to 15, all different within a row; in each aligned block of 128 rows (0 to 127, 128 to 255, ..., all dimensions but the last counted through in order) at most 96 rows name the same one
- w_query: bfloat16 [2048, 2048], P(('seq', 'batch')), may hold values from -0.125 to 0.125
- w_key: bfloat16 [2048, 2048], P(('seq', 'batch')), may hold values from -0.125 to 0.125
- w_value: bfloat16 [2048, 2048], P(('seq', 'batch')), may hold values from -0.125 to 0.125
- w_out: bfloat16 [2048, 2048], P(('seq', 'batch')), may hold values from -3 to 3
- w_router: bfloat16 [2048, 16], P(('seq', 'batch')), may hold values from -0.0625 to 0.0625
- attn_gain: bfloat16 [2048], P(('seq', 'batch')), may hold values from 0.25 to 1.75
- query_gain: bfloat16 [2048], P(('seq', 'batch')), may hold values from 0.25 to 1.75
- key_gain: bfloat16 [2048], P(('seq', 'batch')), may hold values from 0.25 to 1.75
- ffn_gain: bfloat16 [2048], P(('seq', 'batch')), may hold values from 0.25 to 1.75
- w_gate: bfloat16 [16, 2048, 1024], P('seq'), may hold values from -0.125 to 0.125
- w_up: bfloat16 [16, 2048, 1024], P('seq'), may hold values from -0.125 to 0.125
- w_down: bfloat16 [16, 1024, 2048], P('seq'), may hold values from -1 to 1
- out_grad: bfloat16 [4, 1024, 2048], P('batch', 'seq'), may hold values from -6 to 6
Outputs:
- block_out: bfloat16 [4, 1024, 2048], P('batch', 'seq')
- input_grad: float32 [4, 1024, 2048], P('batch', 'seq')
- query_grad: float32 [2048, 2048], P(('seq', 'batch'))
- key_grad: float32 [2048, 2048], P(('seq', 'batch'))
- value_grad: float32 [2048, 2048], P(('seq', 'batch'))
- out_proj_grad: float32 [2048, 2048], P(('seq', 'batch'))
- router_grad: float32 [2048, 16], P(('seq', 'batch'))
- attn_gain_grad: float32 [2048], P(('seq', 'batch'))
- query_gain_grad: float32 [2048], P(('seq', 'batch'))
- key_gain_grad: float32 [2048], P(('seq', 'batch'))
- ffn_gain_grad: float32 [2048], P(('seq', 'batch'))
- gate_grad: float32 [16, 2048, 1024], P('seq', 'batch')
- up_grad: float32 [16, 2048, 1024], P('seq', 'batch')
- down_grad: float32 [16, 1024, 2048], P('seq', 'batch')
- expert_counts: int32 [4, 16], P('batch', 'seq')
Inputs may be any that keep to these rules, and one draw needn't show every extreme that they name: `segments`: along each sequence the ids start at 0 and never fall; the document with id 1 begins within the first 128 positions and ends within the last 128 positions. `expert_ids`: each token names 8 different experts. In the rows of one device no expert is named by more than 96 rows; in some devices' rows an expert is named by exactly 96.
All inputs are finite; a program needn't handle non-finite values.
Results may differ from a plain program's by a relative error of at most 0.03.
Values may be sent and summed in bfloat16 or wider, within the bound.
No kernel may reach another device: no remote copies, remote signals or barrier semaphores. Data moves between devices by JAX's collectives and lax.ppermute only.
A program may use at most 384 MiB of HBM per device.

v0:
```python
import math

import jax
import jax.numpy as jnp
from jax import lax
from jax.sharding import PartitionSpec as P

HEAD_DIM = 128


EPSILON = 1e-05
ROTARY_BASE = 10000.0
MASKED = -1e30


def norm_scale(values):
    return lax.rsqrt(jnp.mean(values * values, axis=-1, keepdims=True) + EPSILON)


def norm_back(grad_normed, unit, scale, gain):
    scaled = grad_normed * gain
    inner = jnp.mean(scaled * unit, axis=-1, keepdims=True)
    return (scale * (scaled - unit * inner), jnp.sum(grad_normed * unit, axis=0))


def rotary_tables(positions, head_dim):
    half = head_dim // 2
    rates = jnp.power(ROTARY_BASE, -jnp.arange(half, dtype=jnp.float32) * (2.0 / head_dim))
    angles = positions.astype(jnp.float32)[:, None] * rates[None, :]
    return (jnp.cos(angles)[:, None, :], jnp.sin(angles)[:, None, :])


def rotate(values, cosine, sine):
    half = values.shape[-1] // 2
    first, second = (values[..., :half], values[..., half:])
    return jnp.concatenate(
        [first * cosine - second * sine, second * cosine + first * sine], axis=-1
    )


def unrotate(gradients, cosine, sine):
    half = gradients.shape[-1] // 2
    first, second = (gradients[..., :half], gradients[..., half:])
    return jnp.concatenate(
        [first * cosine + second * sine, second * cosine - first * sine], axis=-1
    )


def allowed_mask(query_pos, query_doc, doc_all, count):
    key_pos = jnp.arange(count, dtype=jnp.int32)
    return (key_pos[None, :] <= query_pos[:, None]) & (doc_all[None, :] == query_doc[:, None])


def on_device(
    tokens,
    segments,
    expert_ids,
    w_query,
    w_key,
    w_value,
    w_out,
    w_router,
    attn_gain,
    query_gain,
    key_gain,
    ffn_gain,
    w_gate,
    w_up,
    w_down,
    out_grad,
):
    inputs = tokens[0].astype(jnp.float32)
    rows_here, width = inputs.shape
    heads = width // HEAD_DIM
    cycle_size = lax.axis_size("seq")
    offset = lax.axis_index("seq") * rows_here
    doc_all = segments[0]
    positions = offset + jnp.arange(rows_here, dtype=jnp.int32)
    doc_here = lax.dynamic_slice_in_dim(doc_all, offset, rows_here, 0)
    cosine, sine = rotary_tables(positions, HEAD_DIM)
    factor = 1.0 / math.sqrt(HEAD_DIM)
    shared = (
        lax.all_gather(w_query, ("seq", "batch"), axis=0, tiled=True),
        lax.all_gather(w_key, ("seq", "batch"), axis=0, tiled=True),
        lax.all_gather(w_value, ("seq", "batch"), axis=0, tiled=True),
        lax.all_gather(w_out, ("seq", "batch"), axis=0, tiled=True),
        lax.all_gather(w_router, ("seq", "batch"), axis=0, tiled=True),
        lax.all_gather(attn_gain, ("seq", "batch"), axis=0, tiled=True),
        lax.all_gather(query_gain, ("seq", "batch"), axis=0, tiled=True),
        lax.all_gather(key_gain, ("seq", "batch"), axis=0, tiled=True),
        lax.all_gather(ffn_gain, ("seq", "batch"), axis=0, tiled=True),
    )
    query_full, key_full, value_full, out_full, router_full = (
        shared[0],
        shared[1],
        shared[2],
        shared[3],
        shared[4],
    )
    attn_norm_gain = shared[5].astype(jnp.float32)
    query_norm_gain = shared[6].astype(jnp.float32)
    key_norm_gain = shared[7].astype(jnp.float32)
    ffn_norm_gain = shared[8].astype(jnp.float32)
    attn_scale = norm_scale(inputs)
    attn_unit = inputs * attn_scale
    normed = (attn_unit * attn_norm_gain).astype(jnp.bfloat16)
    query_proj = jnp.dot(normed, query_full, preferred_element_type=jnp.float32)
    key_proj = jnp.dot(normed, key_full, preferred_element_type=jnp.float32)
    value_proj = jnp.dot(normed, value_full, preferred_element_type=jnp.float32)
    query_scale = norm_scale(query_proj)
    query_unit = query_proj * query_scale
    key_scale = norm_scale(key_proj)
    key_unit = key_proj * key_scale
    query_heads = rotate(
        (query_unit * query_norm_gain).reshape(rows_here, heads, HEAD_DIM), cosine, sine
    ).astype(jnp.bfloat16)
    key_send = (
        rotate((key_unit * key_norm_gain).reshape(rows_here, heads, HEAD_DIM), cosine, sine)
        .astype(jnp.bfloat16)
        .reshape(rows_here, width)
    )
    value_send = value_proj.astype(jnp.bfloat16)
    piece = (
        lax.all_gather(key_send, "seq", axis=0, tiled=True),
        lax.all_gather(value_send, "seq", axis=0, tiled=True),
    )
    running_max = jnp.full((heads, rows_here), MASKED, jnp.float32)
    running_out = jnp.zeros((rows_here, heads, HEAD_DIM), jnp.float32)
    keys = piece[0].reshape(-1, heads, HEAD_DIM)
    values = piece[1].reshape(-1, heads, HEAD_DIM)
    count = keys.shape[0]
    allowed = allowed_mask(positions, doc_here, doc_all, count)[None]
    scores = (
        jnp.einsum("qhd,khd->hqk", query_heads, keys, preferred_element_type=jnp.float32) * factor
    )
    scores = jnp.where(allowed, scores, MASKED)
    new_max = jnp.maximum(running_max, jnp.max(scores, axis=-1))
    shrink = jnp.exp(running_max - new_max)
    weights = jnp.where(allowed, jnp.exp(scores - new_max[..., None]), 0.0)
    new_sum = jnp.sum(weights, axis=-1)
    mixed = jnp.einsum(
        "hqk,khd->qhd", weights.astype(jnp.bfloat16), values, preferred_element_type=jnp.float32
    )
    final_out = running_out * shrink.T[:, :, None] + mixed
    log_total = new_max + jnp.log(new_sum)
    attn_heads = final_out / new_sum.T[:, :, None]
    mixed_low = attn_heads.reshape(rows_here, width).astype(jnp.bfloat16)
    residual = inputs + jnp.dot(mixed_low, out_full, preferred_element_type=jnp.float32)
    ffn_scale = norm_scale(residual)
    ffn_unit = residual * ffn_scale
    ffn_in = (ffn_unit * ffn_norm_gain).astype(jnp.bfloat16)
    logits = jnp.dot(ffn_in, router_full, preferred_element_type=jnp.float32)
    chances = jax.nn.softmax(logits, axis=-1)
    experts_all = router_full.shape[1]
    owner_experts = w_gate.shape[0]
    choose = expert_ids[0]
    top_count = choose.shape[1]
    picks = choose.reshape(-1)
    chosen = (picks[:, None] == jnp.arange(experts_all, dtype=jnp.int32)[None, :]).astype(jnp.int32)
    ranks = jnp.sum((jnp.cumsum(chosen, axis=0) - 1) * chosen, axis=1)
    capacity = 3 * rows_here * top_count // (2 * experts_all)
    target = picks * capacity + ranks
    choice_table = chosen.reshape(rows_here, top_count, experts_all).astype(jnp.float32)
    gates = jnp.sum(choice_table * chances[:, None, :], axis=-1)
    repeated = jnp.repeat(ffn_in, top_count, axis=0)
    outgoing = jnp.zeros((experts_all * capacity, width), jnp.bfloat16).at[target].set(repeated)
    outgoing = outgoing.reshape(cycle_size, owner_experts, capacity, width)
    local_counts = jnp.sum(chosen, axis=0).reshape(cycle_size, owner_experts)
    arrived, arrived_counts = (
        lax.all_to_all(outgoing, "seq", split_axis=0, concat_axis=0, tiled=True),
        lax.all_to_all(local_counts, "seq", split_axis=0, concat_axis=0, tiled=True),
    )
    counts_here = jnp.sum(arrived_counts, axis=0)
    gate_act = jnp.einsum("sxcd,xdf->sxcf", arrived, w_gate, preferred_element_type=jnp.float32)
    up_act = jnp.einsum("sxcd,xdf->sxcf", arrived, w_up, preferred_element_type=jnp.float32)
    expert_hidden = (jax.nn.silu(gate_act) * up_act).astype(jnp.bfloat16)
    expert_out = jnp.einsum(
        "sxcf,xfd->sxcd", expert_hidden, w_down, preferred_element_type=jnp.float32
    ).astype(jnp.bfloat16)
    returned = lax.all_to_all(expert_out, "seq", split_axis=0, concat_axis=0, tiled=True).reshape(
        experts_all * capacity, width
    )
    picked = returned[target].reshape(rows_here, top_count, width)
    expert_mix = jnp.einsum("tk,tkd->td", gates, picked, preferred_element_type=jnp.float32)
    block_out = (residual + expert_mix).astype(jnp.bfloat16)
    query_back, key_back, value_back, out_back, router_back = (
        lax.all_gather(w_query, ("seq", "batch"), axis=0, tiled=True),
        lax.all_gather(w_key, ("seq", "batch"), axis=0, tiled=True),
        lax.all_gather(w_value, ("seq", "batch"), axis=0, tiled=True),
        lax.all_gather(w_out, ("seq", "batch"), axis=0, tiled=True),
        lax.all_gather(w_router, ("seq", "batch"), axis=0, tiled=True),
    )
    upstream = out_grad[0].astype(jnp.float32)
    grad_rows_out = (
        (gates[:, :, None] * upstream[:, None, :]).astype(jnp.bfloat16).reshape(-1, width)
    )
    grad_gates = jnp.einsum("tkd,td->tk", picked, upstream, preferred_element_type=jnp.float32)
    grad_outgoing = (
        jnp.zeros((experts_all * capacity, width), jnp.bfloat16).at[target].set(grad_rows_out)
    )
    grad_outgoing = grad_outgoing.reshape(cycle_size, owner_experts, capacity, width)
    grad_arrived, expert_in = (
        lax.all_to_all(grad_outgoing, "seq", split_axis=0, concat_axis=0, tiled=True),
        lax.all_to_all(outgoing, "seq", split_axis=0, concat_axis=0, tiled=True),
    )
    gate_keep = jnp.einsum("sxcd,xdf->sxcf", expert_in, w_gate, preferred_element_type=jnp.float32)
    up_keep = jnp.einsum("sxcd,xdf->sxcf", expert_in, w_up, preferred_element_type=jnp.float32)
    hidden_keep = (jax.nn.silu(gate_keep) * up_keep).astype(jnp.bfloat16)
    grad_hidden = jnp.einsum(
        "sxcd,xfd->sxcf", grad_arrived, w_down, preferred_element_type=jnp.float32
    )
    down_term = jnp.einsum(
        "sxcf,sxcd->xfd", hidden_keep, grad_arrived, preferred_element_type=jnp.float32
    )
    sigma = jax.nn.sigmoid(gate_keep)
    grad_gate_act = (grad_hidden * up_keep * sigma * (1.0 + gate_keep * (1.0 - sigma))).astype(
        jnp.bfloat16
    )
    grad_up_act = (grad_hidden * gate_keep * sigma).astype(jnp.bfloat16)
    gate_term = jnp.einsum(
        "sxcd,sxcf->xdf", expert_in, grad_gate_act, preferred_element_type=jnp.float32
    )
    up_term = jnp.einsum(
        "sxcd,sxcf->xdf", expert_in, grad_up_act, preferred_element_type=jnp.float32
    )
    grad_in_rows = (
        jnp.einsum("sxcf,xdf->sxcd", grad_gate_act, w_gate, preferred_element_type=jnp.float32)
        + jnp.einsum("sxcf,xdf->sxcd", grad_up_act, w_up, preferred_element_type=jnp.float32)
    ).astype(jnp.bfloat16)
    grad_back = lax.all_to_all(
        grad_in_rows, "seq", split_axis=0, concat_axis=0, tiled=True
    ).reshape(experts_all * capacity, width)
    grad_ffn_in = jnp.sum(
        grad_back[target].reshape(rows_here, top_count, width), axis=1, dtype=jnp.float32
    )
    grad_chances = jnp.einsum("tk,tke->te", grad_gates, choice_table)
    grad_logits = (
        chances * (grad_chances - jnp.sum(chances * grad_chances, axis=-1, keepdims=True))
    ).astype(jnp.bfloat16)
    router_term = jnp.einsum("td,te->de", ffn_in, grad_logits, preferred_element_type=jnp.float32)
    grad_ffn_in = grad_ffn_in + jnp.einsum(
        "te,de->td", grad_logits, router_back, preferred_element_type=jnp.float32
    )
    grad_res_norm, ffn_gain_term = norm_back(grad_ffn_in, ffn_unit, ffn_scale, ffn_norm_gain)
    grad_residual = upstream + grad_res_norm
    grad_attn = grad_residual.astype(jnp.bfloat16)
    out_term = jnp.einsum("td,te->de", mixed_low, grad_attn, preferred_element_type=jnp.float32)
    grad_mixed = (
        jnp.einsum("te,de->td", grad_attn, out_back, preferred_element_type=jnp.float32)
        .astype(jnp.bfloat16)
        .reshape(rows_here, heads, HEAD_DIM)
    )
    delta = jnp.sum(grad_mixed.astype(jnp.float32) * attn_heads, axis=-1)
    piece = (
        lax.all_gather(key_send, "seq", axis=0, tiled=True),
        lax.all_gather(value_send, "seq", axis=0, tiled=True),
    )
    keys = piece[0].reshape(-1, heads, HEAD_DIM)
    values = piece[1].reshape(-1, heads, HEAD_DIM)
    count = keys.shape[0]
    allowed = allowed_mask(positions, doc_here, doc_all, count)[None]
    scores = (
        jnp.einsum("qhd,khd->hqk", query_heads, keys, preferred_element_type=jnp.float32) * factor
    )
    weights = jnp.where(allowed, jnp.exp(scores - log_total[..., None]), 0.0)
    value_term = jnp.einsum(
        "hqk,qhd->khd", weights.astype(jnp.bfloat16), grad_mixed, preferred_element_type=jnp.float32
    )
    grad_weights = jnp.einsum(
        "qhd,khd->hqk", grad_mixed, values, preferred_element_type=jnp.float32
    )
    grad_scores = (weights * (grad_weights - delta.T[:, :, None])).astype(jnp.bfloat16)
    grad_query = (
        jnp.einsum("hqk,khd->qhd", grad_scores, keys, preferred_element_type=jnp.float32) * factor
    )
    key_term = (
        jnp.einsum("hqk,qhd->khd", grad_scores, query_heads, preferred_element_type=jnp.float32)
        * factor
    )
    key_sums = key_term.reshape(count, width)
    value_sums = value_term.reshape(count, width)
    grad_query_rot, key_sums, value_sums = (grad_query, key_sums, value_sums)
    grad_key_rot, grad_values = (
        lax.psum_scatter(
            key_sums.astype(jnp.bfloat16), "seq", scatter_dimension=0, tiled=True
        ).astype(jnp.float32),
        lax.psum_scatter(
            value_sums.astype(jnp.bfloat16), "seq", scatter_dimension=0, tiled=True
        ).astype(jnp.float32),
    )
    grad_query_normed = unrotate(grad_query_rot, cosine, sine).reshape(rows_here, width)
    grad_key_normed = unrotate(
        grad_key_rot.reshape(rows_here, heads, HEAD_DIM), cosine, sine
    ).reshape(rows_here, width)
    grad_query_proj, query_gain_term = norm_back(
        grad_query_normed, query_unit, query_scale, query_norm_gain
    )
    grad_key_proj, key_gain_term = norm_back(grad_key_normed, key_unit, key_scale, key_norm_gain)
    query_low = grad_query_proj.astype(jnp.bfloat16)
    key_low = grad_key_proj.astype(jnp.bfloat16)
    value_low = grad_values.astype(jnp.bfloat16)
    query_term = jnp.einsum("td,te->de", normed, query_low, preferred_element_type=jnp.float32)
    key_weight_term = jnp.einsum("td,te->de", normed, key_low, preferred_element_type=jnp.float32)
    value_term = jnp.einsum("td,te->de", normed, value_low, preferred_element_type=jnp.float32)
    grad_normed = (
        jnp.einsum("te,de->td", query_low, query_back, preferred_element_type=jnp.float32)
        + jnp.einsum("te,de->td", key_low, key_back, preferred_element_type=jnp.float32)
        + jnp.einsum("te,de->td", value_low, value_back, preferred_element_type=jnp.float32)
    )
    grad_input_norm, attn_gain_term = norm_back(grad_normed, attn_unit, attn_scale, attn_norm_gain)
    grad_input = grad_residual + grad_input_norm
    weight_sums = (
        lax.psum_scatter(query_term, ("seq", "batch"), scatter_dimension=0, tiled=True),
        lax.psum_scatter(key_weight_term, ("seq", "batch"), scatter_dimension=0, tiled=True),
        lax.psum_scatter(value_term, ("seq", "batch"), scatter_dimension=0, tiled=True),
        lax.psum_scatter(out_term, ("seq", "batch"), scatter_dimension=0, tiled=True),
        lax.psum_scatter(router_term, ("seq", "batch"), scatter_dimension=0, tiled=True),
        lax.psum_scatter(attn_gain_term, ("seq", "batch"), scatter_dimension=0, tiled=True),
        lax.psum_scatter(query_gain_term, ("seq", "batch"), scatter_dimension=0, tiled=True),
        lax.psum_scatter(key_gain_term, ("seq", "batch"), scatter_dimension=0, tiled=True),
        lax.psum_scatter(ffn_gain_term, ("seq", "batch"), scatter_dimension=0, tiled=True),
    )
    expert_sums = (
        lax.psum_scatter(
            gate_term.astype(jnp.bfloat16), "batch", scatter_dimension=1, tiled=True
        ).astype(jnp.float32),
        lax.psum_scatter(
            up_term.astype(jnp.bfloat16), "batch", scatter_dimension=1, tiled=True
        ).astype(jnp.float32),
        lax.psum_scatter(
            down_term.astype(jnp.bfloat16), "batch", scatter_dimension=1, tiled=True
        ).astype(jnp.float32),
    )
    return (
        block_out[None],
        grad_input[None],
        weight_sums[0],
        weight_sums[1],
        weight_sums[2],
        weight_sums[3],
        weight_sums[4],
        weight_sums[5],
        weight_sums[6],
        weight_sums[7],
        weight_sums[8],
        expert_sums[0],
        expert_sums[1],
        expert_sums[2],
        counts_here[None],
    )


def solution(mesh):
    in_specs = (
        P("batch", "seq", None),
        P("batch", None),
        P("batch", "seq", None),
        P(("seq", "batch"), None),
        P(("seq", "batch"), None),
        P(("seq", "batch"), None),
        P(("seq", "batch"), None),
        P(("seq", "batch"), None),
        P(("seq", "batch")),
        P(("seq", "batch")),
        P(("seq", "batch")),
        P(("seq", "batch")),
        P("seq", None, None),
        P("seq", None, None),
        P("seq", None, None),
        P("batch", "seq", None),
    )
    out_specs = (
        P("batch", "seq", None),
        P("batch", "seq", None),
        P(("seq", "batch"), None),
        P(("seq", "batch"), None),
        P(("seq", "batch"), None),
        P(("seq", "batch"), None),
        P(("seq", "batch"), None),
        P(("seq", "batch")),
        P(("seq", "batch")),
        P(("seq", "batch")),
        P(("seq", "batch")),
        P("seq", "batch", None),
        P("seq", "batch", None),
        P("seq", "batch", None),
        P("batch", "seq"),
    )
    return jax.shard_map(
        on_device, mesh=mesh, in_specs=in_specs, out_specs=out_specs, check_vma=False
    )
```

profile of v0, /device:TPU:0, one launch (start us, length us, event | category | flops | bytes accessed | tf_op | source)
XLA Modules:
  0.0 3039.9 jit_solution(16456486810373972898)
XLA Ops:
  12.9 42.6 %all-reduce.9 = (bf16[2048]{0:T(1024)(128)(2,1)S(1)}, bf16[2048]{0:T(1024)(128)(2,1)S(1)}, bf16[2048]{0:T(1024)(128)(2,1)S(1)}, bf16[2048]{0:T(1024)(128)(2,1)S(1)}) all-reduce(bf16[2048]{0:T(1024)(128)(2,1)S(1)} %dynamic-update-slice, bf16[2048]{0:T(1024)(128)(2,1)S(1)} %dynamic-update-slice.2, ...), channel_id=1, replica_groups=mesh['seq'=8,'batch'=4] {'seq','batch'}, use_global_device_ids=true, to_apply=%add | all-reduce | flops 8192 | bytes 32768
  57.2 34.4 %all-gather.10.cloned.1.call-done = bf16[2048,2048]{1,0:T(8,128)(2,1)} async-done(((bf16[64,2048]{1,0:T(8,128)(2,1)}), bf16[2048,2048]{1,0:T(8,128)(2,1)}) %all-gather.10.cloned.1.call-update) | async-done | bytes 8388624 | tf_op jit(solution)/shard_map/all_gather | solution.py:84
  91.5 5.0 multiply_reduce_fusion.6
  97.8 72.7 %all-gather.8.cloned.1.call-done = bf16[2048,2048]{1,0:T(8,128)(2,1)} async-done(((bf16[64,2048]{1,0:T(8,128)(2,1)}), bf16[2048,2048]{1,0:T(8,128)(2,1)}) %all-gather.8.cloned.1.call-update) | async-done | bytes 8388624 | tf_op jit(solution)/shard_map/all_gather | solution.py:83
  170.5 4.8 multiply_reduce_fusion.7
  180.1 69.3 %all-gather.14.cloned.1.call-done = bf16[2048,2048]{1,0:T(8,128)(2,1)} async-done(((bf16[64,2048]{1,0:T(8,128)(2,1)}), bf16[2048,2048]{1,0:T(8,128)(2,1)}) %all-gather.14.cloned.1.call-update) | async-done | bytes 8388624 | tf_op jit(solution)/shard_map/all_gather | solution.py:85
  249.4 5.5 convolution_convert_fusion.1
  256.1 4.5 reduce-window.6
  261.9 26.0 all-gather.12.cloned.1.call-done
  287.9 4.6 select_reduce_fusion
  298.8 28.1 all-gather.16.cloned.1.call-done
  326.9 8.7 fusion.138
  335.6 71.5 %all-gather.18.cloned.1.call-done = bf16[2048,2048]{1,0:T(8,128)(2,1)} async-done(((bf16[64,2048]{1,0:T(8,128)(2,1)}), bf16[2048,2048]{1,0:T(8,128)(2,1)}) %all-gather.18.cloned.1.call-update) | async-done | bytes 8388624 | tf_op jit(solution)/shard_map/all_gather | solution.py:86
  407.1 4.7 multiply_reduce_fusion.5
  412.1 10.4 scatter_custom_fusion
  422.5 75.2 %all_to_all.30 = bf16[8,2,96,2048]{3,2,1,0:T(8,128)(2,1)S(1)} all-to-all(bf16[8,2,96,2048]{3,2,1,0:T(8,128)(2,1)} %bitcast.284), channel_id=1, replica_groups=mesh['seq'=8,'batch'=4] {'seq'}, dimensions={0} | all-to-all | bytes 12582912 | tf_op jit(solution)/shard_map/all_to_all | solution.py:170
  497.7 13.1 fusion.6
  510.8 13.8 fusion.20
  524.6 8.8 convert_bitcast_fusion
  536.7 4.9 all-to-all-start.1
  541.6 70.2 %all-gather = bf16[32,64,16]{1,2,0:T(8,128)(2,1)S(1)} all-gather(bf16[1,64,16]{1,2,0:T(8,128)(2,1)S(1)} %bitcast.310), channel_id=1, replica_groups=mesh['seq'=8,'batch'=4] {'seq','batch'}, dimensions={0}, use_global_device_ids=true | all-gather | bytes 67584 | tf_op jit(solution)/shard_map/all_gather | solution.py:87
  613.8 12.8 gather_fusion
  626.6 4.9 fusion.44
  631.8 10.7 scatter_custom_fusion.1
  642.5 77.1 %all_to_all.31 = bf16[8,2,96,2048]{3,2,1,0:T(8,128)(2,1)} all-to-all(bf16[8,2,96,2048]{3,2,1,0:T(8,128)(2,1)} %bitcast.283), channel_id=1, replica_groups=mesh['seq'=8,'batch'=4] {'seq'}, dimensions={0} | all-to-all | bytes 12582912 | tf_op jit(solution)/shard_map/all_to_all | solution.py:203
  719.5 16.4 fusion.17
  735.9 13.4 fusion
  749.3 14.2 fusion.14
  763.6 6.6 copy.127
  770.1 4.8 all-to-all-start.3
  775.4 4.4 fusion.46
  779.8 66.7 %all-to-all-done.3 = bf16[8,2,96,2048]{3,2,1,0:T(8,128)(2,1)} async-done(((bf16[8,2,96,2048]{3,2,1,0:T(8,128)(2,1)}), bf16[8,2,96,2048]{3,2,1,0:T(8,128)(2,1)}, u32[]{:S(2)}, u32[]{:S(2)}) %all-to-all-start.3) | async-done | bytes 6291488 | tf_op jit(solution)/shard_map/all_to_all | solution.py:230
  846.5 12.4 gather_fusion.1
  858.9 5.1 convert_reduce_fusion
  866.8 6.3 convolution_convert_fusion
  873.4 7.7 fusion.69
  881.1 6.6 copy.160
  888.4 7.1 multiply_convert_fusion.1
  900.9 6.4 copy.158
  908.8 12.2 bitcast_convert_fusion
  921.1 11.9 bitcast_convert_fusion.2
  933.2 11.8 bitcast_convert_fusion.1
  946.1 9.4 fusion.107
  956.6 9.7 fusion.124
  966.6 5.7 fusion.77
  972.3 20.3 reduce-scatter.31.cloned.1.call-done
  998.6 3.9 multiply_add_fusion
  1004.3 8.2 fusion.126
  1017.8 8.2 fusion.128
  1030.9 4.5 all-to-all-done.4
  1035.9 94.3 %reduce-scatter.35.cloned.1.call-done = f32[64,16]{1,0:T(8,128)} async-done(((f32[2048,16]{1,0:T(8,128)}), f32[64,16]{1,0:T(8,128)}) %reduce-scatter.35.cloned.1.call-update) | async-done | bytes 4112
  1131.6 6.4 fusion.140
  1138.0 6.4 convolution_add_fusion.2
  1147.6 41.6 %all-reduce.8 = (f32[2048]{0:T(1024)S(1)}, f32[2048]{0:T(1024)S(1)}, f32[2048]{0:T(1024)S(1)}, f32[2048]{0:T(1024)S(1)}) all-reduce(f32[2048]{0:T(1024)S(1)} %get-tuple-element.21, f32[2048]{0:T(1024)S(1)} %get-tuple-element.19, f32[2048]{0:T(1024)S(1)} %get-tuple-element.17, ...), channel_id=9, replica_groups=mesh['seq'=8,'batch'=4] {'seq','batch'}, use_global_device_ids=true, to_apply=%region_29.30.clone | all-reduce | flops 8192 | bytes 65536
  1192.9 81.9 %reduce-scatter.29.cloned.1.call-done = bf16[2,256,2048]{2,1,0:T(8,128)(2,1)} async-done(((bf16[2,1024,2048]{2,1,0:T(8,128)(2,1)}), bf16[2,256,2048]{2,1,0:T(8,128)(2,1)}) %reduce-scatter.29.cloned.1.call-update) | async-done | bytes 2097168 | tf_op jit(solution)/shard_map/reduce_scatter | solution.py:330
  1274.8 4.1 convert_element_type.215
  1278.9 143.6 %reduce-scatter.25.cloned.1.call-done = bf16[2,512,1024]{2,1,0:T(8,128)(2,1)} async-done(((bf16[2,2048,1024]{2,1,0:T(8,128)(2,1)}), bf16[2,512,1024]{2,1,0:T(8,128)(2,1)}) %reduce-scatter.25.cloned.1.call-update) | async-done | bytes 2097168 | tf_op jit(solution)/shard_map/reduce_scatter | solution.py:324
  1422.5 4.1 convert_element_type.211
  1426.6 143.5 %reduce-scatter.27.cloned.1.call-done = bf16[2,512,1024]{2,1,0:T(8,128)(2,1)} async-done(((bf16[2,2048,1024]{2,1,0:T(8,128)(2,1)}), bf16[2,512,1024]{2,1,0:T(8,128)(2,1)}) %reduce-scatter.27.cloned.1.call-update) | async-done | bytes 2097168 | tf_op jit(solution)/shard_map/reduce_scatter | solution.py:327
  1570.1 4.1 convert_element_type.213
  1574.2 363.9 %reduce-scatter.23.cloned.1.call-done = f32[64,2048]{1,0:T(8,128)} async-done(((f32[2048,2048]{1,0:T(8,128)}), f32[64,2048]{1,0:T(8,128)}) %reduce-scatter.23.cloned.1.call-update) | async-done | bytes 524304 | tf_op jit(solution)/shard_map/reduce_scatter | solution.py:316
  1938.0 365.0 %reduce-scatter.21.cloned.1.call-done = f32[64,2048]{1,0:T(8,128)} async-done(((f32[2048,2048]{1,0:T(8,128)}), f32[64,2048]{1,0:T(8,128)}) %reduce-scatter.21.cloned.1.call-update) | async-done | bytes 524304 | tf_op jit(solution)/shard_map/reduce_scatter | solution.py:315
  2303.1 365.0 %reduce-scatter.19.cloned.1.call-done = f32[64,2048]{1,0:T(8,128)} async-done(((f32[2048,2048]{1,0:T(8,128)}), f32[64,2048]{1,0:T(8,128)}) %reduce-scatter.19.cloned.1.call-update) | async-done | bytes 524304 | tf_op jit(solution)/shard_map/reduce_scatter | solution.py:314
  2668.1 365.0 %reduce-scatter.17.cloned.1.call-done = f32[64,2048]{1,0:T(8,128)} async-done(((f32[2048,2048]{1,0:T(8,128)}), f32[64,2048]{1,0:T(8,128)}) %reduce-scatter.17.cloned.1.call-update) | async-done | bytes 524304 | tf_op jit(solution)/shard_map/reduce_scatter | solution.py:313
  (227 shorter events, 67.8 us)
Async XLA Ops:
  7.2 84.4 %all-gather.10.cloned.1.call-start = ((), (), s32[]{:S(2)}) async-start(), calls=%async_computation.16 | async-start | bytes 8650752 | tf_op jit(solution)/shard_map/all_gather | solution.py:84
  7.9 162.6 %all-gather.8.cloned.1.call-start = ((), (), s32[]{:S(2)}) async-start(), calls=%async_computation.15 | async-start | bytes 8650752 | tf_op jit(solution)/shard_map/all_gather | solution.py:83
  8.7 240.8 %all-gather.14.cloned.1.call-start = ((), (), s32[]{:S(2)}) async-start(), calls=%async_computation.18 | async-start | bytes 8650752 | tf_op jit(solution)/shard_map/all_gather | solution.py:85
  9.4 278.5 %all-gather.12.cloned.1.call-start = ((), (), s32[]{:S(2)}) async-start(), calls=%async_computation.17 | async-start | bytes 4718592 | tf_op jit(solution)/shard_map/all_gather | solution.py:124
  55.5 193.9 %copy-start.18 = (f32[2048]{0:T(1024)}, f32[2048]{0:T(1024)S(1)}, u32[]{:S(2)}) copy-start(f32[2048]{0:T(1024)S(1)} %convert_element_type.169) | copy-start | bytes 24580
  55.5 41.0 %copy-start.31 = (f32[2048]{0:T(1024)}, f32[2048]{0:T(1024)S(1)}, u32[]{:S(2)}) copy-start(f32[2048]{0:T(1024)S(1)} %convert_element_type.173) | copy-start | bytes 24580
  55.5 119.8 %copy-start.29 = (f32[2048]{0:T(1024)}, f32[2048]{0:T(1024)S(1)}, u32[]{:S(2)}) copy-start(f32[2048]{0:T(1024)S(1)} %convert_element_type.171) | copy-start | bytes 24580
  56.8 192.6 %copy-start.33 = (f32[128]{0:T(128)}, f32[128]{0:T(128)S(1)}, u32[]{:S(2)}) copy-start(f32[128]{0:T(128)S(1)} %add_rsqrt_fusion.3) | copy-start | bytes 1540
  57.1 120.2 %copy-start.25 = (f32[128,64]{1,0:T(8,128)}, f32[128,64]{1,0:T(8,128)S(1)}, u32[]{:S(2)}) copy-start(f32[128,64]{1,0:T(8,128)S(1)} %get-tuple-element.59) | copy-start | bytes 98308
  57.1 120.2 %copy-start.27 = (f32[128,64]{1,0:T(8,128)}, f32[128,64]{1,0:T(8,128)S(1)}, u32[]{:S(2)}) copy-start(f32[128,64]{1,0:T(8,128)S(1)} %get-tuple-element.60) | copy-start | bytes 98308
  57.1 113.3 %copy-start = (bf16[1,128,2048]{2,1,0:T(8,128)(2,1)S(1)}, bf16[1,128,2048]{2,1,0:T(8,128)(2,1)}, u32[]{:S(2)}) copy-start(bf16[1,128,2048]{2,1,0:T(8,128)(2,1)} %param.16) | copy-start | bytes 1572868
  96.5 78.7 %copy-start.40 = (f32[128]{0:T(128)}, f32[128]{0:T(128)S(1)}, u32[]{:S(2)}) copy-start(f32[128]{0:T(128)S(1)} %add_rsqrt_fusion.1) | copy-start | bytes 1540
  175.3 2.0 copy-start.38
  178.7 109.2 %copy-start.9 = (bf16[128,16,64]{2,0,1:T(8,128)(2,1)}, bf16[128,16,64]{2,0,1:T(8,128)(2,1)S(1)}, u32[]{:S(2)}) copy-start(bf16[128,16,64]{2,0,1:T(8,128)(2,1)S(1)} %get-tuple-element.39) | copy-start | bytes 786436
  178.7 109.2 %copy-start.11 = (bf16[128,16,64]{2,0,1:T(8,128)(2,1)}, bf16[128,16,64]{2,0,1:T(8,128)(2,1)S(1)}, u32[]{:S(2)}) copy-start(bf16[128,16,64]{2,0,1:T(8,128)(2,1)S(1)} %get-tuple-element.40) | copy-start | bytes 786436
  180.0 75.5 %copy-start.35 = (s32[1,128,8]{1,2,0:T(8,128)S(1)}, s32[1,128,8]{1,2,0:T(8,128)}, u32[]{:S(2)}) copy-start(s32[1,128,8]{1,2,0:T(8,128)} %param.18) | copy-start | bytes 12292
  180.1 80.8 %copy-start.42 = (s32[1,1024]{1,0:T(1,128)S(1)}, s32[1,1024]{1,0:T(1,128)}, u32[]{:S(2)}) copy-start(s32[1,1024]{1,0:T(1,128)} %param.17) | copy-start | bytes 12292
  180.1 146.8 %all-gather.16.cloned.1.call-start = ((), (), s32[]{:S(2)}) async-start(), calls=%async_computation.19 | async-start | bytes 4718592 | tf_op jit(solution)/shard_map/all_gather | solution.py:125
  254.9 152.2 %all-gather.18.cloned.1.call-start = ((), (), s32[]{:S(2)}) async-start(), calls=%async_computation.20 | async-start | bytes 8650752 | tf_op jit(solution)/shard_map/all_gather | solution.py:86
  261.9 65.1 %copy-start.20 = (pred[128,1024]{1,0:T(8,128)(4,1)}, pred[128,1024]{1,0:T(8,128)(4,1)S(1)}, u32[]{:S(2)}) copy-start(pred[128,1024]{1,0:T(8,128)(4,1)S(1)} %fusion.106) | copy-start | bytes 393220
  292.4 3.2 copy-start.2
  335.6 76.3 %copy-start.15 = (bf16[128,16,128]{0,2,1:T(8,128)(2,1)}, bf16[128,16,128]{0,2,1:T(8,128)(2,1)S(1)}, u32[]{:S(2)}) copy-start(bf16[128,16,128]{0,2,1:T(8,128)(2,1)S(1)} %get-tuple-element.67) | copy-start | bytes 1572868
  497.7 13.1 copy-start.8
  497.7 26.8 slice-start.2
  510.8 13.8 slice-start.3
  536.7 4.9 copy-start.43
  536.7 75.4 %copy-start.22 = (bf16[1,128,2048]{2,1,0:T(8,128)(2,1)S(1)}, bf16[1,128,2048]{2,1,0:T(8,128)(2,1)}, u32[]{:S(2)}) copy-start(bf16[1,128,2048]{2,1,0:T(8,128)(2,1)} %param.31) | copy-start | bytes 1572868
  536.7 77.1 %all-to-all-start.1 = ((bf16[8,2,96,2048]{3,2,1,0:T(8,128)(2,1)}), bf16[8,2,96,2048]{3,2,1,0:T(8,128)(2,1)}, u32[]{:S(2)}, u32[]{:S(2)}) async-start(bf16[8,2,96,2048]{3,2,1,0:T(8,128)(2,1)} %copy.124), calls=%async_computation.1 | async-start | bytes 12582912 | tf_op jit(solution)/shard_map/all_to_all | solution.py:180
  770.1 76.4 %all-to-all-start.3 = ((bf16[8,2,96,2048]{3,2,1,0:T(8,128)(2,1)}), bf16[8,2,96,2048]{3,2,1,0:T(8,128)(2,1)}, u32[]{:S(2)}, u32[]{:S(2)}) async-start(bf16[8,2,96,2048]{3,2,1,0:T(8,128)(2,1)} %copy.127), calls=%async_computation.3 | async-start | bytes 12582912 | tf_op jit(solution)/shard_map/all_to_all | solution.py:230
  774.9 180.7 %reduce-scatter.33.cloned.1.call-start = ((), (), s32[]{:S(2)}) async-start(), calls=%async_computation.29 | async-start | bytes 4718592
  858.9 6.2 copy-start.17
  866.8 6.6 copy-start.21
  866.8 6.6 copy-start.37
  881.1 7.1 copy-start.24
  887.7 104.8 %reduce-scatter.31.cloned.1.call-start = ((), (), s32[]{:S(2)}) async-start(), calls=%async_computation.28 | async-start | bytes 4718592
  888.3 9.1 copy-start.10
  888.4 9.1 copy-start.12
  895.4 2.0 copy-start.3
  907.3 222.8 %reduce-scatter.35.cloned.1.call-start = ((), (), s32[]{:S(2)}) async-start(), calls=%async_computation.30 | async-start | bytes 1081344
  908.7 366.0 %reduce-scatter.29.cloned.1.call-start = ((), (), s32[]{:S(2)}) async-start(), calls=%async_computation.27 | async-start | bytes 10485760 | tf_op jit(solution)/shard_map/reduce_scatter | solution.py:330
  921.0 501.5 %reduce-scatter.25.cloned.1.call-start = ((), (), s32[]{:S(2)}) async-start(), calls=%async_computation.25 | async-start | bytes 10485760 | tf_op jit(solution)/shard_map/reduce_scatter | solution.py:324
  933.0 637.1 %reduce-scatter.27.cloned.1.call-start = ((), (), s32[]{:S(2)}) async-start(), calls=%async_computation.26 | async-start | bytes 10485760 | tf_op jit(solution)/shard_map/reduce_scatter | solution.py:327
  945.0 1.0 copy-start.16
  945.1 993.0 %reduce-scatter.23.cloned.1.call-start = ((), (), s32[]{:S(2)}) async-start(), calls=%async_computation.24 | async-start | bytes 17301504 | tf_op jit(solution)/shard_map/reduce_scatter | solution.py:316
  955.5 1.1 copy-start.1
  955.5 1.1 copy-start.19
  955.5 1.1 copy-start.34
  955.5 1347.5 %reduce-scatter.21.cloned.1.call-start = ((), (), s32[]{:S(2)}) async-start(), calls=%async_computation.23 | async-start | bytes 17301504 | tf_op jit(solution)/shard_map/reduce_scatter | solution.py:315
  966.3 32.3 %copy-start.26 = (f32[128,64]{1,0:T(8,128)S(1)}, f32[128,64]{1,0:T(8,128)}, u32[]{:S(2)}) copy-start(f32[128,64]{1,0:T(8,128)} %copy-done.25) | copy-start | bytes 98308
  966.3 32.3 %copy-start.28 = (f32[128,64]{1,0:T(8,128)S(1)}, f32[128,64]{1,0:T(8,128)}, u32[]{:S(2)}) copy-start(f32[128,64]{1,0:T(8,128)} %copy-done.27) | copy-start | bytes 98308
  966.3 1701.7 %reduce-scatter.19.cloned.1.call-start = ((), (), s32[]{:S(2)}) async-start(), calls=%async_computation.22 | async-start | bytes 17301504 | tf_op jit(solution)/shard_map/reduce_scatter | solution.py:314
  994.8 7.7 copy-start.7
  994.8 7.7 copy-start.32
  994.8 7.7 copy-start.41
  1012.5 1.2 copy-start.5
  1012.5 1.2 copy-start.30
  1012.5 1.2 copy-start.39
  1012.5 2020.6 %reduce-scatter.17.cloned.1.call-start = ((), (), s32[]{:S(2)}) async-start(), calls=%async_computation.21 | async-start | bytes 17301504 | tf_op jit(solution)/shard_map/reduce_scatter | solution.py:313
  1026.0 112.0 %copy-start.14 = (bf16[128,2048]{1,0:T(8,128)(2,1)S(1)}, bf16[128,2048]{1,0:T(8,128)(2,1)}, u32[]{:S(2)}) copy-start(bf16[128,2048]{1,0:T(8,128)(2,1)} %copy-done.13) | copy-start | bytes 1572868
  1027.3 8.1 all-to-all-start.4
  1131.6 12.9 slice-start
  1138.0 6.5 slice-start.1
  1138.0 6.5 copy-start.23
  1144.5 3.1 copy-start.36
  (4 other events, 3.4 us)
Sparse Core Ops, SparseCore 0:
  10.9 80.5 all-gather.9
  94.5 75.9 all-gather.7
  173.4 75.9 all-gather.13
  251.7 36.0 all-gather.11
  290.2 36.7 all-gather.15
  329.7 77.3 all-gather.17
  887.9 48.9 reduce-scatter.32
  941.2 51.3 reduce-scatter.30
  994.8 135.2 reduce-scatter.34
  1132.5 142.2 reduce-scatter.28
  1277.2 145.2 reduce-scatter.24
  1424.9 145.1 reduce-scatter.26
  1573.1 364.9 reduce-scatter.22
  1940.9 362.1 reduce-scatter.20
  2305.9 362.1 reduce-scatter.18
  2670.9 362.1 reduce-scatter.16
where the time goes:
time: 3050 us; the launch traced here: 3040 us
  waiting for transfers between devices  2320 us (76%)
  blocking collectives  307 us (10%)
  matrix products  242 us (8%)
  local copies, waits for them, and re-layouts  87.7 us (3%)
  other arithmetic  53.3 us (2%)
    reduce_scatter x1, waiting for transfers between devices, on_device(): lax.psum_scatter(value_term, ('seq', 'batch'), scatter_dimension=0, tiled...  365 us
    reduce_scatter x1, waiting for transfers between devices, on_device(): lax.psum_scatter(key_weight_term, ('seq', 'batch'), scatter_dimension=0,...  365 us
    reduce_scatter x1, waiting for transfers between devices, on_device(): lax.psum_scatter(query_term, ('seq', 'batch'), scatter_dimension=0, tiled...  365 us
    reduce_scatter x1, waiting for transfers between devices, on_device(): lax.psum_scatter(out_term, ('seq', 'batch'), scatter_dimension=0, tiled=T...  364 us
    reduce_scatter x1, waiting for transfers between devices, on_device(): lax.psum_scatter(gate_term.astype(jnp.bfloat16), 'batch', scatter_dimensi...  144 us
    reduce_scatter x1, waiting for transfers between devices, on_device(): lax.psum_scatter(up_term.astype(jnp.bfloat16), 'batch', scatter_dimension...  143 us
    unnamed x19, waiting for transfers between devices  117 us
    unnamed x2, blocking collectives  84.2 us
  transfers between devices with their start and end apart: 19, of which 18 were waited for; matrix products, arithmetic and copies ran while one was open for 6% of the time, Pallas kernels for 0%

commit v1 on v0

v1 whole, which is shorter than its diff:
```python
import functools
import math

import jax
import jax.numpy as jnp
from jax import lax
from jax.experimental import pallas as pl
from jax.experimental.pallas import tpu as pltpu
from jax.sharding import PartitionSpec as P

HEAD_DIM = 128
EPSILON = 1e-05
ROTARY_BASE = 10000.0
MASKED = -1e30
BF16 = jnp.bfloat16
F32 = jnp.float32
VMEM_BYTES = 60 * 1024 * 1024


def dot(left, right):
    return lax.dot_general(left, right, (((1,), (0,)), ((), ())), preferred_element_type=F32)


def dot_nt(left, right):
    return lax.dot_general(left, right, (((1,), (1,)), ((), ())), preferred_element_type=F32)


def dot_tn(left, right):
    return lax.dot_general(left, right, (((0,), (0,)), ((), ())), preferred_element_type=F32)


def norm_scale(values):
    return lax.rsqrt(jnp.mean(values * values, axis=-1, keepdims=True) + EPSILON)


def hop(values, axis, mask):
    size = lax.axis_size(axis)
    return lax.ppermute(values, axis, [(i, i ^ mask) for i in range(size)])


def masks_of(size):
    return [2 * m for m in range(size // 2)] + [2 * m + 1 for m in range(size // 2)]


def gather_seq(values):
    size = lax.axis_size("seq")
    near = [values] + [hop(values, "seq", 2 * m) for m in range(1, size // 2)]
    return near + [hop(piece, "seq", 1) for piece in near]


def scatter_seq(parts):
    chips = parts.shape[0] // 2
    both = parts[:chips].astype(F32) + hop(parts[chips:], "seq", 1).astype(F32)
    low = both.astype(BF16)
    total = both[0]
    for m in range(1, chips):
        total = total + hop(low[m], "seq", 2 * m).astype(F32)
    return total


def sum_seq(values, rows):
    size = lax.axis_size("seq")
    masks = masks_of(size)
    place = {mask: r for r, mask in enumerate(masks)}
    total = values
    for mask in range(1, size):
        moved = hop(values, "seq", mask)
        order = [place[masks[r] ^ mask] for r in range(size)]
        total = total + jnp.concatenate([moved[:, o * rows : (o + 1) * rows] for o in order], axis=1)
    return total


def gather_batch(values):
    pieces = [values]
    for t in range(1, lax.axis_size("batch")):
        pieces.append(hop(pieces[t - 1], "batch", 1) if t % 2 and t > 1 else hop(values, "batch", t))
    return pieces


def take_block(values, index):
    return lax.dynamic_index_in_dim(values, index, 0, keepdims=False)


def scatter_batch(blocks, me):
    size = blocks.shape[0]
    if size == 1:
        return blocks[0].astype(F32)
    theirs = jnp.stack([take_block(blocks, me ^ t ^ 1) for t in range(0, size, 2)])
    mine = jnp.stack([take_block(blocks, me ^ t) for t in range(0, size, 2)])
    pair = mine.astype(F32) + hop(theirs, "batch", 1).astype(F32)
    low = pair.astype(BF16)
    total = pair[0]
    for i in range(1, size // 2):
        total = total + hop(low[i], "batch", 2 * i).astype(F32)
    return total


def reorder_kernel(at_ref, *refs):
    *pieces, out_ref, sems = refs
    size = out_ref.shape[0]
    masks = masks_of(size)
    copies = []
    for t, piece in enumerate(pieces):
        for r, mask in enumerate(masks):
            copies.append(
                pltpu.make_async_copy(
                    piece.at[r], out_ref.at[at_ref[0] ^ mask, at_ref[1] ^ t], sems.at[t, r]
                )
            )
    for copy in copies:
        copy.start()
    for copy in copies:
        copy.wait()


def reorder(pieces, here):
    size, rows, columns = pieces[0].shape
    return pl.pallas_call(
        reorder_kernel,
        in_specs=[pl.BlockSpec(memory_space=pltpu.SMEM)]
        + [pl.BlockSpec(memory_space=pl.ANY)] * len(pieces),
        out_specs=pl.BlockSpec(memory_space=pl.ANY),
        out_shape=jax.ShapeDtypeStruct((size, len(pieces), rows, columns), pieces[0].dtype),
        scratch_shapes=[pltpu.SemaphoreType.DMA((len(pieces), size))],
        cost_estimate=pl.CostEstimate(
            flops=0, bytes_accessed=4 * size * len(pieces) * rows * columns, transcendentals=0
        ),
    )(here, *pieces)


def load_heads(place, refs, tables, blocks, rows, queries, keys, values):
    q_ref, k_ref, v_ref, scale_ref, gain_ref = refs
    cos_ref, sin_ref = tables
    for a in range(blocks):
        at = pl.ds(pl.multiple_of(place[a] * rows, rows), rows)
        to = slice(a * rows, (a + 1) * rows)
        cosine, sine = cos_ref[to, :], sin_ref[to, :]
        for i, (source, target) in enumerate(((q_ref, queries), (k_ref, keys))):
            normed = source[at, :] * scale_ref[at, i : i + 1] * gain_ref[i : i + 1, :]
            turned = pltpu.roll(normed, HEAD_DIM // 2, 1)
            target[to, :] = (normed * cosine + turned * sine).astype(BF16)
        values[to, :] = v_ref[at, :].astype(BF16)


def raised_scores(queries, keys, row_ref, col_ref, start, size, factor):
    stop = start + size
    scores = dot_nt(queries[start:stop, :], keys[:stop, :]) * factor
    query_at = lax.broadcasted_iota(jnp.int32, (size, stop), 0) + start
    key_at = lax.broadcasted_iota(jnp.int32, (size, stop), 1)
    allowed = (key_at <= query_at) & (row_ref[start:stop, :] == col_ref[:, :stop])
    scores = jnp.where(allowed, scores, MASKED)
    raised = jnp.exp(scores - jnp.max(scores, axis=-1, keepdims=True))
    return raised, jnp.sum(raised, axis=-1, keepdims=True)


def attend_kernel(
    blocks, size, place, q_ref, k_ref, v_ref, scale_ref, gain_ref, cos_ref, sin_ref, row_ref, col_ref,
    out_ref, queries, keys, values,
):
    total = q_ref.shape[0]
    rows = total // blocks
    refs, tables = (q_ref, k_ref, v_ref, scale_ref, gain_ref), (cos_ref, sin_ref)
    load_heads(place, refs, tables, blocks, rows, queries, keys, values)
    factor = 1.0 / math.sqrt(HEAD_DIM)
    for start in range(0, total, size):
        raised, sums = raised_scores(queries, keys, row_ref, col_ref, start, size, factor)
        mixed = dot(raised.astype(BF16), values[: start + size, :]) / sums
        for i in range(size // rows):
            at = pl.multiple_of(place[start // rows + i] * rows, rows)
            out_ref[pl.ds(at, rows), :] = mixed[i * rows : (i + 1) * rows].astype(BF16)


def attend_back_kernel(
    blocks, size, place, q_ref, k_ref, v_ref, scale_ref, gain_ref, cos_ref, sin_ref, row_ref, col_ref,
    grad_ref, gq_ref, gk_ref, gv_ref, inner_ref, gain_grad_ref, queries, keys, values, key_sum, value_sum,
):
    total = q_ref.shape[0]
    rows = total // blocks
    refs, tables = (q_ref, k_ref, v_ref, scale_ref, gain_ref), (cos_ref, sin_ref)
    load_heads(place, refs, tables, blocks, rows, queries, keys, values)
    factor = 1.0 / math.sqrt(HEAD_DIM)
    key_sum[...] = jnp.zeros_like(key_sum)
    value_sum[...] = jnp.zeros_like(value_sum)
    gain_rows = [jnp.zeros((1, HEAD_DIM), F32), jnp.zeros((1, HEAD_DIM), F32)]

    def finish(i, at, to, gradient, target):
        turned = pltpu.roll(gradient, HEAD_DIM // 2, 1)
        normed = gradient * cos_ref[to, :] - turned * sin_ref[to, :]
        unit = (q_ref, k_ref)[i][at, :] * scale_ref[at, i : i + 1]
        scaled = normed * gain_ref[i : i + 1, :]
        target[at, :] = scaled
        inner_ref[at, i : i + 1] += jnp.sum(scaled * unit, axis=-1, keepdims=True)
        gain_rows[i] += jnp.sum(normed * unit, axis=0, keepdims=True)

    @pl.when(pl.program_id(0) == 0)
    def _():
        inner_ref[...] = jnp.zeros_like(inner_ref)

    for start in range(0, total, size):
        stop = start + size
        raised, sums = raised_scores(queries, keys, row_ref, col_ref, start, size, factor)
        probs = raised * (1.0 / sums)
        pieces = []
        for i in range(size // rows):
            at = pl.multiple_of(place[start // rows + i] * rows, rows)
            pieces.append(grad_ref[pl.ds(at, rows), :])
        grad_mixed = jnp.concatenate(pieces, axis=0) if len(pieces) > 1 else pieces[0]
        grad_weights = dot_nt(grad_mixed, values[:stop, :])
        delta = jnp.sum(probs * grad_weights, axis=-1, keepdims=True)
        grad_scores = (probs * (grad_weights - delta)).astype(BF16)
        grad_queries = dot(grad_scores, keys[:stop, :]) * factor
        key_sum[:stop, :] += dot_tn(grad_scores, queries[start:stop, :])
        value_sum[:stop, :] += dot_tn(probs.astype(BF16), grad_mixed)
        for i in range(size // rows):
            at = pl.ds(pl.multiple_of(place[start // rows + i] * rows, rows), rows)
            to = slice(start + i * rows, start + (i + 1) * rows)
            finish(0, at, to, grad_queries[i * rows : (i + 1) * rows], gq_ref)
    for a in range(blocks):
        at = pl.ds(pl.multiple_of(place[a] * rows, rows), rows)
        to = slice(a * rows, (a + 1) * rows)
        finish(1, at, to, key_sum[to, :] * factor, gk_ref)
        gv_ref[at, :] = value_sum[to, :].astype(BF16)
    gain_grad_ref[0:1, :] = gain_rows[0]
    gain_grad_ref[1:2, :] = gain_rows[1]


def attention(place, qkv, scales, gains, tables, row_docs, col_docs, blocks, grad_mixed=None):
    total = qkv.shape[0]
    heads = qkv.shape[1] // (3 * HEAD_DIM)
    size = min(256, total)
    whole = lambda h: (0, 0)
    column = lambda h: (0, h)
    in_specs = [
        pl.BlockSpec(memory_space=pltpu.SMEM),
        pl.BlockSpec((total, HEAD_DIM), lambda h: (0, h)),
        pl.BlockSpec((total, HEAD_DIM), lambda h: (0, heads + h)),
        pl.BlockSpec((total, HEAD_DIM), lambda h: (0, 2 * heads + h)),
        pl.BlockSpec((total, 2), whole),
        pl.BlockSpec((2, HEAD_DIM), column),
        pl.BlockSpec((total, HEAD_DIM), whole),
        pl.BlockSpec((total, HEAD_DIM), whole),
        pl.BlockSpec((total, 1), whole),
        pl.BlockSpec((1, total), whole),
    ]
    operands = [place, qkv, qkv, qkv, scales, gains, *tables, row_docs, col_docs]
    held = [pltpu.VMEM((total, HEAD_DIM), BF16)] * 3
    params = pltpu.CompilerParams(vmem_limit_bytes=VMEM_BYTES)
    work = total * total * HEAD_DIM * heads
    if grad_mixed is None:
        return pl.pallas_call(
            functools.partial(attend_kernel, blocks, size),
            grid=(heads,),
            in_specs=in_specs,
            out_specs=pl.BlockSpec((total, HEAD_DIM), column),
            out_shape=jax.ShapeDtypeStruct((total, heads * HEAD_DIM), BF16),
            scratch_shapes=held,
            compiler_params=params,
            cost_estimate=pl.CostEstimate(
                flops=4 * work, bytes_accessed=qkv.size * 4, transcendentals=total * total
            ),
        )(*operands)
    return pl.pallas_call(
        functools.partial(attend_back_kernel, blocks, size),
        grid=(heads,),
        in_specs=in_specs + [pl.BlockSpec((total, HEAD_DIM), column)],
        out_specs=[pl.BlockSpec((total, HEAD_DIM), column)] * 3
        + [pl.BlockSpec((total, 2), whole), pl.BlockSpec((2, HEAD_DIM), column)],
        out_shape=[
            jax.ShapeDtypeStruct((total, heads * HEAD_DIM), F32),
            jax.ShapeDtypeStruct((total, heads * HEAD_DIM), F32),
            jax.ShapeDtypeStruct((total, heads * HEAD_DIM), BF16),
            jax.ShapeDtypeStruct((total, 2), F32),
            jax.ShapeDtypeStruct((2, heads * HEAD_DIM), F32),
        ],
        scratch_shapes=held + [pltpu.VMEM((total, HEAD_DIM), F32)] * 2,
        compiler_params=params,
        cost_estimate=pl.CostEstimate(
            flops=10 * work, bytes_accessed=qkv.size * 8, transcendentals=total * total
        ),
    )(*operands, grad_mixed)


def experts_kernel(
    experts, at_ref, x_ref, u_ref, gate_ref, wg_ref, wu_ref, wd_ref,
    out_ref, back_ref, hidden_ref, gate_grad_ref, up_grad_ref,
):
    owned = wg_ref.shape[0]
    rows, width = x_ref.shape
    inputs, upstream = x_ref[...], u_ref[...]
    extra = back_ref.shape[1] - width
    column = lax.broadcasted_iota(jnp.int32, (rows, extra), 1)
    sums = jnp.zeros((rows, extra), F32)
    for e in range(owned):
        gate_act = dot(inputs, wg_ref[e])
        up_act = dot(inputs, wu_ref[e])
        grad_raw = dot_nt(upstream, wd_ref[e])
        gate = gate_ref[:, e : e + 1]
        sigma = jax.nn.sigmoid(gate_act)
        active = gate_act * sigma
        hidden = active * up_act
        grad_gate = jnp.sum(hidden * grad_raw, axis=-1, keepdims=True)
        high = grad_gate.astype(BF16).astype(F32)
        expert = at_ref[0] * owned + e
        sums = jnp.where(column == expert, high, sums)
        sums = jnp.where(column == expert + experts, grad_gate - high, sums)
        grad_hidden = grad_raw * gate
        hidden_ref[e] = (hidden * gate).astype(BF16)
        gate_grad_ref[e] = (grad_hidden * up_act * sigma * (1.0 + gate_act * (1.0 - sigma))).astype(BF16)
        up_grad_ref[e] = (grad_hidden * active).astype(BF16)
    out = dot(hidden_ref[0], wd_ref[0])
    back = dot_nt(gate_grad_ref[0], wg_ref[0]) + dot_nt(up_grad_ref[0], wu_ref[0])
    for e in range(1, owned):
        out += dot(hidden_ref[e], wd_ref[e])
        back += dot_nt(gate_grad_ref[e], wg_ref[e]) + dot_nt(up_grad_ref[e], wu_ref[e])
    out_ref[...] = out.astype(BF16)
    back_ref[:, :width] = back.astype(BF16)
    back_ref[:, width:] = sums.astype(BF16)


def run_experts(at, inputs, upstream, gates, w_gate, w_up, w_down, experts, parts):
    total, width = inputs.shape
    owned, _, hidden = w_gate.shape
    piece = hidden // parts
    size = min(256, total)
    extra = 128 * -(-2 * experts // 128)
    token = lambda i, at: (i, 0)
    once = pl.Buffered(1)
    acts = jax.ShapeDtypeStruct((owned, total, piece), BF16)
    return pl.pallas_call(
        functools.partial(experts_kernel, experts),
        grid_spec=pltpu.PrefetchScalarGridSpec(
            num_scalar_prefetch=1,
            grid=(total // size,),
            in_specs=[
                pl.BlockSpec((size, width), token),
                pl.BlockSpec((size, width), token),
                pl.BlockSpec((size, owned), token),
                pl.BlockSpec((owned, width, piece), lambda i, at: (0, 0, at[1]), pipeline_mode=once),
                pl.BlockSpec((owned, width, piece), lambda i, at: (0, 0, at[1]), pipeline_mode=once),
                pl.BlockSpec((owned, piece, width), lambda i, at: (0, at[1], 0), pipeline_mode=once),
            ],
            out_specs=[
                pl.BlockSpec((size, width), token),
                pl.BlockSpec((size, width + extra), token),
            ]
            + [pl.BlockSpec((owned, size, piece), lambda i, at: (0, i, 0))] * 3,
        ),
        out_shape=[
            jax.ShapeDtypeStruct((total, width), BF16),
            jax.ShapeDtypeStruct((total, width + extra), BF16),
            acts,
            acts,
            acts,
        ],
        compiler_params=pltpu.CompilerParams(vmem_limit_bytes=VMEM_BYTES),
        cost_estimate=pl.CostEstimate(
            flops=12 * total * width * piece * owned,
            bytes_accessed=2 * (4 * total * width + 3 * owned * piece * (total + width)),
            transcendentals=total * piece * owned,
        ),
    )(at, inputs, upstream, gates, w_gate, w_up, w_down)


def on_device(
    tokens,
    segments,
    expert_ids,
    w_query,
    w_key,
    w_value,
    w_out,
    w_router,
    attn_gain,
    query_gain,
    key_gain,
    ffn_gain,
    w_gate,
    w_up,
    w_down,
    out_grad,
):
    seq_size, batch_size = lax.axis_size("seq"), lax.axis_size("batch")
    seq_at, batch_at = lax.axis_index("seq"), lax.axis_index("batch")
    parts = 2 if batch_size % 2 == 0 else 1
    half = batch_size // parts
    part_at = batch_at // half
    here = jnp.stack([seq_at, batch_at]).astype(jnp.int32)
    low_tokens = tokens[0]
    inputs = low_tokens.astype(F32)
    rows, width = inputs.shape
    total = rows * seq_size
    masks = masks_of(seq_size)
    order = seq_at ^ jnp.array(masks, jnp.int32)
    place = jnp.array([masks.index(m) for m in range(seq_size)], jnp.int32)[
        jnp.arange(seq_size, dtype=jnp.int32) ^ seq_at
    ]
    experts = w_router.shape[1]
    owned = w_gate.shape[0]
    wide = width // seq_size
    shard = w_query.shape[0]

    small = jnp.concatenate(
        [w_router] + [g[:, None] for g in (attn_gain, query_gain, key_gain, ffn_gain)], axis=1
    )
    small = jnp.stack([small] + [hop(small, "batch", t) for t in range(1, batch_size)])
    small = jnp.stack([small] + [hop(small, "seq", j) for j in range(1, seq_size)])
    small = small[
        (jnp.arange(seq_size) ^ seq_at)[:, None], (jnp.arange(batch_size) ^ batch_at)[None, :]
    ].reshape(width, experts + 4)
    router = small[:, :experts]
    gains = small[:, experts:].astype(F32).T
    attn_norm_gain, ffn_norm_gain = gains[0], gains[3]
    head_gains = lax.dynamic_slice_in_dim(gains[1:3], seq_at * wide, wide, 1)

    all_tokens = jnp.concatenate(gather_seq(low_tokens), axis=0)
    cut = jnp.concatenate(
        [w.reshape(shard, seq_size, wide).transpose(1, 0, 2) for w in (w_query, w_key, w_value)],
        axis=2,
    )
    moved = jnp.stack(
        [take_block(cut, seq_at)]
        + [hop(take_block(cut, seq_at ^ j), "seq", j) for j in masks[1:]]
    )
    w_heads = reorder(gather_batch(moved), here).reshape(width, 3 * wide)
    out_pieces = gather_batch(w_out)
    w_mix = jnp.stack(out_pieces)[jnp.arange(batch_size) ^ batch_at].reshape(wide, width)

    ids = expert_ids[0].T
    sets = [(out_grad[0], ids)]
    if parts == 2:
        sets.append((hop(out_grad[0], "batch", half), hop(ids, "batch", half)))
    upstreams = [jnp.concatenate(gather_seq(item[0]), axis=0) for item in sets]
    all_ids = [jnp.concatenate(gather_seq(item[1]), axis=1) for item in sets]
    mine = seq_at * owned + jnp.arange(owned, dtype=jnp.int32)
    selected = [jnp.any(item[:, :, None] == mine, axis=0) for item in all_ids]
    counts_here = jnp.sum(selected[0].astype(jnp.int32), axis=0)

    all_inputs = all_tokens.astype(F32)
    normed = (all_inputs * norm_scale(all_inputs) * attn_norm_gain).astype(BF16)
    qkv = dot(normed, w_heads)
    squares = jnp.stack(
        [jnp.sum(jnp.square(qkv[:, i * wide : (i + 1) * wide]), axis=1) for i in range(2)]
    )
    scales = lax.rsqrt(sum_seq(squares, rows) / width + EPSILON).T
    rates = jnp.power(
        ROTARY_BASE, -jnp.arange(HEAD_DIM // 2, dtype=F32) * (2.0 / HEAD_DIM)
    )
    angles = jnp.arange(total, dtype=F32)[:, None] * rates[None, :]
    cosine, sine = jnp.cos(angles), jnp.sin(angles)
    tables = (
        jnp.concatenate([cosine, cosine], axis=1),
        jnp.concatenate([-sine, sine], axis=1),
    )
    attend = functools.partial(
        attention,
        place,
        qkv,
        scales,
        head_gains,
        tables,
        segments[0][:, None],
        segments[0][None, :],
        seq_size,
    )
    mixed_low = attend()
    residual = inputs + scatter_seq(
        dot(mixed_low, w_mix).astype(BF16).reshape(seq_size, rows, width)
    )
    ffn_scale = norm_scale(residual)
    ffn_unit = residual * ffn_scale
    ffn_in = (ffn_unit * ffn_norm_gain).astype(BF16)

    shards = [ffn_in] + ([hop(ffn_in, "batch", half)] if parts == 2 else [])
    at = jnp.stack([seq_at, part_at]).astype(jnp.int32)
    results, all_ffn = [], []
    for values, upstream, chosen in zip(shards, upstreams, selected):
        gathered = jnp.concatenate(gather_seq(values), axis=0)
        chances_all = jax.nn.softmax(dot(gathered, router), axis=-1)
        gates = lax.dynamic_slice_in_dim(chances_all, seq_at * owned, owned, 1) * chosen
        all_ffn.append(gathered)
        results.append(
            run_experts(at, gathered, upstream, gates, w_gate, w_up, w_down, experts, parts)
        )
    back = scatter_seq(results[0][1].reshape(seq_size, rows, -1))
    if parts == 2:
        other = scatter_seq(results[1][1].reshape(seq_size, rows, -1))
        back = back + hop(other.astype(BF16), "batch", half).astype(F32)
    mix = scatter_seq(results[0][0].reshape(seq_size, rows, -1))
    if parts == 2:
        other = scatter_seq(results[1][0].reshape(seq_size, rows, -1))
        mix = mix + hop(other.astype(BF16), "batch", half).astype(F32)
    block_out = (residual + mix).astype(BF16)

    def over_tokens(equation, lefts, rights):
        terms = [
            jnp.einsum(equation, left, right, preferred_element_type=F32)
            for left, right in zip(lefts, rights)
        ]
        return sum(terms[1:], terms[0]).astype(BF16)

    down_term = over_tokens("etf,td->efd", [r[2] for r in results], upstreams)
    gate_term = over_tokens("td,etf->edf", all_ffn, [r[3] for r in results])
    up_term = over_tokens("td,etf->edf", all_ffn, [r[4] for r in results])

    def group_sum(blocks, lead):
        total = take_block(blocks, lead).astype(F32)
        for t in range(1, half):
            total = total + hop(take_block(blocks, lead ^ t), "batch", t).astype(F32)
        return total

    in_group = batch_at % half
    deep = down_term.shape[1] // half
    down_grad = group_sum(
        down_term.reshape(owned, half, deep, width).transpose(1, 0, 2, 3), in_group
    )

    def spread(term):
        deep = width // batch_size
        blocks = term.reshape(owned, parts, half, deep, -1).transpose(2, 1, 0, 3, 4)
        mine = group_sum(blocks, in_group)
        if parts == 1:
            return mine[0]
        keep = take_block(mine, part_at)
        other = hop(take_block(mine, 1 - part_at).astype(BF16), "batch", half).astype(F32)
        return jnp.where(
            part_at == 0,
            jnp.concatenate([keep, other], axis=-1),
            jnp.concatenate([other, keep], axis=-1),
        )

    gate_grad = spread(gate_term)
    up_grad = spread(up_term)

    grad_ffn_in = back[:, :width]
    choices = jnp.any(
        ids[:, :, None] == jnp.arange(experts, dtype=jnp.int32), axis=0
    )
    grad_chances = choices * (
        back[:, width : width + experts] + back[:, width + experts : width + 2 * experts]
    )
    chances = jax.nn.softmax(dot(ffn_in, router), axis=-1)
    grad_logits = (
        chances * (grad_chances - jnp.sum(chances * grad_chances, axis=-1, keepdims=True))
    ).astype(BF16)
    grad_ffn_in = grad_ffn_in + dot_nt(grad_logits, router)
    scaled = grad_ffn_in * ffn_norm_gain
    inner = jnp.mean(scaled * ffn_unit, axis=-1, keepdims=True)
    grad_residual = out_grad[0].astype(F32) + ffn_scale * (scaled - ffn_unit * inner)
    grad_attn = grad_residual.astype(BF16)

    router_term = jnp.concatenate(
        [dot_tn(ffn_in, grad_logits), jnp.sum(grad_ffn_in * ffn_unit, axis=0)[:, None]], axis=1
    ).reshape(seq_size, batch_size, shard, experts + 1)
    router_sum = take_block(router_term, seq_at)
    for j in range(1, seq_size):
        router_sum = router_sum + hop(take_block(router_term, seq_at ^ j), "seq", j)
    router_total = take_block(router_sum, batch_at)
    for t in range(1, batch_size):
        router_total = router_total + hop(take_block(router_sum, batch_at ^ t), "batch", t)
    router_grad, ffn_gain_grad = router_total[:, :experts], router_total[:, experts]

    all_grad = jnp.concatenate(gather_seq(grad_attn), axis=0)
    grad_mixed = dot_nt(all_grad, w_mix).astype(BF16)
    out_proj_grad = scatter_batch(
        dot_tn(mixed_low, all_grad).astype(BF16).reshape(batch_size, shard, width), batch_at
    )
    scaled_q, scaled_k, value_low, inner, gain_terms = attend(grad_mixed=grad_mixed)
    inner = sum_seq(inner.T, rows).T / width
    lows = []
    for i, item in enumerate((scaled_q, scaled_k)):
        scale = scales[:, i : i + 1]
        unit = qkv[:, i * wide : (i + 1) * wide] * scale
        lows.append((scale * (item - unit * inner[:, i : i + 1])).astype(BF16))
    low = jnp.concatenate(lows + [value_low], axis=1)
    grad_normed = scatter_seq(
        dot_nt(low, w_heads).astype(BF16).reshape(seq_size, rows, width)
    )
    heads_term = dot_tn(normed, low).astype(BF16)
    heads_term = heads_term.reshape(seq_size, batch_size, shard, 3 * wide).transpose(1, 0, 2, 3)
    heads_sum = scatter_batch(heads_term, batch_at).astype(BF16)
    pieces = [take_block(heads_sum, seq_at)] + [
        hop(take_block(heads_sum, seq_at ^ j), "seq", j) for j in masks[1:]
    ]
    heads_grad = jnp.stack(pieces)[place].astype(F32)
    query_grad, key_grad, value_grad = (
        heads_grad[:, :, i * wide : (i + 1) * wide].transpose(1, 0, 2).reshape(shard, width)
        for i in range(3)
    )
    gain_blocks = gain_terms.reshape(2, batch_size, shard).transpose(1, 0, 2)
    gain_sum = take_block(gain_blocks, batch_at)
    for t in range(1, batch_size):
        gain_sum = gain_sum + hop(take_block(gain_blocks, batch_at ^ t), "batch", t)

    attn_scale = norm_scale(inputs)
    attn_unit = inputs * attn_scale
    scaled = grad_normed * attn_norm_gain
    inner = jnp.mean(scaled * attn_unit, axis=-1, keepdims=True)
    grad_input = grad_residual + attn_scale * (scaled - attn_unit * inner)
    attn_gain_grad = (
        jnp.sum(
            query_grad * w_query.astype(F32)
            + key_grad * w_key.astype(F32)
            + value_grad * w_value.astype(F32),
            axis=1,
        )
        / attn_gain.astype(F32)
    )
    return (
        block_out[None],
        grad_input[None],
        query_grad,
        key_grad,
        value_grad,
        out_proj_grad,
        router_grad,
        attn_gain_grad,
        gain_sum[0],
        gain_sum[1],
        ffn_gain_grad,
        gate_grad,
        up_grad,
        down_grad,
        counts_here[None],
    )


def solution(mesh):
    in_specs = (
        P("batch", "seq", None),
        P("batch", None),
        P("batch", "seq", None),
        P(("seq", "batch"), None),
        P(("seq", "batch"), None),
        P(("seq", "batch"), None),
        P(("seq", "batch"), None),
        P(("seq", "batch"), None),
        P(("seq", "batch")),
        P(("seq", "batch")),
        P(("seq", "batch")),
        P(("seq", "batch")),
        P("seq", None, None),
        P("seq", None, None),
        P("seq", None, None),
        P("batch", "seq", None),
    )
    out_specs = (
        P("batch", "seq", None),
        P("batch", "seq", None),
        P(("seq", "batch"), None),
        P(("seq", "batch"), None),
        P(("seq", "batch"), None),
        P(("seq", "batch"), None),
        P(("seq", "batch"), None),
        P(("seq", "batch")),
        P(("seq", "batch")),
        P(("seq", "batch")),
        P(("seq", "batch")),
        P("seq", "batch", None),
        P("seq", "batch", None),
        P("seq", "batch", None),
        P("batch", "seq"),
    )
    return jax.shard_map(
        on_device, mesh=mesh, in_specs=in_specs, out_specs=out_specs, check_vma=False
    )
```

time: 3050 us -> 1290 us (0.42)
  waiting for transfers between devices: 2320 us -> 573 us
  blocking collectives: 307 us -> 0 us
  Pallas kernels: 0 us -> 199 us
  matrix products: 242 us -> 73.5 us
  local copies, waits for them, and re-layouts: 87.7 us -> 237 us
  starting transfers between devices: 15 us -> 123 us
    reduce_scatter x7 -> x0, waiting for transfers between devices: 1830 us -> none  [the longest x1 365 us: on_device(): lax.psum_scatter(value_term, ('seq', 'batch'), scatter_dimension=0, tiled...]
    ppermute x0 -> x151, waiting for transfers between devices: none -> 573 us  [hop(): return lax.ppermute(values, axis, [(i, i ^ mask) for i in range(size)])]
    all_gather x6 -> x0, waiting for transfers between devices: 302 us -> none  [the longest x1 72.7 us: on_device(): lax.all_gather(w_query, ('seq', 'batch'), axis=0, tiled=True)]
    pallas_call x0 -> x5, Pallas kernels: none -> 199 us  [the longest x1 97.3 us: reorder(): pl.pallas_call(reorder_kernel, in_specs=[pl.BlockSpec(memory_space=pltpu....]
    dot_general x31 -> x17, matrix products: 241 us -> 73.5 us  [the longest x6 45.1 us: over_tokens(): jnp.einsum(equation, left, right, preferred_element_type=F32)]
    all_to_all x2 -> x0, blocking collectives: 152 us -> none  [the longest x1 77.1 us: on_device(): lax.all_to_all(grad_outgoing, 'seq', split_axis=0, concat_axis=0, tiled=T...]
    ppermute x0 -> x151, starting transfers between devices: none -> 123 us  [hop(): return lax.ppermute(values, axis, [(i, i ^ mask) for i in range(size)])]
    unnamed x19 -> x0, waiting for transfers between devices: 117 us -> none
  transfers between devices with their start and end apart: 19 -> 151, of which waited for: 18 -> 71; matrix products, arithmetic and copies ran while one was open for 6% -> 28% of each run, Pallas kernels for 0% -> 16%
where the time goes in v1:
time: 1290 us; the launch traced here: 1280 us
  waiting for transfers between devices  573 us (44%)
  local copies, waits for them, and re-layouts  237 us (18%)
  Pallas kernels  199 us (15%)
  starting transfers between devices  123 us (10%)
  matrix products  73.5 us (6%)
  other arithmetic  67.9 us (5%)
    ppermute x151, waiting for transfers between devices, hop(): return lax.ppermute(values, axis, [(i, i ^ mask) for i in range(size)])  573 us
    ppermute x151, starting transfers between devices, hop(): return lax.ppermute(values, axis, [(i, i ^ mask) for i in range(size)])  123 us
    unnamed x341, local copies, waits for them, and re-layouts  99.4 us
    pallas_call x1, Pallas kernels, reorder(): pl.pallas_call(reorder_kernel, in_specs=[pl.BlockSpec(memory_space=pltpu....  97.3 us
    pallas_call x2, Pallas kernels, run_experts(): pl.pallas_call(functools.partial(experts_kernel, experts), grid_spec=pltp...  71.2 us
    slice x50, local copies, waits for them, and re-layouts, sum_seq(): moved[:, o * rows:(o + 1) * rows]  50.5 us
    dot_general x6, matrix products, over_tokens(): jnp.einsum(equation, left, right, preferred_element_type=F32)  45.1 us
  transfers between devices with their start and end apart: 151, of which 71 were waited for; matrix products, arithmetic and copies ran while one was open for 28% of the time, Pallas kernels for 16%

profile of v1, /device:TPU:0, one launch (start us, length us, event | category | flops | bytes accessed | tf_op | source)
XLA Modules:
  0.0 1276.0 jit_solution(15251554845384987141)
XLA Ops:
  0.7 4.1 collective-permute-start.82
  65.4 3.4 collective-permute-done.14
  73.6 4.1 collective-permute-done.16
  88.4 4.0 collective-permute-done.19
  94.4 4.1 collective-permute-done.21
  119.7 4.4 collective-permute-done.48
  127.1 7.8 collective-permute-done.49
  135.9 10.0 collective-permute-done
  153.0 29.4 %collective-permute-done.25.refs_2_ = bf16[8,64,768]{2,1,0:T(8,128)(2,1)S(1)} collective-permute-done((bf16[8,64,768]{2,1,0:T(8,128)(2,1)S(1)}, bf16[8,64,768]{2,1,0:T(8,128)(2,1)S(1)}, u32[]{:S(2)}, u32[]{:S(2)}) %collective-permute-start.25) | collective-permute-done | bytes 786464 | tf_op jit(solution)/shard_map/ppermute | solution.py:38
  188.8 15.7 %collective-permute-done.26.refs_3_ = bf16[8,64,768]{2,1,0:T(8,128)(2,1)S(1)} collective-permute-done((bf16[8,64,768]{2,1,0:T(8,128)(2,1)S(1)}, bf16[8,64,768]{2,1,0:T(8,128)(2,1)S(1)}, u32[]{:S(2)}, u32[]{:S(2)}) %collective-permute-start.26) | collective-permute-done | bytes 786464 | tf_op jit(solution)/shard_map/ppermute | solution.py:38
  206.5 97.3 %shard_map.280 = bf16[8,4,64,768]{3,2,1,0:T(8,128)(2,1)} custom-call(s32[2]{0:T(128)} %pad_add_fusion.at_ref, bf16[8,64,768]{2,1,0:T(8,128)(2,1)} %copy-done.43, bf16[8,64,768]{2,1,0:T(8,128)(2,1)} %copy-done.45, bf16[8,64,768]{2,1,0:T(8,128)(2,1)} %copy-done.44, bf16[8,64,768]{2,1,0:T(8,128)(2,1)} %copy-done.46), custom_call_target="tpu_custom_call" | custom-call | bytes 6291456 | tf_op jit(solution)/shard_map/pallas_call | solution.py:118
  303.9 6.7 fusion.28.q_ref.k_ref.v_ref
  320.6 3.6 collective-permute-done.30
  331.1 3.9 collective-permute-done.33
  337.7 10.2 shard_map.281
  368.6 9.7 collective-permute-done.38
  378.3 11.5 collective-permute-done.40
  399.0 18.6 %collective-permute-done.66 = bf16[128,2048]{1,0:T(8,128)(2,1)S(1)} collective-permute-done((bf16[128,2048]{1,0:T(8,128)(2,1)S(1)}, bf16[128,2048]{1,0:T(8,128)(2,1)S(1)}, u32[]{:S(2)}, u32[]{:S(2)}) %collective-permute-start.66) | collective-permute-done | bytes 524320 | tf_op jit(solution)/shard_map/ppermute | solution.py:38
  435.8 35.7 %shard_map.282 = (bf16[1024,2048]{1,0:T(8,128)(2,1)}, bf16[1024,2176]{1,0:T(8,128)(2,1)}, bf16[2,1024,512]{2,1,0:T(8,128)(2,1)}, bf16[2,1024,512]{2,1,0:T(8,128)(2,1)}, bf16[2,1024,512]{2,1,0:T(8,128)(2,1)}) custom-call(s32[2]{0:T(128)} %pad_add_fusion.1.at_ref, bf16[1024,2048]{1,0:T(8,128)(2,1)} %constant_dynamic-update-slice_fusion.56.x_ref, ...), custom_call_target="tpu_custom_call" | custom-call | flops 25769803776 | bytes 35651584 | tf_op jit(solution)/shard_map/pallas_call | solution.py:329
  471.4 4.9 fusion.125
  476.4 9.2 fusion.7
  485.6 6.8 fusion.15
  492.4 7.2 fusion.13
  513.8 35.5 %shard_map.283 = (bf16[1024,2048]{1,0:T(8,128)(2,1)}, bf16[1024,2176]{1,0:T(8,128)(2,1)}, bf16[2,1024,512]{2,1,0:T(8,128)(2,1)}, bf16[2,1024,512]{2,1,0:T(8,128)(2,1)}, bf16[2,1024,512]{2,1,0:T(8,128)(2,1)}) custom-call(s32[2]{0:T(128)} %pad_add_fusion.1.at_ref, bf16[1024,2048]{1,0:T(8,128)(2,1)} %copy-done.16, bf16[1024,2048]{1,0:T(8,128)(2,1)} %copy-done.62, ...), custom_call_target="tpu_custom_call" | custom-call | flops 25769803776 | bytes 35651584 | tf_op jit(solution)/shard_map/pallas_call | solution.py:329
  549.3 4.9 fusion.126
  559.1 7.2 add_convert_fusion
  570.8 8.5 fusion.3
  579.4 6.1 fusion.4
  585.5 7.8 reshape.259
  593.3 11.5 constant_dynamic-slice_fusion
  604.7 7.8 reshape.258
  612.5 10.5 copy.410
  623.0 10.5 copy.409
  633.6 11.4 constant_dynamic-slice_fusion.2
  645.0 10.5 copy.408
  655.5 10.7 copy.407
  668.9 5.3 convert_add_fusion.5
  683.8 31.7 %collective-permute-done.148 = bf16[2,2,512,512]{3,2,1,0:T(8,128)(2,1)S(1)} collective-permute-done((bf16[2,2,512,512]{3,2,1,0:T(8,128)(2,1)}, bf16[2,2,512,512]{3,2,1,0:T(8,128)(2,1)S(1)}, u32[]{:S(2)}, u32[]{:S(2)}) %collective-permute-start.148) | collective-permute-done | bytes 2097184 | tf_op jit(solution)/shard_map/ppermute | solution.py:38
  718.6 4.4 convert_add_fusion.2
  728.1 54.3 %collective-permute-done.146 = bf16[2,2,512,512]{3,2,1,0:T(8,128)(2,1)S(1)} collective-permute-done((bf16[2,2,512,512]{3,2,1,0:T(8,128)(2,1)S(1)}, bf16[2,2,512,512]{3,2,1,0:T(8,128)(2,1)S(1)}, u32[]{:S(2)}, u32[]{:S(2)}) %collective-permute-start.146) | collective-permute-done | bytes 2097184 | tf_op jit(solution)/shard_map/ppermute | solution.py:38
  787.3 21.9 %collective-permute-done.101 = bf16[128,2176]{1,0:T(8,128)(2,1)S(1)} collective-permute-done((bf16[128,2176]{1,0:T(8,128)(2,1)S(1)}, bf16[128,2176]{1,0:T(8,128)(2,1)S(1)}, u32[]{:S(2)}, u32[]{:S(2)}) %collective-permute-start.101) | collective-permute-done | bytes 557088 | tf_op jit(solution)/shard_map/ppermute | solution.py:38
  812.7 7.1 collective-permute-done.92
  822.4 43.6 %collective-permute-done.147 = bf16[2,512,512]{2,1,0:T(8,128)(2,1)S(1)} collective-permute-done((bf16[2,512,512]{2,1,0:T(8,128)(2,1)S(1)}, bf16[2,512,512]{2,1,0:T(8,128)(2,1)S(1)}, u32[]{:S(2)}, u32[]{:S(2)}) %collective-permute-start.147) | collective-permute-done | bytes 1048608 | tf_op jit(solution)/shard_map/ppermute | solution.py:38
  870.6 7.2 collective-permute-done.103
  907.0 11.1 collective-permute-done.104
  918.8 21.1 %collective-permute-done.106 = bf16[128,2048]{1,0:T(8,128)(2,1)S(1)} collective-permute-done((bf16[128,2048]{1,0:T(8,128)(2,1)S(1)}, bf16[128,2048]{1,0:T(8,128)(2,1)S(1)}, u32[]{:S(2)}, u32[]{:S(2)}) %collective-permute-start.106) | collective-permute-done | bytes 524320 | tf_op jit(solution)/shard_map/ppermute | solution.py:38
  946.0 19.8 %shard_map.284 = (f32[1024,256]{1,0:T(8,128)}, f32[1024,256]{1,0:T(8,128)}, bf16[1024,256]{1,0:T(8,128)(2,1)}, f32[1024,2]{1,0:T(8,128)}, f32[2,256]{1,0:T(2,128)}) custom-call(s32[8]{0:T(128)} %copy-done.77, f32[1024,768]{1,0:T(8,128)} %copy-done, f32[1024,768]{1,0:T(8,128)} %copy-done, f32[1024,768]{1,0:T(8,128)} %copy-done, f32[1024,2]{1,0:T(8,128)} %bitcast.456, ...), custom_call_target="tpu_custom_call" | custom-call | flops 2684354560 | bytes 6291456 | tf_op jit(solution)/shard_map/pallas_call | solution.py:262
  976.3 21.9 %collective-permute-done.115 = f32[2,1024]{0,1:T(8,128)S(1)} collective-permute-done((f32[2,1024]{0,1:T(8,128)}, f32[2,1024]{0,1:T(8,128)S(1)}, u32[]{:S(2)}, u32[]{:S(2)}) %collective-permute-start.115) | collective-permute-done | bytes 8224 | tf_op jit(solution)/shard_map/ppermute | solution.py:38
  1001.5 11.0 collective-permute-done.113
  1015.0 9.1 collective-permute-done.112
  1025.5 9.8 collective-permute-done.117
  1107.6 5.2 convolution_convert_fusion.2
  1112.8 3.9 convolution_convert_fusion.1
  1122.4 36.9 %collective-permute-done.122 = bf16[2,8,64,768]{3,2,1,0:T(8,128)(2,1)S(1)} collective-permute-done((bf16[2,8,64,768]{3,2,1,0:T(8,128)(2,1)S(1)}, bf16[2,8,64,768]{3,2,1,0:T(8,128)(2,1)S(1)}, u32[]{:S(2)}, u32[]{:S(2)}) %collective-permute-start.122) | collective-permute-done | bytes 1572896 | tf_op jit(solution)/shard_map/ppermute | solution.py:38
  1164.0 31.8 %collective-permute-done.123 = bf16[8,64,768]{2,1,0:T(8,128)(2,1)S(1)} collective-permute-done((bf16[8,64,768]{2,1,0:T(8,128)(2,1)S(1)}, bf16[8,64,768]{2,1,0:T(8,128)(2,1)S(1)}, u32[]{:S(2)}, u32[]{:S(2)}) %collective-permute-start.123) | collective-permute-done | bytes 786464 | tf_op jit(solution)/shard_map/ppermute | solution.py:38
  1201.9 3.6 collective-permute-done.125
  1206.9 18.8 %collective-permute-done.126 = bf16[64,768]{1,0:T(8,128)(2,1)S(1)} collective-permute-done((bf16[64,768]{1,0:T(8,128)(2,1)S(1)}, bf16[64,768]{1,0:T(8,128)(2,1)S(1)}, u32[]{:S(2)}, u32[]{:S(2)}) %collective-permute-start.126) | collective-permute-done | bytes 98336 | tf_op jit(solution)/shard_map/ppermute | solution.py:38
  1227.9 4.0 collective-permute-done.128
  1232.8 3.8 collective-permute-done.129
  1238.0 4.3 collective-permute-done.130
  1247.1 10.2 collective-permute-done.120
  1257.8 9.9 collective-permute-done.64
  1267.7 3.7 collective-permute-done.94
  1271.4 4.3 fusion.42
  (811 shorter events, 397.9 us)
Async XLA Ops:
  0.7 27.2 %collective-permute-start.82 = (s32[8,128]{1,0:T(8,128)}, s32[8,128]{1,0:T(8,128)S(1)}, u32[]{:S(2)}, u32[]{:S(2)}) collective-permute-start(s32[8,128]{1,0:T(8,128)} %bitcast.516), channel_id=1, source_target_pairs={{0,2},{1,3},{2,0},{3,1},{4,6},{5,7},{6,4},{7,5},{8,10},{9,11},{10,... | collective-permute-start | bytes 12296 | tf_op jit(solution)/shard_map/ppermute | solution.py:38
  4.8 28.1 %collective-permute-start.58 = (s32[8,128]{1,0:T(8,128)}, s32[8,128]{1,0:T(8,128)S(1)}, u32[]{:S(2)}, u32[]{:S(2)}) collective-permute-start(s32[8,128]{1,0:T(8,128)} %bitcast.517), channel_id=1, source_target_pairs={{0,4},{4,0},{8,12},{12,8},{16,20},{20,16},{24,28},{28,24},{1,5},{5... | collective-permute-start | bytes 12296 | tf_op jit(solution)/shard_map/ppermute | solution.py:38
  27.9 76.8 %collective-permute-start.35 = (bf16[64,2048]{1,0:T(8,128)(2,1)S(1)}, bf16[64,2048]{1,0:T(8,128)(2,1)}, u32[]{:S(2)}, u32[]{:S(2)}) collective-permute-start(bf16[64,2048]{1,0:T(8,128)(2,1)S(1)} %copy-done.55), channel_id=1, source_target_pairs={{0,2},{1,3},{2,0},{3,1},{4,6},{5,7},{6,4},{7,5},{8,10},{9,11},{10,... | collective-permute-start | bytes 786440 | tf_op jit(solution)/shard_map/ppermute | solution.py:38
  30.9 78.8 %collective-permute-start.34 = (bf16[64,2048]{1,0:T(8,128)(2,1)S(1)}, bf16[64,2048]{1,0:T(8,128)(2,1)}, u32[]{:S(2)}, u32[]{:S(2)}) collective-permute-start(bf16[64,2048]{1,0:T(8,128)(2,1)S(1)} %copy-done.55), channel_id=1, source_target_pairs={{0,1},{1,0},{2,3},{3,2},{4,5},{5,4},{6,7},{7,6},{8,9},{9,8},{10,11... | collective-permute-start | bytes 786440 | tf_op jit(solution)/shard_map/ppermute | solution.py:38
  31.6 85.5 %collective-permute-start.74 = (bf16[128,2048]{1,0:T(8,128)(2,1)}, bf16[128,2048]{1,0:T(8,128)(2,1)}, u32[]{:S(2)}, u32[]{:S(2)}) collective-permute-start(bf16[128,2048]{1,0:T(8,128)(2,1)} %bitcast.58), channel_id=1, source_target_pairs={{0,2},{1,3},{2,0},{3,1},{4,6},{5,7},{6,4},{7,5},{8,10},{9,11},{10,... | collective-permute-start | bytes 1572872 | tf_op jit(solution)/shard_map/ppermute | solution.py:38
  32.9 318.3 %collective-permute-start.51 = (bf16[128,2048]{1,0:T(8,128)(2,1)}, bf16[128,2048]{1,0:T(8,128)(2,1)}, u32[]{:S(2)}, u32[]{:S(2)}) collective-permute-start(bf16[128,2048]{1,0:T(8,128)(2,1)} %bitcast.58), channel_id=1, source_target_pairs={{0,4},{4,0},{8,12},{12,8},{16,20},{20,16},{24,28},{28,24},{1,5},{5... | collective-permute-start | bytes 1572872 | tf_op jit(solution)/shard_map/ppermute | solution.py:38
  109.8 25.1 %collective-permute-start.49 = (bf16[128,2048]{1,0:T(8,128)(2,1)}, bf16[128,2048]{1,0:T(8,128)(2,1)S(1)}, u32[]{:S(2)}, u32[]{:S(2)}) collective-permute-start(bf16[128,2048]{1,0:T(8,128)(2,1)} %bitcast.58), channel_id=1, source_target_pairs={{0,16},{4,20},{8,24},{12,28},{16,0},{20,4},{24,8},{28,12},{1,17},{... | collective-permute-start | bytes 1572872 | tf_op jit(solution)/shard_map/ppermute | solution.py:38
  113.5 34.3 %collective-permute-start.2 = (bf16[128,2048]{1,0:T(8,128)(2,1)S(1)}, bf16[128,2048]{1,0:T(8,128)(2,1)S(1)}, u32[]{:S(2)}, u32[]{:S(2)}) collective-permute-start(bf16[128,2048]{1,0:T(8,128)(2,1)S(1)} %bitcast.460), channel_id=1, source_target_pairs={{0,24},{4,28},{8,16},{12,20},{16,8},{20,12},{24,0},{28,4},{1,25},{... | collective-permute-start | bytes 1572872 | tf_op jit(solution)/shard_map/ppermute | solution.py:38
  117.1 28.8 %collective-permute-start = (bf16[128,2048]{1,0:T(8,128)(2,1)S(1)}, bf16[128,2048]{1,0:T(8,128)(2,1)S(1)}, u32[]{:S(2)}, u32[]{:S(2)}) collective-permute-start(bf16[128,2048]{1,0:T(8,128)(2,1)S(1)} %bitcast.461), channel_id=1, source_target_pairs={{0,8},{4,12},{8,0},{12,4},{16,24},{20,28},{24,16},{28,20},{1,9},{5... | collective-permute-start | bytes 1572872 | tf_op jit(solution)/shard_map/ppermute | solution.py:38
  124.1 23.5 %collective-permute-start.1 = (bf16[128,2048]{1,0:T(8,128)(2,1)S(1)}, bf16[128,2048]{1,0:T(8,128)(2,1)S(1)}, u32[]{:S(2)}, u32[]{:S(2)}) collective-permute-start(bf16[128,2048]{1,0:T(8,128)(2,1)S(1)} %bitcast.462), channel_id=1, source_target_pairs={{0,16},{4,20},{8,24},{12,28},{16,0},{20,4},{24,8},{28,12},{1,17},{... | collective-permute-start | bytes 1572872 | tf_op jit(solution)/shard_map/ppermute | solution.py:38
  145.9 36.5 %collective-permute-start.25 = (bf16[8,64,768]{2,1,0:T(8,128)(2,1)S(1)}, bf16[8,64,768]{2,1,0:T(8,128)(2,1)S(1)}, u32[]{:S(2)}, u32[]{:S(2)}) collective-permute-start(bf16[8,64,768]{2,1,0:T(8,128)(2,1)S(1)} %constant_dynamic-update-slice_fusion.16.refs_0_), channel_id=1, source_target_pairs={{0,2},{1,3},{2,0},{3,1},{4,6},{5,7},{6,4},{7,5},{8,10},{9,11},{10,... | collective-permute-start | bytes 2359304 | tf_op jit(solution)/shard_map/ppermute | solution.py:38
  148.4 34.1 %collective-permute-start.6 = (bf16[128,2048]{1,0:T(8,128)(2,1)S(1)}, bf16[128,2048]{1,0:T(8,128)(2,1)S(1)}, u32[]{:S(2)}, u32[]{:S(2)}) collective-permute-start(bf16[128,2048]{1,0:T(8,128)(2,1)S(1)} %collective-permute-done.2), channel_id=1, source_target_pairs={{0,4},{4,0},{8,12},{12,8},{16,20},{20,16},{24,28},{28,24},{1,5},{5... | collective-permute-start | bytes 1572872 | tf_op jit(solution)/shard_map/ppermute | solution.py:38
  149.6 161.4 %collective-permute-start.50 = (bf16[128,2048]{1,0:T(8,128)(2,1)}, bf16[128,2048]{1,0:T(8,128)(2,1)}, u32[]{:S(2)}, u32[]{:S(2)}) collective-permute-start(bf16[128,2048]{1,0:T(8,128)(2,1)} %bitcast.58), channel_id=1, source_target_pairs={{0,24},{4,28},{8,16},{12,20},{16,8},{20,12},{24,0},{28,4},{1,25},{... | collective-permute-start | bytes 1572872 | tf_op jit(solution)/shard_map/ppermute | solution.py:38
  151.5 37.2 %collective-permute-start.24 = (bf16[8,64,768]{2,1,0:T(8,128)(2,1)S(1)}, bf16[8,64,768]{2,1,0:T(8,128)(2,1)S(1)}, u32[]{:S(2)}, u32[]{:S(2)}) collective-permute-start(bf16[8,64,768]{2,1,0:T(8,128)(2,1)S(1)} %constant_dynamic-update-slice_fusion.16.refs_0_), channel_id=1, source_target_pairs={{0,1},{1,0},{2,3},{3,2},{4,5},{5,4},{6,7},{7,6},{8,9},{9,8},{10,11... | collective-permute-start | bytes 2359304 | tf_op jit(solution)/shard_map/ppermute | solution.py:38
  182.4 175.4 %collective-permute-start.78 = (bf16[128,2048]{1,0:T(8,128)(2,1)}, bf16[128,2048]{1,0:T(8,128)(2,1)}, u32[]{:S(2)}, u32[]{:S(2)}) collective-permute-start(bf16[128,2048]{1,0:T(8,128)(2,1)} %collective-permute-done.74), channel_id=1, source_target_pairs={{0,4},{4,0},{8,12},{12,8},{16,20},{20,16},{24,28},{28,24},{1,5},{5... | collective-permute-start | bytes 1572872 | tf_op jit(solution)/shard_map/ppermute | solution.py:38
  188.7 167.5 %collective-permute-start.77 = (bf16[128,2048]{1,0:T(8,128)(2,1)}, bf16[128,2048]{1,0:T(8,128)(2,1)}, u32[]{:S(2)}, u32[]{:S(2)}) collective-permute-start(bf16[128,2048]{1,0:T(8,128)(2,1)} %collective-permute-done.74), channel_id=1, source_target_pairs={{0,24},{4,28},{8,16},{12,20},{16,8},{20,12},{24,0},{28,4},{1,25},{... | collective-permute-start | bytes 1572872 | tf_op jit(solution)/shard_map/ppermute | solution.py:38
  205.4 149.6 %collective-permute-start.76 = (bf16[128,2048]{1,0:T(8,128)(2,1)}, bf16[128,2048]{1,0:T(8,128)(2,1)}, u32[]{:S(2)}, u32[]{:S(2)}) collective-permute-start(bf16[128,2048]{1,0:T(8,128)(2,1)} %collective-permute-done.74), channel_id=1, source_target_pairs={{0,16},{4,20},{8,24},{12,28},{16,0},{20,4},{24,8},{28,12},{1,17},{... | collective-permute-start | bytes 1572872 | tf_op jit(solution)/shard_map/ppermute | solution.py:38
  365.1 24.7 %collective-permute-start.40 = (bf16[128,2048]{1,0:T(8,128)(2,1)S(1)}, bf16[128,2048]{1,0:T(8,128)(2,1)S(1)}, u32[]{:S(2)}, u32[]{:S(2)}) collective-permute-start(bf16[128,2048]{1,0:T(8,128)(2,1)S(1)} %get-tuple-element.115), channel_id=1, source_target_pairs={{0,24},{4,28},{8,16},{12,20},{16,8},{20,12},{24,0},{28,4},{1,25},{... | collective-permute-start | bytes 1572872 | tf_op jit(solution)/shard_map/ppermute | solution.py:38
  366.3 24.9 %collective-permute-start.39 = (bf16[128,2048]{1,0:T(8,128)(2,1)S(1)}, bf16[128,2048]{1,0:T(8,128)(2,1)S(1)}, u32[]{:S(2)}, u32[]{:S(2)}) collective-permute-start(bf16[128,2048]{1,0:T(8,128)(2,1)S(1)} %get-tuple-element.116), channel_id=1, source_target_pairs={{0,16},{4,20},{8,24},{12,28},{16,0},{20,4},{24,8},{28,12},{1,17},{... | collective-permute-start | bytes 1572872 | tf_op jit(solution)/shard_map/ppermute | solution.py:38
  393.6 23.9 %collective-permute-start.66 = (bf16[128,2048]{1,0:T(8,128)(2,1)S(1)}, bf16[128,2048]{1,0:T(8,128)(2,1)S(1)}, u32[]{:S(2)}, u32[]{:S(2)}) collective-permute-start(bf16[128,2048]{1,0:T(8,128)(2,1)S(1)} %get-tuple-element.60), channel_id=1, source_target_pairs={{0,2},{1,3},{2,0},{3,1},{4,6},{5,7},{6,4},{7,5},{8,10},{9,11},{10,... | collective-permute-start | bytes 1572872 | tf_op jit(solution)/shard_map/ppermute | solution.py:38
  393.9 31.4 %collective-permute-start.44 = (bf16[128,2048]{1,0:T(8,128)(2,1)S(1)}, bf16[128,2048]{1,0:T(8,128)(2,1)S(1)}, u32[]{:S(2)}, u32[]{:S(2)}) collective-permute-start(bf16[128,2048]{1,0:T(8,128)(2,1)S(1)} %get-tuple-element.60), channel_id=1, source_target_pairs={{0,4},{4,0},{8,12},{12,8},{16,20},{20,16},{24,28},{28,24},{1,5},{5... | collective-permute-start | bytes 1572872 | tf_op jit(solution)/shard_map/ppermute | solution.py:38
  393.9 30.0 %collective-permute-start.43 = (bf16[128,2048]{1,0:T(8,128)(2,1)S(1)}, bf16[128,2048]{1,0:T(8,128)(2,1)S(1)}, u32[]{:S(2)}, u32[]{:S(2)}) collective-permute-start(bf16[128,2048]{1,0:T(8,128)(2,1)S(1)} %get-tuple-element.60), channel_id=1, source_target_pairs={{0,24},{4,28},{8,16},{12,20},{16,8},{20,12},{24,0},{28,4},{1,25},{... | collective-permute-start | bytes 1572872 | tf_op jit(solution)/shard_map/ppermute | solution.py:38
  395.5 27.5 %collective-permute-start.42 = (bf16[128,2048]{1,0:T(8,128)(2,1)S(1)}, bf16[128,2048]{1,0:T(8,128)(2,1)S(1)}, u32[]{:S(2)}, u32[]{:S(2)}) collective-permute-start(bf16[128,2048]{1,0:T(8,128)(2,1)S(1)} %get-tuple-element.60), channel_id=1, source_target_pairs={{0,16},{4,20},{8,24},{12,28},{16,0},{20,4},{24,8},{28,12},{1,17},{... | collective-permute-start | bytes 1572872 | tf_op jit(solution)/shard_map/ppermute | solution.py:38
  396.0 23.8 %collective-permute-start.41 = (bf16[128,2048]{1,0:T(8,128)(2,1)S(1)}, bf16[128,2048]{1,0:T(8,128)(2,1)}, u32[]{:S(2)}, u32[]{:S(2)}) collective-permute-start(bf16[128,2048]{1,0:T(8,128)(2,1)S(1)} %get-tuple-element.60), channel_id=1, source_target_pairs={{0,8},{4,12},{8,0},{12,4},{16,24},{20,28},{24,16},{28,20},{1,9},{5... | collective-permute-start | bytes 1572872 | tf_op jit(solution)/shard_map/ppermute | solution.py:38
  417.6 89.0 %collective-permute-start.70 = (bf16[128,2048]{1,0:T(8,128)(2,1)S(1)}, bf16[128,2048]{1,0:T(8,128)(2,1)}, u32[]{:S(2)}, u32[]{:S(2)}) collective-permute-start(bf16[128,2048]{1,0:T(8,128)(2,1)S(1)} %collective-permute-done.66), channel_id=1, source_target_pairs={{0,4},{4,0},{8,12},{12,8},{16,20},{20,16},{24,28},{28,24},{1,5},{5... | collective-permute-start | bytes 1572872 | tf_op jit(solution)/shard_map/ppermute | solution.py:38
  419.8 85.6 %collective-permute-start.69 = (bf16[128,2048]{1,0:T(8,128)(2,1)S(1)}, bf16[128,2048]{1,0:T(8,128)(2,1)}, u32[]{:S(2)}, u32[]{:S(2)}) collective-permute-start(bf16[128,2048]{1,0:T(8,128)(2,1)S(1)} %collective-permute-done.66), channel_id=1, source_target_pairs={{0,24},{4,28},{8,16},{12,20},{16,8},{20,12},{24,0},{28,4},{1,25},{... | collective-permute-start | bytes 1572872 | tf_op jit(solution)/shard_map/ppermute | solution.py:38
  426.0 77.7 %collective-permute-start.68 = (bf16[128,2048]{1,0:T(8,128)(2,1)S(1)}, bf16[128,2048]{1,0:T(8,128)(2,1)}, u32[]{:S(2)}, u32[]{:S(2)}) collective-permute-start(bf16[128,2048]{1,0:T(8,128)(2,1)S(1)} %collective-permute-done.66), channel_id=1, source_target_pairs={{0,16},{4,20},{8,24},{12,28},{16,0},{20,4},{24,8},{28,12},{1,17},{... | collective-permute-start | bytes 1572872 | tf_op jit(solution)/shard_map/ppermute | solution.py:38
  428.4 72.9 %collective-permute-start.67 = (bf16[128,2048]{1,0:T(8,128)(2,1)S(1)}, bf16[128,2048]{1,0:T(8,128)(2,1)}, u32[]{:S(2)}, u32[]{:S(2)}) collective-permute-start(bf16[128,2048]{1,0:T(8,128)(2,1)S(1)} %collective-permute-done.66), channel_id=1, source_target_pairs={{0,8},{4,12},{8,0},{12,4},{16,24},{20,28},{24,16},{28,20},{1,9},{5... | collective-permute-start | bytes 1572872 | tf_op jit(solution)/shard_map/ppermute | solution.py:38
  476.4 189.8 %collective-permute-start.62 = (bf16[4,128,2048]{2,1,0:T(8,128)(2,1)}, bf16[4,128,2048]{2,1,0:T(8,128)(2,1)}, u32[]{:S(2)}, u32[]{:S(2)}) collective-permute-start(bf16[4,128,2048]{2,1,0:T(8,128)(2,1)} %bitcast.63), channel_id=1, source_target_pairs={{0,4},{4,0},{8,12},{12,8},{16,20},{20,16},{24,28},{28,24},{1,5},{5... | collective-permute-start | bytes 6291464 | tf_op jit(solution)/shard_map/ppermute | solution.py:38
  501.3 174.0 %collective-permute-start.95 = (bf16[4,128,2176]{2,1,0:T(8,128)(2,1)}, bf16[4,128,2176]{2,1,0:T(8,128)(2,1)}, u32[]{:S(2)}, u32[]{:S(2)}) collective-permute-start(bf16[4,128,2176]{2,1,0:T(8,128)(2,1)} %bitcast.76), channel_id=1, source_target_pairs={{0,4},{4,0},{8,12},{12,8},{16,20},{20,16},{24,28},{28,24},{1,5},{5... | collective-permute-start | bytes 6684680 | tf_op jit(solution)/shard_map/ppermute | solution.py:38
  554.3 123.5 %collective-permute-start.90 = (bf16[4,128,2048]{2,1,0:T(8,128)(2,1)}, bf16[4,128,2048]{2,1,0:T(8,128)(2,1)}, u32[]{:S(2)}, u32[]{:S(2)}) collective-permute-start(bf16[4,128,2048]{2,1,0:T(8,128)(2,1)} %bitcast.69), channel_id=1, source_target_pairs={{0,4},{4,0},{8,12},{12,8},{16,20},{20,16},{24,28},{28,24},{1,5},{5... | collective-permute-start | bytes 6291464 | tf_op jit(solution)/shard_map/ppermute | solution.py:38
  557.2 165.7 %collective-permute-start.99 = (bf16[4,128,2176]{2,1,0:T(8,128)(2,1)}, bf16[4,128,2176]{2,1,0:T(8,128)(2,1)}, u32[]{:S(2)}, u32[]{:S(2)}) collective-permute-start(bf16[4,128,2176]{2,1,0:T(8,128)(2,1)} %bitcast.82), channel_id=1, source_target_pairs={{0,4},{4,0},{8,12},{12,8},{16,20},{20,16},{24,28},{28,24},{1,5},{5... | collective-permute-start | bytes 6684680 | tf_op jit(solution)/shard_map/ppermute | solution.py:38
  568.0 150.6 %collective-permute-start.150 = (bf16[2,256,2048]{2,1,0:T(8,128)(2,1)}, bf16[2,256,2048]{2,1,0:T(8,128)(2,1)}, u32[]{:S(2)}, u32[]{:S(2)}) collective-permute-start(bf16[2,256,2048]{2,1,0:T(8,128)(2,1)} %dynamic-slice_bitcast_fusion), channel_id=1, source_target_pairs={{0,1},{1,0},{2,3},{3,2},{4,5},{5,4},{6,7},{7,6},{8,9},{9,8},{10,11... | collective-permute-start | bytes 6291464 | tf_op jit(solution)/shard_map/ppermute | solution.py:38
  666.2 49.3 %collective-permute-start.148 = (bf16[2,2,512,512]{3,2,1,0:T(8,128)(2,1)}, bf16[2,2,512,512]{3,2,1,0:T(8,128)(2,1)S(1)}, u32[]{:S(2)}, u32[]{:S(2)}) collective-permute-start(bf16[2,2,512,512]{3,2,1,0:T(8,128)(2,1)} %bitcast.479), channel_id=1, source_target_pairs={{0,1},{1,0},{2,3},{3,2},{4,5},{5,4},{6,7},{7,6},{8,9},{9,8},{10,11... | collective-permute-start | bytes 6291464 | tf_op jit(solution)/shard_map/ppermute | solution.py:38
  675.3 107.1 %collective-permute-start.146 = (bf16[2,2,512,512]{3,2,1,0:T(8,128)(2,1)S(1)}, bf16[2,2,512,512]{3,2,1,0:T(8,128)(2,1)S(1)}, u32[]{:S(2)}, u32[]{:S(2)}) collective-permute-start(bf16[2,2,512,512]{3,2,1,0:T(8,128)(2,1)S(1)} %bitcast.478), channel_id=1, source_target_pairs={{0,1},{1,0},{2,3},{3,2},{4,5},{5,4},{6,7},{7,6},{8,9},{9,8},{10,11... | collective-permute-start | bytes 6291464 | tf_op jit(solution)/shard_map/ppermute | solution.py:38
  682.9 127.4 %collective-permute-start.91 = (bf16[128,2048]{1,0:T(8,128)(2,1)}, bf16[128,2048]{1,0:T(8,128)(2,1)}, u32[]{:S(2)}, u32[]{:S(2)}) collective-permute-start(bf16[128,2048]{1,0:T(8,128)(2,1)} %get-tuple-element.111), channel_id=1, source_target_pairs={{0,8},{4,12},{8,0},{12,4},{16,24},{20,28},{24,16},{28,20},{1,9},{5... | collective-permute-start | bytes 1572872 | tf_op jit(solution)/shard_map/ppermute | solution.py:38
  716.3 103.5 %collective-permute-start.149 = (bf16[2,512,512]{2,1,0:T(8,128)(2,1)S(1)}, bf16[2,512,512]{2,1,0:T(8,128)(2,1)S(1)}, u32[]{:S(2)}, u32[]{:S(2)}) collective-permute-start(bf16[2,512,512]{2,1,0:T(8,128)(2,1)S(1)} %fusion.45), channel_id=1, source_target_pairs={{0,2},{1,3},{2,0},{3,1},{4,6},{5,7},{6,4},{7,5},{8,10},{9,11},{10,... | collective-permute-start | bytes 3145736 | tf_op jit(solution)/shard_map/ppermute | solution.py:38
  725.3 58.7 %collective-permute-start.100 = (bf16[128,2176]{1,0:T(8,128)(2,1)S(1)}, bf16[128,2176]{1,0:T(8,128)(2,1)S(1)}, u32[]{:S(2)}, u32[]{:S(2)}) collective-permute-start(bf16[128,2176]{1,0:T(8,128)(2,1)S(1)} %get-tuple-element.102), channel_id=1, source_target_pairs={{0,8},{4,12},{8,0},{12,4},{16,24},{20,28},{24,16},{28,20},{1,9},{5... | collective-permute-start | bytes 1671176 | tf_op jit(solution)/shard_map/ppermute | solution.py:38
  727.0 59.3 %collective-permute-start.102 = (bf16[128,2176]{1,0:T(8,128)(2,1)S(1)}, bf16[128,2176]{1,0:T(8,128)(2,1)S(1)}, u32[]{:S(2)}, u32[]{:S(2)}) collective-permute-start(bf16[128,2176]{1,0:T(8,128)(2,1)S(1)} %get-tuple-element.103), channel_id=1, source_target_pairs={{0,24},{4,28},{8,16},{12,20},{16,8},{20,12},{24,0},{28,4},{1,25},{... | collective-permute-start | bytes 1671176 | tf_op jit(solution)/shard_map/ppermute | solution.py:38
  782.4 26.8 %collective-permute-start.101 = (bf16[128,2176]{1,0:T(8,128)(2,1)S(1)}, bf16[128,2176]{1,0:T(8,128)(2,1)S(1)}, u32[]{:S(2)}, u32[]{:S(2)}) collective-permute-start(bf16[128,2176]{1,0:T(8,128)(2,1)S(1)} %get-tuple-element.104), channel_id=1, source_target_pairs={{0,16},{4,20},{8,24},{12,28},{16,0},{20,4},{24,8},{28,12},{1,17},{... | collective-permute-start | bytes 1671176 | tf_op jit(solution)/shard_map/ppermute | solution.py:38
  784.7 26.9 %collective-permute-start.93 = (bf16[128,2048]{1,0:T(8,128)(2,1)S(1)}, bf16[128,2048]{1,0:T(8,128)(2,1)S(1)}, u32[]{:S(2)}, u32[]{:S(2)}) collective-permute-start(bf16[128,2048]{1,0:T(8,128)(2,1)S(1)} %copy-done.54), channel_id=1, source_target_pairs={{0,24},{4,28},{8,16},{12,20},{16,8},{20,12},{24,0},{28,4},{1,25},{... | collective-permute-start | bytes 1572872 | tf_op jit(solution)/shard_map/ppermute | solution.py:38
  786.3 33.5 %collective-permute-start.92 = (bf16[128,2048]{1,0:T(8,128)(2,1)S(1)}, bf16[128,2048]{1,0:T(8,128)(2,1)S(1)}, u32[]{:S(2)}, u32[]{:S(2)}) collective-permute-start(bf16[128,2048]{1,0:T(8,128)(2,1)S(1)} %copy-done.53), channel_id=1, source_target_pairs={{0,16},{4,20},{8,24},{12,28},{16,0},{20,4},{24,8},{28,12},{1,17},{... | collective-permute-start | bytes 1572872 | tf_op jit(solution)/shard_map/ppermute | solution.py:38
  809.2 56.8 %collective-permute-start.147 = (bf16[2,512,512]{2,1,0:T(8,128)(2,1)S(1)}, bf16[2,512,512]{2,1,0:T(8,128)(2,1)S(1)}, u32[]{:S(2)}, u32[]{:S(2)}) collective-permute-start(bf16[2,512,512]{2,1,0:T(8,128)(2,1)S(1)} %fusion.44), channel_id=1, source_target_pairs={{0,2},{1,3},{2,0},{3,1},{4,6},{5,7},{6,4},{7,5},{8,10},{9,11},{10,... | collective-permute-start | bytes 3145736 | tf_op jit(solution)/shard_map/ppermute | solution.py:38
  810.3 60.3 %collective-permute-start.96 = (bf16[128,2176]{1,0:T(8,128)(2,1)S(1)}, bf16[128,2176]{1,0:T(8,128)(2,1)}, u32[]{:S(2)}, u32[]{:S(2)}) collective-permute-start(bf16[128,2176]{1,0:T(8,128)(2,1)S(1)} %get-tuple-element.99), channel_id=1, source_target_pairs={{0,8},{4,12},{8,0},{12,4},{16,24},{20,28},{24,16},{28,20},{1,9},{5... | collective-permute-start | bytes 1671176 | tf_op jit(solution)/shard_map/ppermute | solution.py:38
  811.6 59.0 %collective-permute-start.98 = (bf16[128,2176]{1,0:T(8,128)(2,1)S(1)}, bf16[128,2176]{1,0:T(8,128)(2,1)}, u32[]{:S(2)}, u32[]{:S(2)}) collective-permute-start(bf16[128,2176]{1,0:T(8,128)(2,1)S(1)} %get-tuple-element.100), channel_id=1, source_target_pairs={{0,24},{4,28},{8,16},{12,20},{16,8},{20,12},{24,0},{28,4},{1,25},{... | collective-permute-start | bytes 1671176 | tf_op jit(solution)/shard_map/ppermute | solution.py:38
  819.8 50.9 %collective-permute-start.97 = (bf16[128,2176]{1,0:T(8,128)(2,1)S(1)}, bf16[128,2176]{1,0:T(8,128)(2,1)}, u32[]{:S(2)}, u32[]{:S(2)}) collective-permute-start(bf16[128,2176]{1,0:T(8,128)(2,1)S(1)} %get-tuple-element.101), channel_id=1, source_target_pairs={{0,16},{4,20},{8,24},{12,28},{16,0},{20,4},{24,8},{28,12},{1,17},{... | collective-permute-start | bytes 1671176 | tf_op jit(solution)/shard_map/ppermute | solution.py:38
  819.8 58.1 %collective-permute-start.103 = (bf16[128,2176]{1,0:T(8,128)(2,1)}, bf16[128,2176]{1,0:T(8,128)(2,1)S(1)}, u32[]{:S(2)}, u32[]{:S(2)}) collective-permute-start(bf16[128,2176]{1,0:T(8,128)(2,1)} %fusion.33), channel_id=1, source_target_pairs={{0,2},{1,3},{2,0},{3,1},{4,6},{5,7},{6,4},{7,5},{8,10},{9,11},{10,... | collective-permute-start | bytes 1671176 | tf_op jit(solution)/shard_map/ppermute | solution.py:38
  891.8 366.0 %collective-permute-start.63 = (bf16[128,2048]{1,0:T(8,128)(2,1)}, bf16[128,2048]{1,0:T(8,128)(2,1)}, u32[]{:S(2)}, u32[]{:S(2)}) collective-permute-start(bf16[128,2048]{1,0:T(8,128)(2,1)} %get-tuple-element.108), channel_id=1, source_target_pairs={{0,8},{4,12},{8,0},{12,4},{16,24},{20,28},{24,16},{28,20},{1,9},{5... | collective-permute-start | bytes 1572872 | tf_op jit(solution)/shard_map/ppermute | solution.py:38
  892.7 25.4 %collective-permute-start.104 = (bf16[128,2048]{1,0:T(8,128)(2,1)S(1)}, bf16[128,2048]{1,0:T(8,128)(2,1)S(1)}, u32[]{:S(2)}, u32[]{:S(2)}) collective-permute-start(bf16[128,2048]{1,0:T(8,128)(2,1)S(1)} %get-tuple-element.56), channel_id=1, source_target_pairs={{0,8},{4,12},{8,0},{12,4},{16,24},{20,28},{24,16},{28,20},{1,9},{5... | collective-permute-start | bytes 1572872 | tf_op jit(solution)/shard_map/ppermute | solution.py:38
  901.8 355.9 %collective-permute-start.65 = (bf16[128,2048]{1,0:T(8,128)(2,1)}, bf16[128,2048]{1,0:T(8,128)(2,1)}, u32[]{:S(2)}, u32[]{:S(2)}) collective-permute-start(bf16[128,2048]{1,0:T(8,128)(2,1)} %get-tuple-element.109), channel_id=1, source_target_pairs={{0,24},{4,28},{8,16},{12,20},{16,8},{20,12},{24,0},{28,4},{1,25},{... | collective-permute-start | bytes 1572872 | tf_op jit(solution)/shard_map/ppermute | solution.py:38
  903.2 36.7 %collective-permute-start.106 = (bf16[128,2048]{1,0:T(8,128)(2,1)S(1)}, bf16[128,2048]{1,0:T(8,128)(2,1)S(1)}, u32[]{:S(2)}, u32[]{:S(2)}) collective-permute-start(bf16[128,2048]{1,0:T(8,128)(2,1)S(1)} %get-tuple-element.56), channel_id=1, source_target_pairs={{0,24},{4,28},{8,16},{12,20},{16,8},{20,12},{24,0},{28,4},{1,25},{... | collective-permute-start | bytes 1572872 | tf_op jit(solution)/shard_map/ppermute | solution.py:38
  972.7 26.7 %collective-permute-start.116 = (f32[2,1024]{0,1:T(8,128)}, f32[2,1024]{0,1:T(8,128)S(1)}, u32[]{:S(2)}, u32[]{:S(2)}) collective-permute-start(f32[2,1024]{0,1:T(8,128)} %bitcast.87), channel_id=1, source_target_pairs={{0,24},{4,28},{8,16},{12,20},{16,8},{20,12},{24,0},{28,4},{1,25},{... | collective-permute-start | bytes 24584 | tf_op jit(solution)/shard_map/ppermute | solution.py:38
  973.9 24.2 %collective-permute-start.115 = (f32[2,1024]{0,1:T(8,128)}, f32[2,1024]{0,1:T(8,128)S(1)}, u32[]{:S(2)}, u32[]{:S(2)}) collective-permute-start(f32[2,1024]{0,1:T(8,128)} %bitcast.87), channel_id=1, source_target_pairs={{0,20},{4,16},{8,28},{12,24},{16,4},{20,0},{24,12},{28,8},{1,21},{... | collective-permute-start | bytes 24584 | tf_op jit(solution)/shard_map/ppermute | solution.py:38
  974.4 62.4 %collective-permute-start.114 = (f32[2,1024]{0,1:T(8,128)}, f32[2,1024]{0,1:T(8,128)S(1)}, u32[]{:S(2)}, u32[]{:S(2)}) collective-permute-start(f32[2,1024]{0,1:T(8,128)} %bitcast.87), channel_id=1, source_target_pairs={{0,16},{4,20},{8,24},{12,28},{16,0},{20,4},{24,8},{28,12},{1,17},{... | collective-permute-start | bytes 24584 | tf_op jit(solution)/shard_map/ppermute | solution.py:38
  999.4 24.7 %collective-permute-start.112 = (f32[2,1024]{0,1:T(8,128)}, f32[2,1024]{0,1:T(8,128)S(1)}, u32[]{:S(2)}, u32[]{:S(2)}) collective-permute-start(f32[2,1024]{0,1:T(8,128)} %bitcast.87), channel_id=1, source_target_pairs={{0,8},{4,12},{8,0},{12,4},{16,24},{20,28},{24,16},{28,20},{1,9},{5... | collective-permute-start | bytes 24584 | tf_op jit(solution)/shard_map/ppermute | solution.py:38
  1024.1 58.6 %collective-permute-start.111 = (f32[2,1024]{0,1:T(8,128)}, f32[2,1024]{0,1:T(8,128)}, u32[]{:S(2)}, u32[]{:S(2)}) collective-permute-start(f32[2,1024]{0,1:T(8,128)} %bitcast.87), channel_id=1, source_target_pairs={{0,4},{4,0},{8,12},{12,8},{16,20},{20,16},{24,28},{28,24},{1,5},{5... | collective-permute-start | bytes 24584 | tf_op jit(solution)/shard_map/ppermute | solution.py:38
  1035.2 85.3 %collective-permute-start.131 = (bf16[2,64,2048]{2,1,0:T(8,128)(2,1)}, bf16[2,64,2048]{2,1,0:T(8,128)(2,1)}, u32[]{:S(2)}, u32[]{:S(2)}) collective-permute-start(bf16[2,64,2048]{2,1,0:T(8,128)(2,1)} %pad_maximum_fusion.8), channel_id=1, source_target_pairs={{0,1},{1,0},{2,3},{3,2},{4,5},{5,4},{6,7},{7,6},{8,9},{9,8},{10,11... | collective-permute-start | bytes 1572872 | tf_op jit(solution)/shard_map/ppermute | solution.py:38
  1117.2 42.1 %collective-permute-start.122 = (bf16[2,8,64,768]{3,2,1,0:T(8,128)(2,1)S(1)}, bf16[2,8,64,768]{3,2,1,0:T(8,128)(2,1)S(1)}, u32[]{:S(2)}, u32[]{:S(2)}) collective-permute-start(bf16[2,8,64,768]{3,2,1,0:T(8,128)(2,1)S(1)} %pad_maximum_fusion.1), channel_id=1, source_target_pairs={{0,1},{1,0},{2,3},{3,2},{4,5},{5,4},{6,7},{7,6},{8,9},{9,8},{10,11... | collective-permute-start | bytes 4718600 | tf_op jit(solution)/shard_map/ppermute | solution.py:38
  1119.9 41.0 %collective-permute-start.118 = (bf16[4,128,2048]{2,1,0:T(8,128)(2,1)S(1)}, bf16[4,128,2048]{2,1,0:T(8,128)(2,1)S(1)}, u32[]{:S(2)}, u32[]{:S(2)}) collective-permute-start(bf16[4,128,2048]{2,1,0:T(8,128)(2,1)S(1)} %bitcast.487), channel_id=1, source_target_pairs={{0,4},{4,0},{8,12},{12,8},{16,20},{20,16},{24,28},{28,24},{1,5},{5... | collective-permute-start | bytes 6291464 | tf_op jit(solution)/shard_map/ppermute | solution.py:38
  1121.7 38.4 %collective-permute-start.132 = (bf16[64,2048]{1,0:T(8,128)(2,1)S(1)}, bf16[64,2048]{1,0:T(8,128)(2,1)S(1)}, u32[]{:S(2)}, u32[]{:S(2)}) collective-permute-start(bf16[64,2048]{1,0:T(8,128)(2,1)S(1)} %fusion.70), channel_id=1, source_target_pairs={{0,2},{1,3},{2,0},{3,1},{4,6},{5,7},{6,4},{7,5},{8,10},{9,11},{10,... | collective-permute-start | bytes 786440 | tf_op jit(solution)/shard_map/ppermute | solution.py:38
  1159.8 36.0 %collective-permute-start.123 = (bf16[8,64,768]{2,1,0:T(8,128)(2,1)S(1)}, bf16[8,64,768]{2,1,0:T(8,128)(2,1)S(1)}, u32[]{:S(2)}, u32[]{:S(2)}) collective-permute-start(bf16[8,64,768]{2,1,0:T(8,128)(2,1)S(1)} %fusion.63), channel_id=1, source_target_pairs={{0,2},{1,3},{2,0},{3,1},{4,6},{5,7},{6,4},{7,5},{8,10},{9,11},{10,... | collective-permute-start | bytes 2359304 | tf_op jit(solution)/shard_map/ppermute | solution.py:38
  1198.4 47.2 %collective-permute-start.119 = (bf16[128,2048]{1,0:T(8,128)(2,1)}, bf16[128,2048]{1,0:T(8,128)(2,1)S(1)}, u32[]{:S(2)}, u32[]{:S(2)}) collective-permute-start(bf16[128,2048]{1,0:T(8,128)(2,1)} %get-tuple-element.105), channel_id=1, source_target_pairs={{0,8},{4,12},{8,0},{12,4},{16,24},{20,28},{24,16},{28,20},{1,9},{5... | collective-permute-start | bytes 1572872 | tf_op jit(solution)/shard_map/ppermute | solution.py:38
  1199.4 47.1 %collective-permute-start.121 = (bf16[128,2048]{1,0:T(8,128)(2,1)}, bf16[128,2048]{1,0:T(8,128)(2,1)S(1)}, u32[]{:S(2)}, u32[]{:S(2)}) collective-permute-start(bf16[128,2048]{1,0:T(8,128)(2,1)} %get-tuple-element.106), channel_id=1, source_target_pairs={{0,24},{4,28},{8,16},{12,20},{16,8},{20,12},{24,0},{28,4},{1,25},{... | collective-permute-start | bytes 1572872 | tf_op jit(solution)/shard_map/ppermute | solution.py:38
  1246.5 24.9 %collective-permute-start.94 = (bf16[128,2048]{1,0:T(8,128)(2,1)S(1)}, bf16[128,2048]{1,0:T(8,128)(2,1)S(1)}, u32[]{:S(2)}, u32[]{:S(2)}) collective-permute-start(bf16[128,2048]{1,0:T(8,128)(2,1)S(1)} %copy-done.52), channel_id=1, source_target_pairs={{0,2},{1,3},{2,0},{3,1},{4,6},{5,7},{6,4},{7,5},{8,10},{9,11},{10,... | collective-permute-start | bytes 1572872 | tf_op jit(solution)/shard_map/ppermute | solution.py:38
  (189 other events, 3004.5 us)

commit v2 on v1

v2 whole, which is shorter than its diff:
```python
import functools
import math

import jax
import jax.numpy as jnp
from jax import lax
from jax.experimental import pallas as pl
from jax.experimental.pallas import tpu as pltpu
from jax.sharding import PartitionSpec as P

HEAD_DIM = 128
EPSILON = 1e-05
ROTARY_BASE = 10000.0
MASKED = -1e30
BF16 = jnp.bfloat16
F32 = jnp.float32
VMEM_BYTES = 60 * 1024 * 1024


def dot(left, right):
    return lax.dot_general(left, right, (((1,), (0,)), ((), ())), preferred_element_type=F32)


def dot_nt(left, right):
    return lax.dot_general(left, right, (((1,), (1,)), ((), ())), preferred_element_type=F32)


def dot_tn(left, right):
    return lax.dot_general(left, right, (((0,), (0,)), ((), ())), preferred_element_type=F32)


def norm_scale(values):
    return lax.rsqrt(jnp.mean(values * values, axis=-1, keepdims=True) + EPSILON)


def hop(values, axis, mask):
    size = lax.axis_size(axis)
    return lax.ppermute(values, axis, [(i, i ^ mask) for i in range(size)])


def take_block(values, index, axis=0):
    return lax.dynamic_index_in_dim(values, index, axis, keepdims=False)


def put(buffer, values, starts):
    return lax.dynamic_update_slice(buffer, values, starts)


def after(values, *earlier):
    return lax.optimization_barrier((values, *earlier))[0]


def masks_of(size):
    return [2 * m for m in range(size // 2)] + [2 * m + 1 for m in range(size // 2)]


def gather_near(values):
    return [values] + [hop(values, "seq", 2 * m) for m in range(1, lax.axis_size("seq") // 2)]


def gather_seq(values):
    near = gather_near(values)
    return near + [hop(piece, "seq", 1) for piece in near]


def scatter_seq(near, far):
    chips = lax.axis_size("seq") // 2
    rows = near.shape[0] // chips
    moved = hop(far, "seq", 1)

    def both(m):
        at = slice(m * rows, (m + 1) * rows)
        return near[at].astype(F32) + moved[at].astype(F32)

    sent = [both(m).astype(BF16) for m in range(1, chips)]
    total = both(0)
    for m in range(1, chips):
        total = total + hop(sent[m - 1], "seq", 2 * m).astype(F32)
    return total, sent


def gather_batch(values):
    pieces = [values]
    for t in range(1, lax.axis_size("batch")):
        pieces.append(hop(pieces[t - 1], "batch", 1) if t % 2 and t > 1 else hop(values, "batch", t))
    return pieces


def scatter_batch(blocks, me, kind, *pins):
    size = blocks.shape[0]
    if size == 1:
        return blocks[0].astype(F32)
    theirs = jnp.stack([take_block(blocks, me ^ t ^ 1) for t in range(0, size, 2)])
    moved = after(hop(theirs, "batch", 1), pins[0])
    total = take_block(blocks, me).astype(F32) + moved[0].astype(F32)
    for i in range(1, size // 2):
        pair = take_block(blocks, me ^ (2 * i)).astype(F32) + moved[i].astype(F32)
        total = total + after(hop(pair.astype(kind), "batch", 2 * i), pins[1]).astype(F32)
    return total


def piece_copies(refs, block, per, buffer, slot, sems, first):
    rows = buffer.shape[1] // per
    return [
        pltpu.make_async_copy(
            refs[block * per + i],
            buffer.at[slot, pl.ds(i * rows, rows), :],
            sems.at[slot, first + i],
        )
        for i in range(per)
    ]


def stream(blocks, copies_of):
    step = pl.program_id(0)
    for block in range(blocks):

        @pl.when(step == block)
        def _():
            if block == 0:
                for copy in copies_of(0):
                    copy.start()
            if block + 1 < blocks:
                for copy in copies_of(block + 1):
                    copy.start()
            for copy in copies_of(block):
                copy.wait()


def weight_copies(at_ref, pieces, target, sems):
    return [
        pltpu.make_async_copy(piece, target.at[:, at_ref[1] ^ t], sems.at[t])
        for t, piece in enumerate(pieces)
    ]


def project_pairs_kernel(blocks, per, at_ref, *refs):
    count = blocks * per
    pieces, w_pieces = refs[:count], refs[count : -8]
    gain_ref, normed_ref, pair_ref, square_ref, weight_ref, buffer, sems, w_sems = refs[-8:]
    step = pl.program_id(0)

    @pl.when(step == 0)
    def _():
        for copy in weight_copies(at_ref, w_pieces, weight_ref, w_sems):
            copy.start()

    stream(blocks, lambda block: piece_copies(pieces, block, per, buffer, block % 2, sems, 0))

    @pl.when(step == 0)
    def _():
        for copy in weight_copies(at_ref, w_pieces, weight_ref, w_sems):
            copy.wait()

    values = buffer[step % 2].astype(F32)
    normed = (values * norm_scale(values) * gain_ref[...]).astype(BF16)
    normed_ref[...] = normed
    width = normed.shape[1]
    pair = dot(normed, weight_ref[...].reshape(width, -1))
    pair_ref[...] = pair
    wide = pair.shape[1] // 2
    squared = pair * pair
    high = squared.astype(BF16)
    low = (squared - high.astype(F32)).astype(BF16)
    lane = lax.broadcasted_iota(jnp.int32, (8, 2 * wide), 1)
    line = lax.broadcasted_iota(jnp.int32, (8, 2 * wide), 0)
    pick = (lane // wide == line).astype(BF16)
    sums = (dot_nt(pick, high) + dot_nt(pick, low))[:2]
    rows = normed.shape[0] // per
    for i in range(per):
        at = pl.multiple_of(at_ref[2 + step * per + i] * rows, rows)
        square_ref[:, pl.ds(at, rows)] = sums[:, i * rows : (i + 1) * rows]


def project_pairs(here, pieces, w_pieces, gain):
    rows, width = pieces[0].shape
    seq_size, shard, columns = w_pieces[0].shape
    batch_size = len(w_pieces)
    per = max(1, 256 // rows)
    blocks = len(pieces) // per
    total, size = rows * len(pieces), rows * per
    return pl.pallas_call(
        functools.partial(project_pairs_kernel, blocks, per),
        grid_spec=pltpu.PrefetchScalarGridSpec(
            num_scalar_prefetch=1,
            grid=(blocks,),
            in_specs=[pl.BlockSpec(memory_space=pl.ANY)] * (len(pieces) + batch_size)
            + [pl.BlockSpec((1, width), lambda i, at: (0, 0))],
            out_specs=[
                pl.BlockSpec((size, width), lambda i, at: (i, 0)),
                pl.BlockSpec((size, columns), lambda i, at: (i, 0)),
                pl.BlockSpec((2, total), lambda i, at: (0, 0)),
                pl.BlockSpec((seq_size, batch_size, shard, columns), lambda i, at: (0, 0, 0, 0)),
            ],
            scratch_shapes=[
                pltpu.VMEM((2, size, width), BF16),
                pltpu.SemaphoreType.DMA((2, per)),
                pltpu.SemaphoreType.DMA((batch_size,)),
            ],
        ),
        out_shape=[
            jax.ShapeDtypeStruct((total, width), BF16),
            jax.ShapeDtypeStruct((total, columns), F32),
            jax.ShapeDtypeStruct((2, total), F32),
            jax.ShapeDtypeStruct((seq_size, batch_size, shard, columns), BF16),
        ],
        compiler_params=pltpu.CompilerParams(vmem_limit_bytes=VMEM_BYTES),
        cost_estimate=pl.CostEstimate(
            flops=2 * total * width * columns, bytes_accessed=8 * total * width, transcendentals=0
        ),
    )(here, *pieces, *w_pieces, gain)


def project_values_kernel(at_ref, normed_ref, *refs):
    *w_pieces, value_ref, weight_ref, w_sems = refs

    @pl.when(pl.program_id(0) == 0)
    def _():
        copies = weight_copies(at_ref, w_pieces, weight_ref, w_sems)
        for copy in copies:
            copy.start()
        for copy in copies:
            copy.wait()

    width = normed_ref.shape[1]
    value_ref[...] = dot(normed_ref[...], weight_ref[...].reshape(width, -1)).astype(BF16)


def project_values(here, normed, w_pieces):
    total, width = normed.shape
    seq_size, shard, columns = w_pieces[0].shape
    batch_size = len(w_pieces)
    size = min(512, total)
    return pl.pallas_call(
        project_values_kernel,
        grid_spec=pltpu.PrefetchScalarGridSpec(
            num_scalar_prefetch=1,
            grid=(total // size,),
            in_specs=[pl.BlockSpec((size, width), lambda i, at: (i, 0))]
            + [pl.BlockSpec(memory_space=pl.ANY)] * batch_size,
            out_specs=[
                pl.BlockSpec((size, columns), lambda i, at: (i, 0)),
                pl.BlockSpec((seq_size, batch_size, shard, columns), lambda i, at: (0, 0, 0, 0)),
            ],
            scratch_shapes=[pltpu.SemaphoreType.DMA((batch_size,))],
        ),
        out_shape=[
            jax.ShapeDtypeStruct((total, columns), BF16),
            jax.ShapeDtypeStruct((seq_size, batch_size, shard, columns), BF16),
        ],
        compiler_params=pltpu.CompilerParams(vmem_limit_bytes=VMEM_BYTES),
        cost_estimate=pl.CostEstimate(
            flops=2 * total * width * columns, bytes_accessed=2 * total * width, transcendentals=0
        ),
    )(here, normed, *w_pieces)


def mix_back_kernel(blocks, per, *refs):
    pieces = refs[: blocks * per]
    mixed_ref, weight_ref, back_ref, grad_ref, buffer, total, sems = refs[blocks * per :]
    step = pl.program_id(0)
    stream(blocks, lambda block: piece_copies(pieces, block, per, buffer, block % 2, sems, 0))
    gradient = buffer[step % 2]
    back_ref[...] = dot_nt(gradient, weight_ref[...]).astype(BF16)
    term = dot_tn(mixed_ref[...], gradient)

    @pl.when(step == 0)
    def _():
        total[...] = term

    @pl.when(step > 0)
    def _():
        total[...] += term

    @pl.when(step == blocks - 1)
    def _():
        grad_ref[...] = total[...].astype(BF16)


def mix_back(pieces, mixed, weight):
    rows, width = pieces[0].shape
    wide = weight.shape[0]
    per = max(1, 256 // rows)
    blocks = len(pieces) // per
    total, size = rows * len(pieces), rows * per
    return pl.pallas_call(
        functools.partial(mix_back_kernel, blocks, per),
        grid=(blocks,),
        in_specs=[pl.BlockSpec(memory_space=pl.ANY)] * len(pieces)
        + [
            pl.BlockSpec((size, wide), lambda i: (i, 0)),
            pl.BlockSpec((wide, width), lambda i: (0, 0)),
        ],
        out_specs=[
            pl.BlockSpec((size, wide), lambda i: (i, 0)),
            pl.BlockSpec((wide, width), lambda i: (0, 0)),
        ],
        out_shape=[
            jax.ShapeDtypeStruct((total, wide), BF16),
            jax.ShapeDtypeStruct((wide, width), BF16),
        ],
        scratch_shapes=[
            pltpu.VMEM((2, size, width), BF16),
            pltpu.VMEM((wide, width), F32),
            pltpu.SemaphoreType.DMA((2, per)),
        ],
        compiler_params=pltpu.CompilerParams(vmem_limit_bytes=VMEM_BYTES),
        cost_estimate=pl.CostEstimate(
            flops=4 * total * width * wide, bytes_accessed=4 * total * width, transcendentals=0
        ),
    )(*pieces, mixed, weight)


def load_heads(place, blocks, refs, tables, queries, keys, values):
    q_ref, k_ref, v_ref, scale_ref, gain_ref = refs
    cos_ref, sin_ref = tables
    rows = q_ref.shape[0] // blocks
    for a in range(blocks):
        at = pl.ds(pl.multiple_of(place[a] * rows, rows), rows)
        to = slice(a * rows, (a + 1) * rows)
        for i, (source, target) in enumerate(((q_ref, queries), (k_ref, keys))):
            normed = source[at, :] * scale_ref[to, i : i + 1] * gain_ref[i : i + 1, :]
            turned = pltpu.roll(normed, HEAD_DIM // 2, 1)
            target[to, :] = (normed * cos_ref[to, :] + turned * sin_ref[to, :]).astype(BF16)
        values[to, :] = v_ref[at, :]


def raised_scores(queries, keys, row_ref, col_ref, start, size, factor):
    stop = start + size
    scores = dot_nt(queries[start:stop, :], keys[:stop, :]) * factor
    query_at = lax.broadcasted_iota(jnp.int32, (size, stop), 0) + start
    key_at = lax.broadcasted_iota(jnp.int32, (size, stop), 1)
    allowed = (key_at <= query_at) & (row_ref[start:stop, :] == col_ref[:, :stop])
    scores = jnp.where(allowed, scores, MASKED)
    raised = jnp.exp(scores - jnp.max(scores, axis=-1, keepdims=True))
    return raised, jnp.sum(raised, axis=-1, keepdims=True)


def attend_kernel(
    blocks, size, place, q_ref, k_ref, v_ref, scale_ref, gain_ref, cos_ref, sin_ref, row_ref, col_ref,
    out_ref, queries, keys, values,
):
    total = q_ref.shape[0]
    rows = total // blocks
    refs, tables = (q_ref, k_ref, v_ref, scale_ref, gain_ref), (cos_ref, sin_ref)
    load_heads(place, blocks, refs, tables, queries, keys, values)
    factor = 1.0 / math.sqrt(HEAD_DIM)
    for start in range(0, total, size):
        raised, sums = raised_scores(queries, keys, row_ref, col_ref, start, size, factor)
        mixed = dot(raised.astype(BF16), values[: start + size, :]) / sums
        for i in range(size // rows):
            at = pl.multiple_of(place[start // rows + i] * rows, rows)
            out_ref[pl.ds(at, rows), :] = mixed[i * rows : (i + 1) * rows].astype(BF16)


def attend_back_kernel(
    blocks, size, place, q_ref, k_ref, v_ref, scale_ref, gain_ref, cos_ref, sin_ref, row_ref, col_ref,
    grad_ref, gq_ref, gk_ref, gv_ref, inner_ref, gain_grad_ref, queries, keys, values, key_sum, value_sum,
):
    total = q_ref.shape[0]
    rows = total // blocks
    refs, tables = (q_ref, k_ref, v_ref, scale_ref, gain_ref), (cos_ref, sin_ref)
    load_heads(place, blocks, refs, tables, queries, keys, values)
    factor = 1.0 / math.sqrt(HEAD_DIM)
    key_sum[...] = jnp.zeros_like(key_sum)
    value_sum[...] = jnp.zeros_like(value_sum)
    gain_rows = [jnp.zeros((1, HEAD_DIM), F32), jnp.zeros((1, HEAD_DIM), F32)]

    def finish(i, a, gradient, target):
        at = pl.ds(pl.multiple_of(place[a] * rows, rows), rows)
        to = slice(a * rows, (a + 1) * rows)
        turned = pltpu.roll(gradient, HEAD_DIM // 2, 1)
        normed = gradient * cos_ref[to, :] - turned * sin_ref[to, :]
        unit = (q_ref, k_ref)[i][at, :] * scale_ref[to, i : i + 1]
        scaled = normed * gain_ref[i : i + 1, :]
        target[at, :] = scaled
        inner_ref[to, i : i + 1] += jnp.sum(scaled * unit, axis=-1, keepdims=True)
        gain_rows[i] += jnp.sum(normed * unit, axis=0, keepdims=True)

    @pl.when(pl.program_id(0) == 0)
    def _():
        inner_ref[...] = jnp.zeros_like(inner_ref)

    for start in range(0, total, size):
        stop = start + size
        raised, sums = raised_scores(queries, keys, row_ref, col_ref, start, size, factor)
        probs = raised * (1.0 / sums)
        pieces = []
        for i in range(size // rows):
            at = pl.multiple_of(place[start // rows + i] * rows, rows)
            pieces.append(grad_ref[pl.ds(at, rows), :])
        grad_mixed = jnp.concatenate(pieces, axis=0) if len(pieces) > 1 else pieces[0]
        grad_weights = dot_nt(grad_mixed, values[:stop, :])
        delta = jnp.sum(probs * grad_weights, axis=-1, keepdims=True)
        grad_scores = (probs * (grad_weights - delta)).astype(BF16)
        grad_queries = dot(grad_scores, keys[:stop, :]) * factor
        key_sum[:stop, :] += dot_tn(grad_scores, queries[start:stop, :])
        value_sum[:stop, :] += dot_tn(probs.astype(BF16), grad_mixed)
        for i in range(size // rows):
            finish(0, start // rows + i, grad_queries[i * rows : (i + 1) * rows], gq_ref)
    for a in range(blocks):
        to = slice(a * rows, (a + 1) * rows)
        finish(1, a, key_sum[to, :] * factor, gk_ref)
        gv_ref[pl.ds(pl.multiple_of(place[a] * rows, rows), rows), :] = value_sum[to, :].astype(BF16)
    gain_grad_ref[0:1, :] = gain_rows[0]
    gain_grad_ref[1:2, :] = gain_rows[1]


def attention(place, pairs, values, scales, gains, tables, row_docs, col_docs, grad_mixed=None):
    total = pairs.shape[0]
    blocks = place.shape[0]
    heads = values.shape[1] // HEAD_DIM
    size = max(256, total // blocks)
    whole = lambda h: (0, 0)
    column = lambda h: (0, h)
    in_specs = [
        pl.BlockSpec(memory_space=pltpu.SMEM),
        pl.BlockSpec((total, HEAD_DIM), lambda h: (0, h)),
        pl.BlockSpec((total, HEAD_DIM), lambda h: (0, heads + h)),
        pl.BlockSpec((total, HEAD_DIM), column),
        pl.BlockSpec((total, 2), whole),
        pl.BlockSpec((2, HEAD_DIM), column),
        pl.BlockSpec((total, HEAD_DIM), whole),
        pl.BlockSpec((total, HEAD_DIM), whole),
        pl.BlockSpec((total, 1), whole),
        pl.BlockSpec((1, total), whole),
    ]
    operands = [place, pairs, pairs, values, scales, gains, *tables, row_docs, col_docs]
    held = [pltpu.VMEM((total, HEAD_DIM), BF16)] * 3
    params = pltpu.CompilerParams(vmem_limit_bytes=VMEM_BYTES)
    work = total * total * HEAD_DIM * heads
    if grad_mixed is None:
        return pl.pallas_call(
            functools.partial(attend_kernel, blocks, size),
            grid=(heads,),
            in_specs=in_specs,
            out_specs=pl.BlockSpec((total, HEAD_DIM), column),
            out_shape=jax.ShapeDtypeStruct((total, heads * HEAD_DIM), BF16),
            scratch_shapes=held,
            compiler_params=params,
            cost_estimate=pl.CostEstimate(
                flops=4 * work, bytes_accessed=pairs.size * 8, transcendentals=total * total
            ),
        )(*operands)
    return pl.pallas_call(
        functools.partial(attend_back_kernel, blocks, size),
        grid=(heads,),
        in_specs=in_specs + [pl.BlockSpec((total, HEAD_DIM), column)],
        out_specs=[pl.BlockSpec((total, HEAD_DIM), column)] * 3
        + [pl.BlockSpec((total, 2), whole), pl.BlockSpec((2, HEAD_DIM), column)],
        out_shape=[
            jax.ShapeDtypeStruct((total, heads * HEAD_DIM), F32),
            jax.ShapeDtypeStruct((total, heads * HEAD_DIM), F32),
            jax.ShapeDtypeStruct((total, heads * HEAD_DIM), BF16),
            jax.ShapeDtypeStruct((total, 2), F32),
            jax.ShapeDtypeStruct((2, heads * HEAD_DIM), F32),
        ],
        scratch_shapes=held + [pltpu.VMEM((total, HEAD_DIM), F32)] * 2,
        compiler_params=params,
        cost_estimate=pl.CostEstimate(
            flops=10 * work, bytes_accessed=pairs.size * 16, transcendentals=total * total
        ),
    )(*operands, grad_mixed)


def router_chances(inputs, router, experts):
    logits = dot(inputs, router)
    column = lax.broadcasted_iota(jnp.int32, logits.shape, 1)
    logits = jnp.where(column < experts, logits, MASKED)
    raised = jnp.exp(logits - jnp.max(logits, axis=-1, keepdims=True))
    return raised / jnp.sum(raised, axis=-1, keepdims=True)


def acts_kernel(experts, blocks, per, k, at_ref, *refs):
    count = blocks * per
    pieces = refs[:count]
    (
        side_ref, router_ref, wg_ref, wu_ref, wd_ref,
        x_out, u_out, hidden_ref, gate_grad_ref, up_grad_ref, sums_ref, x_buffer, u_buffer, sems,
    ) = refs[count:]
    step = pl.program_id(0)
    sides = [side_ref.at[at_ref[2 + r], k] for r in range(count)]

    def copies_of(block):
        slot = block % 2
        return piece_copies(pieces, block, per, x_buffer, slot, sems, 0) + piece_copies(
            sides, block, per, u_buffer, slot, sems, per
        )

    stream(blocks, copies_of)
    owned, width, _ = wg_ref.shape
    inputs, upstream = x_buffer[step % 2], u_buffer[step % 2, :, :width]
    chosen = u_buffer[step % 2, :, width:].astype(F32)
    x_out[...] = inputs
    u_out[...] = upstream
    gates = router_chances(inputs, router_ref[...], experts) * chosen
    gate_at = lax.broadcasted_iota(jnp.int32, gates.shape, 1)
    column = lax.broadcasted_iota(jnp.int32, sums_ref.shape, 1)
    sums = jnp.zeros(sums_ref.shape, F32)
    for e in range(owned):
        gate_act = dot(inputs, wg_ref[e])
        up_act = dot(inputs, wu_ref[e])
        grad_raw = dot_nt(upstream, wd_ref[e])
        expert = at_ref[0] * owned + e
        gate = jnp.sum(jnp.where(gate_at == expert, gates, 0.0), axis=-1, keepdims=True)
        sigma = jax.nn.sigmoid(gate_act)
        active = gate_act * sigma
        hidden = active * up_act
        grad_gate = jnp.sum(hidden * grad_raw, axis=-1, keepdims=True)
        high = grad_gate.astype(BF16).astype(F32)
        sums = jnp.where(column == expert, high, sums)
        sums = jnp.where(column == expert + experts, grad_gate - high, sums)
        grad_hidden = grad_raw * gate
        hidden_ref[e] = (hidden * gate).astype(BF16)
        gate_grad_ref[e] = (grad_hidden * up_act * sigma * (1.0 + gate_act * (1.0 - sigma))).astype(BF16)
        up_grad_ref[e] = (grad_hidden * active).astype(BF16)
    sums_ref[...] = sums.astype(BF16)


def run_acts(at, pieces, sides, k, router, w_gate, w_up, w_down, experts, parts):
    rows, width = pieces[0].shape
    total = rows * len(pieces)
    owned, _, hidden = w_gate.shape
    piece = hidden // parts
    per = max(1, 256 // rows)
    blocks, size = len(pieces) // per, rows * per
    extra = 128 * -(-2 * experts // 128)
    lanes = router.shape[1]
    token = lambda i, at: (i, 0)
    once = pl.Buffered(1)
    acts = jax.ShapeDtypeStruct((owned, total, piece), BF16)
    act_spec = pl.BlockSpec((owned, size, piece), lambda i, at: (0, i, 0))
    return pl.pallas_call(
        functools.partial(acts_kernel, experts, blocks, per, k),
        grid_spec=pltpu.PrefetchScalarGridSpec(
            num_scalar_prefetch=1,
            grid=(blocks,),
            in_specs=[pl.BlockSpec(memory_space=pl.ANY)] * (len(pieces) + 1)
            + [
                pl.BlockSpec((width, lanes), lambda i, at: (0, 0), pipeline_mode=once),
                pl.BlockSpec((owned, width, piece), lambda i, at: (0, 0, at[1]), pipeline_mode=once),
                pl.BlockSpec((owned, width, piece), lambda i, at: (0, 0, at[1]), pipeline_mode=once),
                pl.BlockSpec((owned, piece, width), lambda i, at: (0, at[1], 0), pipeline_mode=once),
            ],
            out_specs=[pl.BlockSpec((size, width), token)] * 2
            + [act_spec] * 3
            + [pl.BlockSpec((size, extra), token)],
            scratch_shapes=[
                pltpu.VMEM((2, size, width), BF16),
                pltpu.VMEM((2, size, width + lanes), BF16),
                pltpu.SemaphoreType.DMA((2, 2 * per)),
            ],
        ),
        out_shape=[
            jax.ShapeDtypeStruct((total, width), BF16),
            jax.ShapeDtypeStruct((total, width), BF16),
            acts,
            acts,
            acts,
            jax.ShapeDtypeStruct((total, extra), BF16),
        ],
        compiler_params=pltpu.CompilerParams(vmem_limit_bytes=VMEM_BYTES),
        cost_estimate=pl.CostEstimate(
            flops=6 * total * width * piece * owned,
            bytes_accessed=2 * (4 * total * width + 3 * owned * piece * (total + width)),
            transcendentals=total * piece * owned,
        ),
    )(at, *pieces, sides, router, w_gate, w_up, w_down)


def split_store(values, near_ref, far_ref):
    middle = pl.num_programs(0) // 2

    @pl.when(pl.program_id(0) < middle)
    def _():
        near_ref[...] = values

    @pl.when(pl.program_id(0) >= middle)
    def _():
        far_ref[...] = values


def rows_back_kernel(at_ref, gate_ref, up_ref, sums_ref, wg_ref, wu_ref, near_ref, far_ref):
    back = dot_nt(gate_ref[0], wg_ref[0]) + dot_nt(up_ref[0], wu_ref[0])
    for e in range(1, wg_ref.shape[0]):
        back += dot_nt(gate_ref[e], wg_ref[e]) + dot_nt(up_ref[e], wu_ref[e])
    split_store(jnp.concatenate([back.astype(BF16), sums_ref[...]], axis=1), near_ref, far_ref)


def rows_out_kernel(sets, blocks, per, at_ref, *refs):
    *hidden_refs, wd_ref, out_ref = refs
    step = pl.program_id(0)
    rows = out_ref.shape[4]
    for k, hidden_ref in enumerate(hidden_refs):

        @pl.when(step // blocks == k)
        def _():
            out = dot(hidden_ref[0], wd_ref[0])
            for e in range(1, wd_ref.shape[0]):
                out += dot(hidden_ref[e], wd_ref[e])
            for i in range(per):
                at = at_ref[2 + (step - k * blocks) * per + i] // 2 % per
                out_ref[0, at, 0, 0] = out[i * rows : (i + 1) * rows].astype(BF16)


def run_out(at, hiddens, w_down, rows):
    owned, total, piece = hiddens[0].shape
    sets, width = len(hiddens), w_down.shape[2]
    seq_size = total // rows
    per = max(1, 256 // rows)
    size, blocks = rows * per, seq_size // per

    def hidden_at(k):
        return lambda i, at: (0, jnp.clip(i - k * blocks, 0, blocks - 1), 0)

    def out_at(i, at):
        first = at[2 + (i % blocks) * per]
        return (first // (2 * per), 0, first % 2, i // blocks, 0, 0)

    out = pl.pallas_call(
        functools.partial(rows_out_kernel, sets, blocks, per),
        grid_spec=pltpu.PrefetchScalarGridSpec(
            num_scalar_prefetch=1,
            grid=(sets * blocks,),
            in_specs=[pl.BlockSpec((owned, size, piece), hidden_at(k)) for k in range(sets)]
            + [
                pl.BlockSpec(
                    (owned, piece, width), lambda i, at: (0, at[1], 0), pipeline_mode=pl.Buffered(1)
                )
            ],
            out_specs=pl.BlockSpec((1, per, 1, 1, rows, width), out_at),
        ),
        out_shape=jax.ShapeDtypeStruct((seq_size // (2 * per), per, 2, sets, rows, width), BF16),
        compiler_params=pltpu.CompilerParams(vmem_limit_bytes=VMEM_BYTES),
        cost_estimate=pl.CostEstimate(
            flops=2 * sets * total * width * piece * owned,
            bytes_accessed=2 * sets * total * (width + owned * piece),
            transcendentals=0,
        ),
    )(at, *hiddens, w_down)
    return out.reshape(seq_size, sets, rows, width)


def run_back(at, gates, ups, sums, w_gate, w_up):
    owned, total, piece = gates.shape
    size = min(256, total // 2)
    middle = total // (2 * size)
    width, extra = w_gate.shape[1], sums.shape[1]
    act_spec = pl.BlockSpec((owned, size, piece), lambda i, at: (0, i, 0))
    weight_spec = pl.BlockSpec(
        (owned, width, piece), lambda i, at: (0, 0, at[1]), pipeline_mode=pl.Buffered(1)
    )
    out = jax.ShapeDtypeStruct((total // 2, width + extra), BF16)
    return pl.pallas_call(
        rows_back_kernel,
        grid_spec=pltpu.PrefetchScalarGridSpec(
            num_scalar_prefetch=1,
            grid=(total // size,),
            in_specs=[act_spec] * 2
            + [pl.BlockSpec((size, extra), lambda i, at: (i, 0))]
            + [weight_spec] * 2,
            out_specs=[
                pl.BlockSpec((size, width + extra), lambda i, at: (jnp.minimum(i, middle - 1), 0)),
                pl.BlockSpec((size, width + extra), lambda i, at: (jnp.maximum(i - middle, 0), 0)),
            ],
        ),
        out_shape=[out, out],
        compiler_params=pltpu.CompilerParams(vmem_limit_bytes=VMEM_BYTES),
        cost_estimate=pl.CostEstimate(
            flops=4 * total * width * piece * owned,
            bytes_accessed=2 * (total * width + 2 * owned * piece * (total + width)),
            transcendentals=0,
        ),
    )(at, gates, ups, sums, w_gate, w_up)


def down_kernel(sets, at_ref, *refs):
    out_ref = refs[-1]
    for e in range(out_ref.shape[1]):
        term = dot_tn(refs[0][e], refs[sets][...])
        for i in range(1, sets):
            term += dot_tn(refs[i][e], refs[sets + i][...])
        out_ref[0, e] = term.astype(BF16)


def down_blocks(targets, hiddens, upstreams, group, width):
    owned, total, piece = hiddens[0].shape
    deep = piece // group
    sets, count = len(hiddens), targets.shape[0]
    wide = min(512, width)
    return pl.pallas_call(
        functools.partial(down_kernel, sets),
        grid_spec=pltpu.PrefetchScalarGridSpec(
            num_scalar_prefetch=1,
            grid=(count, width // wide),
            in_specs=[pl.BlockSpec((owned, total, deep), lambda g, j, at: (0, 0, at[g]))] * sets
            + [pl.BlockSpec((total, wide), lambda g, j, at: (0, j))] * sets,
            out_specs=pl.BlockSpec((1, owned, deep, wide), lambda g, j, at: (g, 0, 0, j)),
        ),
        out_shape=jax.ShapeDtypeStruct((count, owned, deep, width), BF16),
        compiler_params=pltpu.CompilerParams(vmem_limit_bytes=VMEM_BYTES),
        cost_estimate=pl.CostEstimate(
            flops=2 * sets * count * owned * total * deep * width,
            bytes_accessed=2 * sets * total * (width + owned * deep),
            transcendentals=0,
        ),
    )(targets, *hiddens, *upstreams)


def in_kernel(sets, at_ref, *refs):
    out_ref = refs[-1]
    for e in range(out_ref.shape[2]):
        term = dot_tn(refs[0][...], refs[sets][e])
        for i in range(1, sets):
            term += dot_tn(refs[i][...], refs[sets + i][e])
        out_ref[0, 0, e] = term.astype(BF16)


def in_blocks(targets, inputs, acts, group, parts):
    owned, total, piece = acts[0].shape
    width = inputs[0].shape[1]
    deep = width // (group * parts)
    sets, count = len(inputs), targets.shape[0]
    held = pl.BlockSpec((owned, total, piece), lambda g, p, at: (0, 0, 0), pipeline_mode=pl.Buffered(1))
    return pl.pallas_call(
        functools.partial(in_kernel, sets),
        grid_spec=pltpu.PrefetchScalarGridSpec(
            num_scalar_prefetch=1,
            grid=(count, parts),
            in_specs=[pl.BlockSpec((total, deep), lambda g, p, at: (0, p * group + at[g]))] * sets
            + [held] * sets,
            out_specs=pl.BlockSpec((1, 1, owned, deep, piece), lambda g, p, at: (g, p, 0, 0, 0)),
        ),
        out_shape=jax.ShapeDtypeStruct((count, parts, owned, deep, piece), BF16),
        compiler_params=pltpu.CompilerParams(vmem_limit_bytes=VMEM_BYTES),
        cost_estimate=pl.CostEstimate(
            flops=2 * sets * count * parts * owned * total * deep * piece,
            bytes_accessed=4 * sets * owned * total * piece,
            transcendentals=0,
        ),
    )(targets, *inputs, *acts)


def on_device(
    tokens,
    segments,
    expert_ids,
    w_query,
    w_key,
    w_value,
    w_out,
    w_router,
    attn_gain,
    query_gain,
    key_gain,
    ffn_gain,
    w_gate,
    w_up,
    w_down,
    out_grad,
):
    seq_size, batch_size = lax.axis_size("seq"), lax.axis_size("batch")
    seq_at, batch_at = lax.axis_index("seq"), lax.axis_index("batch")
    parts = 2 if batch_size % 2 == 0 else 1
    half = batch_size // parts
    part_at, in_group = batch_at // half, batch_at % half
    low_tokens = tokens[0]
    inputs = low_tokens.astype(F32)
    rows, width = inputs.shape
    total = rows * seq_size
    experts = w_router.shape[1]
    owned = w_gate.shape[0]
    wide = width // seq_size
    shard = w_query.shape[0]

    masks = masks_of(seq_size)
    order = seq_at ^ jnp.array(masks, jnp.int32)
    place = jnp.array([masks.index(m) for m in range(seq_size)], jnp.int32)[
        jnp.arange(seq_size, dtype=jnp.int32) ^ seq_at
    ]

    def reordered(values, by):
        return values.reshape(-1, seq_size, rows)[:, by].reshape(values.shape)

    masks = masks_of(seq_size)
    order = seq_at ^ jnp.array(masks, jnp.int32)
    place = jnp.array([masks.index(m) for m in range(seq_size)], jnp.int32)[
        jnp.arange(seq_size, dtype=jnp.int32) ^ seq_at
    ]
    here = jnp.concatenate([jnp.stack([seq_at, batch_at]).astype(jnp.int32), order])

    def reordered(values, by):
        return values.reshape(-1, seq_size, rows)[:, by].reshape(values.shape)

    masks = masks_of(seq_size)
    order = seq_at ^ jnp.array(masks, jnp.int32)
    place = jnp.array([masks.index(m) for m in range(seq_size)], jnp.int32)[
        jnp.arange(seq_size, dtype=jnp.int32) ^ seq_at
    ]
    here = jnp.concatenate([jnp.stack([seq_at, batch_at]).astype(jnp.int32), order])
    at = jnp.concatenate([jnp.stack([seq_at, part_at]).astype(jnp.int32), order])

    def reordered(values, by):
        return values.reshape(-1, seq_size, rows)[:, by].reshape(values.shape)

    near_tokens = gather_near(low_tokens)

    def columns_of(*weights):
        cut = [w.reshape(shard, seq_size, wide).transpose(1, 0, 2) for w in weights]
        return lax.all_to_all(jnp.concatenate(cut, axis=2), "seq", split_axis=0, concat_axis=0, tiled=True)

    pair_cut = columns_of(w_query, w_key)

    lanes = 128 * -(-(experts + 4) // 128)
    gains = jnp.stack([attn_gain, query_gain, key_gain, ffn_gain], axis=1)
    small = jnp.zeros((shard, lanes), BF16)
    small = put(put(small, w_router, (0, 0)), gains, (0, experts))
    small = lax.all_gather(small, "batch", axis=0, tiled=True)
    router = lax.all_gather(small, "seq", axis=0, tiled=True)
    gains = router[:, experts : experts + 4].astype(F32).T
    attn_norm_gain, ffn_norm_gain = gains[0], gains[3]
    head_gains = lax.dynamic_slice_in_dim(gains[1:3], seq_at * wide, wide, 1)

    pair_pieces = gather_batch(after(pair_cut, router))
    value_cut = columns_of(after(w_value, pair_cut))
    value_pieces = gather_batch(after(value_cut, *pair_pieces[2:3]))
    token_pieces = near_tokens + [hop(piece, "seq", 1) for piece in near_tokens]
    w_mix = jnp.zeros((batch_size, shard, width), BF16)
    for t, piece in enumerate(gather_batch(after(w_out, *value_pieces[2:3]))):
        w_mix = put(w_mix, piece[None], (batch_at ^ t, 0, 0))
    w_mix = w_mix.reshape(wide, width)

    ids = expert_ids[0]
    choices = jnp.any(ids[:, :, None] == jnp.arange(lanes, dtype=jnp.int32), axis=1)
    side = jnp.concatenate([out_grad[0], choices.astype(BF16)], axis=1)
    sides = jnp.stack([side] + ([hop(side, "batch", half)] if parts == 2 else []))
    sides = lax.all_gather(after(sides, *near_tokens), "seq", axis=0)
    counts = jnp.sum(sides[:, 0, :, width:].astype(F32), axis=(0, 1)).astype(jnp.int32)
    counts_here = lax.dynamic_slice_in_dim(counts, seq_at * owned, owned, 0)

    normed, pairs, squares, pair_weights = project_pairs(
        here, token_pieces, pair_pieces, attn_norm_gain[None]
    )
    values, value_weights = project_values(here, normed, value_pieces)
    pair_weights, value_weights = (w.reshape(width, -1) for w in (pair_weights, value_weights))

    def sum_seq(values):
        return jnp.sum(lax.all_gather(values, "seq", axis=0), axis=0)

    scales = lax.rsqrt(sum_seq(squares) / width + EPSILON)
    rates = jnp.power(
        ROTARY_BASE, -jnp.arange(HEAD_DIM // 2, dtype=F32) * (2.0 / HEAD_DIM)
    )
    angles = jnp.arange(total, dtype=F32)[:, None] * rates[None, :]
    cosine, sine = jnp.cos(angles), jnp.sin(angles)
    tables = (
        jnp.concatenate([cosine, cosine], axis=1),
        jnp.concatenate([-sine, sine], axis=1),
    )
    attend = functools.partial(
        attention,
        place,
        pairs,
        values,
        scales.T,
        head_gains,
        tables,
        segments[0][:, None],
        segments[0][None, :],
    )
    mixed_low = attend()
    middle = total // 2
    far = dot(mixed_low[middle:], w_mix).astype(BF16)
    residual = inputs + scatter_seq(dot(mixed_low[:middle], w_mix).astype(BF16), far)[0]
    ffn_scale = norm_scale(residual)
    ffn_unit = residual * ffn_scale
    ffn_in = (ffn_unit * ffn_norm_gain).astype(BF16)

    def acts_of(k, pieces):
        return run_acts(at, pieces, sides, k, router, w_gate, w_up, w_down, experts, parts)

    ffn_pieces = gather_seq(ffn_in)
    results = [acts_of(0, ffn_pieces)]
    if parts == 2:
        partner = hop(ffn_in, "batch", half)
        near = gather_near(after(partner, *ffn_pieces))
        near = [after(piece, results[0][0]) for piece in near]
        results.append(acts_of(1, near + [hop(piece, "seq", 1) for piece in near]))
    all_ffn, upstreams, hiddens, gate_acts, up_acts, sums = zip(*results)
    own = in_group[None].astype(jnp.int32)
    others = jnp.stack([in_group ^ t for t in range(1, half)]).astype(jnp.int32) if half > 1 else None
    down = functools.partial(down_blocks, hiddens=hiddens, upstreams=upstreams, group=half, width=width)
    into = functools.partial(in_blocks, inputs=all_ffn, group=half, parts=parts)

    def send_group(theirs):
        return [hop(theirs[t - 1], "batch", t) for t in range(1, half)]

    def group_sum(mine, moved):
        total = mine[0].astype(F32)
        for item in moved:
            total = total + item.astype(F32)
        return total

    def swap_part(summed):
        return hop(take_block(summed, 1 - part_at).astype(BF16), "batch", half)

    gate_moved = up_moved = down_moved = ()
    at_back = at
    if half > 1:
        gate_theirs = into(others, acts=gate_acts)
        gate_moved = send_group(gate_theirs)
        at_back = after(at, gate_theirs)
    backs, sent = [], []
    for k in reversed(range(parts)):
        pair = run_back(at_back, gate_acts[k], up_acts[k], sums[k], w_gate, w_up)
        summed, low = scatter_seq(*pair)
        backs.insert(0, summed)
        sent += low
        at_back = after(at, *pair)
    back = backs[0]
    if parts == 2:
        back = back + hop(backs[1].astype(BF16), "batch", half).astype(F32)

    grad_ffn_in = back[:, :width]
    grad_chances = choices[:, :experts] * (
        back[:, width : width + experts] + back[:, width + experts : width + 2 * experts]
    )
    chances = router_chances(ffn_in, router, experts)[:, :experts]
    grad_logits = (
        chances * (grad_chances - jnp.sum(chances * grad_chances, axis=-1, keepdims=True))
    ).astype(BF16)
    grad_ffn_in = grad_ffn_in + dot_nt(grad_logits, router[:, :experts])
    scaled = grad_ffn_in * ffn_norm_gain
    inner = jnp.mean(scaled * ffn_unit, axis=-1, keepdims=True)
    grad_residual = out_grad[0].astype(F32) + ffn_scale * (scaled - ffn_unit * inner)
    grad_attn = grad_residual.astype(BF16)

    later = own
    if half > 1:
        up_theirs = into(after(others, *sent), acts=up_acts)
        down_theirs = down(after(others, up_theirs))
        up_moved = send_group(after(up_theirs, grad_attn))
        later = after(own, down_theirs)
    mix = run_out(after(at, *sent, later), hiddens, w_down, rows)
    later = after(later, mix)
    gate_mine = into(later, acts=gate_acts)
    up_mine = into(later, acts=up_acts)
    down_mine = down(later)
    gate_sum = group_sum(gate_mine, [after(item, grad_attn) for item in gate_moved])
    gate_other = swap_part(gate_sum) if parts == 2 else None
    mix = lax.psum_scatter(mix, "seq", scatter_dimension=0)

    grad_pieces = gather_seq(grad_attn)
    grad_mixed, out_term = mix_back(grad_pieces, mixed_low, w_mix)
    scaled_q, scaled_k, value_low, inner, gain_terms = attend(grad_mixed=grad_mixed)
    inner = reordered(sum_seq(inner.T), order).T / width
    rel_scales = reordered(scales, order).T
    lows = []
    for i, item in enumerate((scaled_q, scaled_k)):
        scale = rel_scales[:, i : i + 1]
        unit = pairs[:, i * wide : (i + 1) * wide] * scale
        lows.append((scale * (item - unit * inner[:, i : i + 1])).astype(BF16))
    pair_low = jnp.concatenate(lows, axis=1)

    def rows_of(at):
        return (dot_nt(pair_low[at], pair_weights) + dot_nt(value_low[at], value_weights)).astype(BF16)

    far = rows_of(slice(middle, total))
    grad_normed, sent = scatter_seq(rows_of(slice(0, middle)), far)

    def head_sums(values):
        term = dot_tn(normed, values).astype(BF16).reshape(seq_size * batch_size, shard, -1)
        term = lax.all_to_all(term, ("seq", "batch"), split_axis=0, concat_axis=0, tiled=True)
        term = after(term, grad_normed).reshape(seq_size, batch_size, shard, -1)
        return jnp.sum(term.astype(F32), axis=1)

    value_sums = head_sums(value_low)
    pair_sums = head_sums(after(pair_low, far))
    query_grad, key_grad, value_grad = (
        item.transpose(1, 0, 2).reshape(shard, width)
        for item in (pair_sums[:, :, :wide], pair_sums[:, :, wide:], value_sums)
    )

    def spread(summed, other):
        if parts == 1:
            return summed[0]
        keep, other = take_block(summed, part_at), after(other, grad_normed).astype(F32)
        return jnp.where(
            part_at == 0,
            jnp.concatenate([keep, other], axis=-1),
            jnp.concatenate([other, keep], axis=-1),
        )

    up_sum = group_sum(up_mine, [after(item, value_low) for item in up_moved])
    up_other = swap_part(up_sum) if parts == 2 else None
    if half > 1:
        down_moved = [
            after(item, grad_normed) for item in send_group(after(down_theirs, value_low, *up_moved))
        ]
    down_grad = group_sum(down_mine, down_moved)
    gate_grad = spread(gate_sum, gate_other)
    up_grad = spread(up_sum, up_other)
    out_proj_grad = scatter_batch(
        out_term.reshape(batch_size, shard, width), batch_at, BF16, value_low, grad_normed
    )
    gain_blocks = gain_terms.reshape(2, batch_size, shard).transpose(1, 0, 2)
    gain_sum = scatter_batch(gain_blocks, batch_at, F32, pair_low, grad_normed)

    mine = mix[0].astype(F32)
    if parts == 2:
        mine = mine + after(hop(after(mix[1], value_low), "batch", half), grad_normed).astype(F32)
    block_out = (residual + mine).astype(BF16)

    router_term = jnp.concatenate(
        [dot_tn(grad_logits, ffn_in), jnp.sum(grad_ffn_in * ffn_unit, axis=0)[None]], axis=0
    )
    router_term = router_term.reshape(experts + 1, seq_size * batch_size, shard).transpose(1, 0, 2)
    router_sum = lax.all_to_all(router_term, ("seq", "batch"), split_axis=0, concat_axis=0, tiled=True)
    router_sum = jnp.sum(after(router_sum, value_low), axis=0)
    router_grad, ffn_gain_grad = router_sum[:experts].T, router_sum[experts]

    attn_scale = norm_scale(inputs)
    attn_unit = inputs * attn_scale
    scaled = grad_normed * attn_norm_gain
    inner = jnp.mean(scaled * attn_unit, axis=-1, keepdims=True)
    grad_input = grad_residual + attn_scale * (scaled - attn_unit * inner)
    attn_gain_grad = (
        jnp.sum(
            query_grad * w_query.astype(F32)
            + key_grad * w_key.astype(F32)
            + value_grad * w_value.astype(F32),
            axis=1,
        )
        / attn_gain.astype(F32)
    )
    return (
        block_out[None],
        grad_input[None],
        query_grad,
        key_grad,
        value_grad,
        out_proj_grad,
        router_grad,
        attn_gain_grad,
        gain_sum[0],
        gain_sum[1],
        ffn_gain_grad,
        gate_grad,
        up_grad,
        down_grad,
        counts_here[None],
    )


def solution(mesh):
    in_specs = (
        P("batch", "seq", None),
        P("batch", None),
        P("batch", "seq", None),
        P(("seq", "batch"), None),
        P(("seq", "batch"), None),
        P(("seq", "batch"), None),
        P(("seq", "batch"), None),
        P(("seq", "batch"), None),
        P(("seq", "batch")),
        P(("seq", "batch")),
        P(("seq", "batch")),
        P(("seq", "batch")),
        P("seq", None, None),
        P("seq", None, None),
        P("seq", None, None),
        P("batch", "seq", None),
    )
    out_specs = (
        P("batch", "seq", None),
        P("batch", "seq", None),
        P(("seq", "batch"), None),
        P(("seq", "batch"), None),
        P(("seq", "batch"), None),
        P(("seq", "batch"), None),
        P(("seq", "batch"), None),
        P(("seq", "batch")),
        P(("seq", "batch")),
        P(("seq", "batch")),
        P(("seq", "batch")),
        P("seq", "batch", None),
        P("seq", "batch", None),
        P("seq", "batch", None),
        P("batch", "seq"),
    )
    return jax.shard_map(
        on_device, mesh=mesh, in_specs=in_specs, out_specs=out_specs, check_vma=False
    )
```

time: 1290 us -> 720 us (0.56)
  waiting for transfers between devices: 573 us -> 258 us
  local copies, waits for them, and re-layouts: 237 us -> 29.5 us
  matrix products: 73.5 us -> 18.9 us
  blocking collectives: 0 us -> 45 us
  starting transfers between devices: 123 us -> 84.7 us
    ppermute x151 -> x66, waiting for transfers between devices: 573 us -> 240 us  [hop(): return lax.ppermute(values, axis, [(i, i ^ mask) for i in range(size)])]
    unnamed x341 -> x143, local copies, waits for them, and re-layouts: 99.4 us -> 9.93 us
    slice x58 -> x1, local copies, waits for them, and re-layouts: 67.8 us -> 0.62 us  [on_device(): scale = rel_scales[:, i:i + 1]]
    ppermute x151 -> x66, starting transfers between devices: 123 us -> 64.4 us  [hop(): return lax.ppermute(values, axis, [(i, i ^ mask) for i in range(size)])]
    dot_general x6 -> x0, matrix products: 45.1 us -> none  [over_tokens(): jnp.einsum(equation, left, right, preferred_element_type=F32)]
    all_gather x0 -> x4, blocking collectives: none -> 45 us  [the longest x2 18.5 us: sum_seq(): return jnp.sum(lax.all_gather(values, 'seq', axis=0), axis=0)]
    another operation x6 -> x2, local copies, waits for them, and re-layouts: 22.9 us -> 0.13 us  [the longest x1 0.11 us: on_device(): gains = jnp.stack([attn_gain, query_gain, key_gain, ffn_gain], axis=1)]
    all_to_all x0 -> x5, starting transfers between devices: none -> 20.2 us  [the longest x2 7.98 us: head_sums(): lax.all_to_all(term, ('seq', 'batch'), split_axis=0, concat_axis=0, tiled...]
  transfers between devices with their start and end apart: 151 -> 73, of which waited for: 71 -> 29; matrix products, arithmetic and copies ran while one was open for 28% -> 13% of each run, Pallas kernels for 16% -> 22%
where the time goes in v2:
time: 720 us; the launch traced here: 712 us
  waiting for transfers between devices  258 us (36%)
  Pallas kernels  204 us (28%)
  starting transfers between devices  84.7 us (12%)
  other arithmetic  56.8 us (8%)
  blocking collectives  45 us (6%)
  local copies, waits for them, and re-layouts  29.5 us (4%)
  matrix products  18.9 us (3%)
  between operations  15.6 us (2%)
    ppermute x66, waiting for transfers between devices, hop(): return lax.ppermute(values, axis, [(i, i ^ mask) for i in range(size)])  240 us
    ppermute x66, starting transfers between devices, hop(): return lax.ppermute(values, axis, [(i, i ^ mask) for i in range(size)])  64.4 us
    pallas_call x2, Pallas kernels, run_acts(): pl.pallas_call(functools.partial(acts_kernel, experts, blocks, per, k), g...  50.1 us
    pallas_call x4, Pallas kernels, in_blocks(): pl.pallas_call(functools.partial(in_kernel, sets), grid_spec=pltpu.Prefet...  34.8 us
    pallas_call x2, Pallas kernels, run_back(): pl.pallas_call(rows_back_kernel, grid_spec=pltpu.PrefetchScalarGridSpec(n...  32.2 us
    pallas_call x1, Pallas kernels, attention(): pl.pallas_call(functools.partial(attend_back_kernel, blocks, size), grid=...  19.7 us
    pallas_call x2, Pallas kernels, down_blocks(): pl.pallas_call(functools.partial(down_kernel, sets), grid_spec=pltpu.Pref...  18.9 us
    all_gather x2, blocking collectives, sum_seq(): return jnp.sum(lax.all_gather(values, 'seq', axis=0), axis=0)  18.5 us
  transfers between devices with their start and end apart: 73, of which 29 were waited for; matrix products, arithmetic and copies ran while one was open for 13% of the time, Pallas kernels for 22%

profile of v2, /device:TPU:0, one launch (start us, length us, event | category | flops | bytes accessed | tf_op | source)
XLA Modules:
  0.0 712.4 jit_solution(1392925602697458440)
XLA Ops:
  9.5 4.1 collective-permute-start.27
  13.6 2.4 collective-permute-start.2
  17.1 21.1 %collective-permute-done.27 = bf16[128,2176]{1,0:T(8,128)(2,1)S(1)} collective-permute-done((bf16[128,2176]{1,0:T(8,128)(2,1)S(1)}, bf16[128,2176]{1,0:T(8,128)(2,1)S(1)}, u32[]{:S(2)}, u32[]{:S(2)}) %collective-permute-start.27) | collective-permute-done | bytes 557088 | tf_op jit(solution)/shard_map/ppermute | solution.py:38
  40.7 4.2 all-to-all-start
  45.4 13.2 %all_gather.24 = bf16[256,128]{1,0:T(8,128)(2,1)S(1)} all-gather(bf16[64,128]{1,0:T(8,128)(2,1)S(1)} %dynamic_update_slice.19), channel_id=1, replica_groups=mesh['seq'=8,'batch'=4] {'batch'}, dimensions={0}, use_global_device_ids=true | all-gather | bytes 81920 | tf_op jit(solution)/shard_map/all_gather | solution.py:818
  58.7 13.3 %all_gather.25 = bf16[2048,128]{0,1:T(8,128)(2,1)S(1)} all-gather(bf16[256,128]{0,1:T(8,128)(2,1)S(1)} %copy.138), channel_id=1, replica_groups=mesh['seq'=8,'batch'=4] {'seq'}, dimensions={0}, use_global_device_ids=true | all-gather | bytes 589824 | tf_op jit(solution)/shard_map/all_gather | solution.py:819
  76.0 3.5 all-to-all-start.1
  80.9 8.6 %all-to-all-done.1.refs_0_ = bf16[8,64,256]{2,1,0:T(8,128)(2,1)S(1)} async-done(((bf16[8,64,256]{2,1,0:T(8,128)(2,1)}), bf16[8,64,256]{2,1,0:T(8,128)(2,1)S(1)}, u32[]{:S(2)}, u32[]{:S(2)}) %all-to-all-start.1) | async-done | bytes 262176 | tf_op jit(solution)/shard_map/all_to_all | solution.py:810
  89.5 9.8 %collective-permute-done.8.refs_10_ = bf16[8,64,512]{2,1,0:T(8,128)(2,1)} collective-permute-done((bf16[8,64,512]{2,1,0:T(8,128)(2,1)}, bf16[8,64,512]{2,1,0:T(8,128)(2,1)}, u32[]{:S(2)}, u32[]{:S(2)}) %collective-permute-start.8) | collective-permute-done | bytes 524320 | tf_op jit(solution)/shard_map/ppermute | solution.py:38
  104.6 8.5 %collective-permute-done.11.refs_2_ = bf16[8,64,256]{2,1,0:T(8,128)(2,1)} collective-permute-done((bf16[8,64,256]{2,1,0:T(8,128)(2,1)S(1)}, bf16[8,64,256]{2,1,0:T(8,128)(2,1)}, u32[]{:S(2)}, u32[]{:S(2)}) %collective-permute-start.11) | collective-permute-done | bytes 262176 | tf_op jit(solution)/shard_map/ppermute | solution.py:38
  113.9 8.7 %collective-permute-done.7.refs_9_ = bf16[8,64,512]{2,1,0:T(8,128)(2,1)S(1)} collective-permute-done((bf16[8,64,512]{2,1,0:T(8,128)(2,1)}, bf16[8,64,512]{2,1,0:T(8,128)(2,1)S(1)}, u32[]{:S(2)}, u32[]{:S(2)}) %collective-permute-start.7) | collective-permute-done | bytes 524320 | tf_op jit(solution)/shard_map/ppermute | solution.py:38
  122.6 3.0 collective-permute-start.14
  128.4 11.1 %collective-permute-done.9.refs_11_ = bf16[8,64,512]{2,1,0:T(8,128)(2,1)} collective-permute-done((bf16[8,64,512]{2,1,0:T(8,128)(2,1)}, bf16[8,64,512]{2,1,0:T(8,128)(2,1)}, u32[]{:S(2)}, u32[]{:S(2)}) %collective-permute-start.9) | collective-permute-done | bytes 524320 | tf_op jit(solution)/shard_map/ppermute | solution.py:38
  139.5 9.7 %shard_map.289 = (bf16[1024,2048]{1,0:T(8,128)(2,1)}, f32[1024,512]{1,0:T(8,128)}, f32[2,1024]{1,0:T(2,128)}, bf16[8,4,64,512]{3,2,1,0:T(8,128)(2,1)}) custom-call(s32[10]{0:T(128)} %get-tuple-element.189.at_ref, bf16[128,2048]{1,0:T(8,128)(2,1)} %bitcast.191, bf16[128,2048]{1,0:T(8,128)(2,1)} %copy-done.62, bf16[128,2048]{1,0:T(8,128)(2,1)} %copy-done.61, ...), custom_call_target="tpu_custom_call" | custom-call | flops 2147483648 | bytes 16777216 | tf_op jit(solution)/shard_map/pallas_call | solution.py:182
  149.3 9.2 %all-gather.3 = f32[8,2,1024]{2,1,0:T(2,128)S(1)} all-gather(f32[1,2,1024]{2,1,0:T(2,128)} %bitcast.228), channel_id=2, replica_groups=mesh['seq'=8,'batch'=4] {'seq'}, dimensions={0}, use_global_device_ids=true | all-gather | bytes 73728 | tf_op jit(solution)/shard_map/all_gather | solution.py:848
  159.8 5.8 shard_map.290
  165.6 10.1 %shard_map.291.refs_8_ = bf16[1024,256]{1,0:T(8,128)(2,1)} custom-call(s32[8]{0:T(128)} %gather_fusion, f32[1024,512]{1,0:T(8,128)} %get-tuple-element.79.q_ref.k_ref, f32[1024,512]{1,0:T(8,128)} %get-tuple-element.79.q_ref.k_ref, bf16[1024,256]{1,0:T(8,128)(2,1)} %get-tuple-element.83.v_ref, f32[1024,2]{1,0:T(8,128)} %get-tuple-element.172.scale_ref, ...), custom_call_target="tpu_custom_call" | custom-call | flops 1073741824 | bytes 4194304 | tf_op jit(solution)/shard_map/pallas_call | solution.py:433
  178.8 3.1 collective-permute-done.16
  186.1 11.3 %collective-permute-done.17 = bf16[128,2048]{1,0:T(8,128)(2,1)S(1)} collective-permute-done((bf16[128,2048]{1,0:T(8,128)(2,1)S(1)}, bf16[128,2048]{1,0:T(8,128)(2,1)S(1)}, u32[]{:S(2)}, u32[]{:S(2)}) %collective-permute-start.17) | collective-permute-done | bytes 524320 | tf_op jit(solution)/shard_map/ppermute | solution.py:38
  197.4 11.2 %collective-permute-done.19 = bf16[128,2048]{1,0:T(8,128)(2,1)S(1)} collective-permute-done((bf16[128,2048]{1,0:T(8,128)(2,1)S(1)}, bf16[128,2048]{1,0:T(8,128)(2,1)S(1)}, u32[]{:S(2)}, u32[]{:S(2)}) %collective-permute-start.19) | collective-permute-done | bytes 524320 | tf_op jit(solution)/shard_map/ppermute | solution.py:38
  214.4 2.8 collective-permute-start.28
  217.1 9.6 %collective-permute-done.22.refs_3_ = bf16[128,2048]{1,0:T(8,128)(2,1)} collective-permute-done((bf16[128,2048]{1,0:T(8,128)(2,1)S(1)}, bf16[128,2048]{1,0:T(8,128)(2,1)}, u32[]{:S(2)}, u32[]{:S(2)}) %collective-permute-start.22) | collective-permute-done | bytes 524320 | tf_op jit(solution)/shard_map/ppermute | solution.py:38
  226.8 9.1 %collective-permute-done.21.refs_2_ = bf16[128,2048]{1,0:T(8,128)(2,1)} collective-permute-done((bf16[128,2048]{1,0:T(8,128)(2,1)S(1)}, bf16[128,2048]{1,0:T(8,128)(2,1)}, u32[]{:S(2)}, u32[]{:S(2)}) %collective-permute-start.21) | collective-permute-done | bytes 524320 | tf_op jit(solution)/shard_map/ppermute | solution.py:38
  242.3 25.0 %shard_map.292 = (bf16[1024,2048]{1,0:T(8,128)(2,1)}, bf16[1024,2048]{1,0:T(8,128)(2,1)}, bf16[2,1024,512]{2,1,0:T(8,128)(2,1)}, bf16[2,1024,512]{2,1,0:T(8,128)...) custom-call(s32[10]{0:T(128)} %get-tuple-element.113.at_ref, bf16[128,2048]{1,0:T(8,128)(2,1)} %copy-done.12, ...), custom_call_target="tpu_custom_call" | custom-call | flops 12884901888 | bytes 35651584 | tf_op jit(solution)/shard_map/pallas_call | solution.py:533
  271.9 25.1 %shard_map.293 = (bf16[1024,2048]{1,0:T(8,128)(2,1)}, bf16[1024,2048]{1,0:T(8,128)(2,1)}, bf16[2,1024,512]{2,1,0:T(8,128)(2,1)}, bf16[2,1024,512]{2,1,0:T(8,128)...) custom-call(s32[10]{0:T(128)} %get-tuple-element.113.at_ref, bf16[128,2048]{1,0:T(8,128)(2,1)} %copy-done.63, ...), custom_call_target="tpu_custom_call" | custom-call | flops 12884901888 | bytes 35651584 | tf_op jit(solution)/shard_map/pallas_call | solution.py:533
  297.0 8.7 %shard_map.294 = bf16[1,2,2,512,512]{4,3,2,1,0:T(8,128)(2,1)} custom-call(s32[1]{0:T(128)} %bitcast.21.at_ref, bf16[1024,2048]{1,0:T(8,128)(2,1)} %get-tuple-element.87.refs_0_, bf16[1024,2048]{1,0:T(8,128)(2,1)} %get-tuple-element.93.refs_1_, bf16[2,1024,512]{2,1,0:T(8,128)(2,1)} %get-tuple-element.94.refs_2_.gate_ref, ...), custom_call_target="tpu_custom_call" | custom-call | flops 4294967296 | bytes 8388608 | tf_op jit(solution)/shard_map/pallas_call | solution.py:725
  305.7 16.1 %shard_map.295 = (bf16[512,2176]{1,0:T(8,128)(2,1)}, bf16[512,2176]{1,0:T(8,128)(2,1)}) custom-call(s32[10]{0:T(128)} %get-tuple-element.113.at_ref, bf16[2,1024,512]{2,1,0:T(8,128)(2,1)} %get-tuple-element.95.refs_3_.gate_ref, bf16[2,1024,512]{2,1,0:T(8,128)(2,1)} %get-tuple-element.97.up_ref.refs_3_, bf16[1024,128]{1,0:T(8,128)(2,1)} %get-tuple-element.98.sums_ref, ...), custom_call_target="tpu_custom_call" | custom-call | flops 8589934592 | bytes 16777216 | tf_op jit(solution)/shard_map/pallas_call | solution.py:654
  321.9 16.1 %shard_map.296 = (bf16[512,2176]{1,0:T(8,128)(2,1)}, bf16[512,2176]{1,0:T(8,128)(2,1)}) custom-call(s32[10]{0:T(128)} %get-tuple-element.113.at_ref, bf16[2,1024,512]{2,1,0:T(8,128)(2,1)} %get-tuple-element.94.refs_2_.gate_ref, bf16[2,1024,512]{2,1,0:T(8,128)(2,1)} %get-tuple-element.102.up_ref.refs_2_, bf16[1024,128]{1,0:T(8,128)(2,1)} %get-tuple-element.103.sums_ref, ...), custom_call_target="tpu_custom_call" | custom-call | flops 8589934592 | bytes 16777216 | tf_op jit(solution)/shard_map/pallas_call | solution.py:654
  343.5 3.4 add_convert_fusion.6
  350.3 2.8 add_convert_fusion.3
  354.6 8.8 %shard_map.297 = bf16[1,2,2,512,512]{4,3,2,1,0:T(8,128)(2,1)} custom-call(s32[1]{0:T(128)} %bitcast.21.at_ref, bf16[1024,2048]{1,0:T(8,128)(2,1)} %get-tuple-element.87.refs_0_, bf16[1024,2048]{1,0:T(8,128)(2,1)} %get-tuple-element.93.refs_1_, bf16[2,1024,512]{2,1,0:T(8,128)(2,1)} %get-tuple-element.102.up_ref.refs_2_, ...), custom_call_target="tpu_custom_call" | custom-call | flops 4294967296 | bytes 8388608 | tf_op jit(solution)/shard_map/pallas_call | solution.py:725
  363.4 8.8 %shard_map.298 = bf16[1,2,256,2048]{3,2,1,0:T(8,128)(2,1)} custom-call(s32[1]{0:T(128)} %bitcast.21.at_ref, bf16[2,1024,512]{2,1,0:T(8,128)(2,1)} %get-tuple-element.108.refs_0_, bf16[2,1024,512]{2,1,0:T(8,128)(2,1)} %get-tuple-element.109.refs_1_, bf16[1024,2048]{1,0:T(8,128)(2,1)} %get-tuple-element.110.refs_2_, bf16[1024,2048]{1,0:T(8,128)(2,1)} %get-tuple-element.111.refs_3_), custom_call_target="tpu_custom_call" | custom-call | flops 4294967296 | bytes 10485760 | tf_op jit(solution)/shard_map/pallas_call | solution.py:691
  372.2 15.1 %shard_map.299 = bf16[2,2,2,2,128,2048]{5,4,3,2,1,0:T(8,128)(2,1)} custom-call(s32[10]{0:T(128)} %get-tuple-element.113.at_ref, bf16[2,1024,512]{2,1,0:T(8,128)(2,1)} %get-tuple-element.108.refs_0_, bf16[2,1024,512]{2,1,0:T(8,128)(2,1)} %get-tuple-element.109.refs_1_, bf16[2,1024,2048]{2,1,0:T(8,128)(2,1)} %refs_2_.1), custom_call_target="tpu_custom_call" | custom-call | flops 8589934592 | bytes 12582912 | tf_op jit(solution)/shard_map/pallas_call | solution.py:620
  389.4 2.9 add_convert_fusion.2
  394.5 10.0 %shard_map.304 = bf16[1,2,256,2048]{3,2,1,0:T(8,128)(2,1)} custom-call(s32[1]{0:T(128)} %bitcast.28.at_ref, bf16[2,1024,512]{2,1,0:T(8,128)(2,1)} %get-tuple-element.108.refs_0_, bf16[2,1024,512]{2,1,0:T(8,128)(2,1)} %get-tuple-element.109.refs_1_, bf16[1024,2048]{1,0:T(8,128)(2,1)} %get-tuple-element.110.refs_2_, bf16[1024,2048]{1,0:T(8,128)(2,1)} %get-tuple-element.111.refs_3_), custom_call_target="tpu_custom_call" | custom-call | flops 4294967296 | bytes 10485760 | tf_op jit(solution)/shard_map/pallas_call | solution.py:691
  404.6 8.6 %shard_map.303 = bf16[1,2,2,512,512]{4,3,2,1,0:T(8,128)(2,1)} custom-call(s32[1]{0:T(128)} %bitcast.28.at_ref, bf16[1024,2048]{1,0:T(8,128)(2,1)} %get-tuple-element.87.refs_0_, bf16[1024,2048]{1,0:T(8,128)(2,1)} %get-tuple-element.93.refs_1_, bf16[2,1024,512]{2,1,0:T(8,128)(2,1)} %get-tuple-element.102.up_ref.refs_2_, ...), custom_call_target="tpu_custom_call" | custom-call | flops 4294967296 | bytes 8388608 | tf_op jit(solution)/shard_map/pallas_call | solution.py:725
  414.0 4.3 collective-permute-done.44
  426.2 8.7 %shard_map.302 = bf16[1,2,2,512,512]{4,3,2,1,0:T(8,128)(2,1)} custom-call(s32[1]{0:T(128)} %bitcast.28.at_ref, bf16[1024,2048]{1,0:T(8,128)(2,1)} %get-tuple-element.87.refs_0_, bf16[1024,2048]{1,0:T(8,128)(2,1)} %get-tuple-element.93.refs_1_, bf16[2,1024,512]{2,1,0:T(8,128)(2,1)} %get-tuple-element.94.refs_2_.gate_ref, ...), custom_call_target="tpu_custom_call" | custom-call | flops 4294967296 | bytes 8388608 | tf_op jit(solution)/shard_map/pallas_call | solution.py:725
  438.0 4.5 all-to-all-start.4
  444.5 5.3 collective-permute-done.47.refs_3_
  449.7 10.3 %collective-permute-done.46.refs_2_ = bf16[128,2048]{1,0:T(8,128)(2,1)} collective-permute-done((bf16[128,2048]{1,0:T(8,128)(2,1)}, bf16[128,2048]{1,0:T(8,128)(2,1)}, u32[]{:S(2)}, u32[]{:S(2)}) %collective-permute-start.46) | collective-permute-done | bytes 524320 | tf_op jit(solution)/shard_map/ppermute | solution.py:38
  469.1 7.9 %shard_map.300 = (bf16[1024,256]{1,0:T(8,128)(2,1)}, bf16[256,2048]{1,0:T(8,128)(2,1)}) custom-call(bf16[128,2048]{1,0:T(8,128)(2,1)} %fusion.38.refs_0_, bf16[128,2048]{1,0:T(8,128)(2,1)} %collective-permute-done.45.refs_1_, bf16[128,2048]{1,0:T(8,128)(2,1)} %collective-permute-done.46.refs_2_, bf16[128,2048]{1,0:T(8,128)(2,1)} %collective-permute-done.47.refs_3_, ...), custom_call_target="tpu_custom_call" | custom-call | flops 2147483648 | bytes 8388608 | tf_op jit(solution)/shard_map/pallas_call | solution.py:286
  476.9 19.7 %shard_map.301 = (f32[1024,256]{1,0:T(8,128)}, f32[1024,256]{1,0:T(8,128)}, bf16[1024,256]{1,0:T(8,128)(2,1)}, f32[1024,2]{1,0:T(8,128)}, f32[2,256]{1,0:T(2,128)}) custom-call(s32[8]{0:T(128)} %gather_fusion, f32[1024,512]{1,0:T(8,128)} %get-tuple-element.79.q_ref.k_ref, f32[1024,512]{1,0:T(8,128)} %get-tuple-element.79.q_ref.k_ref, ...), custom_call_target="tpu_custom_call" | custom-call | flops 2684354560 | bytes 8388608 | tf_op jit(solution)/shard_map/pallas_call | solution.py:445
  500.8 9.3 %all-gather.4 = f32[8,2,1024]{2,1,0:T(2,128)S(1)} all-gather(f32[1,2,1024]{2,1,0:T(2,128)S(1)} %copy.148), channel_id=4, replica_groups=mesh['seq'=8,'batch'=4] {'seq'}, dimensions={0}, use_global_device_ids=true | all-gather | bytes 73728 | tf_op jit(solution)/shard_map/all_gather | solution.py:848
  512.2 4.5 convolution_convert_fusion.3
  516.8 3.7 all-to-all-start.3
  524.4 2.6 add_convert_fusion
  529.5 3.8 convolution_convert_fusion
  533.3 2.6 add_convert_fusion.1
  536.4 9.4 %all-to-all-done.3 = bf16[32,64,256]{2,1,0:T(8,128)(2,1)} async-done(((bf16[32,64,256]{2,1,0:T(8,128)(2,1)}), bf16[32,64,256]{2,1,0:T(8,128)(2,1)}, u32[]{:S(2)}, u32[]{:S(2)}) %all-to-all-start.3) | async-done | bytes 1048608 | tf_op jit(solution)/shard_map/all_to_all | solution.py:973
  545.8 4.3 all-to-all-start.2
  550.1 3.0 convert_add_fusion.1
  557.4 2.4 collective-permute-start.64
  562.8 20.1 %collective-permute-done.54 = bf16[128,2048]{1,0:T(8,128)(2,1)S(1)} collective-permute-done((bf16[128,2048]{1,0:T(8,128)(2,1)S(1)}, bf16[128,2048]{1,0:T(8,128)(2,1)S(1)}, u32[]{:S(2)}, u32[]{:S(2)}) %collective-permute-start.54) | collective-permute-done | bytes 524320 | tf_op jit(solution)/shard_map/ppermute | solution.py:38
  583.5 14.2 %collective-permute-done.56 = bf16[128,2048]{1,0:T(8,128)(2,1)S(1)} collective-permute-done((bf16[128,2048]{1,0:T(8,128)(2,1)S(1)}, bf16[128,2048]{1,0:T(8,128)(2,1)S(1)}, u32[]{:S(2)}, u32[]{:S(2)}) %collective-permute-start.56) | collective-permute-done | bytes 524320 | tf_op jit(solution)/shard_map/ppermute | solution.py:38
  598.1 2.5 collective-permute-start.58
  600.6 2.5 fusion.2
  603.1 49.7 %collective-permute-done.60 = f32[2,64]{1,0:T(2,128)S(1)} collective-permute-done((f32[2,64]{1,0:T(2,128)S(1)}, f32[2,64]{1,0:T(2,128)S(1)}, u32[]{:S(2)}, u32[]{:S(2)}) %collective-permute-start.60) | collective-permute-done | bytes 544 | tf_op jit(solution)/shard_map/ppermute | solution.py:38
  652.7 5.3 collective-permute-done.58
  663.4 2.9 maximum_select_fusion
  666.4 2.9 maximum_select_fusion.1
  671.7 2.8 convert_add_fusion
  677.0 3.4 collective-permute-start.52
  682.9 20.6 %collective-permute-done.52 = bf16[128,2048]{1,0:T(8,128)(2,1)S(1)} collective-permute-done((bf16[128,2048]{1,0:T(8,128)(2,1)S(1)}, bf16[128,2048]{1,0:T(8,128)(2,1)S(1)}, u32[]{:S(2)}, u32[]{:S(2)}) %collective-permute-start.52) | collective-permute-done | bytes 524320 | tf_op jit(solution)/shard_map/ppermute | solution.py:38
  (365 shorter events, 118.8 us)
Async XLA Ops:
  7.2 235.1 %all-gather.7.cloned.1.call-start = ((), (), s32[]{:S(2)}) async-start(), calls=%async_computation.7 | async-start | bytes 10027008 | tf_op jit(solution)/shard_map/all_gather | solution.py:837
  9.5 28.7 %collective-permute-start.27 = (bf16[128,2176]{1,0:T(8,128)(2,1)S(1)}, bf16[128,2176]{1,0:T(8,128)(2,1)S(1)}, u32[]{:S(2)}, u32[]{:S(2)}) collective-permute-start(bf16[128,2176]{1,0:T(8,128)(2,1)S(1)} %get-tuple-element.170), channel_id=1, source_target_pairs={{0,2},{1,3},{2,0},{3,1},{4,6},{5,7},{6,4},{7,5},{8,10},{9,11},{10,... | collective-permute-start | bytes 1671176 | tf_op jit(solution)/shard_map/ppermute | solution.py:38
  13.6 25.7 %collective-permute-start.2 = (bf16[128,2048]{1,0:T(8,128)(2,1)}, bf16[128,2048]{1,0:T(8,128)(2,1)S(1)}, u32[]{:S(2)}, u32[]{:S(2)}) collective-permute-start(bf16[128,2048]{1,0:T(8,128)(2,1)} %bitcast.188), channel_id=1, source_target_pairs={{0,24},{4,28},{8,16},{12,20},{16,8},{20,12},{24,0},{28,4},{1,25},{... | collective-permute-start | bytes 1572872 | tf_op jit(solution)/shard_map/ppermute | solution.py:38
  16.1 23.3 %collective-permute-start.1 = (bf16[128,2048]{1,0:T(8,128)(2,1)}, bf16[128,2048]{1,0:T(8,128)(2,1)S(1)}, u32[]{:S(2)}, u32[]{:S(2)}) collective-permute-start(bf16[128,2048]{1,0:T(8,128)(2,1)} %bitcast.189), channel_id=1, source_target_pairs={{0,16},{4,20},{8,24},{12,28},{16,0},{20,4},{24,8},{28,12},{1,17},{... | collective-permute-start | bytes 1572872 | tf_op jit(solution)/shard_map/ppermute | solution.py:38
  16.6 22.9 %collective-permute-start = (bf16[128,2048]{1,0:T(8,128)(2,1)}, bf16[128,2048]{1,0:T(8,128)(2,1)S(1)}, u32[]{:S(2)}, u32[]{:S(2)}) collective-permute-start(bf16[128,2048]{1,0:T(8,128)(2,1)} %bitcast.190), channel_id=1, source_target_pairs={{0,8},{4,12},{8,0},{12,4},{16,24},{20,28},{24,16},{28,20},{1,9},{5... | collective-permute-start | bytes 1572872 | tf_op jit(solution)/shard_map/ppermute | solution.py:38
  39.5 65.1 %collective-permute-start.3 = (bf16[128,2048]{1,0:T(8,128)(2,1)S(1)}, bf16[128,2048]{1,0:T(8,128)(2,1)}, u32[]{:S(2)}, u32[]{:S(2)}) collective-permute-start(bf16[128,2048]{1,0:T(8,128)(2,1)S(1)} %bitcast.192), channel_id=1, source_target_pairs={{0,4},{4,0},{8,12},{12,8},{16,20},{20,16},{24,28},{28,24},{1,5},{5... | collective-permute-start | bytes 1572872 | tf_op jit(solution)/shard_map/ppermute | solution.py:38
  40.7 32.0 %all-to-all-start = ((bf16[8,64,512]{2,1,0:T(8,128)(2,1)}), bf16[8,64,512]{2,1,0:T(8,128)(2,1)}, u32[]{:S(2)}, u32[]{:S(2)}) async-start(bf16[8,64,512]{2,1,0:T(8,128)(2,1)} %pad_maximum_fusion.3), calls=%async_computation | async-start | bytes 1048576 | tf_op jit(solution)/shard_map/all_to_all | solution.py:810
  72.6 26.6 %collective-permute-start.8 = (bf16[8,64,512]{2,1,0:T(8,128)(2,1)}, bf16[8,64,512]{2,1,0:T(8,128)(2,1)}, u32[]{:S(2)}, u32[]{:S(2)}) collective-permute-start(bf16[8,64,512]{2,1,0:T(8,128)(2,1)} %all-to-all-done.refs_8_), channel_id=1, source_target_pairs={{0,2},{1,3},{2,0},{3,1},{4,6},{5,7},{6,4},{7,5},{8,10},{9,11},{10,... | collective-permute-start | bytes 1572872 | tf_op jit(solution)/shard_map/ppermute | solution.py:38
  76.0 13.5 %all-to-all-start.1 = ((bf16[8,64,256]{2,1,0:T(8,128)(2,1)}), bf16[8,64,256]{2,1,0:T(8,128)(2,1)S(1)}, u32[]{:S(2)}, u32[]{:S(2)}) async-start(bf16[8,64,256]{2,1,0:T(8,128)(2,1)} %bitcast.181), calls=%async_computation.1 | async-start | bytes 524288 | tf_op jit(solution)/shard_map/all_to_all | solution.py:810
  79.5 596.3 %reduce-scatter.2.cloned.1.call-start = ((), (), s32[]{:S(2)}) async-start(), calls=%async_computation.6 | async-start | bytes 9437184 | tf_op jit(solution)/shard_map/reduce_scatter | solution.py:951
  99.3 13.8 %collective-permute-start.11 = (bf16[8,64,256]{2,1,0:T(8,128)(2,1)S(1)}, bf16[8,64,256]{2,1,0:T(8,128)(2,1)}, u32[]{:S(2)}, u32[]{:S(2)}) collective-permute-start(bf16[8,64,256]{2,1,0:T(8,128)(2,1)S(1)} %all-to-all-done.1.refs_0_), channel_id=1, source_target_pairs={{0,2},{1,3},{2,0},{3,1},{4,6},{5,7},{6,4},{7,5},{8,10},{9,11},{10,... | collective-permute-start | bytes 786440 | tf_op jit(solution)/shard_map/ppermute | solution.py:38
  102.0 20.5 %collective-permute-start.7 = (bf16[8,64,512]{2,1,0:T(8,128)(2,1)}, bf16[8,64,512]{2,1,0:T(8,128)(2,1)S(1)}, u32[]{:S(2)}, u32[]{:S(2)}) collective-permute-start(bf16[8,64,512]{2,1,0:T(8,128)(2,1)} %all-to-all-done.refs_8_), channel_id=1, source_target_pairs={{0,1},{1,0},{2,3},{3,2},{4,5},{5,4},{6,7},{7,6},{8,9},{9,8},{10,11... | collective-permute-start | bytes 1572872 | tf_op jit(solution)/shard_map/ppermute | solution.py:38
  104.1 18.5 %collective-permute-start.6 = (bf16[128,2048]{1,0:T(8,128)(2,1)}, bf16[128,2048]{1,0:T(8,128)(2,1)S(1)}, u32[]{:S(2)}, u32[]{:S(2)}) collective-permute-start(bf16[128,2048]{1,0:T(8,128)(2,1)} %copy-done.60), channel_id=1, source_target_pairs={{0,4},{4,0},{8,12},{12,8},{16,20},{20,16},{24,28},{28,24},{1,5},{5... | collective-permute-start | bytes 1572872 | tf_op jit(solution)/shard_map/ppermute | solution.py:38
  104.1 21.5 %collective-permute-start.5 = (bf16[128,2048]{1,0:T(8,128)(2,1)}, bf16[128,2048]{1,0:T(8,128)(2,1)S(1)}, u32[]{:S(2)}, u32[]{:S(2)}) collective-permute-start(bf16[128,2048]{1,0:T(8,128)(2,1)} %copy-done.61), channel_id=1, source_target_pairs={{0,4},{4,0},{8,12},{12,8},{16,20},{20,16},{24,28},{28,24},{1,5},{5... | collective-permute-start | bytes 1572872 | tf_op jit(solution)/shard_map/ppermute | solution.py:38
  104.6 21.8 %collective-permute-start.4 = (bf16[128,2048]{1,0:T(8,128)(2,1)}, bf16[128,2048]{1,0:T(8,128)(2,1)S(1)}, u32[]{:S(2)}, u32[]{:S(2)}) collective-permute-start(bf16[128,2048]{1,0:T(8,128)(2,1)} %copy-done.62), channel_id=1, source_target_pairs={{0,4},{4,0},{8,12},{12,8},{16,20},{20,16},{24,28},{28,24},{1,5},{5... | collective-permute-start | bytes 1572872 | tf_op jit(solution)/shard_map/ppermute | solution.py:38
  113.1 26.4 %collective-permute-start.9 = (bf16[8,64,512]{2,1,0:T(8,128)(2,1)}, bf16[8,64,512]{2,1,0:T(8,128)(2,1)}, u32[]{:S(2)}, u32[]{:S(2)}) collective-permute-start(bf16[8,64,512]{2,1,0:T(8,128)(2,1)} %collective-permute-done.8.refs_10_), channel_id=1, source_target_pairs={{0,1},{1,0},{2,3},{3,2},{4,5},{5,4},{6,7},{7,6},{8,9},{9,8},{10,11... | collective-permute-start | bytes 1572872 | tf_op jit(solution)/shard_map/ppermute | solution.py:38
  122.6 37.2 %collective-permute-start.10 = (bf16[8,64,256]{2,1,0:T(8,128)(2,1)S(1)}, bf16[8,64,256]{2,1,0:T(8,128)(2,1)}, u32[]{:S(2)}, u32[]{:S(2)}) collective-permute-start(bf16[8,64,256]{2,1,0:T(8,128)(2,1)S(1)} %all-to-all-done.1.refs_0_), channel_id=1, source_target_pairs={{0,1},{1,0},{2,3},{3,2},{4,5},{5,4},{6,7},{7,6},{8,9},{9,8},{10,11... | collective-permute-start | bytes 786440 | tf_op jit(solution)/shard_map/ppermute | solution.py:38
  122.6 36.2 %collective-permute-start.14 = (bf16[64,2048]{1,0:T(8,128)(2,1)S(1)}, bf16[64,2048]{1,0:T(8,128)(2,1)S(1)}, u32[]{:S(2)}, u32[]{:S(2)}) collective-permute-start(bf16[64,2048]{1,0:T(8,128)(2,1)S(1)} %copy-done.39), channel_id=1, source_target_pairs={{0,2},{1,3},{2,0},{3,1},{4,6},{5,7},{6,4},{7,5},{8,10},{9,11},{10,... | collective-permute-start | bytes 786440 | tf_op jit(solution)/shard_map/ppermute | solution.py:38
  125.5 33.3 %collective-permute-start.13 = (bf16[64,2048]{1,0:T(8,128)(2,1)S(1)}, bf16[64,2048]{1,0:T(8,128)(2,1)S(1)}, u32[]{:S(2)}, u32[]{:S(2)}) collective-permute-start(bf16[64,2048]{1,0:T(8,128)(2,1)S(1)} %copy-done.39), channel_id=1, source_target_pairs={{0,1},{1,0},{2,3},{3,2},{4,5},{5,4},{6,7},{7,6},{8,9},{9,8},{10,11... | collective-permute-start | bytes 786440 | tf_op jit(solution)/shard_map/ppermute | solution.py:38
  127.1 32.6 %collective-permute-start.12 = (bf16[8,64,256]{2,1,0:T(8,128)(2,1)}, bf16[8,64,256]{2,1,0:T(8,128)(2,1)}, u32[]{:S(2)}, u32[]{:S(2)}) collective-permute-start(bf16[8,64,256]{2,1,0:T(8,128)(2,1)} %collective-permute-done.11.refs_2_), channel_id=1, source_target_pairs={{0,1},{1,0},{2,3},{3,2},{4,5},{5,4},{6,7},{7,6},{8,9},{9,8},{10,11... | collective-permute-start | bytes 786440 | tf_op jit(solution)/shard_map/ppermute | solution.py:38
  158.8 16.9 %collective-permute-start.15 = (bf16[64,2048]{1,0:T(8,128)(2,1)S(1)}, bf16[64,2048]{1,0:T(8,128)(2,1)S(1)}, u32[]{:S(2)}, u32[]{:S(2)}) collective-permute-start(bf16[64,2048]{1,0:T(8,128)(2,1)S(1)} %collective-permute-done.14), channel_id=1, source_target_pairs={{0,1},{1,0},{2,3},{3,2},{4,5},{5,4},{6,7},{7,6},{8,9},{9,8},{10,11... | collective-permute-start | bytes 786440 | tf_op jit(solution)/shard_map/ppermute | solution.py:38
  182.6 14.8 %collective-permute-start.17 = (bf16[128,2048]{1,0:T(8,128)(2,1)S(1)}, bf16[128,2048]{1,0:T(8,128)(2,1)S(1)}, u32[]{:S(2)}, u32[]{:S(2)}) collective-permute-start(bf16[128,2048]{1,0:T(8,128)(2,1)S(1)} %get-tuple-element.158), channel_id=1, source_target_pairs={{0,8},{4,12},{8,0},{12,4},{16,24},{20,28},{24,16},{28,20},{1,9},{5... | collective-permute-start | bytes 1572872 | tf_op jit(solution)/shard_map/ppermute | solution.py:38
  183.7 24.9 %collective-permute-start.19 = (bf16[128,2048]{1,0:T(8,128)(2,1)S(1)}, bf16[128,2048]{1,0:T(8,128)(2,1)S(1)}, u32[]{:S(2)}, u32[]{:S(2)}) collective-permute-start(bf16[128,2048]{1,0:T(8,128)(2,1)S(1)} %get-tuple-element.159), channel_id=1, source_target_pairs={{0,24},{4,28},{8,16},{12,20},{16,8},{20,12},{24,0},{28,4},{1,25},{... | collective-permute-start | bytes 1572872 | tf_op jit(solution)/shard_map/ppermute | solution.py:38
  185.2 24.8 %collective-permute-start.18 = (bf16[128,2048]{1,0:T(8,128)(2,1)S(1)}, bf16[128,2048]{1,0:T(8,128)(2,1)S(1)}, u32[]{:S(2)}, u32[]{:S(2)}) collective-permute-start(bf16[128,2048]{1,0:T(8,128)(2,1)S(1)} %get-tuple-element.160), channel_id=1, source_target_pairs={{0,16},{4,20},{8,24},{12,28},{16,0},{20,4},{24,8},{28,12},{1,17},{... | collective-permute-start | bytes 1572872 | tf_op jit(solution)/shard_map/ppermute | solution.py:38
  210.8 15.9 %collective-permute-start.22 = (bf16[128,2048]{1,0:T(8,128)(2,1)S(1)}, bf16[128,2048]{1,0:T(8,128)(2,1)}, u32[]{:S(2)}, u32[]{:S(2)}) collective-permute-start(bf16[128,2048]{1,0:T(8,128)(2,1)S(1)} %multiply_convert_fusion.2.refs_0_), channel_id=1, source_target_pairs={{0,24},{4,28},{8,16},{12,20},{16,8},{20,12},{24,0},{28,4},{1,25},{... | collective-permute-start | bytes 1572872 | tf_op jit(solution)/shard_map/ppermute | solution.py:38
  212.3 23.5 %collective-permute-start.21 = (bf16[128,2048]{1,0:T(8,128)(2,1)S(1)}, bf16[128,2048]{1,0:T(8,128)(2,1)}, u32[]{:S(2)}, u32[]{:S(2)}) collective-permute-start(bf16[128,2048]{1,0:T(8,128)(2,1)S(1)} %multiply_convert_fusion.2.refs_0_), channel_id=1, source_target_pairs={{0,16},{4,20},{8,24},{12,28},{16,0},{20,4},{24,8},{28,12},{1,17},{... | collective-permute-start | bytes 1572872 | tf_op jit(solution)/shard_map/ppermute | solution.py:38
  213.3 22.5 %collective-permute-start.20 = (bf16[128,2048]{1,0:T(8,128)(2,1)S(1)}, bf16[128,2048]{1,0:T(8,128)(2,1)}, u32[]{:S(2)}, u32[]{:S(2)}) collective-permute-start(bf16[128,2048]{1,0:T(8,128)(2,1)S(1)} %multiply_convert_fusion.2.refs_0_), channel_id=1, source_target_pairs={{0,8},{4,12},{8,0},{12,4},{16,24},{20,28},{24,16},{28,20},{1,9},{5... | collective-permute-start | bytes 1572872 | tf_op jit(solution)/shard_map/ppermute | solution.py:38
  214.4 24.0 %collective-permute-start.28 = (bf16[128,2048]{1,0:T(8,128)(2,1)S(1)}, bf16[128,2048]{1,0:T(8,128)(2,1)S(1)}, u32[]{:S(2)}, u32[]{:S(2)}) collective-permute-start(bf16[128,2048]{1,0:T(8,128)(2,1)S(1)} %multiply_convert_fusion.2.refs_0_), channel_id=1, source_target_pairs={{0,2},{1,3},{2,0},{3,1},{4,6},{5,7},{6,4},{7,5},{8,10},{9,11},{10,... | collective-permute-start | bytes 1572872 | tf_op jit(solution)/shard_map/ppermute | solution.py:38
  217.1 21.2 %collective-permute-start.23 = (bf16[128,2048]{1,0:T(8,128)(2,1)S(1)}, bf16[128,2048]{1,0:T(8,128)(2,1)}, u32[]{:S(2)}, u32[]{:S(2)}) collective-permute-start(bf16[128,2048]{1,0:T(8,128)(2,1)S(1)} %multiply_convert_fusion.2.refs_0_), channel_id=1, source_target_pairs={{0,4},{4,0},{8,12},{12,8},{16,20},{20,16},{24,28},{28,24},{1,5},{5... | collective-permute-start | bytes 1572872 | tf_op jit(solution)/shard_map/ppermute | solution.py:38
  226.8 11.6 %collective-permute-start.26 = (bf16[128,2048]{1,0:T(8,128)(2,1)}, bf16[128,2048]{1,0:T(8,128)(2,1)}, u32[]{:S(2)}, u32[]{:S(2)}) collective-permute-start(bf16[128,2048]{1,0:T(8,128)(2,1)} %collective-permute-done.22.refs_3_), channel_id=1, source_target_pairs={{0,4},{4,0},{8,12},{12,8},{16,20},{20,16},{24,28},{28,24},{1,5},{5... | collective-permute-start | bytes 1572872 | tf_op jit(solution)/shard_map/ppermute | solution.py:38
  238.8 28.5 %collective-permute-start.31 = (bf16[128,2048]{1,0:T(8,128)(2,1)S(1)}, bf16[128,2048]{1,0:T(8,128)(2,1)}, u32[]{:S(2)}, u32[]{:S(2)}) collective-permute-start(bf16[128,2048]{1,0:T(8,128)(2,1)S(1)} %collective-permute-done.28.refs_0_), channel_id=1, source_target_pairs={{0,24},{4,28},{8,16},{12,20},{16,8},{20,12},{24,0},{28,4},{1,25},{... | collective-permute-start | bytes 1572872 | tf_op jit(solution)/shard_map/ppermute | solution.py:38
  240.3 27.0 %collective-permute-start.30 = (bf16[128,2048]{1,0:T(8,128)(2,1)S(1)}, bf16[128,2048]{1,0:T(8,128)(2,1)}, u32[]{:S(2)}, u32[]{:S(2)}) collective-permute-start(bf16[128,2048]{1,0:T(8,128)(2,1)S(1)} %collective-permute-done.28.refs_0_), channel_id=1, source_target_pairs={{0,16},{4,20},{8,24},{12,28},{16,0},{20,4},{24,8},{28,12},{1,17},{... | collective-permute-start | bytes 1572872 | tf_op jit(solution)/shard_map/ppermute | solution.py:38
  241.3 26.1 %collective-permute-start.29 = (bf16[128,2048]{1,0:T(8,128)(2,1)S(1)}, bf16[128,2048]{1,0:T(8,128)(2,1)}, u32[]{:S(2)}, u32[]{:S(2)}) collective-permute-start(bf16[128,2048]{1,0:T(8,128)(2,1)S(1)} %collective-permute-done.28.refs_0_), channel_id=1, source_target_pairs={{0,8},{4,12},{8,0},{12,4},{16,24},{20,28},{24,16},{28,20},{1,9},{5... | collective-permute-start | bytes 1572872 | tf_op jit(solution)/shard_map/ppermute | solution.py:38
  321.7 21.7 %collective-permute-start.36 = (bf16[512,2176]{1,0:T(8,128)(2,1)}, bf16[512,2176]{1,0:T(8,128)(2,1)}, u32[]{:S(2)}, u32[]{:S(2)}) collective-permute-start(bf16[512,2176]{1,0:T(8,128)(2,1)} %get-tuple-element.100), channel_id=1, source_target_pairs={{0,4},{4,0},{8,12},{12,8},{16,20},{20,16},{24,28},{28,24},{1,5},{5... | collective-permute-start | bytes 6684680 | tf_op jit(solution)/shard_map/ppermute | solution.py:38
  338.0 12.3 %collective-permute-start.37 = (bf16[512,2176]{1,0:T(8,128)(2,1)}, bf16[512,2176]{1,0:T(8,128)(2,1)}, u32[]{:S(2)}, u32[]{:S(2)}) collective-permute-start(bf16[512,2176]{1,0:T(8,128)(2,1)} %get-tuple-element.105), channel_id=1, source_target_pairs={{0,4},{4,0},{8,12},{12,8},{16,20},{20,16},{24,28},{28,24},{1,5},{5... | collective-permute-start | bytes 6684680 | tf_op jit(solution)/shard_map/ppermute | solution.py:38
  342.6 99.9 %collective-permute-start.61 = (bf16[2,2,512,512]{3,2,1,0:T(8,128)(2,1)}, bf16[2,2,512,512]{3,2,1,0:T(8,128)(2,1)}, u32[]{:S(2)}, u32[]{:S(2)}) collective-permute-start(bf16[2,2,512,512]{3,2,1,0:T(8,128)(2,1)} %bitcast.243), channel_id=1, source_target_pairs={{0,1},{1,0},{2,3},{3,2},{4,5},{5,4},{6,7},{7,6},{8,9},{9,8},{10,11... | collective-permute-start | bytes 6291464 | tf_op jit(solution)/shard_map/ppermute | solution.py:38
  346.8 40.5 %collective-permute-start.43 = (bf16[128,2176]{1,0:T(8,128)(2,1)}, bf16[128,2176]{1,0:T(8,128)(2,1)}, u32[]{:S(2)}, u32[]{:S(2)}) collective-permute-start(bf16[128,2176]{1,0:T(8,128)(2,1)} %get-tuple-element.152), channel_id=1, source_target_pairs={{0,24},{4,28},{8,16},{12,20},{16,8},{20,12},{24,0},{28,4},{1,25},{... | collective-permute-start | bytes 1671176 | tf_op jit(solution)/shard_map/ppermute | solution.py:38
  348.3 40.1 %collective-permute-start.42 = (bf16[128,2176]{1,0:T(8,128)(2,1)}, bf16[128,2176]{1,0:T(8,128)(2,1)}, u32[]{:S(2)}, u32[]{:S(2)}) collective-permute-start(bf16[128,2176]{1,0:T(8,128)(2,1)} %get-tuple-element.153), channel_id=1, source_target_pairs={{0,16},{4,20},{8,24},{12,28},{16,0},{20,4},{24,8},{28,12},{1,17},{... | collective-permute-start | bytes 1671176 | tf_op jit(solution)/shard_map/ppermute | solution.py:38
  349.2 40.2 %collective-permute-start.41 = (bf16[128,2176]{1,0:T(8,128)(2,1)}, bf16[128,2176]{1,0:T(8,128)(2,1)}, u32[]{:S(2)}, u32[]{:S(2)}) collective-permute-start(bf16[128,2176]{1,0:T(8,128)(2,1)} %get-tuple-element.154), channel_id=1, source_target_pairs={{0,8},{4,12},{8,0},{12,4},{16,24},{20,28},{24,16},{28,20},{1,9},{5... | collective-permute-start | bytes 1671176 | tf_op jit(solution)/shard_map/ppermute | solution.py:38
  353.1 60.1 %collective-permute-start.40 = (bf16[128,2176]{1,0:T(8,128)(2,1)}, bf16[128,2176]{1,0:T(8,128)(2,1)S(1)}, u32[]{:S(2)}, u32[]{:S(2)}) collective-permute-start(bf16[128,2176]{1,0:T(8,128)(2,1)} %get-tuple-element.149), channel_id=1, source_target_pairs={{0,24},{4,28},{8,16},{12,20},{16,8},{20,12},{24,0},{28,4},{1,25},{... | collective-permute-start | bytes 1671176 | tf_op jit(solution)/shard_map/ppermute | solution.py:38
  387.3 25.8 %collective-permute-start.39 = (bf16[128,2176]{1,0:T(8,128)(2,1)}, bf16[128,2176]{1,0:T(8,128)(2,1)S(1)}, u32[]{:S(2)}, u32[]{:S(2)}) collective-permute-start(bf16[128,2176]{1,0:T(8,128)(2,1)} %get-tuple-element.150), channel_id=1, source_target_pairs={{0,16},{4,20},{8,24},{12,28},{16,0},{20,4},{24,8},{28,12},{1,17},{... | collective-permute-start | bytes 1671176 | tf_op jit(solution)/shard_map/ppermute | solution.py:38
  388.4 24.8 %collective-permute-start.38 = (bf16[128,2176]{1,0:T(8,128)(2,1)S(1)}, bf16[128,2176]{1,0:T(8,128)(2,1)}, u32[]{:S(2)}, u32[]{:S(2)}) collective-permute-start(bf16[128,2176]{1,0:T(8,128)(2,1)S(1)} %get-tuple-element.151), channel_id=1, source_target_pairs={{0,8},{4,12},{8,0},{12,4},{16,24},{20,28},{24,16},{28,20},{1,9},{5... | collective-permute-start | bytes 1671176 | tf_op jit(solution)/shard_map/ppermute | solution.py:38
  392.3 26.0 %collective-permute-start.44 = (bf16[128,2176]{1,0:T(8,128)(2,1)}, bf16[128,2176]{1,0:T(8,128)(2,1)}, u32[]{:S(2)}, u32[]{:S(2)}) collective-permute-start(bf16[128,2176]{1,0:T(8,128)(2,1)} %add_convert_fusion.2), channel_id=1, source_target_pairs={{0,2},{1,3},{2,0},{3,1},{4,6},{5,7},{6,4},{7,5},{8,10},{9,11},{10,... | collective-permute-start | bytes 1671176 | tf_op jit(solution)/shard_map/ppermute | solution.py:38
  422.7 27.0 %collective-permute-start.47 = (bf16[128,2048]{1,0:T(8,128)(2,1)}, bf16[128,2048]{1,0:T(8,128)(2,1)}, u32[]{:S(2)}, u32[]{:S(2)}) collective-permute-start(bf16[128,2048]{1,0:T(8,128)(2,1)} %fusion.38.refs_0_), channel_id=1, source_target_pairs={{0,24},{4,28},{8,16},{12,20},{16,8},{20,12},{24,0},{28,4},{1,25},{... | collective-permute-start | bytes 1572872 | tf_op jit(solution)/shard_map/ppermute | solution.py:38
  424.2 35.8 %collective-permute-start.46 = (bf16[128,2048]{1,0:T(8,128)(2,1)}, bf16[128,2048]{1,0:T(8,128)(2,1)}, u32[]{:S(2)}, u32[]{:S(2)}) collective-permute-start(bf16[128,2048]{1,0:T(8,128)(2,1)} %fusion.38.refs_0_), channel_id=1, source_target_pairs={{0,16},{4,20},{8,24},{12,28},{16,0},{20,4},{24,8},{28,12},{1,17},{... | collective-permute-start | bytes 1572872 | tf_op jit(solution)/shard_map/ppermute | solution.py:38
  425.2 34.9 %collective-permute-start.45 = (bf16[128,2048]{1,0:T(8,128)(2,1)}, bf16[128,2048]{1,0:T(8,128)(2,1)}, u32[]{:S(2)}, u32[]{:S(2)}) collective-permute-start(bf16[128,2048]{1,0:T(8,128)(2,1)} %fusion.38.refs_0_), channel_id=1, source_target_pairs={{0,8},{4,12},{8,0},{12,4},{16,24},{20,28},{24,16},{28,20},{1,9},{5... | collective-permute-start | bytes 1572872 | tf_op jit(solution)/shard_map/ppermute | solution.py:38
  434.9 32.0 %collective-permute-start.48 = (bf16[128,2048]{1,0:T(8,128)(2,1)}, bf16[128,2048]{1,0:T(8,128)(2,1)}, u32[]{:S(2)}, u32[]{:S(2)}) collective-permute-start(bf16[128,2048]{1,0:T(8,128)(2,1)} %fusion.38.refs_0_), channel_id=1, source_target_pairs={{0,4},{4,0},{8,12},{12,8},{16,20},{20,16},{24,28},{28,24},{1,5},{5... | collective-permute-start | bytes 1572872 | tf_op jit(solution)/shard_map/ppermute | solution.py:38
  438.0 27.4 %all-to-all-start.4 = ((f32[32,1,1088]{2,1,0:T(1,128)}), f32[32,1,1088]{2,1,0:T(1,128)S(1)}, u32[]{:S(2)}, u32[]{:S(2)}) async-start(f32[32,1,1088]{2,1,0:T(1,128)} %reshape.233), calls=%async_computation.5 | async-start | bytes 294912 | tf_op jit(solution)/shard_map/all_to_all | solution.py:1018
  442.5 93.9 %collective-permute-start.63 = (bf16[2,2,512,512]{3,2,1,0:T(8,128)(2,1)}, bf16[2,2,512,512]{3,2,1,0:T(8,128)(2,1)}, u32[]{:S(2)}, u32[]{:S(2)}) collective-permute-start(bf16[2,2,512,512]{3,2,1,0:T(8,128)(2,1)} %bitcast.242), channel_id=1, source_target_pairs={{0,1},{1,0},{2,3},{3,2},{4,5},{5,4},{6,7},{7,6},{8,9},{9,8},{10,11... | collective-permute-start | bytes 6291464 | tf_op jit(solution)/shard_map/ppermute | solution.py:38
  449.7 19.3 %collective-permute-start.51 = (bf16[128,2048]{1,0:T(8,128)(2,1)}, bf16[128,2048]{1,0:T(8,128)(2,1)}, u32[]{:S(2)}, u32[]{:S(2)}) collective-permute-start(bf16[128,2048]{1,0:T(8,128)(2,1)} %collective-permute-done.47.refs_3_), channel_id=1, source_target_pairs={{0,4},{4,0},{8,12},{12,8},{16,20},{20,16},{24,28},{28,24},{1,5},{5... | collective-permute-start | bytes 1572872 | tf_op jit(solution)/shard_map/ppermute | solution.py:38
  467.0 193.3 %collective-permute-start.62 = (bf16[2,512,512]{2,1,0:T(8,128)(2,1)}, bf16[2,512,512]{2,1,0:T(8,128)(2,1)}, u32[]{:S(2)}, u32[]{:S(2)}) collective-permute-start(bf16[2,512,512]{2,1,0:T(8,128)(2,1)} %fusion.8), channel_id=1, source_target_pairs={{0,2},{1,3},{2,0},{3,1},{4,6},{5,7},{6,4},{7,5},{8,10},{9,11},{10,... | collective-permute-start | bytes 3145736 | tf_op jit(solution)/shard_map/ppermute | solution.py:38
  498.8 37.6 %collective-permute-start.59 = (f32[2,2,64]{2,1,0:T(2,128)S(1)}, f32[2,2,64]{2,1,0:T(2,128)S(1)}, u32[]{:S(2)}, u32[]{:S(2)}) collective-permute-start(f32[2,2,64]{2,1,0:T(2,128)S(1)} %pad_maximum_fusion.7), channel_id=1, source_target_pairs={{0,1},{1,0},{2,3},{3,2},{4,5},{5,4},{6,7},{7,6},{8,9},{9,8},{10,11... | collective-permute-start | bytes 3080 | tf_op jit(solution)/shard_map/ppermute | solution.py:38
  512.2 24.2 %collective-permute-start.57 = (bf16[2,64,2048]{2,1,0:T(8,128)(2,1)}, bf16[2,64,2048]{2,1,0:T(8,128)(2,1)}, u32[]{:S(2)}, u32[]{:S(2)}) collective-permute-start(bf16[2,64,2048]{2,1,0:T(8,128)(2,1)} %pad_maximum_fusion.6), channel_id=1, source_target_pairs={{0,1},{1,0},{2,3},{3,2},{4,5},{5,4},{6,7},{7,6},{8,9},{9,8},{10,11... | collective-permute-start | bytes 1572872 | tf_op jit(solution)/shard_map/ppermute | solution.py:38
  516.8 29.0 %all-to-all-start.3 = ((bf16[32,64,256]{2,1,0:T(8,128)(2,1)}), bf16[32,64,256]{2,1,0:T(8,128)(2,1)}, u32[]{:S(2)}, u32[]{:S(2)}) async-start(bf16[32,64,256]{2,1,0:T(8,128)(2,1)} %bitcast.209), calls=%async_computation.4 | async-start | bytes 2097152 | tf_op jit(solution)/shard_map/all_to_all | solution.py:973
  527.0 26.2 %collective-permute-start.53 = (bf16[512,2048]{1,0:T(8,128)(2,1)}, bf16[512,2048]{1,0:T(8,128)(2,1)}, u32[]{:S(2)}, u32[]{:S(2)}) collective-permute-start(bf16[512,2048]{1,0:T(8,128)(2,1)} %add_convert_fusion), channel_id=1, source_target_pairs={{0,4},{4,0},{8,12},{12,8},{16,20},{20,16},{24,28},{28,24},{1,5},{5... | collective-permute-start | bytes 6291464 | tf_op jit(solution)/shard_map/ppermute | solution.py:38
  545.8 128.7 %all-to-all-start.2 = ((bf16[32,64,512]{2,1,0:T(8,128)(2,1)}), bf16[32,64,512]{2,1,0:T(8,128)(2,1)S(1)}, u32[]{:S(2)}, u32[]{:S(2)}) async-start(bf16[32,64,512]{2,1,0:T(8,128)(2,1)} %bitcast.203), calls=%async_computation.3 | async-start | bytes 4194304 | tf_op jit(solution)/shard_map/all_to_all | solution.py:973
  555.3 27.7 %collective-permute-start.54 = (bf16[128,2048]{1,0:T(8,128)(2,1)S(1)}, bf16[128,2048]{1,0:T(8,128)(2,1)S(1)}, u32[]{:S(2)}, u32[]{:S(2)}) collective-permute-start(bf16[128,2048]{1,0:T(8,128)(2,1)S(1)} %get-tuple-element.155), channel_id=1, source_target_pairs={{0,8},{4,12},{8,0},{12,4},{16,24},{20,28},{24,16},{28,20},{1,9},{5... | collective-permute-start | bytes 1572872 | tf_op jit(solution)/shard_map/ppermute | solution.py:38
  557.4 104.5 %collective-permute-start.64 = (bf16[2,512,512]{2,1,0:T(8,128)(2,1)S(1)}, bf16[2,512,512]{2,1,0:T(8,128)(2,1)S(1)}, u32[]{:S(2)}, u32[]{:S(2)}) collective-permute-start(bf16[2,512,512]{2,1,0:T(8,128)(2,1)S(1)} %fusion.9), channel_id=1, source_target_pairs={{0,2},{1,3},{2,0},{3,1},{4,6},{5,7},{6,4},{7,5},{8,10},{9,11},{10,... | collective-permute-start | bytes 3145736 | tf_op jit(solution)/shard_map/ppermute | solution.py:38
  559.8 37.9 %collective-permute-start.56 = (bf16[128,2048]{1,0:T(8,128)(2,1)S(1)}, bf16[128,2048]{1,0:T(8,128)(2,1)S(1)}, u32[]{:S(2)}, u32[]{:S(2)}) collective-permute-start(bf16[128,2048]{1,0:T(8,128)(2,1)S(1)} %get-tuple-element.156), channel_id=1, source_target_pairs={{0,24},{4,28},{8,16},{12,20},{16,8},{20,12},{24,0},{28,4},{1,25},{... | collective-permute-start | bytes 1572872 | tf_op jit(solution)/shard_map/ppermute | solution.py:38
  561.3 36.8 %collective-permute-start.55 = (bf16[128,2048]{1,0:T(8,128)(2,1)S(1)}, bf16[128,2048]{1,0:T(8,128)(2,1)S(1)}, u32[]{:S(2)}, u32[]{:S(2)}) collective-permute-start(bf16[128,2048]{1,0:T(8,128)(2,1)S(1)} %get-tuple-element.157), channel_id=1, source_target_pairs={{0,16},{4,20},{8,24},{12,28},{16,0},{20,4},{24,8},{28,12},{1,17},{... | collective-permute-start | bytes 1572872 | tf_op jit(solution)/shard_map/ppermute | solution.py:38
  583.0 88.7 %collective-permute-start.65 = (bf16[2,256,2048]{2,1,0:T(8,128)(2,1)S(1)}, bf16[2,256,2048]{2,1,0:T(8,128)(2,1)S(1)}, u32[]{:S(2)}, u32[]{:S(2)}) collective-permute-start(bf16[2,256,2048]{2,1,0:T(8,128)(2,1)S(1)} %bitcast.241), channel_id=1, source_target_pairs={{0,1},{1,0},{2,3},{3,2},{4,5},{5,4},{6,7},{7,6},{8,9},{9,8},{10,11... | collective-permute-start | bytes 6291464 | tf_op jit(solution)/shard_map/ppermute | solution.py:38
  597.6 55.1 %collective-permute-start.60 = (f32[2,64]{1,0:T(2,128)S(1)}, f32[2,64]{1,0:T(2,128)S(1)}, u32[]{:S(2)}, u32[]{:S(2)}) collective-permute-start(f32[2,64]{1,0:T(2,128)S(1)} %bitcast_add_fusion.1), channel_id=1, source_target_pairs={{0,2},{1,3},{2,0},{3,1},{4,6},{5,7},{6,4},{7,5},{8,10},{9,11},{10,... | collective-permute-start | bytes 1544 | tf_op jit(solution)/shard_map/ppermute | solution.py:38
  598.1 60.0 %collective-permute-start.58 = (bf16[64,2048]{1,0:T(8,128)(2,1)S(1)}, bf16[64,2048]{1,0:T(8,128)(2,1)S(1)}, u32[]{:S(2)}, u32[]{:S(2)}) collective-permute-start(bf16[64,2048]{1,0:T(8,128)(2,1)S(1)} %fusion.20), channel_id=1, source_target_pairs={{0,2},{1,3},{2,0},{3,1},{4,6},{5,7},{6,4},{7,5},{8,10},{9,11},{10,... | collective-permute-start | bytes 786440 | tf_op jit(solution)/shard_map/ppermute | solution.py:38
  677.0 26.6 %collective-permute-start.52 = (bf16[128,2048]{1,0:T(8,128)(2,1)S(1)}, bf16[128,2048]{1,0:T(8,128)(2,1)S(1)}, u32[]{:S(2)}, u32[]{:S(2)}) collective-permute-start(bf16[128,2048]{1,0:T(8,128)(2,1)S(1)} %slice_bitcast_fusion.2), channel_id=1, source_target_pairs={{0,2},{1,3},{2,0},{3,1},{4,6},{5,7},{6,4},{7,5},{8,10},{9,11},{10,... | collective-permute-start | bytes 1572872 | tf_op jit(solution)/shard_map/ppermute | solution.py:38
  (78 other events, 1523.3 us)
Sparse Core Ops, SparseCore 0:
  39.6 63.8 all-gather.6
  387.4 94.1 reduce-scatter.1

commit v3 on v2

--- a/solution.py
+++ b/solution.py
@@ -60,6 +60,7 @@
 
 def gather_seq(values):
     near = gather_near(values)
+    near[0] = after(values, *near[1:2])
     return near + [hop(piece, "seq", 1) for piece in near]
 
 
@@ -79,10 +80,23 @@
     return total, sent
 
 
-def gather_batch(values):
+def scatter_chips(near, far):
+    size = lax.axis_size("seq")
+    sent = (near.astype(F32) + hop(far, "seq", 1).astype(F32)).astype(BF16)
+    groups = [list(range(core, size, 2)) for core in range(2)]
+    moved = lax.all_to_all(
+        sent, "seq", split_axis=0, concat_axis=0, axis_index_groups=groups, tiled=True
+    )
+    return jnp.sum(moved.astype(F32), axis=0), sent
+
+
+def gather_batch(values, *pins):
     pieces = [values]
     for t in range(1, lax.axis_size("batch")):
-        pieces.append(hop(pieces[t - 1], "batch", 1) if t % 2 and t > 1 else hop(values, "batch", t))
+        if t % 2 and t > 1:
+            pieces.append(hop(after(pieces[t - 1], *pieces[1 : t - 1], *pins), "batch", 1))
+        else:
+            pieces.append(hop(values, "batch", t))
     return pieces
 
 
@@ -128,8 +142,9 @@
 
 
 def weight_copies(at_ref, pieces, target, sems):
+    shard = target.shape[2]
     return [
-        pltpu.make_async_copy(piece, target.at[:, at_ref[1] ^ t], sems.at[t])
+        pltpu.make_async_copy(piece.at[:, pl.ds(0, shard)], target.at[:, at_ref[1] ^ t], sems.at[t])
         for t, piece in enumerate(pieces)
     ]
 
@@ -172,9 +187,9 @@
         square_ref[:, pl.ds(at, rows)] = sums[:, i * rows : (i + 1) * rows]
 
 
-def project_pairs(here, pieces, w_pieces, gain):
+def project_pairs(here, pieces, w_pieces, shard, gain):
     rows, width = pieces[0].shape
-    seq_size, shard, columns = w_pieces[0].shape
+    seq_size, _, columns = w_pieces[0].shape
     batch_size = len(w_pieces)
     per = max(1, 256 // rows)
     blocks = len(pieces) // per
@@ -464,14 +479,14 @@
 
 
 def router_chances(inputs, router, experts):
-    logits = dot(inputs, router)
+    logits = dot_nt(inputs, router)
     column = lax.broadcasted_iota(jnp.int32, logits.shape, 1)
     logits = jnp.where(column < experts, logits, MASKED)
     raised = jnp.exp(logits - jnp.max(logits, axis=-1, keepdims=True))
     return raised / jnp.sum(raised, axis=-1, keepdims=True)
 
 
-def acts_kernel(experts, blocks, per, k, at_ref, *refs):
+def acts_kernel(experts, blocks, per, at_ref, *refs):
     count = blocks * per
     pieces = refs[:count]
     (
@@ -479,7 +494,7 @@
         x_out, u_out, hidden_ref, gate_grad_ref, up_grad_ref, sums_ref, x_buffer, u_buffer, sems,
     ) = refs[count:]
     step = pl.program_id(0)
-    sides = [side_ref.at[at_ref[2 + r], k] for r in range(count)]
+    sides = [side_ref.at[at_ref[2 + r]] for r in range(count)]
 
     def copies_of(block):
         slot = block % 2
@@ -517,7 +532,7 @@
     sums_ref[...] = sums.astype(BF16)
 
 
-def run_acts(at, pieces, sides, k, router, w_gate, w_up, w_down, experts, parts):
+def run_acts(at, pieces, sides, router, w_gate, w_up, w_down, experts, parts):
     rows, width = pieces[0].shape
     total = rows * len(pieces)
     owned, _, hidden = w_gate.shape
@@ -525,19 +540,19 @@
     per = max(1, 256 // rows)
     blocks, size = len(pieces) // per, rows * per
     extra = 128 * -(-2 * experts // 128)
-    lanes = router.shape[1]
+    lanes = router.shape[0]
     token = lambda i, at: (i, 0)
     once = pl.Buffered(1)
     acts = jax.ShapeDtypeStruct((owned, total, piece), BF16)
     act_spec = pl.BlockSpec((owned, size, piece), lambda i, at: (0, i, 0))
     return pl.pallas_call(
-        functools.partial(acts_kernel, experts, blocks, per, k),
+        functools.partial(acts_kernel, experts, blocks, per),
         grid_spec=pltpu.PrefetchScalarGridSpec(
             num_scalar_prefetch=1,
             grid=(blocks,),
             in_specs=[pl.BlockSpec(memory_space=pl.ANY)] * (len(pieces) + 1)
             + [
-                pl.BlockSpec((width, lanes), lambda i, at: (0, 0), pipeline_mode=once),
+                pl.BlockSpec((lanes, width), lambda i, at: (0, 0), pipeline_mode=once),
                 pl.BlockSpec((owned, width, piece), lambda i, at: (0, 0, at[1]), pipeline_mode=once),
                 pl.BlockSpec((owned, width, piece), lambda i, at: (0, 0, at[1]), pipeline_mode=once),
                 pl.BlockSpec((owned, piece, width), lambda i, at: (0, at[1], 0), pipeline_mode=once),
@@ -568,23 +583,23 @@
     )(at, *pieces, sides, router, w_gate, w_up, w_down)
 
 
-def split_store(values, near_ref, far_ref):
-    middle = pl.num_programs(0) // 2
-
-    @pl.when(pl.program_id(0) < middle)
-    def _():
-        near_ref[...] = values
-
-    @pl.when(pl.program_id(0) >= middle)
-    def _():
-        far_ref[...] = values
-
-
-def rows_back_kernel(at_ref, gate_ref, up_ref, sums_ref, wg_ref, wu_ref, near_ref, far_ref):
+def rows_back_kernel(blocks, per, at_ref, gate_ref, up_ref, sums_ref, wg_ref, wu_ref, near_ref, far_ref):
     back = dot_nt(gate_ref[0], wg_ref[0]) + dot_nt(up_ref[0], wu_ref[0])
     for e in range(1, wg_ref.shape[0]):
         back += dot_nt(gate_ref[e], wg_ref[e]) + dot_nt(up_ref[e], wu_ref[e])
-    split_store(jnp.concatenate([back.astype(BF16), sums_ref[...]], axis=1), near_ref, far_ref)
+    back = back.astype(BF16)
+    step = pl.program_id(0)
+    rows, width = near_ref.shape[2], back.shape[1]
+
+    def store(out_ref):
+        for i in range(per):
+            at = at_ref[2 + step * per + i] // 2 % per
+            part = slice(i * rows, (i + 1) * rows)
+            out_ref[0, at, :, :width] = back[part]
+            out_ref[0, at, :, width:] = sums_ref[part, :]
+
+    pl.when(step < blocks // 2)(lambda: store(near_ref))
+    pl.when(step >= blocks // 2)(lambda: store(far_ref))
 
 
 def rows_out_kernel(sets, blocks, per, at_ref, *refs):
@@ -641,28 +656,34 @@
     return out.reshape(seq_size, sets, rows, width)
 
 
-def run_back(at, gates, ups, sums, w_gate, w_up):
+def run_back(at, gates, ups, sums, w_gate, w_up, rows):
     owned, total, piece = gates.shape
-    size = min(256, total // 2)
-    middle = total // (2 * size)
+    chips = total // (2 * rows)
+    per = max(1, 256 // rows)
+    size, blocks = rows * per, total // (rows * per)
+    middle = blocks // 2
     width, extra = w_gate.shape[1], sums.shape[1]
     act_spec = pl.BlockSpec((owned, size, piece), lambda i, at: (0, i, 0))
     weight_spec = pl.BlockSpec(
         (owned, width, piece), lambda i, at: (0, 0, at[1]), pipeline_mode=pl.Buffered(1)
     )
-    out = jax.ShapeDtypeStruct((total // 2, width + extra), BF16)
-    return pl.pallas_call(
-        rows_back_kernel,
+
+    def out_spec(first, last):
+        return pl.BlockSpec(
+            (1, per, rows, width + extra),
+            lambda i, at: (at[2 + jnp.clip(i, first, last) * per] // (2 * per), 0, 0, 0),
+        )
+
+    out = jax.ShapeDtypeStruct((chips // per, per, rows, width + extra), BF16)
+    results = pl.pallas_call(
+        functools.partial(rows_back_kernel, blocks, per),
         grid_spec=pltpu.PrefetchScalarGridSpec(
             num_scalar_prefetch=1,
-            grid=(total // size,),
+            grid=(blocks,),
             in_specs=[act_spec] * 2
             + [pl.BlockSpec((size, extra), lambda i, at: (i, 0))]
             + [weight_spec] * 2,
-            out_specs=[
-                pl.BlockSpec((size, width + extra), lambda i, at: (jnp.minimum(i, middle - 1), 0)),
-                pl.BlockSpec((size, width + extra), lambda i, at: (jnp.maximum(i - middle, 0), 0)),
-            ],
+            out_specs=[out_spec(0, middle - 1), out_spec(middle, blocks - 1)],
         ),
         out_shape=[out, out],
         compiler_params=pltpu.CompilerParams(vmem_limit_bytes=VMEM_BYTES),
@@ -672,6 +693,7 @@
             transcendentals=0,
         ),
     )(at, gates, ups, sums, w_gate, w_up)
+    return [item.reshape(chips, rows, width + extra) for item in results]
 
 
 def down_kernel(sets, at_ref, *refs):
@@ -805,41 +827,56 @@
 
     near_tokens = gather_near(low_tokens)
 
-    def columns_of(*weights):
-        cut = [w.reshape(shard, seq_size, wide).transpose(1, 0, 2) for w in weights]
-        return lax.all_to_all(jnp.concatenate(cut, axis=2), "seq", split_axis=0, concat_axis=0, tiled=True)
-
-    pair_cut = columns_of(w_query, w_key)
-
-    lanes = 128 * -(-(experts + 4) // 128)
-    gains = jnp.stack([attn_gain, query_gain, key_gain, ffn_gain], axis=1)
-    small = jnp.zeros((shard, lanes), BF16)
-    small = put(put(small, w_router, (0, 0)), gains, (0, experts))
-    small = lax.all_gather(small, "batch", axis=0, tiled=True)
-    router = lax.all_gather(small, "seq", axis=0, tiled=True)
-    gains = router[:, experts : experts + 4].astype(F32).T
+    def cut_of(*weights):
+        return jnp.concatenate(
+            [w.reshape(shard, seq_size, wide).transpose(1, 0, 2) for w in weights], axis=2
+        )
+
+    def exchange(blocks):
+        return lax.all_to_all(blocks, "seq", split_axis=0, concat_axis=0, tiled=True)
+
+    small = jnp.concatenate(
+        [jnp.stack([attn_gain, query_gain, key_gain, ffn_gain]), w_router.T], axis=0
+    )
+    items, fit = experts + 4, 2 * wide // shard
+    deep = 8 * -(-items // (8 * fit))
+    small = jnp.pad(small, ((0, deep * fit - items), (0, 0))).reshape(1, deep, 2 * wide)
+    small = jnp.broadcast_to(small, (seq_size, deep, 2 * wide))
+    pair_cut = exchange(jnp.concatenate([cut_of(w_query, w_key), small], axis=1))
+
+    ids = expert_ids[0]
+    lanes = 128 * -(-experts // 128)
+    choices = jnp.any(ids[:, :, None] == jnp.arange(lanes, dtype=jnp.int32), axis=1)
+    side = jnp.concatenate([out_grad[0], choices.astype(BF16)], axis=1)
+    partner = [hop(side, "batch", half)] if parts == 2 else []
+    token_pieces = near_tokens + [hop(after(piece, pair_cut, *partner), "seq", 1) for piece in near_tokens]
+    value_cut = exchange(after(cut_of(w_value), pair_cut))
+    pair_pieces = gather_batch(after(pair_cut, *token_pieces), value_cut)
+    value_pieces = gather_batch(after(value_cut, *pair_pieces[2:3]), *pair_pieces)
+    out_pieces = gather_batch(after(w_out, *pair_pieces), *value_pieces)
+    small = jnp.stack([item[:, shard:] for item in pair_pieces])
+    small = small.reshape(batch_size, seq_size, deep * fit, shard)[
+        jnp.arange(batch_size, dtype=jnp.int32) ^ batch_at
+    ]
+    small = small.transpose(2, 1, 0, 3).reshape(deep * fit, width)
+    gains = small[:4].astype(F32)
     attn_norm_gain, ffn_norm_gain = gains[0], gains[3]
     head_gains = lax.dynamic_slice_in_dim(gains[1:3], seq_at * wide, wide, 1)
-
-    pair_pieces = gather_batch(after(pair_cut, router))
-    value_cut = columns_of(after(w_value, pair_cut))
-    value_pieces = gather_batch(after(value_cut, *pair_pieces[2:3]))
-    token_pieces = near_tokens + [hop(piece, "seq", 1) for piece in near_tokens]
+    router = jnp.pad(small[4:items], ((0, lanes - experts), (0, 0)))
     w_mix = jnp.zeros((batch_size, shard, width), BF16)
-    for t, piece in enumerate(gather_batch(after(w_out, *value_pieces[2:3]))):
+    for t, piece in enumerate(out_pieces):
         w_mix = put(w_mix, piece[None], (batch_at ^ t, 0, 0))
     w_mix = w_mix.reshape(wide, width)
 
-    ids = expert_ids[0]
-    choices = jnp.any(ids[:, :, None] == jnp.arange(lanes, dtype=jnp.int32), axis=1)
-    side = jnp.concatenate([out_grad[0], choices.astype(BF16)], axis=1)
-    sides = jnp.stack([side] + ([hop(side, "batch", half)] if parts == 2 else []))
-    sides = lax.all_gather(after(sides, *near_tokens), "seq", axis=0)
-    counts = jnp.sum(sides[:, 0, :, width:].astype(F32), axis=(0, 1)).astype(jnp.int32)
+    sides = [
+        lax.all_gather(after(item, *pins), "seq", axis=0)
+        for item, pins in zip([side, *partner], ([value_cut, *pair_pieces[1:3]], pair_pieces))
+    ]
+    counts = jnp.sum(sides[0][:, :, width:].astype(F32), axis=(0, 1)).astype(jnp.int32)
     counts_here = lax.dynamic_slice_in_dim(counts, seq_at * owned, owned, 0)
 
     normed, pairs, squares, pair_weights = project_pairs(
-        here, token_pieces, pair_pieces, attn_norm_gain[None]
+        here, token_pieces, pair_pieces, shard, after(attn_norm_gain[None], *value_pieces[:3])
     )
     values, value_weights = project_values(here, normed, value_pieces)
     pair_weights, value_weights = (w.reshape(width, -1) for w in (pair_weights, value_weights))
@@ -868,7 +905,7 @@
         segments[0][:, None],
         segments[0][None, :],
     )
-    mixed_low = attend()
+    mixed_low = after(attend(), sides[0])
     middle = total // 2
     far = dot(mixed_low[middle:], w_mix).astype(BF16)
     residual = inputs + scatter_seq(dot(mixed_low[:middle], w_mix).astype(BF16), far)[0]
@@ -877,7 +914,7 @@
     ffn_in = (ffn_unit * ffn_norm_gain).astype(BF16)
 
     def acts_of(k, pieces):
-        return run_acts(at, pieces, sides, k, router, w_gate, w_up, w_down, experts, parts)
+        return run_acts(at, pieces, sides[k], router, w_gate, w_up, w_down, experts, parts)
 
     ffn_pieces = gather_seq(ffn_in)
     results = [acts_of(0, ffn_pieces)]
@@ -895,6 +932,11 @@
     def send_group(theirs):
         return [hop(theirs[t - 1], "batch", t) for t in range(1, half)]
 
+    def gather_group(theirs):
+        groups = [list(range(first, first + half)) for first in range(0, batch_size, half)]
+        blocks = lax.all_gather(theirs, "batch", axis=0, axis_index_groups=groups)
+        return [take_block(blocks, in_group ^ t)[t - 1] for t in range(1, half)]
+
     def group_sum(mine, moved):
         total = mine[0].astype(F32)
         for item in moved:
@@ -912,14 +954,30 @@
         at_back = after(at, gate_theirs)
     backs, sent = [], []
     for k in reversed(range(parts)):
-        pair = run_back(at_back, gate_acts[k], up_acts[k], sums[k], w_gate, w_up)
-        summed, low = scatter_seq(*pair)
+        near, far = run_back(at_back, gate_acts[k], up_acts[k], sums[k], w_gate, w_up, rows)
+        if half > 1 and not sent:
+            up_theirs = into(after(others, near), acts=up_acts)
+            near = after(near, up_theirs)
+        if k == 0:
+            mix = run_out(after(at, near), hiddens, w_down, rows)
+            far = after(far, mix, *backs, *gate_moved)
+        summed, low = scatter_chips(near, far)
         backs.insert(0, summed)
-        sent += low
-        at_back = after(at, *pair)
-    back = backs[0]
+        sent.append(low)
+        at_back = after(at, low)
+    gate_mine = last = into(after(own, *sent), acts=gate_acts)
+    other = hop(backs[1].astype(BF16), "batch", half) if parts == 2 else gate_mine
+    if half > 1:
+        last = down_theirs = down(after(others, gate_mine))
+    gate_sum = group_sum(gate_mine, gate_moved)
+    up_mine = into(after(own, last, other), acts=up_acts)
+    gate_other = swap_part(gate_sum) if parts == 2 else gate_sum
+    if half > 1:
+        up_moved = gather_group(up_theirs)
+        down_moved = gather_group(down_theirs)
+    back = after(backs[0], up_mine, gate_sum)
     if parts == 2:
-        back = back + hop(backs[1].astype(BF16), "batch", half).astype(F32)
+        back = back + other.astype(F32)
 
     grad_ffn_in = back[:, :width]
     grad_chances = choices[:, :experts] * (
@@ -929,31 +987,27 @@
     grad_logits = (
         chances * (grad_chances - jnp.sum(chances * grad_chances, axis=-1, keepdims=True))
     ).astype(BF16)
-    grad_ffn_in = grad_ffn_in + dot_nt(grad_logits, router[:, :experts])
+    grad_ffn_in = grad_ffn_in + dot(grad_logits, router[:experts])
     scaled = grad_ffn_in * ffn_norm_gain
     inner = jnp.mean(scaled * ffn_unit, axis=-1, keepdims=True)
     grad_residual = out_grad[0].astype(F32) + ffn_scale * (scaled - ffn_unit * inner)
     grad_attn = grad_residual.astype(BF16)
 
-    later = own
-    if half > 1:
-        up_theirs = into(after(others, *sent), acts=up_acts)
-        down_theirs = down(after(others, up_theirs))
-        up_moved = send_group(after(up_theirs, grad_attn))
-        later = after(own, down_theirs)
-    mix = run_out(after(at, *sent, later), hiddens, w_down, rows)
-    later = after(later, mix)
-    gate_mine = into(later, acts=gate_acts)
-    up_mine = into(later, acts=up_acts)
-    down_mine = down(later)
-    gate_sum = group_sum(gate_mine, [after(item, grad_attn) for item in gate_moved])
-    gate_other = swap_part(gate_sum) if parts == 2 else None
-    mix = lax.psum_scatter(mix, "seq", scatter_dimension=0)
-
-    grad_pieces = gather_seq(grad_attn)
-    grad_mixed, out_term = mix_back(grad_pieces, mixed_low, w_mix)
+    grad_near = gather_near(grad_attn)
+    arrived = grad_near[1:]
+    up_sum = group_sum(up_mine, [after(item, grad_attn) for item in up_moved])
+    grad_near[0] = after(grad_attn, up_sum, *arrived)
+    grad_pieces = grad_near + [hop(piece, "seq", 1) for piece in grad_near]
+    up_other = swap_part(up_sum) if parts == 2 else up_sum
+    grad_mixed, out_term = mix_back(grad_pieces, after(mixed_low, gate_other), w_mix)
+    mix = lax.psum_scatter(after(mix, grad_mixed), "seq", scatter_dimension=0)
     scaled_q, scaled_k, value_low, inner, gain_terms = attend(grad_mixed=grad_mixed)
-    inner = reordered(sum_seq(inner.T), order).T / width
+
+    def term_of(values):
+        return dot_tn(normed, values).astype(BF16).reshape(seq_size * batch_size, shard, -1)
+
+    value_term = term_of(value_low)
+    inner = reordered(sum_seq(after(inner.T, value_term)), order).T / width
     rel_scales = reordered(scales, order).T
     lows = []
     for i, item in enumerate((scaled_q, scaled_k)):
@@ -961,21 +1015,49 @@
         unit = pairs[:, i * wide : (i + 1) * wide] * scale
         lows.append((scale * (item - unit * inner[:, i : i + 1])).astype(BF16))
     pair_low = jnp.concatenate(lows, axis=1)
+    pair_term = term_of(pair_low)
+    late_low = after(pair_low, pair_term)
 
     def rows_of(at):
-        return (dot_nt(pair_low[at], pair_weights) + dot_nt(value_low[at], value_weights)).astype(BF16)
+        return (dot_nt(late_low[at], pair_weights) + dot_nt(value_low[at], value_weights)).astype(BF16)
 
     far = rows_of(slice(middle, total))
-    grad_normed, sent = scatter_seq(rows_of(slice(0, middle)), far)
-
-    def head_sums(values):
-        term = dot_tn(normed, values).astype(BF16).reshape(seq_size * batch_size, shard, -1)
+    grad_normed, _ = scatter_seq(rows_of(slice(0, middle)), far)
+    mix_other = hop(after(mix[1], value_low), "batch", half) if parts == 2 else mix
+    grad_normed = after(grad_normed, mix_other)
+    down_mine = down(after(own, grad_normed))
+
+    def head_sums(term, extra):
+        term = jnp.concatenate([term, *extra], axis=1)
         term = lax.all_to_all(term, ("seq", "batch"), split_axis=0, concat_axis=0, tiled=True)
-        term = after(term, grad_normed).reshape(seq_size, batch_size, shard, -1)
-        return jnp.sum(term.astype(F32), axis=1)
-
-    value_sums = head_sums(value_low)
-    pair_sums = head_sums(after(pair_low, far))
+        term = after(term, grad_normed)
+        total = jnp.sum(term[:, :shard].reshape(seq_size, batch_size, shard, -1).astype(F32), axis=1)
+        return total, jnp.sum(term[:, shard:].astype(F32), axis=0)
+
+    def two_parts(values):
+        high = values.astype(BF16)
+        return jnp.concatenate([high, (values - high.astype(F32)).astype(BF16)], axis=0)
+
+    def in_rows(items):
+        fit = wide // shard
+        deep = 8 * -(-items.shape[0] // (8 * fit))
+        items = jnp.pad(items, ((0, deep * fit - items.shape[0]), (0, 0), (0, 0), (0, 0)))
+        return items.transpose(1, 2, 0, 3).reshape(seq_size * batch_size, deep, wide)
+
+    router_term = jnp.concatenate(
+        [dot_tn(grad_logits, ffn_in), jnp.sum(grad_ffn_in * ffn_unit, axis=0)[None]], axis=0
+    )
+    router_items = two_parts(router_term).reshape(-1, seq_size, batch_size, shard)
+    gain_items = two_parts(gain_terms).reshape(4, 1, batch_size, shard)
+    mine_only = (jnp.arange(seq_size) == seq_at)[None, :, None, None]
+    gain_items = jnp.where(mine_only, gain_items, jnp.zeros_like(gain_items))
+    items = in_rows(jnp.concatenate([gain_items, router_items], axis=0))
+    value_sums, items = head_sums(value_term, [items])
+    items = items.reshape(-1, shard)
+    gain_sum = items[0:2] + items[2:4]
+    router_sum = items[4 : 5 + experts] + items[5 + experts : 6 + 2 * experts]
+    router_grad, ffn_gain_grad = router_sum[:experts].T, router_sum[experts]
+    pair_sums, _ = head_sums(pair_term, [])
     query_grad, key_grad, value_grad = (
         item.transpose(1, 0, 2).reshape(shard, width)
         for item in (pair_sums[:, :, :wide], pair_sums[:, :, wide:], value_sums)
@@ -984,40 +1066,24 @@
     def spread(summed, other):
         if parts == 1:
             return summed[0]
-        keep, other = take_block(summed, part_at), after(other, grad_normed).astype(F32)
+        keep, other = take_block(summed, part_at), other.astype(F32)
         return jnp.where(
             part_at == 0,
             jnp.concatenate([keep, other], axis=-1),
             jnp.concatenate([other, keep], axis=-1),
         )
 
-    up_sum = group_sum(up_mine, [after(item, value_low) for item in up_moved])
-    up_other = swap_part(up_sum) if parts == 2 else None
-    if half > 1:
-        down_moved = [
-            after(item, grad_normed) for item in send_group(after(down_theirs, value_low, *up_moved))
-        ]
-    down_grad = group_sum(down_mine, down_moved)
-    gate_grad = spread(gate_sum, gate_other)
-    up_grad = spread(up_sum, up_other)
+    down_grad = group_sum(down_mine, [after(item, pair_term) for item in down_moved])
+    gate_grad = spread(gate_sum, after(gate_other, pair_term))
+    up_grad = spread(up_sum, after(up_other, grad_normed))
     out_proj_grad = scatter_batch(
-        out_term.reshape(batch_size, shard, width), batch_at, BF16, value_low, grad_normed
-    )
-    gain_blocks = gain_terms.reshape(2, batch_size, shard).transpose(1, 0, 2)
-    gain_sum = scatter_batch(gain_blocks, batch_at, F32, pair_low, grad_normed)
+        out_term.reshape(batch_size, shard, width), batch_at, BF16, far, grad_normed
+    )
 
     mine = mix[0].astype(F32)
     if parts == 2:
-        mine = mine + after(hop(after(mix[1], value_low), "batch", half), grad_normed).astype(F32)
+        mine = mine + mix_other.astype(F32)
     block_out = (residual + mine).astype(BF16)
-
-    router_term = jnp.concatenate(
-        [dot_tn(grad_logits, ffn_in), jnp.sum(grad_ffn_in * ffn_unit, axis=0)[None]], axis=0
-    )
-    router_term = router_term.reshape(experts + 1, seq_size * batch_size, shard).transpose(1, 0, 2)
-    router_sum = lax.all_to_all(router_term, ("seq", "batch"), split_axis=0, concat_axis=0, tiled=True)
-    router_sum = jnp.sum(after(router_sum, value_low), axis=0)
-    router_grad, ffn_gain_grad = router_sum[:experts].T, router_sum[experts]
 
     attn_scale = norm_scale(inputs)
     attn_unit = inputs * attn_scale

time: 720 us -> 697 us (0.968)
  waiting for transfers between devices: 258 us -> 212 us
  local copies, waits for them, and re-layouts: 29.5 us -> 48.2 us
  starting transfers between devices: 84.7 us -> 76.7 us
    ppermute x66 -> x56, waiting for transfers between devices: 240 us -> 194 us  [hop(): return lax.ppermute(values, axis, [(i, i ^ mask) for i in range(size)])]
    all_to_all x0 -> x2, blocking collectives: none -> 31.5 us  [exchange(): lax.all_to_all(blocks, 'seq', split_axis=0, concat_axis=0, tiled=True)]
    all_gather x2 -> x0, blocking collectives: 26.4 us -> none  [the longest x1 13.3 us: on_device(): router = lax.all_gather(small, 'seq', axis=0, tiled=True)]
    reduce_scatter x1, waiting for transfers between devices: 0.01 us -> 17.3 us  [on_device(): mix = lax.psum_scatter(after(mix, grad_mixed), 'seq', scatter_dimension=0)]
    all_to_all x2, waiting for transfers between devices: 9.39 us -> 0.01 us  [head_sums(): lax.all_to_all(term, ('seq', 'batch'), split_axis=0, concat_axis=0, tiled...]
    all_to_all x3 -> x2, waiting for transfers between devices: 8.6 us -> 0.01 us  [scatter_chips(): lax.all_to_all(sent, 'seq', split_axis=0, concat_axis=0, axis_index_group...]
    ppermute x66 -> x56, starting transfers between devices: 64.4 us -> 58.6 us  [hop(): return lax.ppermute(values, axis, [(i, i ^ mask) for i in range(size)])]
  transfers between devices with their start and end apart: 73 -> 65, of which waited for: 29 -> 29; matrix products, arithmetic and copies ran while one was open for 13% -> 15% of each run, Pallas kernels for 22% -> 22%
where the time goes in v3:
time: 697 us; the launch traced here: 689 us
  waiting for transfers between devices  212 us (30%)
  Pallas kernels  205 us (29%)
  starting transfers between devices  76.7 us (11%)
  other arithmetic  61.3 us (9%)
  blocking collectives  50.1 us (7%)
  local copies, waits for them, and re-layouts  48.2 us (7%)
  matrix products  20 us (3%)
  between operations  15.2 us (2%)
    ppermute x56, waiting for transfers between devices, hop(): return lax.ppermute(values, axis, [(i, i ^ mask) for i in range(size)])  194 us
    ppermute x56, starting transfers between devices, hop(): return lax.ppermute(values, axis, [(i, i ^ mask) for i in range(size)])  58.6 us
    pallas_call x2, Pallas kernels, run_acts(): pl.pallas_call(functools.partial(acts_kernel, experts, blocks, per), grid...  50.8 us
    pallas_call x4, Pallas kernels, in_blocks(): pl.pallas_call(functools.partial(in_kernel, sets), grid_spec=pltpu.Prefet...  35.1 us
    pallas_call x2, Pallas kernels, run_back(): pl.pallas_call(functools.partial(rows_back_kernel, blocks, per), grid_spe...  32.5 us
    all_to_all x2, blocking collectives, exchange(): lax.all_to_all(blocks, 'seq', split_axis=0, concat_axis=0, tiled=True)  31.5 us
    pallas_call x1, Pallas kernels, attention(): pl.pallas_call(functools.partial(attend_back_kernel, blocks, size), grid=...  19.9 us
    all_gather x2, blocking collectives, sum_seq(): return jnp.sum(lax.all_gather(values, 'seq', axis=0), axis=0)  18.6 us
  transfers between devices with their start and end apart: 65, of which 29 were waited for; matrix products, arithmetic and copies ran while one was open for 15% of the time, Pallas kernels for 22%

profile of v3, /device:TPU:0, one launch (start us, length us, event | category | flops | bytes accessed | tf_op | source)
XLA Modules:
  0.0 688.7 jit_solution(13079791786880154558)
XLA Ops:
  7.2 4.0 collective-permute-start.2
  14.1 3.1 collective-permute-start.3
  19.9 21.1 %all_to_all.30.refs_8_ = bf16[8,72,512]{2,1,0:T(8,128)(2,1)S(1)} all-to-all(bf16[8,72,512]{2,1,0:T(8,128)(2,1)S(1)} %pad_maximum_fusion.2), channel_id=1, replica_groups=mesh['seq'=8,'batch'=4] {'seq'}, dimensions={0} | all-to-all | bytes 1179648 | tf_op jit(solution)/shard_map/all_to_all | solution.py:836
  45.6 2.6 collective-permute-start.9
  49.8 10.4 %all_to_all.31.refs_0_ = bf16[8,64,256]{2,1,0:T(8,128)(2,1)S(1)} all-to-all(bf16[8,64,256]{2,1,0:T(8,128)(2,1)S(1)} %bitcast.197), channel_id=1, replica_groups=mesh['seq'=8,'batch'=4] {'seq'}, dimensions={0} | all-to-all | bytes 524288 | tf_op jit(solution)/shard_map/all_to_all | solution.py:836
  60.2 14.4 %collective-permute-done.9.refs_10_ = bf16[8,72,512]{2,1,0:T(8,128)(2,1)S(1)} collective-permute-done((bf16[8,72,512]{2,1,0:T(8,128)(2,1)S(1)}, bf16[8,72,512]{2,1,0:T(8,128)(2,1)S(1)}, u32[]{:S(2)}, u32[]{:S(2)}) %collective-permute-start.9) | collective-permute-done | bytes 589856 | tf_op jit(solution)/shard_map/ppermute | solution.py:38
  79.0 3.1 collective-permute-start.12
  87.8 10.5 %collective-permute-done.10.refs_11_ = bf16[8,72,512]{2,1,0:T(8,128)(2,1)} collective-permute-done((bf16[8,72,512]{2,1,0:T(8,128)(2,1)}, bf16[8,72,512]{2,1,0:T(8,128)(2,1)}, u32[]{:S(2)}, u32[]{:S(2)}) %collective-permute-start.10) | collective-permute-done | bytes 589856 | tf_op jit(solution)/shard_map/ppermute | solution.py:38
  99.8 2.5 collective-permute-start.14
  102.2 6.3 collective-permute-done.11.refs_1_
  111.2 9.7 %shard_map.289 = (bf16[1024,2048]{1,0:T(8,128)(2,1)}, f32[1024,512]{1,0:T(8,128)}, f32[2,1024]{1,0:T(2,128)}, bf16[8,4,64,512]{3,2,1,0:T(8,128)(2,1)}) custom-call(s32[10]{0:T(128)} %get-tuple-element.205.at_ref, bf16[128,2048]{1,0:T(8,128)(2,1)} %bitcast.175, bf16[128,2048]{1,0:T(8,128)(2,1)} %collective-permute-done.refs_1_, ...), custom_call_target="tpu_custom_call" | custom-call | flops 2147483648 | bytes 16777216 | tf_op jit(solution)/shard_map/pallas_call | solution.py:197
  121.0 9.3 %all-gather.6 = f32[8,2,1024]{2,1,0:T(2,128)S(1)} all-gather(f32[1,2,1024]{2,1,0:T(2,128)} %bitcast.211), channel_id=2, replica_groups=mesh['seq'=8,'batch'=4] {'seq'}, dimensions={0}, use_global_device_ids=true | all-gather | bytes 73728 | tf_op jit(solution)/shard_map/all_gather | solution.py:885
  134.5 6.2 shard_map.290
  140.7 10.1 %shard_map.291.refs_8_ = bf16[1024,256]{1,0:T(8,128)(2,1)} custom-call(s32[8]{0:T(128)} %gather_fusion, f32[1024,512]{1,0:T(8,128)} %get-tuple-element.100.q_ref.k_ref, f32[1024,512]{1,0:T(8,128)} %get-tuple-element.100.q_ref.k_ref, bf16[1024,256]{1,0:T(8,128)(2,1)} %get-tuple-element.103.v_ref, f32[1024,2]{1,0:T(8,128)} %get-tuple-element.193.scale_ref, ...), custom_call_target="tpu_custom_call" | custom-call | flops 1073741824 | bytes 4194304 | tf_op jit(solution)/shard_map/pallas_call | solution.py:448
  153.7 3.4 collective-permute-done.17
  162.5 14.5 %collective-permute-done.18 = bf16[128,2048]{1,0:T(8,128)(2,1)S(1)} collective-permute-done((bf16[128,2048]{1,0:T(8,128)(2,1)}, bf16[128,2048]{1,0:T(8,128)(2,1)S(1)}, u32[]{:S(2)}, u32[]{:S(2)}) %collective-permute-start.18) | collective-permute-done | bytes 524320 | tf_op jit(solution)/shard_map/ppermute | solution.py:38
  176.9 11.9 %collective-permute-done.20 = bf16[128,2048]{1,0:T(8,128)(2,1)S(1)} collective-permute-done((bf16[128,2048]{1,0:T(8,128)(2,1)}, bf16[128,2048]{1,0:T(8,128)(2,1)S(1)}, u32[]{:S(2)}, u32[]{:S(2)}) %collective-permute-start.20) | collective-permute-done | bytes 524320 | tf_op jit(solution)/shard_map/ppermute | solution.py:38
  195.6 2.4 collective-permute-start.28
  198.0 8.9 %collective-permute-done.21.refs_1_ = bf16[128,2048]{1,0:T(8,128)(2,1)S(1)} collective-permute-done((bf16[128,2048]{1,0:T(8,128)(2,1)S(1)}, bf16[128,2048]{1,0:T(8,128)(2,1)S(1)}, u32[]{:S(2)}, u32[]{:S(2)}) %collective-permute-start.21) | collective-permute-done | bytes 524320 | tf_op jit(solution)/shard_map/ppermute | solution.py:38
  206.9 10.2 %collective-permute-done.23.refs_3_ = bf16[128,2048]{1,0:T(8,128)(2,1)S(1)} collective-permute-done((bf16[128,2048]{1,0:T(8,128)(2,1)S(1)}, bf16[128,2048]{1,0:T(8,128)(2,1)S(1)}, u32[]{:S(2)}, u32[]{:S(2)}) %collective-permute-start.23) | collective-permute-done | bytes 524320 | tf_op jit(solution)/shard_map/ppermute | solution.py:38
  225.6 25.3 %shard_map.292 = (bf16[1024,2048]{1,0:T(8,128)(2,1)}, bf16[1024,2048]{1,0:T(8,128)(2,1)}, bf16[2,1024,512]{2,1,0:T(8,128)(2,1)}, bf16[2,1024,512]{2,1,0:T(8,128)...) custom-call(s32[10]{0:T(128)} %get-tuple-element.131.at_ref, bf16[128,2048]{1,0:T(8,128)(2,1)} %copy-done.23, ...), custom_call_target="tpu_custom_call" | custom-call | flops 12884901888 | bytes 35651584 | tf_op jit(solution)/shard_map/pallas_call | solution.py:548
  255.3 25.5 %shard_map.293 = (bf16[1024,2048]{1,0:T(8,128)(2,1)}, bf16[1024,2048]{1,0:T(8,128)(2,1)}, bf16[2,1024,512]{2,1,0:T(8,128)(2,1)}, bf16[2,1024,512]{2,1,0:T(8,128)...) custom-call(s32[10]{0:T(128)} %get-tuple-element.131.at_ref, bf16[128,2048]{1,0:T(8,128)(2,1)} %copy-done.55, ...), custom_call_target="tpu_custom_call" | custom-call | flops 12884901888 | bytes 35651584 | tf_op jit(solution)/shard_map/pallas_call | solution.py:548
  280.8 8.6 %shard_map.294 = bf16[1,2,2,512,512]{4,3,2,1,0:T(8,128)(2,1)} custom-call(s32[1]{0:T(128)} %bitcast.26.at_ref, bf16[1024,2048]{1,0:T(8,128)(2,1)} %get-tuple-element.110.refs_0_, bf16[1024,2048]{1,0:T(8,128)(2,1)} %get-tuple-element.117.refs_1_, bf16[2,1024,512]{2,1,0:T(8,128)(2,1)} %get-tuple-element.118.refs_2_.gate_ref, ...), custom_call_target="tpu_custom_call" | custom-call | flops 4294967296 | bytes 8388608 | tf_op jit(solution)/shard_map/pallas_call | solution.py:747
  289.4 16.2 %shard_map.295 = (bf16[2,2,128,2176]{3,2,1,0:T(8,128)(2,1)}, bf16[2,2,128,2176]{3,2,1,0:T(8,128)(2,1)}) custom-call(s32[10]{0:T(128)} %get-tuple-element.131.at_ref, bf16[2,1024,512]{2,1,0:T(8,128)(2,1)} %get-tuple-element.119.refs_3_.gate_ref, bf16[2,1024,512]{2,1,0:T(8,128)(2,1)} %get-tuple-element.121.up_ref.refs_3_, ...), custom_call_target="tpu_custom_call" | custom-call | flops 8589934592 | bytes 16777216 | tf_op jit(solution)/shard_map/pallas_call | solution.py:678
  307.4 8.8 %shard_map.296 = bf16[1,2,2,512,512]{4,3,2,1,0:T(8,128)(2,1)} custom-call(s32[1]{0:T(128)} %bitcast.26.at_ref, bf16[1024,2048]{1,0:T(8,128)(2,1)} %get-tuple-element.110.refs_0_, bf16[1024,2048]{1,0:T(8,128)(2,1)} %get-tuple-element.117.refs_1_, bf16[2,1024,512]{2,1,0:T(8,128)(2,1)} %get-tuple-element.125.refs_2_.up_ref, ...), custom_call_target="tpu_custom_call" | custom-call | flops 4294967296 | bytes 8388608 | tf_op jit(solution)/shard_map/pallas_call | solution.py:747
  316.2 3.5 add_convert_fusion.1
  319.7 3.6 all-to-all-start.2
  324.1 15.4 %shard_map.298 = bf16[2,2,2,2,128,2048]{5,4,3,2,1,0:T(8,128)(2,1)} custom-call(s32[10]{0:T(128)} %get-tuple-element.131.at_ref, bf16[2,1024,512]{2,1,0:T(8,128)(2,1)} %get-tuple-element.132.refs_0_, bf16[2,1024,512]{2,1,0:T(8,128)(2,1)} %get-tuple-element.133.refs_1_, bf16[2,1024,2048]{2,1,0:T(8,128)(2,1)} %refs_2_.1), custom_call_target="tpu_custom_call" | custom-call | flops 8589934592 | bytes 12582912 | tf_op jit(solution)/shard_map/pallas_call | solution.py:635
  339.5 16.3 %shard_map.297 = (bf16[2,2,128,2176]{3,2,1,0:T(8,128)(2,1)}, bf16[2,2,128,2176]{3,2,1,0:T(8,128)(2,1)}) custom-call(s32[10]{0:T(128)} %get-tuple-element.131.at_ref, bf16[2,1024,512]{2,1,0:T(8,128)(2,1)} %get-tuple-element.118.refs_2_.gate_ref, bf16[2,1024,512]{2,1,0:T(8,128)(2,1)} %get-tuple-element.125.refs_2_.up_ref, ...), custom_call_target="tpu_custom_call" | custom-call | flops 8589934592 | bytes 16777216 | tf_op jit(solution)/shard_map/pallas_call | solution.py:678
  356.9 13.9 %collective-permute-done.37 = bf16[2,2,512,512]{3,2,1,0:T(8,128)(2,1)} collective-permute-done((bf16[2,2,512,512]{3,2,1,0:T(8,128)(2,1)}, bf16[2,2,512,512]{3,2,1,0:T(8,128)(2,1)}, u32[]{:S(2)}, u32[]{:S(2)}) %collective-permute-start.37) | collective-permute-done | bytes 2097184 | tf_op jit(solution)/shard_map/ppermute | solution.py:38
  375.4 3.5 add_convert_fusion
  379.0 3.6 all-to-all-start.3
  382.6 8.6 %shard_map.299 = bf16[1,2,2,512,512]{4,3,2,1,0:T(8,128)(2,1)} custom-call(s32[1]{0:T(128)} %bitcast.34.at_ref, bf16[1024,2048]{1,0:T(8,128)(2,1)} %get-tuple-element.110.refs_0_, bf16[1024,2048]{1,0:T(8,128)(2,1)} %get-tuple-element.117.refs_1_, bf16[2,1024,512]{2,1,0:T(8,128)(2,1)} %get-tuple-element.118.refs_2_.gate_ref, ...), custom_call_target="tpu_custom_call" | custom-call | flops 4294967296 | bytes 8388608 | tf_op jit(solution)/shard_map/pallas_call | solution.py:747
  391.3 8.8 %shard_map.300 = bf16[1,2,256,2048]{3,2,1,0:T(8,128)(2,1)} custom-call(s32[1]{0:T(128)} %bitcast.26.at_ref, bf16[2,1024,512]{2,1,0:T(8,128)(2,1)} %get-tuple-element.132.refs_0_, bf16[2,1024,512]{2,1,0:T(8,128)(2,1)} %get-tuple-element.133.refs_1_, bf16[1024,2048]{1,0:T(8,128)(2,1)} %get-tuple-element.138.refs_2_, bf16[1024,2048]{1,0:T(8,128)(2,1)} %get-tuple-element.139.refs_3_), custom_call_target="tpu_custom_call" | custom-call | flops 4294967296 | bytes 10485760 | tf_op jit(solution)/shard_map/pallas_call | solution.py:713
  400.2 2.9 convert_add_fusion.2
  408.3 9.0 %shard_map.301 = bf16[1,2,2,512,512]{4,3,2,1,0:T(8,128)(2,1)} custom-call(s32[1]{0:T(128)} %bitcast.34.at_ref, bf16[1024,2048]{1,0:T(8,128)(2,1)} %get-tuple-element.110.refs_0_, bf16[1024,2048]{1,0:T(8,128)(2,1)} %get-tuple-element.117.refs_1_, bf16[2,1024,512]{2,1,0:T(8,128)(2,1)} %get-tuple-element.125.refs_2_.up_ref, ...), custom_call_target="tpu_custom_call" | custom-call | flops 4294967296 | bytes 8388608 | tf_op jit(solution)/shard_map/pallas_call | solution.py:747
  421.2 2.8 collective-permute-start.42
  427.0 2.7 convert_add_fusion.1
  429.7 7.2 %collective-permute-done.42.refs_3_ = bf16[128,2048]{1,0:T(8,128)(2,1)S(1)} collective-permute-done((bf16[128,2048]{1,0:T(8,128)(2,1)S(1)}, bf16[128,2048]{1,0:T(8,128)(2,1)S(1)}, u32[]{:S(2)}, u32[]{:S(2)}) %collective-permute-start.42) | collective-permute-done | bytes 524320 | tf_op jit(solution)/shard_map/ppermute | solution.py:38
  436.9 10.2 %collective-permute-done.41.refs_2_ = bf16[128,2048]{1,0:T(8,128)(2,1)} collective-permute-done((bf16[128,2048]{1,0:T(8,128)(2,1)S(1)}, bf16[128,2048]{1,0:T(8,128)(2,1)}, u32[]{:S(2)}, u32[]{:S(2)}) %collective-permute-start.41) | collective-permute-done | bytes 524320 | tf_op jit(solution)/shard_map/ppermute | solution.py:38
  448.4 6.7 collective-permute-done.47
  456.7 7.8 %shard_map.302 = (bf16[1024,256]{1,0:T(8,128)(2,1)}, bf16[256,2048]{1,0:T(8,128)(2,1)}) custom-call(bf16[128,2048]{1,0:T(8,128)(2,1)} %copy-done.40, bf16[128,2048]{1,0:T(8,128)(2,1)} %collective-permute-done.40.refs_1_, bf16[128,2048]{1,0:T(8,128)(2,1)} %collective-permute-done.41.refs_2_, bf16[128,2048]{1,0:T(8,128)(2,1)} %copy-done.60, ...), custom_call_target="tpu_custom_call" | custom-call | flops 2147483648 | bytes 8388608 | tf_op jit(solution)/shard_map/pallas_call | solution.py:301
  468.2 3.1 dynamic-slice_bitcast_fusion.3
  472.0 2.8 fusion.9
  474.9 19.9 %shard_map.303 = (f32[1024,256]{1,0:T(8,128)}, f32[1024,256]{1,0:T(8,128)}, bf16[1024,256]{1,0:T(8,128)(2,1)}, f32[1024,2]{1,0:T(8,128)}, f32[2,256]{1,0:T(2,128)}) custom-call(s32[8]{0:T(128)} %gather_fusion, f32[1024,512]{1,0:T(8,128)} %get-tuple-element.100.q_ref.k_ref, f32[1024,512]{1,0:T(8,128)} %get-tuple-element.100.q_ref.k_ref, ...), custom_call_target="tpu_custom_call" | custom-call | flops 2684354560 | bytes 8388608 | tf_op jit(solution)/shard_map/pallas_call | solution.py:460
  496.5 4.8 convolution_convert_fusion.3
  502.5 9.4 %all-gather.7 = f32[8,2,1024]{2,1,0:T(2,128)S(1)} all-gather(f32[1,2,1024]{2,1,0:T(2,128)S(1)} %copy.142), channel_id=6, replica_groups=mesh['seq'=8,'batch'=4] {'seq'}, dimensions={0}, use_global_device_ids=true | all-gather | bytes 73728 | tf_op jit(solution)/shard_map/all_gather | solution.py:885
  517.6 3.8 convolution_convert_fusion
  522.5 6.6 all-to-all-start.5
  531.1 2.7 add_convert_fusion.2
  535.6 2.4 collective-permute-start.53
  541.2 2.9 maximum_select_fusion
  545.4 19.5 %collective-permute-done.53 = bf16[2,64,2048]{2,1,0:T(8,128)(2,1)} collective-permute-done((bf16[2,64,2048]{2,1,0:T(8,128)(2,1)S(1)}, bf16[2,64,2048]{2,1,0:T(8,128)(2,1)}, u32[]{:S(2)}, u32[]{:S(2)}) %collective-permute-start.53) | collective-permute-done | bytes 524320 | tf_op jit(solution)/shard_map/ppermute | solution.py:38
  565.0 4.1 all-to-all-start.4
  570.8 2.6 collective-permute-start.54
  573.4 2.8 add_convert_fusion.6
  579.8 3.2 dynamic-slice_bitcast_fusion
  582.9 17.3 %reduce-scatter.2.cloned.1.call-done = bf16[1,2,128,2048]{3,2,1,0:T(8,128)(2,1)} async-done(((bf16[8,2,128,2048]{3,2,1,0:T(8,128)(2,1)}), bf16[1,2,128,2048]{3,2,1,0:T(8,128)(2,1)}) %reduce-scatter.2.cloned.1.call-update) | async-done | bytes 1048592 | tf_op jit(solution)/shard_map/reduce_scatter | solution.py:1003
  601.3 8.7 %collective-permute-done.50 = bf16[128,2048]{1,0:T(8,128)(2,1)S(1)} collective-permute-done((bf16[128,2048]{1,0:T(8,128)(2,1)}, bf16[128,2048]{1,0:T(8,128)(2,1)S(1)}, u32[]{:S(2)}, u32[]{:S(2)}) %collective-permute-start.50) | collective-permute-done | bytes 524320 | tf_op jit(solution)/shard_map/ppermute | solution.py:38
  611.4 10.6 %collective-permute-done.52 = bf16[128,2048]{1,0:T(8,128)(2,1)S(1)} collective-permute-done((bf16[128,2048]{1,0:T(8,128)(2,1)}, bf16[128,2048]{1,0:T(8,128)(2,1)S(1)}, u32[]{:S(2)}, u32[]{:S(2)}) %collective-permute-start.52) | collective-permute-done | bytes 524320 | tf_op jit(solution)/shard_map/ppermute | solution.py:38
  624.7 27.1 %collective-permute-done.48 = bf16[128,2048]{1,0:T(8,128)(2,1)S(1)} collective-permute-done((bf16[128,2048]{1,0:T(8,128)(2,1)S(1)}, bf16[128,2048]{1,0:T(8,128)(2,1)S(1)}, u32[]{:S(2)}, u32[]{:S(2)}) %collective-permute-start.48) | collective-permute-done | bytes 524320 | tf_op jit(solution)/shard_map/ppermute | solution.py:38
  655.4 8.7 %shard_map.304 = bf16[1,2,256,2048]{3,2,1,0:T(8,128)(2,1)} custom-call(s32[1]{0:T(128)} %bitcast.34.at_ref, bf16[2,1024,512]{2,1,0:T(8,128)(2,1)} %get-tuple-element.132.refs_0_, bf16[2,1024,512]{2,1,0:T(8,128)(2,1)} %get-tuple-element.133.refs_1_, bf16[1024,2048]{1,0:T(8,128)(2,1)} %get-tuple-element.138.refs_2_, bf16[1024,2048]{1,0:T(8,128)(2,1)} %get-tuple-element.139.refs_3_), custom_call_target="tpu_custom_call" | custom-call | flops 4294967296 | bytes 10485760 | tf_op jit(solution)/shard_map/pallas_call | solution.py:713
  673.2 2.8 convert_add_fusion
  678.0 2.9 maximum_select_fusion.1
  (371 shorter events, 129.2 us)
Async XLA Ops:
  7.2 143.7 %all-gather.13.cloned.1.call-start = ((), (), s32[]{:S(2)}) async-start(), calls=%async_computation.8 | async-start | bytes 5013504 | tf_op jit(solution)/shard_map/all_gather | solution.py:872
  7.2 33.9 %collective-permute-start.2 = (bf16[128,2048]{1,0:T(8,128)(2,1)}, bf16[128,2048]{1,0:T(8,128)(2,1)}, u32[]{:S(2)}, u32[]{:S(2)}) collective-permute-start(bf16[128,2048]{1,0:T(8,128)(2,1)} %bitcast.172), channel_id=1, source_target_pairs={{0,24},{4,28},{8,16},{12,20},{16,8},{20,12},{24,0},{28,4},{1,25},{... | collective-permute-start | bytes 1572872 | tf_op jit(solution)/shard_map/ppermute | solution.py:38
  11.2 29.9 %collective-permute-start.1 = (bf16[128,2048]{1,0:T(8,128)(2,1)}, bf16[128,2048]{1,0:T(8,128)(2,1)}, u32[]{:S(2)}, u32[]{:S(2)}) collective-permute-start(bf16[128,2048]{1,0:T(8,128)(2,1)} %bitcast.173), channel_id=1, source_target_pairs={{0,16},{4,20},{8,24},{12,28},{16,0},{20,4},{24,8},{28,12},{1,17},{... | collective-permute-start | bytes 1572872 | tf_op jit(solution)/shard_map/ppermute | solution.py:38
  11.7 29.4 %collective-permute-start = (bf16[128,2048]{1,0:T(8,128)(2,1)}, bf16[128,2048]{1,0:T(8,128)(2,1)}, u32[]{:S(2)}, u32[]{:S(2)}) collective-permute-start(bf16[128,2048]{1,0:T(8,128)(2,1)} %bitcast.174), channel_id=1, source_target_pairs={{0,8},{4,12},{8,0},{12,4},{16,24},{20,28},{24,16},{28,20},{1,9},{5... | collective-permute-start | bytes 1572872 | tf_op jit(solution)/shard_map/ppermute | solution.py:38
  14.1 27.0 %collective-permute-start.3 = (bf16[128,2176]{1,0:T(8,128)(2,1)S(1)}, bf16[128,2176]{1,0:T(8,128)(2,1)S(1)}, u32[]{:S(2)}, u32[]{:S(2)}) collective-permute-start(bf16[128,2176]{1,0:T(8,128)(2,1)S(1)} %pad_maximum_fusion.3), channel_id=1, source_target_pairs={{0,2},{1,3},{2,0},{3,1},{4,6},{5,7},{6,4},{7,5},{8,10},{9,11},{10,... | collective-permute-start | bytes 1671176 | tf_op jit(solution)/shard_map/ppermute | solution.py:38
  41.1 2.0 collective-permute-start.4
  41.2 2.9 collective-permute-start.5
  41.7 3.1 collective-permute-start.6
  41.8 3.8 collective-permute-start.7
  45.6 29.0 %collective-permute-start.9 = (bf16[8,72,512]{2,1,0:T(8,128)(2,1)S(1)}, bf16[8,72,512]{2,1,0:T(8,128)(2,1)S(1)}, u32[]{:S(2)}, u32[]{:S(2)}) collective-permute-start(bf16[8,72,512]{2,1,0:T(8,128)(2,1)S(1)} %all_to_all.30.refs_8_), channel_id=1, source_target_pairs={{0,2},{1,3},{2,0},{3,1},{4,6},{5,7},{6,4},{7,5},{8,10},{9,11},{10,... | collective-permute-start | bytes 1769480 | tf_op jit(solution)/shard_map/ppermute | solution.py:38
  48.2 27.2 %collective-permute-start.8 = (bf16[8,72,512]{2,1,0:T(8,128)(2,1)S(1)}, bf16[8,72,512]{2,1,0:T(8,128)(2,1)}, u32[]{:S(2)}, u32[]{:S(2)}) collective-permute-start(bf16[8,72,512]{2,1,0:T(8,128)(2,1)S(1)} %all_to_all.30.refs_8_), channel_id=1, source_target_pairs={{0,1},{1,0},{2,3},{3,2},{4,5},{5,4},{6,7},{7,6},{8,9},{9,8},{10,11... | collective-permute-start | bytes 1769480 | tf_op jit(solution)/shard_map/ppermute | solution.py:38
  75.4 176.7 %all-gather.15.cloned.1.call-start = ((), (), s32[]{:S(2)}) async-start(), calls=%async_computation.9 | async-start | bytes 5013504 | tf_op jit(solution)/shard_map/all_gather | solution.py:872
  76.1 22.2 %collective-permute-start.10 = (bf16[8,72,512]{2,1,0:T(8,128)(2,1)}, bf16[8,72,512]{2,1,0:T(8,128)(2,1)}, u32[]{:S(2)}, u32[]{:S(2)}) collective-permute-start(bf16[8,72,512]{2,1,0:T(8,128)(2,1)} %copy-done.48), channel_id=1, source_target_pairs={{0,1},{1,0},{2,3},{3,2},{4,5},{5,4},{6,7},{7,6},{8,9},{9,8},{10,11... | collective-permute-start | bytes 1769480 | tf_op jit(solution)/shard_map/ppermute | solution.py:38
  79.0 23.2 %collective-permute-start.12 = (bf16[8,64,256]{2,1,0:T(8,128)(2,1)S(1)}, bf16[8,64,256]{2,1,0:T(8,128)(2,1)}, u32[]{:S(2)}, u32[]{:S(2)}) collective-permute-start(bf16[8,64,256]{2,1,0:T(8,128)(2,1)S(1)} %all_to_all.31.refs_0_), channel_id=1, source_target_pairs={{0,2},{1,3},{2,0},{3,1},{4,6},{5,7},{6,4},{7,5},{8,10},{9,11},{10,... | collective-permute-start | bytes 786440 | tf_op jit(solution)/shard_map/ppermute | solution.py:38
  82.1 26.4 %collective-permute-start.11 = (bf16[8,64,256]{2,1,0:T(8,128)(2,1)S(1)}, bf16[8,64,256]{2,1,0:T(8,128)(2,1)}, u32[]{:S(2)}, u32[]{:S(2)}) collective-permute-start(bf16[8,64,256]{2,1,0:T(8,128)(2,1)S(1)} %all_to_all.31.refs_0_), channel_id=1, source_target_pairs={{0,1},{1,0},{2,3},{3,2},{4,5},{5,4},{6,7},{7,6},{8,9},{9,8},{10,11... | collective-permute-start | bytes 786440 | tf_op jit(solution)/shard_map/ppermute | solution.py:38
  98.3 34.0 %collective-permute-start.15 = (bf16[64,2048]{1,0:T(8,128)(2,1)S(1)}, bf16[64,2048]{1,0:T(8,128)(2,1)S(1)}, u32[]{:S(2)}, u32[]{:S(2)}) collective-permute-start(bf16[64,2048]{1,0:T(8,128)(2,1)S(1)} %copy-done.45), channel_id=1, source_target_pairs={{0,2},{1,3},{2,0},{3,1},{4,6},{5,7},{6,4},{7,5},{8,10},{9,11},{10,... | collective-permute-start | bytes 786440 | tf_op jit(solution)/shard_map/ppermute | solution.py:38
  99.8 32.6 %collective-permute-start.14 = (bf16[64,2048]{1,0:T(8,128)(2,1)S(1)}, bf16[64,2048]{1,0:T(8,128)(2,1)S(1)}, u32[]{:S(2)}, u32[]{:S(2)}) collective-permute-start(bf16[64,2048]{1,0:T(8,128)(2,1)S(1)} %copy-done.45), channel_id=1, source_target_pairs={{0,1},{1,0},{2,3},{3,2},{4,5},{5,4},{6,7},{7,6},{8,9},{9,8},{10,11... | collective-permute-start | bytes 786440 | tf_op jit(solution)/shard_map/ppermute | solution.py:38
  111.2 21.1 %collective-permute-start.13 = (bf16[8,64,256]{2,1,0:T(8,128)(2,1)}, bf16[8,64,256]{2,1,0:T(8,128)(2,1)S(1)}, u32[]{:S(2)}, u32[]{:S(2)}) collective-permute-start(bf16[8,64,256]{2,1,0:T(8,128)(2,1)} %collective-permute-done.12.refs_2_), channel_id=1, source_target_pairs={{0,1},{1,0},{2,3},{3,2},{4,5},{5,4},{6,7},{7,6},{8,9},{9,8},{10,11... | collective-permute-start | bytes 786440 | tf_op jit(solution)/shard_map/ppermute | solution.py:38
  132.3 18.5 %collective-permute-start.16 = (bf16[64,2048]{1,0:T(8,128)(2,1)S(1)}, bf16[64,2048]{1,0:T(8,128)(2,1)S(1)}, u32[]{:S(2)}, u32[]{:S(2)}) collective-permute-start(bf16[64,2048]{1,0:T(8,128)(2,1)S(1)} %collective-permute-done.15), channel_id=1, source_target_pairs={{0,1},{1,0},{2,3},{3,2},{4,5},{5,4},{6,7},{7,6},{8,9},{9,8},{10,11... | collective-permute-start | bytes 786440 | tf_op jit(solution)/shard_map/ppermute | solution.py:38
  152.8 4.2 collective-permute-start.17
  158.9 18.0 %collective-permute-start.18 = (bf16[128,2048]{1,0:T(8,128)(2,1)}, bf16[128,2048]{1,0:T(8,128)(2,1)S(1)}, u32[]{:S(2)}, u32[]{:S(2)}) collective-permute-start(bf16[128,2048]{1,0:T(8,128)(2,1)} %get-tuple-element.182), channel_id=1, source_target_pairs={{0,8},{4,12},{8,0},{12,4},{16,24},{20,28},{24,16},{28,20},{1,9},{5... | collective-permute-start | bytes 1572872 | tf_op jit(solution)/shard_map/ppermute | solution.py:38
  160.1 28.7 %collective-permute-start.20 = (bf16[128,2048]{1,0:T(8,128)(2,1)}, bf16[128,2048]{1,0:T(8,128)(2,1)S(1)}, u32[]{:S(2)}, u32[]{:S(2)}) collective-permute-start(bf16[128,2048]{1,0:T(8,128)(2,1)} %get-tuple-element.183), channel_id=1, source_target_pairs={{0,24},{4,28},{8,16},{12,20},{16,8},{20,12},{24,0},{28,4},{1,25},{... | collective-permute-start | bytes 1572872 | tf_op jit(solution)/shard_map/ppermute | solution.py:38
  161.6 28.0 %collective-permute-start.19 = (bf16[128,2048]{1,0:T(8,128)(2,1)}, bf16[128,2048]{1,0:T(8,128)(2,1)}, u32[]{:S(2)}, u32[]{:S(2)}) collective-permute-start(bf16[128,2048]{1,0:T(8,128)(2,1)} %get-tuple-element.184), channel_id=1, source_target_pairs={{0,16},{4,20},{8,24},{12,28},{16,0},{20,4},{24,8},{28,12},{1,17},{... | collective-permute-start | bytes 1572872 | tf_op jit(solution)/shard_map/ppermute | solution.py:38
  192.1 14.9 %collective-permute-start.21 = (bf16[128,2048]{1,0:T(8,128)(2,1)S(1)}, bf16[128,2048]{1,0:T(8,128)(2,1)S(1)}, u32[]{:S(2)}, u32[]{:S(2)}) collective-permute-start(bf16[128,2048]{1,0:T(8,128)(2,1)S(1)} %multiply_convert_fusion.2.refs_0_), channel_id=1, source_target_pairs={{0,8},{4,12},{8,0},{12,4},{16,24},{20,28},{24,16},{28,20},{1,9},{5... | collective-permute-start | bytes 1572872 | tf_op jit(solution)/shard_map/ppermute | solution.py:38
  192.7 24.4 %collective-permute-start.23 = (bf16[128,2048]{1,0:T(8,128)(2,1)S(1)}, bf16[128,2048]{1,0:T(8,128)(2,1)S(1)}, u32[]{:S(2)}, u32[]{:S(2)}) collective-permute-start(bf16[128,2048]{1,0:T(8,128)(2,1)S(1)} %multiply_convert_fusion.2.refs_0_), channel_id=1, source_target_pairs={{0,24},{4,28},{8,16},{12,20},{16,8},{20,12},{24,0},{28,4},{1,25},{... | collective-permute-start | bytes 1572872 | tf_op jit(solution)/shard_map/ppermute | solution.py:38
  194.1 24.5 %collective-permute-start.22 = (bf16[128,2048]{1,0:T(8,128)(2,1)S(1)}, bf16[128,2048]{1,0:T(8,128)(2,1)}, u32[]{:S(2)}, u32[]{:S(2)}) collective-permute-start(bf16[128,2048]{1,0:T(8,128)(2,1)S(1)} %multiply_convert_fusion.2.refs_0_), channel_id=1, source_target_pairs={{0,16},{4,20},{8,24},{12,28},{16,0},{20,4},{24,8},{28,12},{1,17},{... | collective-permute-start | bytes 1572872 | tf_op jit(solution)/shard_map/ppermute | solution.py:38
  195.6 25.6 %collective-permute-start.28 = (bf16[128,2048]{1,0:T(8,128)(2,1)S(1)}, bf16[128,2048]{1,0:T(8,128)(2,1)S(1)}, u32[]{:S(2)}, u32[]{:S(2)}) collective-permute-start(bf16[128,2048]{1,0:T(8,128)(2,1)S(1)} %multiply_convert_fusion.2.refs_0_), channel_id=1, source_target_pairs={{0,2},{1,3},{2,0},{3,1},{4,6},{5,7},{6,4},{7,5},{8,10},{9,11},{10,... | collective-permute-start | bytes 1572872 | tf_op jit(solution)/shard_map/ppermute | solution.py:38
  217.1 4.1 collective-permute-start.27
  218.6 3.0 collective-permute-start.26
  218.6 3.0 collective-permute-start.24
  219.1 3.0 collective-permute-start.25
  222.1 28.9 %collective-permute-start.31 = (bf16[128,2048]{1,0:T(8,128)(2,1)S(1)}, bf16[128,2048]{1,0:T(8,128)(2,1)S(1)}, u32[]{:S(2)}, u32[]{:S(2)}) collective-permute-start(bf16[128,2048]{1,0:T(8,128)(2,1)S(1)} %collective-permute-done.28.refs_0_), channel_id=1, source_target_pairs={{0,24},{4,28},{8,16},{12,20},{16,8},{20,12},{24,0},{28,4},{1,25},{... | collective-permute-start | bytes 1572872 | tf_op jit(solution)/shard_map/ppermute | solution.py:38
  223.7 27.4 %collective-permute-start.30 = (bf16[128,2048]{1,0:T(8,128)(2,1)S(1)}, bf16[128,2048]{1,0:T(8,128)(2,1)S(1)}, u32[]{:S(2)}, u32[]{:S(2)}) collective-permute-start(bf16[128,2048]{1,0:T(8,128)(2,1)S(1)} %collective-permute-done.28.refs_0_), channel_id=1, source_target_pairs={{0,16},{4,20},{8,24},{12,28},{16,0},{20,4},{24,8},{28,12},{1,17},{... | collective-permute-start | bytes 1572872 | tf_op jit(solution)/shard_map/ppermute | solution.py:38
  224.0 27.1 %collective-permute-start.29 = (bf16[128,2048]{1,0:T(8,128)(2,1)S(1)}, bf16[128,2048]{1,0:T(8,128)(2,1)}, u32[]{:S(2)}, u32[]{:S(2)}) collective-permute-start(bf16[128,2048]{1,0:T(8,128)(2,1)S(1)} %collective-permute-done.28.refs_0_), channel_id=1, source_target_pairs={{0,8},{4,12},{8,0},{12,4},{16,24},{20,28},{24,16},{28,20},{1,9},{5... | collective-permute-start | bytes 1572872 | tf_op jit(solution)/shard_map/ppermute | solution.py:38
  251.1 3.7 collective-permute-start.33
  251.6 3.1 collective-permute-start.34
  251.7 3.6 collective-permute-start.35
  305.7 10.5 %collective-permute-start.36 = (bf16[4,128,2176]{2,1,0:T(8,128)(2,1)}, bf16[4,128,2176]{2,1,0:T(8,128)(2,1)}, u32[]{:S(2)}, u32[]{:S(2)}) collective-permute-start(bf16[4,128,2176]{2,1,0:T(8,128)(2,1)} %bitcast.220), channel_id=1, source_target_pairs={{0,4},{4,0},{8,12},{12,8},{16,20},{20,16},{24,28},{28,24},{1,5},{5... | collective-permute-start | bytes 6684680 | tf_op jit(solution)/shard_map/ppermute | solution.py:38
  305.8 65.1 %collective-permute-start.37 = (bf16[2,2,512,512]{3,2,1,0:T(8,128)(2,1)}, bf16[2,2,512,512]{3,2,1,0:T(8,128)(2,1)}, u32[]{:S(2)}, u32[]{:S(2)}) collective-permute-start(bf16[2,2,512,512]{3,2,1,0:T(8,128)(2,1)} %bitcast.33), channel_id=1, source_target_pairs={{0,1},{1,0},{2,3},{3,2},{4,5},{5,4},{6,7},{7,6},{8,9},{9,8},{10,11... | collective-permute-start | bytes 6291464 | tf_op jit(solution)/shard_map/ppermute | solution.py:38
  319.7 36.1 %all-to-all-start.2 = ((bf16[4,128,2176]{2,1,0:T(8,128)(2,1)}), bf16[4,128,2176]{2,1,0:T(8,128)(2,1)S(1)}, u32[]{:S(2)}, u32[]{:S(2)}) async-start(bf16[4,128,2176]{2,1,0:T(8,128)(2,1)} %add_convert_fusion.1), calls=%async_computation.2 | async-start | bytes 4456448 | tf_op jit(solution)/shard_map/all_to_all | solution.py:87
  323.3 101.3 %all-gather.17.cloned.1.call-start = ((), (), s32[]{:S(2)}) async-start(), calls=%async_computation.10 | async-start | bytes 6291456 | tf_op jit(solution)/shard_map/all_gather | solution.py:937
  370.9 4.6 collective-permute-start.38
  372.5 30.6 %collective-permute-start.39 = (bf16[128,2176]{1,0:T(8,128)(2,1)}, bf16[128,2176]{1,0:T(8,128)(2,1)}, u32[]{:S(2)}, u32[]{:S(2)}) collective-permute-start(bf16[128,2176]{1,0:T(8,128)(2,1)} %convert_reduce_fusion.1), channel_id=1, source_target_pairs={{0,2},{1,3},{2,0},{3,1},{4,6},{5,7},{6,4},{7,5},{8,10},{9,11},{10,... | collective-permute-start | bytes 1671176 | tf_op jit(solution)/shard_map/ppermute | solution.py:38
  379.0 38.4 %all-to-all-start.3 = ((bf16[4,128,2176]{2,1,0:T(8,128)(2,1)}), bf16[4,128,2176]{2,1,0:T(8,128)(2,1)S(1)}, u32[]{:S(2)}, u32[]{:S(2)}) async-start(bf16[4,128,2176]{2,1,0:T(8,128)(2,1)} %add_convert_fusion), calls=%async_computation.3 | async-start | bytes 4456448 | tf_op jit(solution)/shard_map/all_to_all | solution.py:87
  382.6 197.2 %all-gather.19.cloned.1.call-start = ((), (), s32[]{:S(2)}) async-start(), calls=%async_computation.11 | async-start | bytes 6291456 | tf_op jit(solution)/shard_map/all_gather | solution.py:937
  400.1 200.1 %reduce-scatter.2.cloned.1.call-start = ((), (), s32[]{:S(2)}) async-start(), calls=%async_computation.7 | async-start | bytes 9437184 | tf_op jit(solution)/shard_map/reduce_scatter | solution.py:1003
  406.1 49.0 %collective-permute-start.47 = (bf16[2,512,512]{2,1,0:T(8,128)(2,1)}, bf16[2,512,512]{2,1,0:T(8,128)(2,1)}, u32[]{:S(2)}, u32[]{:S(2)}) collective-permute-start(bf16[2,512,512]{2,1,0:T(8,128)(2,1)} %fusion.8), channel_id=1, source_target_pairs={{0,2},{1,3},{2,0},{3,1},{4,6},{5,7},{6,4},{7,5},{8,10},{9,11},{10,... | collective-permute-start | bytes 3145736 | tf_op jit(solution)/shard_map/ppermute | solution.py:38
  421.2 15.8 %collective-permute-start.42 = (bf16[128,2048]{1,0:T(8,128)(2,1)S(1)}, bf16[128,2048]{1,0:T(8,128)(2,1)S(1)}, u32[]{:S(2)}, u32[]{:S(2)}) collective-permute-start(bf16[128,2048]{1,0:T(8,128)(2,1)S(1)} %get-tuple-element.143.refs_0_), channel_id=1, source_target_pairs={{0,24},{4,28},{8,16},{12,20},{16,8},{20,12},{24,0},{28,4},{1,25},{... | collective-permute-start | bytes 1572872 | tf_op jit(solution)/shard_map/ppermute | solution.py:38
  424.0 23.1 %collective-permute-start.41 = (bf16[128,2048]{1,0:T(8,128)(2,1)S(1)}, bf16[128,2048]{1,0:T(8,128)(2,1)}, u32[]{:S(2)}, u32[]{:S(2)}) collective-permute-start(bf16[128,2048]{1,0:T(8,128)(2,1)S(1)} %get-tuple-element.143.refs_0_), channel_id=1, source_target_pairs={{0,16},{4,20},{8,24},{12,28},{16,0},{20,4},{24,8},{28,12},{1,17},{... | collective-permute-start | bytes 1572872 | tf_op jit(solution)/shard_map/ppermute | solution.py:38
  424.6 22.8 %collective-permute-start.40 = (bf16[128,2048]{1,0:T(8,128)(2,1)S(1)}, bf16[128,2048]{1,0:T(8,128)(2,1)}, u32[]{:S(2)}, u32[]{:S(2)}) collective-permute-start(bf16[128,2048]{1,0:T(8,128)(2,1)S(1)} %get-tuple-element.143.refs_0_), channel_id=1, source_target_pairs={{0,8},{4,12},{8,0},{12,4},{16,24},{20,28},{24,16},{28,20},{1,9},{5... | collective-permute-start | bytes 1572872 | tf_op jit(solution)/shard_map/ppermute | solution.py:38
  447.3 7.7 %collective-permute-start.46 = (bf16[128,2048]{1,0:T(8,128)(2,1)S(1)}, bf16[128,2048]{1,0:T(8,128)(2,1)S(1)}, u32[]{:S(2)}, u32[]{:S(2)}) collective-permute-start(bf16[128,2048]{1,0:T(8,128)(2,1)S(1)} %collective-permute-done.42.refs_3_), channel_id=1, source_target_pairs={{0,4},{4,0},{8,12},{12,8},{16,20},{20,16},{24,28},{28,24},{1,5},{5... | collective-permute-start | bytes 1572872 | tf_op jit(solution)/shard_map/ppermute | solution.py:38
  447.3 7.7 %collective-permute-start.45 = (bf16[128,2048]{1,0:T(8,128)(2,1)}, bf16[128,2048]{1,0:T(8,128)(2,1)S(1)}, u32[]{:S(2)}, u32[]{:S(2)}) collective-permute-start(bf16[128,2048]{1,0:T(8,128)(2,1)} %collective-permute-done.41.refs_2_), channel_id=1, source_target_pairs={{0,4},{4,0},{8,12},{12,8},{16,20},{20,16},{24,28},{28,24},{1,5},{5... | collective-permute-start | bytes 1572872 | tf_op jit(solution)/shard_map/ppermute | solution.py:38
  447.9 7.2 %collective-permute-start.43 = (bf16[128,2048]{1,0:T(8,128)(2,1)S(1)}, bf16[128,2048]{1,0:T(8,128)(2,1)S(1)}, u32[]{:S(2)}, u32[]{:S(2)}) collective-permute-start(bf16[128,2048]{1,0:T(8,128)(2,1)S(1)} %get-tuple-element.143.refs_0_), channel_id=1, source_target_pairs={{0,4},{4,0},{8,12},{12,8},{16,20},{20,16},{24,28},{28,24},{1,5},{5... | collective-permute-start | bytes 1572872 | tf_op jit(solution)/shard_map/ppermute | solution.py:38
  447.9 8.9 %collective-permute-start.44 = (bf16[128,2048]{1,0:T(8,128)(2,1)}, bf16[128,2048]{1,0:T(8,128)(2,1)}, u32[]{:S(2)}, u32[]{:S(2)}) collective-permute-start(bf16[128,2048]{1,0:T(8,128)(2,1)} %collective-permute-done.40.refs_1_), channel_id=1, source_target_pairs={{0,4},{4,0},{8,12},{12,8},{16,20},{20,16},{24,28},{28,24},{1,5},{5... | collective-permute-start | bytes 1572872 | tf_op jit(solution)/shard_map/ppermute | solution.py:38
  474.7 177.0 %collective-permute-start.55 = (bf16[2,512,512]{2,1,0:T(8,128)(2,1)}, bf16[2,512,512]{2,1,0:T(8,128)(2,1)}, u32[]{:S(2)}, u32[]{:S(2)}) collective-permute-start(bf16[2,512,512]{2,1,0:T(8,128)(2,1)} %fusion.9), channel_id=1, source_target_pairs={{0,2},{1,3},{2,0},{3,1},{4,6},{5,7},{6,4},{7,5},{8,10},{9,11},{10,... | collective-permute-start | bytes 3145736 | tf_op jit(solution)/shard_map/ppermute | solution.py:38
  522.5 42.4 %all-to-all-start.5 = ((bf16[32,80,256]{2,1,0:T(8,128)(2,1)}), bf16[32,80,256]{2,1,0:T(8,128)(2,1)}, u32[]{:S(2)}, u32[]{:S(2)}) async-start(bf16[32,80,256]{2,1,0:T(8,128)(2,1)} %pad_maximum_fusion), calls=%async_computation.6 | async-start | bytes 2621440 | tf_op jit(solution)/shard_map/all_to_all | solution.py:1032
  533.7 39.7 %collective-permute-start.49 = (bf16[512,2048]{1,0:T(8,128)(2,1)}, bf16[512,2048]{1,0:T(8,128)(2,1)}, u32[]{:S(2)}, u32[]{:S(2)}) collective-permute-start(bf16[512,2048]{1,0:T(8,128)(2,1)} %add_convert_fusion.2), channel_id=1, source_target_pairs={{0,4},{4,0},{8,12},{12,8},{16,20},{20,16},{24,28},{28,24},{1,5},{5... | collective-permute-start | bytes 6291464 | tf_op jit(solution)/shard_map/ppermute | solution.py:38
  535.6 29.3 %collective-permute-start.53 = (bf16[2,64,2048]{2,1,0:T(8,128)(2,1)S(1)}, bf16[2,64,2048]{2,1,0:T(8,128)(2,1)}, u32[]{:S(2)}, u32[]{:S(2)}) collective-permute-start(bf16[2,64,2048]{2,1,0:T(8,128)(2,1)S(1)} %pad_maximum_fusion.7), channel_id=1, source_target_pairs={{0,1},{1,0},{2,3},{3,2},{4,5},{5,4},{6,7},{7,6},{8,9},{9,8},{10,11... | collective-permute-start | bytes 1572872 | tf_op jit(solution)/shard_map/ppermute | solution.py:38
  565.0 101.1 %all-to-all-start.4 = ((bf16[32,64,512]{2,1,0:T(8,128)(2,1)}), bf16[32,64,512]{2,1,0:T(8,128)(2,1)}, u32[]{:S(2)}, u32[]{:S(2)}) async-start(bf16[32,64,512]{2,1,0:T(8,128)(2,1)} %bitcast.188), calls=%async_computation.5 | async-start | bytes 4194304 | tf_op jit(solution)/shard_map/all_to_all | solution.py:1032
  570.8 80.9 %collective-permute-start.54 = (bf16[64,2048]{1,0:T(8,128)(2,1)}, bf16[64,2048]{1,0:T(8,128)(2,1)S(1)}, u32[]{:S(2)}, u32[]{:S(2)}) collective-permute-start(bf16[64,2048]{1,0:T(8,128)(2,1)} %fusion.24), channel_id=1, source_target_pairs={{0,2},{1,3},{2,0},{3,1},{4,6},{5,7},{6,4},{7,5},{8,10},{9,11},{10,... | collective-permute-start | bytes 786440 | tf_op jit(solution)/shard_map/ppermute | solution.py:38
  576.3 33.7 %collective-permute-start.50 = (bf16[128,2048]{1,0:T(8,128)(2,1)}, bf16[128,2048]{1,0:T(8,128)(2,1)S(1)}, u32[]{:S(2)}, u32[]{:S(2)}) collective-permute-start(bf16[128,2048]{1,0:T(8,128)(2,1)} %get-tuple-element.179), channel_id=1, source_target_pairs={{0,8},{4,12},{8,0},{12,4},{16,24},{20,28},{24,16},{28,20},{1,9},{5... | collective-permute-start | bytes 1572872 | tf_op jit(solution)/shard_map/ppermute | solution.py:38
  577.7 44.2 %collective-permute-start.52 = (bf16[128,2048]{1,0:T(8,128)(2,1)}, bf16[128,2048]{1,0:T(8,128)(2,1)S(1)}, u32[]{:S(2)}, u32[]{:S(2)}) collective-permute-start(bf16[128,2048]{1,0:T(8,128)(2,1)} %get-tuple-element.180), channel_id=1, source_target_pairs={{0,24},{4,28},{8,16},{12,20},{16,8},{20,12},{24,0},{28,4},{1,25},{... | collective-permute-start | bytes 1572872 | tf_op jit(solution)/shard_map/ppermute | solution.py:38
  579.2 43.5 %collective-permute-start.51 = (bf16[128,2048]{1,0:T(8,128)(2,1)}, bf16[128,2048]{1,0:T(8,128)(2,1)}, u32[]{:S(2)}, u32[]{:S(2)}) collective-permute-start(bf16[128,2048]{1,0:T(8,128)(2,1)} %get-tuple-element.181), channel_id=1, source_target_pairs={{0,16},{4,20},{8,24},{12,28},{16,0},{20,4},{24,8},{28,12},{1,17},{... | collective-permute-start | bytes 1572872 | tf_op jit(solution)/shard_map/ppermute | solution.py:38
  610.0 41.8 %collective-permute-start.48 = (bf16[128,2048]{1,0:T(8,128)(2,1)S(1)}, bf16[128,2048]{1,0:T(8,128)(2,1)S(1)}, u32[]{:S(2)}, u32[]{:S(2)}) collective-permute-start(bf16[128,2048]{1,0:T(8,128)(2,1)S(1)} %slice_bitcast_fusion.2), channel_id=1, source_target_pairs={{0,2},{1,3},{2,0},{3,1},{4,6},{5,7},{6,4},{7,5},{8,10},{9,11},{10,... | collective-permute-start | bytes 1572872 | tf_op jit(solution)/shard_map/ppermute | solution.py:38
  (66 other events, 735.5 us)
Sparse Core Ops, SparseCore 0:
  75.6 38.7 all-gather.12
  130.6 39.8 all-gather.14
  325.7 88.0 all-gather.16
  415.3 76.0 all-gather.18
  494.7 105.5 reduce-scatter.1

commit v4 on v3

--- a/solution.py
+++ b/solution.py
@@ -876,7 +876,7 @@
     counts_here = lax.dynamic_slice_in_dim(counts, seq_at * owned, owned, 0)
 
     normed, pairs, squares, pair_weights = project_pairs(
-        here, token_pieces, pair_pieces, shard, after(attn_norm_gain[None], *value_pieces[:3])
+        here, token_pieces, pair_pieces, shard, attn_norm_gain[None]
     )
     values, value_weights = project_values(here, normed, value_pieces)
     pair_weights, value_weights = (w.reshape(width, -1) for w in (pair_weights, value_weights))
@@ -1022,10 +1022,10 @@
         return (dot_nt(late_low[at], pair_weights) + dot_nt(value_low[at], value_weights)).astype(BF16)
 
     far = rows_of(slice(middle, total))
-    grad_normed, _ = scatter_seq(rows_of(slice(0, middle)), far)
+    grad_normed, low = scatter_seq(rows_of(slice(0, middle)), far)
     mix_other = hop(after(mix[1], value_low), "batch", half) if parts == 2 else mix
     grad_normed = after(grad_normed, mix_other)
-    down_mine = down(after(own, grad_normed))
+    down_mine = down(after(own, *low))
 
     def head_sums(term, extra):
         term = jnp.concatenate([term, *extra], axis=1)

time: 697 us -> 684 us (0.981)
  waiting for transfers between devices: 212 us -> 199 us
    reduce_scatter x1, waiting for transfers between devices: 17.3 us -> 0.01 us  [on_device(): mix = lax.psum_scatter(after(mix, grad_mixed), 'seq', scatter_dimension=0)]
  transfers between devices with their start and end apart: 65 -> 65, of which waited for: 29 -> 28; matrix products, arithmetic and copies ran while one was open for 15% -> 17% of each run, Pallas kernels for 22% -> 23%
where the time goes in v4:
time: 684 us; the launch traced here: 676 us
  Pallas kernels  205 us (30%)
  waiting for transfers between devices  199 us (29%)
  starting transfers between devices  73.8 us (11%)
  other arithmetic  61.9 us (9%)
  blocking collectives  50.2 us (7%)
  local copies, waits for them, and re-layouts  49.9 us (7%)
  matrix products  20.6 us (3%)
  between operations  15.5 us (2%)
    ppermute x56, waiting for transfers between devices, hop(): return lax.ppermute(values, axis, [(i, i ^ mask) for i in range(size)])  198 us
    ppermute x56, starting transfers between devices, hop(): return lax.ppermute(values, axis, [(i, i ^ mask) for i in range(size)])  57.4 us
    pallas_call x2, Pallas kernels, run_acts(): pl.pallas_call(functools.partial(acts_kernel, experts, blocks, per), grid...  50.8 us
    pallas_call x4, Pallas kernels, in_blocks(): pl.pallas_call(functools.partial(in_kernel, sets), grid_spec=pltpu.Prefet...  34.8 us
    pallas_call x2, Pallas kernels, run_back(): pl.pallas_call(functools.partial(rows_back_kernel, blocks, per), grid_spe...  32.5 us
    all_to_all x2, blocking collectives, exchange(): lax.all_to_all(blocks, 'seq', split_axis=0, concat_axis=0, tiled=True)  31.5 us
    pallas_call x1, Pallas kernels, attention(): pl.pallas_call(functools.partial(attend_back_kernel, blocks, size), grid=...  19.9 us
    all_gather x2, blocking collectives, sum_seq(): return jnp.sum(lax.all_gather(values, 'seq', axis=0), axis=0)  18.7 us
  transfers between devices with their start and end apart: 65, of which 28 were waited for; matrix products, arithmetic and copies ran while one was open for 17% of the time, Pallas kernels for 23%

profile of v4, /device:TPU:0, one launch (start us, length us, event | category | flops | bytes accessed | tf_op | source)
XLA Modules:
  0.0 675.8 jit_solution(2213176871357229750)
XLA Ops:
  7.2 4.0 collective-permute-start.2
  14.1 3.1 collective-permute-start.3
  19.9 21.1 %all_to_all.30.refs_8_ = bf16[8,72,512]{2,1,0:T(8,128)(2,1)S(1)} all-to-all(bf16[8,72,512]{2,1,0:T(8,128)(2,1)S(1)} %pad_maximum_fusion.2), channel_id=1, replica_groups=mesh['seq'=8,'batch'=4] {'seq'}, dimensions={0} | all-to-all | bytes 1179648 | tf_op jit(solution)/shard_map/all_to_all | solution.py:836
  45.6 2.6 collective-permute-start.9
  49.8 10.4 %all_to_all.31.refs_0_ = bf16[8,64,256]{2,1,0:T(8,128)(2,1)S(1)} all-to-all(bf16[8,64,256]{2,1,0:T(8,128)(2,1)S(1)} %bitcast.197), channel_id=1, replica_groups=mesh['seq'=8,'batch'=4] {'seq'}, dimensions={0} | all-to-all | bytes 524288 | tf_op jit(solution)/shard_map/all_to_all | solution.py:836
  60.2 14.4 %collective-permute-done.9.refs_10_ = bf16[8,72,512]{2,1,0:T(8,128)(2,1)S(1)} collective-permute-done((bf16[8,72,512]{2,1,0:T(8,128)(2,1)S(1)}, bf16[8,72,512]{2,1,0:T(8,128)(2,1)S(1)}, u32[]{:S(2)}, u32[]{:S(2)}) %collective-permute-start.9) | collective-permute-done | bytes 589856 | tf_op jit(solution)/shard_map/ppermute | solution.py:38
  79.1 3.1 collective-permute-start.12
  87.8 10.6 %collective-permute-done.10.refs_11_ = bf16[8,72,512]{2,1,0:T(8,128)(2,1)} collective-permute-done((bf16[8,72,512]{2,1,0:T(8,128)(2,1)}, bf16[8,72,512]{2,1,0:T(8,128)(2,1)}, u32[]{:S(2)}, u32[]{:S(2)}) %collective-permute-start.10) | collective-permute-done | bytes 589856 | tf_op jit(solution)/shard_map/ppermute | solution.py:38
  99.8 2.5 collective-permute-start.14
  102.3 6.3 collective-permute-done.11.refs_1_
  111.3 9.7 %shard_map.289 = (bf16[1024,2048]{1,0:T(8,128)(2,1)}, f32[1024,512]{1,0:T(8,128)}, f32[2,1024]{1,0:T(2,128)}, bf16[8,4,64,512]{3,2,1,0:T(8,128)(2,1)}) custom-call(s32[10]{0:T(128)} %get-tuple-element.203.at_ref, bf16[128,2048]{1,0:T(8,128)(2,1)} %bitcast.175, bf16[128,2048]{1,0:T(8,128)(2,1)} %collective-permute-done.refs_1_, ...), custom_call_target="tpu_custom_call" | custom-call | flops 2147483648 | bytes 16777216 | tf_op jit(solution)/shard_map/pallas_call | solution.py:197
  121.0 9.3 %all-gather.6 = f32[8,2,1024]{2,1,0:T(2,128)S(1)} all-gather(f32[1,2,1024]{2,1,0:T(2,128)} %bitcast.211), channel_id=2, replica_groups=mesh['seq'=8,'batch'=4] {'seq'}, dimensions={0}, use_global_device_ids=true | all-gather | bytes 73728 | tf_op jit(solution)/shard_map/all_gather | solution.py:885
  134.5 6.2 shard_map.290
  140.7 10.1 %shard_map.291.refs_8_ = bf16[1024,256]{1,0:T(8,128)(2,1)} custom-call(s32[8]{0:T(128)} %gather_fusion, f32[1024,512]{1,0:T(8,128)} %get-tuple-element.97.q_ref.k_ref, f32[1024,512]{1,0:T(8,128)} %get-tuple-element.97.q_ref.k_ref, bf16[1024,256]{1,0:T(8,128)(2,1)} %get-tuple-element.101.v_ref, f32[1024,2]{1,0:T(8,128)} %get-tuple-element.191.scale_ref, ...), custom_call_target="tpu_custom_call" | custom-call | flops 1073741824 | bytes 4194304 | tf_op jit(solution)/shard_map/pallas_call | solution.py:448
  153.7 3.4 collective-permute-done.17
  162.5 14.5 %collective-permute-done.18 = bf16[128,2048]{1,0:T(8,128)(2,1)S(1)} collective-permute-done((bf16[128,2048]{1,0:T(8,128)(2,1)}, bf16[128,2048]{1,0:T(8,128)(2,1)S(1)}, u32[]{:S(2)}, u32[]{:S(2)}) %collective-permute-start.18) | collective-permute-done | bytes 524320 | tf_op jit(solution)/shard_map/ppermute | solution.py:38
  177.0 11.9 %collective-permute-done.20 = bf16[128,2048]{1,0:T(8,128)(2,1)S(1)} collective-permute-done((bf16[128,2048]{1,0:T(8,128)(2,1)}, bf16[128,2048]{1,0:T(8,128)(2,1)S(1)}, u32[]{:S(2)}, u32[]{:S(2)}) %collective-permute-start.20) | collective-permute-done | bytes 524320 | tf_op jit(solution)/shard_map/ppermute | solution.py:38
  189.6 2.3 multiply_reduce_fusion.2
  195.6 2.4 collective-permute-start.28
  198.0 8.9 %collective-permute-done.21.refs_1_ = bf16[128,2048]{1,0:T(8,128)(2,1)S(1)} collective-permute-done((bf16[128,2048]{1,0:T(8,128)(2,1)S(1)}, bf16[128,2048]{1,0:T(8,128)(2,1)S(1)}, u32[]{:S(2)}, u32[]{:S(2)}) %collective-permute-start.21) | collective-permute-done | bytes 524320 | tf_op jit(solution)/shard_map/ppermute | solution.py:38
  207.0 10.2 %collective-permute-done.23.refs_3_ = bf16[128,2048]{1,0:T(8,128)(2,1)S(1)} collective-permute-done((bf16[128,2048]{1,0:T(8,128)(2,1)S(1)}, bf16[128,2048]{1,0:T(8,128)(2,1)S(1)}, u32[]{:S(2)}, u32[]{:S(2)}) %collective-permute-start.23) | collective-permute-done | bytes 524320 | tf_op jit(solution)/shard_map/ppermute | solution.py:38
  225.6 25.3 %shard_map.292 = (bf16[1024,2048]{1,0:T(8,128)(2,1)}, bf16[1024,2048]{1,0:T(8,128)(2,1)}, bf16[2,1024,512]{2,1,0:T(8,128)(2,1)}, bf16[2,1024,512]{2,1,0:T(8,128)...) custom-call(s32[10]{0:T(128)} %get-tuple-element.129.at_ref, bf16[128,2048]{1,0:T(8,128)(2,1)} %copy-done.22, ...), custom_call_target="tpu_custom_call" | custom-call | flops 12884901888 | bytes 35651584 | tf_op jit(solution)/shard_map/pallas_call | solution.py:548
  255.3 25.5 %shard_map.293 = (bf16[1024,2048]{1,0:T(8,128)(2,1)}, bf16[1024,2048]{1,0:T(8,128)(2,1)}, bf16[2,1024,512]{2,1,0:T(8,128)(2,1)}, bf16[2,1024,512]{2,1,0:T(8,128)...) custom-call(s32[10]{0:T(128)} %get-tuple-element.129.at_ref, bf16[128,2048]{1,0:T(8,128)(2,1)} %copy-done.53, ...), custom_call_target="tpu_custom_call" | custom-call | flops 12884901888 | bytes 35651584 | tf_op jit(solution)/shard_map/pallas_call | solution.py:548
  280.8 8.6 %shard_map.294 = bf16[1,2,2,512,512]{4,3,2,1,0:T(8,128)(2,1)} custom-call(s32[1]{0:T(128)} %bitcast.26.at_ref, bf16[1024,2048]{1,0:T(8,128)(2,1)} %get-tuple-element.108.refs_0_, bf16[1024,2048]{1,0:T(8,128)(2,1)} %get-tuple-element.115.refs_1_, bf16[2,1024,512]{2,1,0:T(8,128)(2,1)} %get-tuple-element.116.refs_2_.gate_ref, ...), custom_call_target="tpu_custom_call" | custom-call | flops 4294967296 | bytes 8388608 | tf_op jit(solution)/shard_map/pallas_call | solution.py:747
  289.4 16.2 %shard_map.295 = (bf16[2,2,128,2176]{3,2,1,0:T(8,128)(2,1)}, bf16[2,2,128,2176]{3,2,1,0:T(8,128)(2,1)}) custom-call(s32[10]{0:T(128)} %get-tuple-element.129.at_ref, bf16[2,1024,512]{2,1,0:T(8,128)(2,1)} %get-tuple-element.117.refs_3_.gate_ref, bf16[2,1024,512]{2,1,0:T(8,128)(2,1)} %get-tuple-element.119.up_ref.refs_3_, ...), custom_call_target="tpu_custom_call" | custom-call | flops 8589934592 | bytes 16777216 | tf_op jit(solution)/shard_map/pallas_call | solution.py:678
  307.4 8.8 %shard_map.296 = bf16[1,2,2,512,512]{4,3,2,1,0:T(8,128)(2,1)} custom-call(s32[1]{0:T(128)} %bitcast.26.at_ref, bf16[1024,2048]{1,0:T(8,128)(2,1)} %get-tuple-element.108.refs_0_, bf16[1024,2048]{1,0:T(8,128)(2,1)} %get-tuple-element.115.refs_1_, bf16[2,1024,512]{2,1,0:T(8,128)(2,1)} %get-tuple-element.123.refs_2_.up_ref, ...), custom_call_target="tpu_custom_call" | custom-call | flops 4294967296 | bytes 8388608 | tf_op jit(solution)/shard_map/pallas_call | solution.py:747
  316.1 3.5 add_convert_fusion.1
  319.7 3.6 all-to-all-start.2
  324.0 15.6 %shard_map.298 = bf16[2,2,2,2,128,2048]{5,4,3,2,1,0:T(8,128)(2,1)} custom-call(s32[10]{0:T(128)} %get-tuple-element.129.at_ref, bf16[2,1024,512]{2,1,0:T(8,128)(2,1)} %get-tuple-element.130.refs_0_, bf16[2,1024,512]{2,1,0:T(8,128)(2,1)} %get-tuple-element.131.refs_1_, bf16[2,1024,2048]{2,1,0:T(8,128)(2,1)} %refs_2_.1), custom_call_target="tpu_custom_call" | custom-call | flops 8589934592 | bytes 12582912 | tf_op jit(solution)/shard_map/pallas_call | solution.py:635
  339.6 16.3 %shard_map.297 = (bf16[2,2,128,2176]{3,2,1,0:T(8,128)(2,1)}, bf16[2,2,128,2176]{3,2,1,0:T(8,128)(2,1)}) custom-call(s32[10]{0:T(128)} %get-tuple-element.129.at_ref, bf16[2,1024,512]{2,1,0:T(8,128)(2,1)} %get-tuple-element.116.refs_2_.gate_ref, bf16[2,1024,512]{2,1,0:T(8,128)(2,1)} %get-tuple-element.123.refs_2_.up_ref, ...), custom_call_target="tpu_custom_call" | custom-call | flops 8589934592 | bytes 16777216 | tf_op jit(solution)/shard_map/pallas_call | solution.py:678
  357.1 13.8 %collective-permute-done.37 = bf16[2,2,512,512]{3,2,1,0:T(8,128)(2,1)} collective-permute-done((bf16[2,2,512,512]{3,2,1,0:T(8,128)(2,1)}, bf16[2,2,512,512]{3,2,1,0:T(8,128)(2,1)}, u32[]{:S(2)}, u32[]{:S(2)}) %collective-permute-start.37) | collective-permute-done | bytes 2097184 | tf_op jit(solution)/shard_map/ppermute | solution.py:38
  372.5 2.3 collective-permute-start.39
  375.5 3.5 add_convert_fusion
  379.0 3.6 all-to-all-start.3
  382.7 8.6 %shard_map.299 = bf16[1,2,2,512,512]{4,3,2,1,0:T(8,128)(2,1)} custom-call(s32[1]{0:T(128)} %bitcast.34.at_ref, bf16[1024,2048]{1,0:T(8,128)(2,1)} %get-tuple-element.108.refs_0_, bf16[1024,2048]{1,0:T(8,128)(2,1)} %get-tuple-element.115.refs_1_, bf16[2,1024,512]{2,1,0:T(8,128)(2,1)} %get-tuple-element.116.refs_2_.gate_ref, ...), custom_call_target="tpu_custom_call" | custom-call | flops 4294967296 | bytes 8388608 | tf_op jit(solution)/shard_map/pallas_call | solution.py:747
  391.3 8.8 %shard_map.300 = bf16[1,2,256,2048]{3,2,1,0:T(8,128)(2,1)} custom-call(s32[1]{0:T(128)} %bitcast.26.at_ref, bf16[2,1024,512]{2,1,0:T(8,128)(2,1)} %get-tuple-element.130.refs_0_, bf16[2,1024,512]{2,1,0:T(8,128)(2,1)} %get-tuple-element.131.refs_1_, bf16[1024,2048]{1,0:T(8,128)(2,1)} %get-tuple-element.136.refs_2_, bf16[1024,2048]{1,0:T(8,128)(2,1)} %get-tuple-element.137.refs_3_), custom_call_target="tpu_custom_call" | custom-call | flops 4294967296 | bytes 10485760 | tf_op jit(solution)/shard_map/pallas_call | solution.py:713
  400.2 2.9 convert_add_fusion.2
  408.3 8.8 %shard_map.301 = bf16[1,2,2,512,512]{4,3,2,1,0:T(8,128)(2,1)} custom-call(s32[1]{0:T(128)} %bitcast.34.at_ref, bf16[1024,2048]{1,0:T(8,128)(2,1)} %get-tuple-element.108.refs_0_, bf16[1024,2048]{1,0:T(8,128)(2,1)} %get-tuple-element.115.refs_1_, bf16[2,1024,512]{2,1,0:T(8,128)(2,1)} %get-tuple-element.123.refs_2_.up_ref, ...), custom_call_target="tpu_custom_call" | custom-call | flops 4294967296 | bytes 8388608 | tf_op jit(solution)/shard_map/pallas_call | solution.py:747
  420.9 2.8 collective-permute-start.42
  426.8 2.7 convert_add_fusion.1
  429.4 7.2 %collective-permute-done.42.refs_3_ = bf16[128,2048]{1,0:T(8,128)(2,1)S(1)} collective-permute-done((bf16[128,2048]{1,0:T(8,128)(2,1)S(1)}, bf16[128,2048]{1,0:T(8,128)(2,1)S(1)}, u32[]{:S(2)}, u32[]{:S(2)}) %collective-permute-start.42) | collective-permute-done | bytes 524320 | tf_op jit(solution)/shard_map/ppermute | solution.py:38
  436.6 10.1 %collective-permute-done.41.refs_2_ = bf16[128,2048]{1,0:T(8,128)(2,1)} collective-permute-done((bf16[128,2048]{1,0:T(8,128)(2,1)S(1)}, bf16[128,2048]{1,0:T(8,128)(2,1)}, u32[]{:S(2)}, u32[]{:S(2)}) %collective-permute-start.41) | collective-permute-done | bytes 524320 | tf_op jit(solution)/shard_map/ppermute | solution.py:38
  448.0 7.1 %collective-permute-done.47 = bf16[2,512,512]{2,1,0:T(8,128)(2,1)} collective-permute-done((bf16[2,512,512]{2,1,0:T(8,128)(2,1)}, bf16[2,512,512]{2,1,0:T(8,128)(2,1)}, u32[]{:S(2)}, u32[]{:S(2)}) %collective-permute-start.47) | collective-permute-done | bytes 1048608 | tf_op jit(solution)/shard_map/ppermute | solution.py:38
  456.7 7.8 %shard_map.302 = (bf16[1024,256]{1,0:T(8,128)(2,1)}, bf16[256,2048]{1,0:T(8,128)(2,1)}) custom-call(bf16[128,2048]{1,0:T(8,128)(2,1)} %copy-done.38, bf16[128,2048]{1,0:T(8,128)(2,1)} %collective-permute-done.40.refs_1_, bf16[128,2048]{1,0:T(8,128)(2,1)} %collective-permute-done.41.refs_2_, bf16[128,2048]{1,0:T(8,128)(2,1)} %copy-done.58, ...), custom_call_target="tpu_custom_call" | custom-call | flops 2147483648 | bytes 8388608 | tf_op jit(solution)/shard_map/pallas_call | solution.py:301
  468.3 3.1 dynamic-slice_bitcast_fusion.3
  472.0 2.7 fusion.9
  474.7 3.2 dynamic-slice_bitcast_fusion.2
  478.0 19.9 %shard_map.303 = (f32[1024,256]{1,0:T(8,128)}, f32[1024,256]{1,0:T(8,128)}, bf16[1024,256]{1,0:T(8,128)(2,1)}, f32[1024,2]{1,0:T(8,128)}, f32[2,256]{1,0:T(2,128)}) custom-call(s32[8]{0:T(128)} %gather_fusion, f32[1024,512]{1,0:T(8,128)} %get-tuple-element.97.q_ref.k_ref, f32[1024,512]{1,0:T(8,128)} %get-tuple-element.97.q_ref.k_ref, ...), custom_call_target="tpu_custom_call" | custom-call | flops 2684354560 | bytes 8388608 | tf_op jit(solution)/shard_map/pallas_call | solution.py:460
  499.6 5.4 convolution_convert_fusion.3
  506.3 9.4 %all-gather.7 = f32[8,2,1024]{2,1,0:T(2,128)S(1)} all-gather(f32[1,2,1024]{2,1,0:T(2,128)S(1)} %copy.142), channel_id=6, replica_groups=mesh['seq'=8,'batch'=4] {'seq'}, dimensions={0}, use_global_device_ids=true | all-gather | bytes 73728 | tf_op jit(solution)/shard_map/all_gather | solution.py:885
  522.2 3.8 convolution_convert_fusion
  527.2 5.5 all-to-all-start.5
  534.6 2.7 add_convert_fusion.2
  542.7 2.9 maximum_select_fusion
  547.0 20.9 %collective-permute-done.53 = bf16[2,64,2048]{2,1,0:T(8,128)(2,1)S(1)} collective-permute-done((bf16[2,64,2048]{2,1,0:T(8,128)(2,1)S(1)}, bf16[2,64,2048]{2,1,0:T(8,128)(2,1)S(1)}, u32[]{:S(2)}, u32[]{:S(2)}) %collective-permute-start.53) | collective-permute-done | bytes 524320 | tf_op jit(solution)/shard_map/ppermute | solution.py:38
  571.0 3.2 dynamic-slice_bitcast_fusion
  574.2 3.5 all-to-all-start.4
  577.7 2.9 add_convert_fusion.6
  584.1 8.9 %shard_map.304 = bf16[1,2,256,2048]{3,2,1,0:T(8,128)(2,1)} custom-call(s32[1]{0:T(128)} %bitcast.34.at_ref, bf16[2,1024,512]{2,1,0:T(8,128)(2,1)} %get-tuple-element.130.refs_0_, bf16[2,1024,512]{2,1,0:T(8,128)(2,1)} %get-tuple-element.131.refs_1_, bf16[1024,2048]{1,0:T(8,128)(2,1)} %get-tuple-element.136.refs_2_, bf16[1024,2048]{1,0:T(8,128)(2,1)} %get-tuple-element.137.refs_3_), custom_call_target="tpu_custom_call" | custom-call | flops 4294967296 | bytes 10485760 | tf_op jit(solution)/shard_map/pallas_call | solution.py:713
  593.0 4.4 convert_add_fusion
  598.5 11.1 %collective-permute-done.50 = bf16[128,2048]{1,0:T(8,128)(2,1)} collective-permute-done((bf16[128,2048]{1,0:T(8,128)(2,1)}, bf16[128,2048]{1,0:T(8,128)(2,1)}, u32[]{:S(2)}, u32[]{:S(2)}) %collective-permute-start.50) | collective-permute-done | bytes 524320 | tf_op jit(solution)/shard_map/ppermute | solution.py:38
  610.7 13.6 %collective-permute-done.52 = bf16[128,2048]{1,0:T(8,128)(2,1)} collective-permute-done((bf16[128,2048]{1,0:T(8,128)(2,1)}, bf16[128,2048]{1,0:T(8,128)(2,1)}, u32[]{:S(2)}, u32[]{:S(2)}) %collective-permute-start.52) | collective-permute-done | bytes 524320 | tf_op jit(solution)/shard_map/ppermute | solution.py:38
  626.4 24.2 %collective-permute-done.48 = bf16[128,2048]{1,0:T(8,128)(2,1)S(1)} collective-permute-done((bf16[128,2048]{1,0:T(8,128)(2,1)S(1)}, bf16[128,2048]{1,0:T(8,128)(2,1)S(1)}, u32[]{:S(2)}, u32[]{:S(2)}) %collective-permute-start.48) | collective-permute-done | bytes 524320 | tf_op jit(solution)/shard_map/ppermute | solution.py:38
  664.9 2.9 maximum_select_fusion.1
  (367 shorter events, 125.9 us)
Async XLA Ops:
  7.2 143.7 %all-gather.13.cloned.1.call-start = ((), (), s32[]{:S(2)}) async-start(), calls=%async_computation.8 | async-start | bytes 5013504 | tf_op jit(solution)/shard_map/all_gather | solution.py:872
  7.2 33.9 %collective-permute-start.2 = (bf16[128,2048]{1,0:T(8,128)(2,1)}, bf16[128,2048]{1,0:T(8,128)(2,1)}, u32[]{:S(2)}, u32[]{:S(2)}) collective-permute-start(bf16[128,2048]{1,0:T(8,128)(2,1)} %bitcast.172), channel_id=1, source_target_pairs={{0,24},{4,28},{8,16},{12,20},{16,8},{20,12},{24,0},{28,4},{1,25},{... | collective-permute-start | bytes 1572872 | tf_op jit(solution)/shard_map/ppermute | solution.py:38
  11.2 29.9 %collective-permute-start.1 = (bf16[128,2048]{1,0:T(8,128)(2,1)}, bf16[128,2048]{1,0:T(8,128)(2,1)}, u32[]{:S(2)}, u32[]{:S(2)}) collective-permute-start(bf16[128,2048]{1,0:T(8,128)(2,1)} %bitcast.173), channel_id=1, source_target_pairs={{0,16},{4,20},{8,24},{12,28},{16,0},{20,4},{24,8},{28,12},{1,17},{... | collective-permute-start | bytes 1572872 | tf_op jit(solution)/shard_map/ppermute | solution.py:38
  11.7 29.4 %collective-permute-start = (bf16[128,2048]{1,0:T(8,128)(2,1)}, bf16[128,2048]{1,0:T(8,128)(2,1)}, u32[]{:S(2)}, u32[]{:S(2)}) collective-permute-start(bf16[128,2048]{1,0:T(8,128)(2,1)} %bitcast.174), channel_id=1, source_target_pairs={{0,8},{4,12},{8,0},{12,4},{16,24},{20,28},{24,16},{28,20},{1,9},{5... | collective-permute-start | bytes 1572872 | tf_op jit(solution)/shard_map/ppermute | solution.py:38
  14.1 27.0 %collective-permute-start.3 = (bf16[128,2176]{1,0:T(8,128)(2,1)S(1)}, bf16[128,2176]{1,0:T(8,128)(2,1)S(1)}, u32[]{:S(2)}, u32[]{:S(2)}) collective-permute-start(bf16[128,2176]{1,0:T(8,128)(2,1)S(1)} %pad_maximum_fusion.3), channel_id=1, source_target_pairs={{0,2},{1,3},{2,0},{3,1},{4,6},{5,7},{6,4},{7,5},{8,10},{9,11},{10,... | collective-permute-start | bytes 1671176 | tf_op jit(solution)/shard_map/ppermute | solution.py:38
  41.1 2.0 collective-permute-start.4
  41.2 2.9 collective-permute-start.5
  41.7 3.1 collective-permute-start.6
  41.8 3.8 collective-permute-start.7
  45.6 29.0 %collective-permute-start.9 = (bf16[8,72,512]{2,1,0:T(8,128)(2,1)S(1)}, bf16[8,72,512]{2,1,0:T(8,128)(2,1)S(1)}, u32[]{:S(2)}, u32[]{:S(2)}) collective-permute-start(bf16[8,72,512]{2,1,0:T(8,128)(2,1)S(1)} %all_to_all.30.refs_8_), channel_id=1, source_target_pairs={{0,2},{1,3},{2,0},{3,1},{4,6},{5,7},{6,4},{7,5},{8,10},{9,11},{10,... | collective-permute-start | bytes 1769480 | tf_op jit(solution)/shard_map/ppermute | solution.py:38
  48.2 27.2 %collective-permute-start.8 = (bf16[8,72,512]{2,1,0:T(8,128)(2,1)S(1)}, bf16[8,72,512]{2,1,0:T(8,128)(2,1)}, u32[]{:S(2)}, u32[]{:S(2)}) collective-permute-start(bf16[8,72,512]{2,1,0:T(8,128)(2,1)S(1)} %all_to_all.30.refs_8_), channel_id=1, source_target_pairs={{0,1},{1,0},{2,3},{3,2},{4,5},{5,4},{6,7},{7,6},{8,9},{9,8},{10,11... | collective-permute-start | bytes 1769480 | tf_op jit(solution)/shard_map/ppermute | solution.py:38
  75.4 176.7 %all-gather.15.cloned.1.call-start = ((), (), s32[]{:S(2)}) async-start(), calls=%async_computation.9 | async-start | bytes 5013504 | tf_op jit(solution)/shard_map/all_gather | solution.py:872
  76.2 22.2 %collective-permute-start.10 = (bf16[8,72,512]{2,1,0:T(8,128)(2,1)}, bf16[8,72,512]{2,1,0:T(8,128)(2,1)}, u32[]{:S(2)}, u32[]{:S(2)}) collective-permute-start(bf16[8,72,512]{2,1,0:T(8,128)(2,1)} %copy-done.46), channel_id=1, source_target_pairs={{0,1},{1,0},{2,3},{3,2},{4,5},{5,4},{6,7},{7,6},{8,9},{9,8},{10,11... | collective-permute-start | bytes 1769480 | tf_op jit(solution)/shard_map/ppermute | solution.py:38
  79.1 23.2 %collective-permute-start.12 = (bf16[8,64,256]{2,1,0:T(8,128)(2,1)S(1)}, bf16[8,64,256]{2,1,0:T(8,128)(2,1)}, u32[]{:S(2)}, u32[]{:S(2)}) collective-permute-start(bf16[8,64,256]{2,1,0:T(8,128)(2,1)S(1)} %all_to_all.31.refs_0_), channel_id=1, source_target_pairs={{0,2},{1,3},{2,0},{3,1},{4,6},{5,7},{6,4},{7,5},{8,10},{9,11},{10,... | collective-permute-start | bytes 786440 | tf_op jit(solution)/shard_map/ppermute | solution.py:38
  82.2 26.4 %collective-permute-start.11 = (bf16[8,64,256]{2,1,0:T(8,128)(2,1)S(1)}, bf16[8,64,256]{2,1,0:T(8,128)(2,1)}, u32[]{:S(2)}, u32[]{:S(2)}) collective-permute-start(bf16[8,64,256]{2,1,0:T(8,128)(2,1)S(1)} %all_to_all.31.refs_0_), channel_id=1, source_target_pairs={{0,1},{1,0},{2,3},{3,2},{4,5},{5,4},{6,7},{7,6},{8,9},{9,8},{10,11... | collective-permute-start | bytes 786440 | tf_op jit(solution)/shard_map/ppermute | solution.py:38
  98.4 34.0 %collective-permute-start.15 = (bf16[64,2048]{1,0:T(8,128)(2,1)S(1)}, bf16[64,2048]{1,0:T(8,128)(2,1)S(1)}, u32[]{:S(2)}, u32[]{:S(2)}) collective-permute-start(bf16[64,2048]{1,0:T(8,128)(2,1)S(1)} %copy-done.43), channel_id=1, source_target_pairs={{0,2},{1,3},{2,0},{3,1},{4,6},{5,7},{6,4},{7,5},{8,10},{9,11},{10,... | collective-permute-start | bytes 786440 | tf_op jit(solution)/shard_map/ppermute | solution.py:38
  99.8 32.6 %collective-permute-start.14 = (bf16[64,2048]{1,0:T(8,128)(2,1)S(1)}, bf16[64,2048]{1,0:T(8,128)(2,1)S(1)}, u32[]{:S(2)}, u32[]{:S(2)}) collective-permute-start(bf16[64,2048]{1,0:T(8,128)(2,1)S(1)} %copy-done.43), channel_id=1, source_target_pairs={{0,1},{1,0},{2,3},{3,2},{4,5},{5,4},{6,7},{7,6},{8,9},{9,8},{10,11... | collective-permute-start | bytes 786440 | tf_op jit(solution)/shard_map/ppermute | solution.py:38
  111.3 21.1 %collective-permute-start.13 = (bf16[8,64,256]{2,1,0:T(8,128)(2,1)}, bf16[8,64,256]{2,1,0:T(8,128)(2,1)S(1)}, u32[]{:S(2)}, u32[]{:S(2)}) collective-permute-start(bf16[8,64,256]{2,1,0:T(8,128)(2,1)} %collective-permute-done.12.refs_2_), channel_id=1, source_target_pairs={{0,1},{1,0},{2,3},{3,2},{4,5},{5,4},{6,7},{7,6},{8,9},{9,8},{10,11... | collective-permute-start | bytes 786440 | tf_op jit(solution)/shard_map/ppermute | solution.py:38
  132.4 18.5 %collective-permute-start.16 = (bf16[64,2048]{1,0:T(8,128)(2,1)S(1)}, bf16[64,2048]{1,0:T(8,128)(2,1)S(1)}, u32[]{:S(2)}, u32[]{:S(2)}) collective-permute-start(bf16[64,2048]{1,0:T(8,128)(2,1)S(1)} %collective-permute-done.15), channel_id=1, source_target_pairs={{0,1},{1,0},{2,3},{3,2},{4,5},{5,4},{6,7},{7,6},{8,9},{9,8},{10,11... | collective-permute-start | bytes 786440 | tf_op jit(solution)/shard_map/ppermute | solution.py:38
  152.9 4.2 collective-permute-start.17
  158.9 18.0 %collective-permute-start.18 = (bf16[128,2048]{1,0:T(8,128)(2,1)}, bf16[128,2048]{1,0:T(8,128)(2,1)S(1)}, u32[]{:S(2)}, u32[]{:S(2)}) collective-permute-start(bf16[128,2048]{1,0:T(8,128)(2,1)} %get-tuple-element.180), channel_id=1, source_target_pairs={{0,8},{4,12},{8,0},{12,4},{16,24},{20,28},{24,16},{28,20},{1,9},{5... | collective-permute-start | bytes 1572872 | tf_op jit(solution)/shard_map/ppermute | solution.py:38
  160.1 28.7 %collective-permute-start.20 = (bf16[128,2048]{1,0:T(8,128)(2,1)}, bf16[128,2048]{1,0:T(8,128)(2,1)S(1)}, u32[]{:S(2)}, u32[]{:S(2)}) collective-permute-start(bf16[128,2048]{1,0:T(8,128)(2,1)} %get-tuple-element.181), channel_id=1, source_target_pairs={{0,24},{4,28},{8,16},{12,20},{16,8},{20,12},{24,0},{28,4},{1,25},{... | collective-permute-start | bytes 1572872 | tf_op jit(solution)/shard_map/ppermute | solution.py:38
  161.6 28.0 %collective-permute-start.19 = (bf16[128,2048]{1,0:T(8,128)(2,1)}, bf16[128,2048]{1,0:T(8,128)(2,1)}, u32[]{:S(2)}, u32[]{:S(2)}) collective-permute-start(bf16[128,2048]{1,0:T(8,128)(2,1)} %get-tuple-element.182), channel_id=1, source_target_pairs={{0,16},{4,20},{8,24},{12,28},{16,0},{20,4},{24,8},{28,12},{1,17},{... | collective-permute-start | bytes 1572872 | tf_op jit(solution)/shard_map/ppermute | solution.py:38
  192.1 14.9 %collective-permute-start.21 = (bf16[128,2048]{1,0:T(8,128)(2,1)S(1)}, bf16[128,2048]{1,0:T(8,128)(2,1)S(1)}, u32[]{:S(2)}, u32[]{:S(2)}) collective-permute-start(bf16[128,2048]{1,0:T(8,128)(2,1)S(1)} %multiply_convert_fusion.2.refs_0_), channel_id=1, source_target_pairs={{0,8},{4,12},{8,0},{12,4},{16,24},{20,28},{24,16},{28,20},{1,9},{5... | collective-permute-start | bytes 1572872 | tf_op jit(solution)/shard_map/ppermute | solution.py:38
  192.7 24.4 %collective-permute-start.23 = (bf16[128,2048]{1,0:T(8,128)(2,1)S(1)}, bf16[128,2048]{1,0:T(8,128)(2,1)S(1)}, u32[]{:S(2)}, u32[]{:S(2)}) collective-permute-start(bf16[128,2048]{1,0:T(8,128)(2,1)S(1)} %multiply_convert_fusion.2.refs_0_), channel_id=1, source_target_pairs={{0,24},{4,28},{8,16},{12,20},{16,8},{20,12},{24,0},{28,4},{1,25},{... | collective-permute-start | bytes 1572872 | tf_op jit(solution)/shard_map/ppermute | solution.py:38
  194.2 24.4 %collective-permute-start.22 = (bf16[128,2048]{1,0:T(8,128)(2,1)S(1)}, bf16[128,2048]{1,0:T(8,128)(2,1)}, u32[]{:S(2)}, u32[]{:S(2)}) collective-permute-start(bf16[128,2048]{1,0:T(8,128)(2,1)S(1)} %multiply_convert_fusion.2.refs_0_), channel_id=1, source_target_pairs={{0,16},{4,20},{8,24},{12,28},{16,0},{20,4},{24,8},{28,12},{1,17},{... | collective-permute-start | bytes 1572872 | tf_op jit(solution)/shard_map/ppermute | solution.py:38
  195.6 25.6 %collective-permute-start.28 = (bf16[128,2048]{1,0:T(8,128)(2,1)S(1)}, bf16[128,2048]{1,0:T(8,128)(2,1)S(1)}, u32[]{:S(2)}, u32[]{:S(2)}) collective-permute-start(bf16[128,2048]{1,0:T(8,128)(2,1)S(1)} %multiply_convert_fusion.2.refs_0_), channel_id=1, source_target_pairs={{0,2},{1,3},{2,0},{3,1},{4,6},{5,7},{6,4},{7,5},{8,10},{9,11},{10,... | collective-permute-start | bytes 1572872 | tf_op jit(solution)/shard_map/ppermute | solution.py:38
  217.1 4.1 collective-permute-start.27
  218.6 3.0 collective-permute-start.26
  218.6 3.0 collective-permute-start.24
  219.1 3.0 collective-permute-start.25
  222.2 28.9 %collective-permute-start.31 = (bf16[128,2048]{1,0:T(8,128)(2,1)S(1)}, bf16[128,2048]{1,0:T(8,128)(2,1)S(1)}, u32[]{:S(2)}, u32[]{:S(2)}) collective-permute-start(bf16[128,2048]{1,0:T(8,128)(2,1)S(1)} %collective-permute-done.28.refs_0_), channel_id=1, source_target_pairs={{0,24},{4,28},{8,16},{12,20},{16,8},{20,12},{24,0},{28,4},{1,25},{... | collective-permute-start | bytes 1572872 | tf_op jit(solution)/shard_map/ppermute | solution.py:38
  223.7 27.4 %collective-permute-start.30 = (bf16[128,2048]{1,0:T(8,128)(2,1)S(1)}, bf16[128,2048]{1,0:T(8,128)(2,1)S(1)}, u32[]{:S(2)}, u32[]{:S(2)}) collective-permute-start(bf16[128,2048]{1,0:T(8,128)(2,1)S(1)} %collective-permute-done.28.refs_0_), channel_id=1, source_target_pairs={{0,16},{4,20},{8,24},{12,28},{16,0},{20,4},{24,8},{28,12},{1,17},{... | collective-permute-start | bytes 1572872 | tf_op jit(solution)/shard_map/ppermute | solution.py:38
  224.0 27.1 %collective-permute-start.29 = (bf16[128,2048]{1,0:T(8,128)(2,1)S(1)}, bf16[128,2048]{1,0:T(8,128)(2,1)}, u32[]{:S(2)}, u32[]{:S(2)}) collective-permute-start(bf16[128,2048]{1,0:T(8,128)(2,1)S(1)} %collective-permute-done.28.refs_0_), channel_id=1, source_target_pairs={{0,8},{4,12},{8,0},{12,4},{16,24},{20,28},{24,16},{28,20},{1,9},{5... | collective-permute-start | bytes 1572872 | tf_op jit(solution)/shard_map/ppermute | solution.py:38
  251.1 3.7 collective-permute-start.33
  251.6 3.1 collective-permute-start.34
  251.7 3.6 collective-permute-start.35
  305.7 10.5 %collective-permute-start.36 = (bf16[4,128,2176]{2,1,0:T(8,128)(2,1)}, bf16[4,128,2176]{2,1,0:T(8,128)(2,1)}, u32[]{:S(2)}, u32[]{:S(2)}) collective-permute-start(bf16[4,128,2176]{2,1,0:T(8,128)(2,1)} %bitcast.220), channel_id=1, source_target_pairs={{0,4},{4,0},{8,12},{12,8},{16,20},{20,16},{24,28},{28,24},{1,5},{5... | collective-permute-start | bytes 6684680 | tf_op jit(solution)/shard_map/ppermute | solution.py:38
  305.8 65.1 %collective-permute-start.37 = (bf16[2,2,512,512]{3,2,1,0:T(8,128)(2,1)}, bf16[2,2,512,512]{3,2,1,0:T(8,128)(2,1)}, u32[]{:S(2)}, u32[]{:S(2)}) collective-permute-start(bf16[2,2,512,512]{3,2,1,0:T(8,128)(2,1)} %bitcast.33), channel_id=1, source_target_pairs={{0,1},{1,0},{2,3},{3,2},{4,5},{5,4},{6,7},{7,6},{8,9},{9,8},{10,11... | collective-permute-start | bytes 6291464 | tf_op jit(solution)/shard_map/ppermute | solution.py:38
  319.7 36.2 %all-to-all-start.2 = ((bf16[4,128,2176]{2,1,0:T(8,128)(2,1)}), bf16[4,128,2176]{2,1,0:T(8,128)(2,1)S(1)}, u32[]{:S(2)}, u32[]{:S(2)}) async-start(bf16[4,128,2176]{2,1,0:T(8,128)(2,1)} %add_convert_fusion.1), calls=%async_computation.2 | async-start | bytes 4456448 | tf_op jit(solution)/shard_map/all_to_all | solution.py:87
  323.3 101.0 %all-gather.17.cloned.1.call-start = ((), (), s32[]{:S(2)}) async-start(), calls=%async_computation.10 | async-start | bytes 6291456 | tf_op jit(solution)/shard_map/all_gather | solution.py:937
  370.9 4.6 collective-permute-start.38
  372.5 30.6 %collective-permute-start.39 = (bf16[128,2176]{1,0:T(8,128)(2,1)}, bf16[128,2176]{1,0:T(8,128)(2,1)}, u32[]{:S(2)}, u32[]{:S(2)}) collective-permute-start(bf16[128,2176]{1,0:T(8,128)(2,1)} %convert_reduce_fusion.1), channel_id=1, source_target_pairs={{0,2},{1,3},{2,0},{3,1},{4,6},{5,7},{6,4},{7,5},{8,10},{9,11},{10,... | collective-permute-start | bytes 1671176 | tf_op jit(solution)/shard_map/ppermute | solution.py:38
  379.0 38.1 %all-to-all-start.3 = ((bf16[4,128,2176]{2,1,0:T(8,128)(2,1)}), bf16[4,128,2176]{2,1,0:T(8,128)(2,1)S(1)}, u32[]{:S(2)}, u32[]{:S(2)}) async-start(bf16[4,128,2176]{2,1,0:T(8,128)(2,1)} %add_convert_fusion), calls=%async_computation.3 | async-start | bytes 4456448 | tf_op jit(solution)/shard_map/all_to_all | solution.py:87
  382.6 188.4 %all-gather.19.cloned.1.call-start = ((), (), s32[]{:S(2)}) async-start(), calls=%async_computation.11 | async-start | bytes 6291456 | tf_op jit(solution)/shard_map/all_gather | solution.py:937
  400.1 197.3 %reduce-scatter.2.cloned.1.call-start = ((), (), s32[]{:S(2)}) async-start(), calls=%async_computation.7 | async-start | bytes 9437184 | tf_op jit(solution)/shard_map/reduce_scatter | solution.py:1003
  406.1 49.0 %collective-permute-start.47 = (bf16[2,512,512]{2,1,0:T(8,128)(2,1)}, bf16[2,512,512]{2,1,0:T(8,128)(2,1)}, u32[]{:S(2)}, u32[]{:S(2)}) collective-permute-start(bf16[2,512,512]{2,1,0:T(8,128)(2,1)} %fusion.8), channel_id=1, source_target_pairs={{0,2},{1,3},{2,0},{3,1},{4,6},{5,7},{6,4},{7,5},{8,10},{9,11},{10,... | collective-permute-start | bytes 3145736 | tf_op jit(solution)/shard_map/ppermute | solution.py:38
  420.9 15.8 %collective-permute-start.42 = (bf16[128,2048]{1,0:T(8,128)(2,1)S(1)}, bf16[128,2048]{1,0:T(8,128)(2,1)S(1)}, u32[]{:S(2)}, u32[]{:S(2)}) collective-permute-start(bf16[128,2048]{1,0:T(8,128)(2,1)S(1)} %get-tuple-element.141.refs_0_), channel_id=1, source_target_pairs={{0,24},{4,28},{8,16},{12,20},{16,8},{20,12},{24,0},{28,4},{1,25},{... | collective-permute-start | bytes 1572872 | tf_op jit(solution)/shard_map/ppermute | solution.py:38
  423.7 23.0 %collective-permute-start.41 = (bf16[128,2048]{1,0:T(8,128)(2,1)S(1)}, bf16[128,2048]{1,0:T(8,128)(2,1)}, u32[]{:S(2)}, u32[]{:S(2)}) collective-permute-start(bf16[128,2048]{1,0:T(8,128)(2,1)S(1)} %get-tuple-element.141.refs_0_), channel_id=1, source_target_pairs={{0,16},{4,20},{8,24},{12,28},{16,0},{20,4},{24,8},{28,12},{1,17},{... | collective-permute-start | bytes 1572872 | tf_op jit(solution)/shard_map/ppermute | solution.py:38
  424.3 22.7 %collective-permute-start.40 = (bf16[128,2048]{1,0:T(8,128)(2,1)S(1)}, bf16[128,2048]{1,0:T(8,128)(2,1)}, u32[]{:S(2)}, u32[]{:S(2)}) collective-permute-start(bf16[128,2048]{1,0:T(8,128)(2,1)S(1)} %get-tuple-element.141.refs_0_), channel_id=1, source_target_pairs={{0,8},{4,12},{8,0},{12,4},{16,24},{20,28},{24,16},{28,20},{1,9},{5... | collective-permute-start | bytes 1572872 | tf_op jit(solution)/shard_map/ppermute | solution.py:38
  447.0 8.1 %collective-permute-start.46 = (bf16[128,2048]{1,0:T(8,128)(2,1)S(1)}, bf16[128,2048]{1,0:T(8,128)(2,1)S(1)}, u32[]{:S(2)}, u32[]{:S(2)}) collective-permute-start(bf16[128,2048]{1,0:T(8,128)(2,1)S(1)} %collective-permute-done.42.refs_3_), channel_id=1, source_target_pairs={{0,4},{4,0},{8,12},{12,8},{16,20},{20,16},{24,28},{28,24},{1,5},{5... | collective-permute-start | bytes 1572872 | tf_op jit(solution)/shard_map/ppermute | solution.py:38
  447.0 8.1 %collective-permute-start.45 = (bf16[128,2048]{1,0:T(8,128)(2,1)}, bf16[128,2048]{1,0:T(8,128)(2,1)S(1)}, u32[]{:S(2)}, u32[]{:S(2)}) collective-permute-start(bf16[128,2048]{1,0:T(8,128)(2,1)} %collective-permute-done.41.refs_2_), channel_id=1, source_target_pairs={{0,4},{4,0},{8,12},{12,8},{16,20},{20,16},{24,28},{28,24},{1,5},{5... | collective-permute-start | bytes 1572872 | tf_op jit(solution)/shard_map/ppermute | solution.py:38
  447.5 7.6 %collective-permute-start.43 = (bf16[128,2048]{1,0:T(8,128)(2,1)S(1)}, bf16[128,2048]{1,0:T(8,128)(2,1)S(1)}, u32[]{:S(2)}, u32[]{:S(2)}) collective-permute-start(bf16[128,2048]{1,0:T(8,128)(2,1)S(1)} %get-tuple-element.141.refs_0_), channel_id=1, source_target_pairs={{0,4},{4,0},{8,12},{12,8},{16,20},{20,16},{24,28},{28,24},{1,5},{5... | collective-permute-start | bytes 1572872 | tf_op jit(solution)/shard_map/ppermute | solution.py:38
  447.5 9.2 %collective-permute-start.44 = (bf16[128,2048]{1,0:T(8,128)(2,1)}, bf16[128,2048]{1,0:T(8,128)(2,1)}, u32[]{:S(2)}, u32[]{:S(2)}) collective-permute-start(bf16[128,2048]{1,0:T(8,128)(2,1)} %collective-permute-done.40.refs_1_), channel_id=1, source_target_pairs={{0,4},{4,0},{8,12},{12,8},{16,20},{20,16},{24,28},{28,24},{1,5},{5... | collective-permute-start | bytes 1572872 | tf_op jit(solution)/shard_map/ppermute | solution.py:38
  474.7 175.9 %collective-permute-start.55 = (bf16[2,512,512]{2,1,0:T(8,128)(2,1)}, bf16[2,512,512]{2,1,0:T(8,128)(2,1)}, u32[]{:S(2)}, u32[]{:S(2)}) collective-permute-start(bf16[2,512,512]{2,1,0:T(8,128)(2,1)} %fusion.9), channel_id=1, source_target_pairs={{0,2},{1,3},{2,0},{3,1},{4,6},{5,7},{6,4},{7,5},{8,10},{9,11},{10,... | collective-permute-start | bytes 3145736 | tf_op jit(solution)/shard_map/ppermute | solution.py:38
  527.2 47.1 %all-to-all-start.5 = ((bf16[32,80,256]{2,1,0:T(8,128)(2,1)}), bf16[32,80,256]{2,1,0:T(8,128)(2,1)}, u32[]{:S(2)}, u32[]{:S(2)}) async-start(bf16[32,80,256]{2,1,0:T(8,128)(2,1)} %pad_maximum_fusion), calls=%async_computation.6 | async-start | bytes 2621440 | tf_op jit(solution)/shard_map/all_to_all | solution.py:1032
  537.2 40.5 %collective-permute-start.49 = (bf16[512,2048]{1,0:T(8,128)(2,1)}, bf16[512,2048]{1,0:T(8,128)(2,1)}, u32[]{:S(2)}, u32[]{:S(2)}) collective-permute-start(bf16[512,2048]{1,0:T(8,128)(2,1)} %add_convert_fusion.2), channel_id=1, source_target_pairs={{0,4},{4,0},{8,12},{12,8},{16,20},{20,16},{24,28},{28,24},{1,5},{5... | collective-permute-start | bytes 6291464 | tf_op jit(solution)/shard_map/ppermute | solution.py:38
  537.7 30.2 %collective-permute-start.53 = (bf16[2,64,2048]{2,1,0:T(8,128)(2,1)S(1)}, bf16[2,64,2048]{2,1,0:T(8,128)(2,1)S(1)}, u32[]{:S(2)}, u32[]{:S(2)}) collective-permute-start(bf16[2,64,2048]{2,1,0:T(8,128)(2,1)S(1)} %pad_maximum_fusion.7), channel_id=1, source_target_pairs={{0,1},{1,0},{2,3},{3,2},{4,5},{5,4},{6,7},{7,6},{8,9},{9,8},{10,11... | collective-permute-start | bytes 1572872 | tf_op jit(solution)/shard_map/ppermute | solution.py:38
  568.7 81.9 %collective-permute-start.54 = (bf16[64,2048]{1,0:T(8,128)(2,1)}, bf16[64,2048]{1,0:T(8,128)(2,1)S(1)}, u32[]{:S(2)}, u32[]{:S(2)}) collective-permute-start(bf16[64,2048]{1,0:T(8,128)(2,1)} %fusion.24), channel_id=1, source_target_pairs={{0,2},{1,3},{2,0},{3,1},{4,6},{5,7},{6,4},{7,5},{8,10},{9,11},{10,... | collective-permute-start | bytes 786440 | tf_op jit(solution)/shard_map/ppermute | solution.py:38
  574.2 82.0 %all-to-all-start.4 = ((bf16[32,64,512]{2,1,0:T(8,128)(2,1)}), bf16[32,64,512]{2,1,0:T(8,128)(2,1)}, u32[]{:S(2)}, u32[]{:S(2)}) async-start(bf16[32,64,512]{2,1,0:T(8,128)(2,1)} %bitcast.188), calls=%async_computation.5 | async-start | bytes 4194304 | tf_op jit(solution)/shard_map/all_to_all | solution.py:1032
  580.6 29.0 %collective-permute-start.50 = (bf16[128,2048]{1,0:T(8,128)(2,1)}, bf16[128,2048]{1,0:T(8,128)(2,1)}, u32[]{:S(2)}, u32[]{:S(2)}) collective-permute-start(bf16[128,2048]{1,0:T(8,128)(2,1)} %get-tuple-element.177), channel_id=1, source_target_pairs={{0,8},{4,12},{8,0},{12,4},{16,24},{20,28},{24,16},{28,20},{1,9},{5... | collective-permute-start | bytes 1572872 | tf_op jit(solution)/shard_map/ppermute | solution.py:38
  582.2 42.1 %collective-permute-start.52 = (bf16[128,2048]{1,0:T(8,128)(2,1)}, bf16[128,2048]{1,0:T(8,128)(2,1)}, u32[]{:S(2)}, u32[]{:S(2)}) collective-permute-start(bf16[128,2048]{1,0:T(8,128)(2,1)} %get-tuple-element.178), channel_id=1, source_target_pairs={{0,24},{4,28},{8,16},{12,20},{16,8},{20,12},{24,0},{28,4},{1,25},{... | collective-permute-start | bytes 1572872 | tf_op jit(solution)/shard_map/ppermute | solution.py:38
  583.7 40.6 %collective-permute-start.51 = (bf16[128,2048]{1,0:T(8,128)(2,1)}, bf16[128,2048]{1,0:T(8,128)(2,1)}, u32[]{:S(2)}, u32[]{:S(2)}) collective-permute-start(bf16[128,2048]{1,0:T(8,128)(2,1)} %get-tuple-element.179), channel_id=1, source_target_pairs={{0,16},{4,20},{8,24},{12,28},{16,0},{20,4},{24,8},{28,12},{1,17},{... | collective-permute-start | bytes 1572872 | tf_op jit(solution)/shard_map/ppermute | solution.py:38
  609.6 41.0 %collective-permute-start.48 = (bf16[128,2048]{1,0:T(8,128)(2,1)S(1)}, bf16[128,2048]{1,0:T(8,128)(2,1)S(1)}, u32[]{:S(2)}, u32[]{:S(2)}) collective-permute-start(bf16[128,2048]{1,0:T(8,128)(2,1)S(1)} %slice_bitcast_fusion.2), channel_id=1, source_target_pairs={{0,2},{1,3},{2,0},{3,1},{4,6},{5,7},{6,4},{7,5},{8,10},{9,11},{10,... | collective-permute-start | bytes 1572872 | tf_op jit(solution)/shard_map/ppermute | solution.py:38
  (64 other events, 738.2 us)
Sparse Core Ops, SparseCore 0:
  75.6 38.7 all-gather.12
  130.7 39.8 all-gather.14
  325.7 88.0 all-gather.16
  415.2 76.1 all-gather.18
  494.7 83.9 reduce-scatter.1

commit v5 on v4

--- a/solution.py
+++ b/solution.py
@@ -852,7 +852,7 @@
     token_pieces = near_tokens + [hop(after(piece, pair_cut, *partner), "seq", 1) for piece in near_tokens]
     value_cut = exchange(after(cut_of(w_value), pair_cut))
     pair_pieces = gather_batch(after(pair_cut, *token_pieces), value_cut)
-    value_pieces = gather_batch(after(value_cut, *pair_pieces[2:3]), *pair_pieces)
+    value_pieces = gather_batch(after(value_cut, *pair_pieces))
     out_pieces = gather_batch(after(w_out, *pair_pieces), *value_pieces)
     small = jnp.stack([item[:, shard:] for item in pair_pieces])
     small = small.reshape(batch_size, seq_size, deep * fit, shard)[

time: 684 us -> 677 us (0.990)
  waiting for transfers between devices: 199 us -> 191 us
    ppermute x56, waiting for transfers between devices: 198 us -> 191 us  [hop(): return lax.ppermute(values, axis, [(i, i ^ mask) for i in range(size)])]
where the time goes in v5:
time: 677 us; the launch traced here: 669 us
  Pallas kernels  205 us (30%)
  waiting for transfers between devices  191 us (28%)
  starting transfers between devices  75.8 us (11%)
  other arithmetic  61.9 us (9%)
  blocking collectives  50 us (7%)
  local copies, waits for them, and re-layouts  48.8 us (7%)
  matrix products  20.5 us (3%)
  between operations  15.5 us (2%)
    ppermute x56, waiting for transfers between devices, hop(): return lax.ppermute(values, axis, [(i, i ^ mask) for i in range(size)])  191 us
    ppermute x56, starting transfers between devices, hop(): return lax.ppermute(values, axis, [(i, i ^ mask) for i in range(size)])  58.8 us
    pallas_call x2, Pallas kernels, run_acts(): pl.pallas_call(functools.partial(acts_kernel, experts, blocks, per), grid...  50.7 us
    pallas_call x4, Pallas kernels, in_blocks(): pl.pallas_call(functools.partial(in_kernel, sets), grid_spec=pltpu.Prefet...  34.9 us
    pallas_call x2, Pallas kernels, run_back(): pl.pallas_call(functools.partial(rows_back_kernel, blocks, per), grid_spe...  32.5 us
    all_to_all x2, blocking collectives, exchange(): lax.all_to_all(blocks, 'seq', split_axis=0, concat_axis=0, tiled=True)  31.5 us
    pallas_call x1, Pallas kernels, attention(): pl.pallas_call(functools.partial(attend_back_kernel, blocks, size), grid=...  19.9 us
    all_gather x2, blocking collectives, sum_seq(): return jnp.sum(lax.all_gather(values, 'seq', axis=0), axis=0)  18.5 us
  transfers between devices with their start and end apart: 65, of which 28 were waited for; matrix products, arithmetic and copies ran while one was open for 17% of the time, Pallas kernels for 23%

profile of v5, /device:TPU:0, one launch (start us, length us, event | category | flops | bytes accessed | tf_op | source)
XLA Modules:
  0.0 668.8 jit_solution(17430708177416269729)
XLA Ops:
  7.2 4.0 collective-permute-start.2
  14.1 3.1 collective-permute-start.3
  19.9 21.1 %all_to_all.30.refs_8_ = bf16[8,72,512]{2,1,0:T(8,128)(2,1)S(1)} all-to-all(bf16[8,72,512]{2,1,0:T(8,128)(2,1)S(1)} %pad_maximum_fusion.2), channel_id=1, replica_groups=mesh['seq'=8,'batch'=4] {'seq'}, dimensions={0} | all-to-all | bytes 1179648 | tf_op jit(solution)/shard_map/all_to_all | solution.py:836
  45.6 2.6 collective-permute-start.9
  49.8 10.4 %all_to_all.31.refs_0_ = bf16[8,64,256]{2,1,0:T(8,128)(2,1)S(1)} all-to-all(bf16[8,64,256]{2,1,0:T(8,128)(2,1)S(1)} %bitcast.197), channel_id=1, replica_groups=mesh['seq'=8,'batch'=4] {'seq'}, dimensions={0} | all-to-all | bytes 524288 | tf_op jit(solution)/shard_map/all_to_all | solution.py:836
  60.2 14.4 %collective-permute-done.9.refs_10_ = bf16[8,72,512]{2,1,0:T(8,128)(2,1)S(1)} collective-permute-done((bf16[8,72,512]{2,1,0:T(8,128)(2,1)S(1)}, bf16[8,72,512]{2,1,0:T(8,128)(2,1)S(1)}, u32[]{:S(2)}, u32[]{:S(2)}) %collective-permute-start.9) | collective-permute-done | bytes 589856 | tf_op jit(solution)/shard_map/ppermute | solution.py:38
  84.8 8.3 %collective-permute-done.10.refs_11_ = bf16[8,72,512]{2,1,0:T(8,128)(2,1)S(1)} collective-permute-done((bf16[8,72,512]{2,1,0:T(8,128)(2,1)}, bf16[8,72,512]{2,1,0:T(8,128)(2,1)S(1)}, u32[]{:S(2)}, u32[]{:S(2)}) %collective-permute-start.10) | collective-permute-done | bytes 589856 | tf_op jit(solution)/shard_map/ppermute | solution.py:38
  93.1 3.0 collective-permute-start.12
  100.1 9.7 %shard_map.289 = (bf16[1024,2048]{1,0:T(8,128)(2,1)}, f32[1024,512]{1,0:T(8,128)}, f32[2,1024]{1,0:T(2,128)}, bf16[8,4,64,512]{3,2,1,0:T(8,128)(2,1)}) custom-call(s32[10]{0:T(128)} %get-tuple-element.203.at_ref, bf16[128,2048]{1,0:T(8,128)(2,1)} %bitcast.175, bf16[128,2048]{1,0:T(8,128)(2,1)} %collective-permute-done.refs_1_, ...), custom_call_target="tpu_custom_call" | custom-call | flops 2147483648 | bytes 16777216 | tf_op jit(solution)/shard_map/pallas_call | solution.py:197
  109.9 9.3 %all-gather.6 = f32[8,2,1024]{2,1,0:T(2,128)S(1)} all-gather(f32[1,2,1024]{2,1,0:T(2,128)} %bitcast.211), channel_id=2, replica_groups=mesh['seq'=8,'batch'=4] {'seq'}, dimensions={0}, use_global_device_ids=true | all-gather | bytes 73728 | tf_op jit(solution)/shard_map/all_gather | solution.py:885
  123.1 6.8 %collective-permute-done.13.refs_3_ = bf16[8,64,256]{2,1,0:T(8,128)(2,1)S(1)} collective-permute-done((bf16[8,64,256]{2,1,0:T(8,128)(2,1)S(1)}, bf16[8,64,256]{2,1,0:T(8,128)(2,1)S(1)}, u32[]{:S(2)}, u32[]{:S(2)}) %collective-permute-start.13) | collective-permute-done | bytes 262176 | tf_op jit(solution)/shard_map/ppermute | solution.py:38
  131.7 6.0 shard_map.290
  137.7 10.1 %shard_map.291.refs_8_ = bf16[1024,256]{1,0:T(8,128)(2,1)} custom-call(s32[8]{0:T(128)} %gather_fusion, f32[1024,512]{1,0:T(8,128)} %get-tuple-element.97.q_ref.k_ref, f32[1024,512]{1,0:T(8,128)} %get-tuple-element.97.q_ref.k_ref, bf16[1024,256]{1,0:T(8,128)(2,1)} %get-tuple-element.101.v_ref, f32[1024,2]{1,0:T(8,128)} %get-tuple-element.191.scale_ref, ...), custom_call_target="tpu_custom_call" | custom-call | flops 1073741824 | bytes 4194304 | tf_op jit(solution)/shard_map/pallas_call | solution.py:448
  150.6 3.4 collective-permute-done.17
  159.4 11.4 %collective-permute-done.18 = bf16[128,2048]{1,0:T(8,128)(2,1)S(1)} collective-permute-done((bf16[128,2048]{1,0:T(8,128)(2,1)}, bf16[128,2048]{1,0:T(8,128)(2,1)S(1)}, u32[]{:S(2)}, u32[]{:S(2)}) %collective-permute-start.18) | collective-permute-done | bytes 524320 | tf_op jit(solution)/shard_map/ppermute | solution.py:38
  170.8 11.4 %collective-permute-done.20 = bf16[128,2048]{1,0:T(8,128)(2,1)S(1)} collective-permute-done((bf16[128,2048]{1,0:T(8,128)(2,1)}, bf16[128,2048]{1,0:T(8,128)(2,1)S(1)}, u32[]{:S(2)}, u32[]{:S(2)}) %collective-permute-start.20) | collective-permute-done | bytes 524320 | tf_op jit(solution)/shard_map/ppermute | solution.py:38
  189.7 2.9 collective-permute-start.28
  192.5 8.5 %collective-permute-done.21.refs_1_ = bf16[128,2048]{1,0:T(8,128)(2,1)S(1)} collective-permute-done((bf16[128,2048]{1,0:T(8,128)(2,1)S(1)}, bf16[128,2048]{1,0:T(8,128)(2,1)S(1)}, u32[]{:S(2)}, u32[]{:S(2)}) %collective-permute-start.21) | collective-permute-done | bytes 524320 | tf_op jit(solution)/shard_map/ppermute | solution.py:38
  201.0 9.0 %collective-permute-done.23.refs_3_ = bf16[128,2048]{1,0:T(8,128)(2,1)S(1)} collective-permute-done((bf16[128,2048]{1,0:T(8,128)(2,1)S(1)}, bf16[128,2048]{1,0:T(8,128)(2,1)S(1)}, u32[]{:S(2)}, u32[]{:S(2)}) %collective-permute-start.23) | collective-permute-done | bytes 524320 | tf_op jit(solution)/shard_map/ppermute | solution.py:38
  218.5 25.2 %shard_map.292 = (bf16[1024,2048]{1,0:T(8,128)(2,1)}, bf16[1024,2048]{1,0:T(8,128)(2,1)}, bf16[2,1024,512]{2,1,0:T(8,128)(2,1)}, bf16[2,1024,512]{2,1,0:T(8,128)...) custom-call(s32[10]{0:T(128)} %get-tuple-element.129.at_ref, bf16[128,2048]{1,0:T(8,128)(2,1)} %copy-done.22, ...), custom_call_target="tpu_custom_call" | custom-call | flops 12884901888 | bytes 35651584 | tf_op jit(solution)/shard_map/pallas_call | solution.py:548
  248.1 25.5 %shard_map.293 = (bf16[1024,2048]{1,0:T(8,128)(2,1)}, bf16[1024,2048]{1,0:T(8,128)(2,1)}, bf16[2,1024,512]{2,1,0:T(8,128)(2,1)}, bf16[2,1024,512]{2,1,0:T(8,128)...) custom-call(s32[10]{0:T(128)} %get-tuple-element.129.at_ref, bf16[128,2048]{1,0:T(8,128)(2,1)} %copy-done.56, ...), custom_call_target="tpu_custom_call" | custom-call | flops 12884901888 | bytes 35651584 | tf_op jit(solution)/shard_map/pallas_call | solution.py:548
  273.6 8.7 %shard_map.294 = bf16[1,2,2,512,512]{4,3,2,1,0:T(8,128)(2,1)} custom-call(s32[1]{0:T(128)} %bitcast.26.at_ref, bf16[1024,2048]{1,0:T(8,128)(2,1)} %get-tuple-element.108.refs_0_, bf16[1024,2048]{1,0:T(8,128)(2,1)} %get-tuple-element.115.refs_1_, bf16[2,1024,512]{2,1,0:T(8,128)(2,1)} %get-tuple-element.116.refs_2_.gate_ref, ...), custom_call_target="tpu_custom_call" | custom-call | flops 4294967296 | bytes 8388608 | tf_op jit(solution)/shard_map/pallas_call | solution.py:747
  282.3 16.2 %shard_map.295 = (bf16[2,2,128,2176]{3,2,1,0:T(8,128)(2,1)}, bf16[2,2,128,2176]{3,2,1,0:T(8,128)(2,1)}) custom-call(s32[10]{0:T(128)} %get-tuple-element.129.at_ref, bf16[2,1024,512]{2,1,0:T(8,128)(2,1)} %get-tuple-element.117.refs_3_.gate_ref, bf16[2,1024,512]{2,1,0:T(8,128)(2,1)} %get-tuple-element.119.up_ref.refs_3_, ...), custom_call_target="tpu_custom_call" | custom-call | flops 8589934592 | bytes 16777216 | tf_op jit(solution)/shard_map/pallas_call | solution.py:678
  299.3 8.7 %shard_map.296 = bf16[1,2,2,512,512]{4,3,2,1,0:T(8,128)(2,1)} custom-call(s32[1]{0:T(128)} %bitcast.26.at_ref, bf16[1024,2048]{1,0:T(8,128)(2,1)} %get-tuple-element.108.refs_0_, bf16[1024,2048]{1,0:T(8,128)(2,1)} %get-tuple-element.115.refs_1_, bf16[2,1024,512]{2,1,0:T(8,128)(2,1)} %get-tuple-element.123.refs_2_.up_ref, ...), custom_call_target="tpu_custom_call" | custom-call | flops 4294967296 | bytes 8388608 | tf_op jit(solution)/shard_map/pallas_call | solution.py:747
  308.1 3.5 add_convert_fusion.1
  311.6 3.6 all-to-all-start.2
  316.0 15.6 %shard_map.298 = bf16[2,2,2,2,128,2048]{5,4,3,2,1,0:T(8,128)(2,1)} custom-call(s32[10]{0:T(128)} %get-tuple-element.129.at_ref, bf16[2,1024,512]{2,1,0:T(8,128)(2,1)} %get-tuple-element.130.refs_0_, bf16[2,1024,512]{2,1,0:T(8,128)(2,1)} %get-tuple-element.131.refs_1_, bf16[2,1024,2048]{2,1,0:T(8,128)(2,1)} %refs_2_.1), custom_call_target="tpu_custom_call" | custom-call | flops 8589934592 | bytes 12582912 | tf_op jit(solution)/shard_map/pallas_call | solution.py:635
  331.5 16.2 %shard_map.297 = (bf16[2,2,128,2176]{3,2,1,0:T(8,128)(2,1)}, bf16[2,2,128,2176]{3,2,1,0:T(8,128)(2,1)}) custom-call(s32[10]{0:T(128)} %get-tuple-element.129.at_ref, bf16[2,1024,512]{2,1,0:T(8,128)(2,1)} %get-tuple-element.116.refs_2_.gate_ref, bf16[2,1024,512]{2,1,0:T(8,128)(2,1)} %get-tuple-element.123.refs_2_.up_ref, ...), custom_call_target="tpu_custom_call" | custom-call | flops 8589934592 | bytes 16777216 | tf_op jit(solution)/shard_map/pallas_call | solution.py:678
  349.0 14.0 %collective-permute-done.37 = bf16[2,2,512,512]{3,2,1,0:T(8,128)(2,1)} collective-permute-done((bf16[2,2,512,512]{3,2,1,0:T(8,128)(2,1)}, bf16[2,2,512,512]{3,2,1,0:T(8,128)(2,1)}, u32[]{:S(2)}, u32[]{:S(2)}) %collective-permute-start.37) | collective-permute-done | bytes 2097184 | tf_op jit(solution)/shard_map/ppermute | solution.py:38
  364.5 3.8 collective-permute-start.39
  368.4 3.6 add_convert_fusion
  371.9 3.6 all-to-all-start.3
  375.6 8.7 %shard_map.299 = bf16[1,2,2,512,512]{4,3,2,1,0:T(8,128)(2,1)} custom-call(s32[1]{0:T(128)} %bitcast.34.at_ref, bf16[1024,2048]{1,0:T(8,128)(2,1)} %get-tuple-element.108.refs_0_, bf16[1024,2048]{1,0:T(8,128)(2,1)} %get-tuple-element.115.refs_1_, bf16[2,1024,512]{2,1,0:T(8,128)(2,1)} %get-tuple-element.116.refs_2_.gate_ref, ...), custom_call_target="tpu_custom_call" | custom-call | flops 4294967296 | bytes 8388608 | tf_op jit(solution)/shard_map/pallas_call | solution.py:747
  384.3 8.8 %shard_map.300 = bf16[1,2,256,2048]{3,2,1,0:T(8,128)(2,1)} custom-call(s32[1]{0:T(128)} %bitcast.26.at_ref, bf16[2,1024,512]{2,1,0:T(8,128)(2,1)} %get-tuple-element.130.refs_0_, bf16[2,1024,512]{2,1,0:T(8,128)(2,1)} %get-tuple-element.131.refs_1_, bf16[1024,2048]{1,0:T(8,128)(2,1)} %get-tuple-element.136.refs_2_, bf16[1024,2048]{1,0:T(8,128)(2,1)} %get-tuple-element.137.refs_3_), custom_call_target="tpu_custom_call" | custom-call | flops 4294967296 | bytes 10485760 | tf_op jit(solution)/shard_map/pallas_call | solution.py:713
  393.2 2.9 convert_add_fusion.2
  399.3 2.9 collective-permute-start.47
  402.2 8.8 %shard_map.301 = bf16[1,2,2,512,512]{4,3,2,1,0:T(8,128)(2,1)} custom-call(s32[1]{0:T(128)} %bitcast.34.at_ref, bf16[1024,2048]{1,0:T(8,128)(2,1)} %get-tuple-element.108.refs_0_, bf16[1024,2048]{1,0:T(8,128)(2,1)} %get-tuple-element.115.refs_1_, bf16[2,1024,512]{2,1,0:T(8,128)(2,1)} %get-tuple-element.123.refs_2_.up_ref, ...), custom_call_target="tpu_custom_call" | custom-call | flops 4294967296 | bytes 8388608 | tf_op jit(solution)/shard_map/pallas_call | solution.py:747
  414.7 2.8 collective-permute-start.42
  420.8 2.7 convert_add_fusion.1
  423.5 7.0 %collective-permute-done.42.refs_3_ = bf16[128,2048]{1,0:T(8,128)(2,1)S(1)} collective-permute-done((bf16[128,2048]{1,0:T(8,128)(2,1)S(1)}, bf16[128,2048]{1,0:T(8,128)(2,1)S(1)}, u32[]{:S(2)}, u32[]{:S(2)}) %collective-permute-start.42) | collective-permute-done | bytes 524320 | tf_op jit(solution)/shard_map/ppermute | solution.py:38
  430.5 10.2 %collective-permute-done.41.refs_2_ = bf16[128,2048]{1,0:T(8,128)(2,1)} collective-permute-done((bf16[128,2048]{1,0:T(8,128)(2,1)S(1)}, bf16[128,2048]{1,0:T(8,128)(2,1)}, u32[]{:S(2)}, u32[]{:S(2)}) %collective-permute-start.41) | collective-permute-done | bytes 524320 | tf_op jit(solution)/shard_map/ppermute | solution.py:38
  441.9 6.6 collective-permute-done.47
  450.1 7.9 %shard_map.302 = (bf16[1024,256]{1,0:T(8,128)(2,1)}, bf16[256,2048]{1,0:T(8,128)(2,1)}) custom-call(bf16[128,2048]{1,0:T(8,128)(2,1)} %copy-done.38, bf16[128,2048]{1,0:T(8,128)(2,1)} %collective-permute-done.40.refs_1_, bf16[128,2048]{1,0:T(8,128)(2,1)} %collective-permute-done.41.refs_2_, bf16[128,2048]{1,0:T(8,128)(2,1)} %copy-done.61, ...), custom_call_target="tpu_custom_call" | custom-call | flops 2147483648 | bytes 8388608 | tf_op jit(solution)/shard_map/pallas_call | solution.py:301
  461.7 3.1 dynamic-slice_bitcast_fusion.3
  465.4 2.7 fusion.9
  468.2 3.1 dynamic-slice_bitcast_fusion.2
  471.4 19.9 %shard_map.303 = (f32[1024,256]{1,0:T(8,128)}, f32[1024,256]{1,0:T(8,128)}, bf16[1024,256]{1,0:T(8,128)(2,1)}, f32[1024,2]{1,0:T(8,128)}, f32[2,256]{1,0:T(2,128)}) custom-call(s32[8]{0:T(128)} %gather_fusion, f32[1024,512]{1,0:T(8,128)} %get-tuple-element.97.q_ref.k_ref, f32[1024,512]{1,0:T(8,128)} %get-tuple-element.97.q_ref.k_ref, ...), custom_call_target="tpu_custom_call" | custom-call | flops 2684354560 | bytes 8388608 | tf_op jit(solution)/shard_map/pallas_call | solution.py:460
  493.0 5.3 convolution_convert_fusion.3
  499.6 9.2 %all-gather.7 = f32[8,2,1024]{2,1,0:T(2,128)S(1)} all-gather(f32[1,2,1024]{2,1,0:T(2,128)S(1)} %copy.142), channel_id=6, replica_groups=mesh['seq'=8,'batch'=4] {'seq'}, dimensions={0}, use_global_device_ids=true | all-gather | bytes 73728 | tf_op jit(solution)/shard_map/all_gather | solution.py:885
  514.6 3.8 convolution_convert_fusion
  519.5 6.1 all-to-all-start.5
  527.6 2.7 add_convert_fusion.2
  535.6 2.9 maximum_select_fusion
  539.9 20.9 %collective-permute-done.53 = bf16[2,64,2048]{2,1,0:T(8,128)(2,1)S(1)} collective-permute-done((bf16[2,64,2048]{2,1,0:T(8,128)(2,1)S(1)}, bf16[2,64,2048]{2,1,0:T(8,128)(2,1)S(1)}, u32[]{:S(2)}, u32[]{:S(2)}) %collective-permute-start.53) | collective-permute-done | bytes 524320 | tf_op jit(solution)/shard_map/ppermute | solution.py:38
  561.7 2.3 collective-permute-start.54
  564.0 3.2 dynamic-slice_bitcast_fusion
  567.2 3.5 all-to-all-start.4
  570.7 2.9 add_convert_fusion.6
  577.1 8.9 %shard_map.304 = bf16[1,2,256,2048]{3,2,1,0:T(8,128)(2,1)} custom-call(s32[1]{0:T(128)} %bitcast.34.at_ref, bf16[2,1024,512]{2,1,0:T(8,128)(2,1)} %get-tuple-element.130.refs_0_, bf16[2,1024,512]{2,1,0:T(8,128)(2,1)} %get-tuple-element.131.refs_1_, bf16[1024,2048]{1,0:T(8,128)(2,1)} %get-tuple-element.136.refs_2_, bf16[1024,2048]{1,0:T(8,128)(2,1)} %get-tuple-element.137.refs_3_), custom_call_target="tpu_custom_call" | custom-call | flops 4294967296 | bytes 10485760 | tf_op jit(solution)/shard_map/pallas_call | solution.py:713
  586.0 4.4 convert_add_fusion
  591.4 11.2 %collective-permute-done.50 = bf16[128,2048]{1,0:T(8,128)(2,1)} collective-permute-done((bf16[128,2048]{1,0:T(8,128)(2,1)}, bf16[128,2048]{1,0:T(8,128)(2,1)}, u32[]{:S(2)}, u32[]{:S(2)}) %collective-permute-start.50) | collective-permute-done | bytes 524320 | tf_op jit(solution)/shard_map/ppermute | solution.py:38
  603.7 13.5 %collective-permute-done.52 = bf16[128,2048]{1,0:T(8,128)(2,1)} collective-permute-done((bf16[128,2048]{1,0:T(8,128)(2,1)}, bf16[128,2048]{1,0:T(8,128)(2,1)}, u32[]{:S(2)}, u32[]{:S(2)}) %collective-permute-start.52) | collective-permute-done | bytes 524320 | tf_op jit(solution)/shard_map/ppermute | solution.py:38
  619.3 24.3 %collective-permute-done.48 = bf16[128,2048]{1,0:T(8,128)(2,1)S(1)} collective-permute-done((bf16[128,2048]{1,0:T(8,128)(2,1)S(1)}, bf16[128,2048]{1,0:T(8,128)(2,1)S(1)}, u32[]{:S(2)}, u32[]{:S(2)}) %collective-permute-start.48) | collective-permute-done | bytes 524320 | tf_op jit(solution)/shard_map/ppermute | solution.py:38
  657.9 2.9 maximum_select_fusion.1
  (373 shorter events, 123.6 us)
Async XLA Ops:
  7.2 140.7 %all-gather.13.cloned.1.call-start = ((), (), s32[]{:S(2)}) async-start(), calls=%async_computation.8 | async-start | bytes 5013504 | tf_op jit(solution)/shard_map/all_gather | solution.py:872
  7.2 33.9 %collective-permute-start.2 = (bf16[128,2048]{1,0:T(8,128)(2,1)}, bf16[128,2048]{1,0:T(8,128)(2,1)}, u32[]{:S(2)}, u32[]{:S(2)}) collective-permute-start(bf16[128,2048]{1,0:T(8,128)(2,1)} %bitcast.172), channel_id=1, source_target_pairs={{0,24},{4,28},{8,16},{12,20},{16,8},{20,12},{24,0},{28,4},{1,25},{... | collective-permute-start | bytes 1572872 | tf_op jit(solution)/shard_map/ppermute | solution.py:38
  11.2 29.9 %collective-permute-start.1 = (bf16[128,2048]{1,0:T(8,128)(2,1)}, bf16[128,2048]{1,0:T(8,128)(2,1)}, u32[]{:S(2)}, u32[]{:S(2)}) collective-permute-start(bf16[128,2048]{1,0:T(8,128)(2,1)} %bitcast.173), channel_id=1, source_target_pairs={{0,16},{4,20},{8,24},{12,28},{16,0},{20,4},{24,8},{28,12},{1,17},{... | collective-permute-start | bytes 1572872 | tf_op jit(solution)/shard_map/ppermute | solution.py:38
  11.7 29.4 %collective-permute-start = (bf16[128,2048]{1,0:T(8,128)(2,1)}, bf16[128,2048]{1,0:T(8,128)(2,1)}, u32[]{:S(2)}, u32[]{:S(2)}) collective-permute-start(bf16[128,2048]{1,0:T(8,128)(2,1)} %bitcast.174), channel_id=1, source_target_pairs={{0,8},{4,12},{8,0},{12,4},{16,24},{20,28},{24,16},{28,20},{1,9},{5... | collective-permute-start | bytes 1572872 | tf_op jit(solution)/shard_map/ppermute | solution.py:38
  14.1 27.0 %collective-permute-start.3 = (bf16[128,2176]{1,0:T(8,128)(2,1)S(1)}, bf16[128,2176]{1,0:T(8,128)(2,1)S(1)}, u32[]{:S(2)}, u32[]{:S(2)}) collective-permute-start(bf16[128,2176]{1,0:T(8,128)(2,1)S(1)} %pad_maximum_fusion.3), channel_id=1, source_target_pairs={{0,2},{1,3},{2,0},{3,1},{4,6},{5,7},{6,4},{7,5},{8,10},{9,11},{10,... | collective-permute-start | bytes 1671176 | tf_op jit(solution)/shard_map/ppermute | solution.py:38
  41.2 2.9 collective-permute-start.5
  41.7 3.1 collective-permute-start.6
  41.8 3.8 collective-permute-start.7
  45.6 29.0 %collective-permute-start.9 = (bf16[8,72,512]{2,1,0:T(8,128)(2,1)S(1)}, bf16[8,72,512]{2,1,0:T(8,128)(2,1)S(1)}, u32[]{:S(2)}, u32[]{:S(2)}) collective-permute-start(bf16[8,72,512]{2,1,0:T(8,128)(2,1)S(1)} %all_to_all.30.refs_8_), channel_id=1, source_target_pairs={{0,2},{1,3},{2,0},{3,1},{4,6},{5,7},{6,4},{7,5},{8,10},{9,11},{10,... | collective-permute-start | bytes 1769480 | tf_op jit(solution)/shard_map/ppermute | solution.py:38
  48.2 27.2 %collective-permute-start.8 = (bf16[8,72,512]{2,1,0:T(8,128)(2,1)S(1)}, bf16[8,72,512]{2,1,0:T(8,128)(2,1)}, u32[]{:S(2)}, u32[]{:S(2)}) collective-permute-start(bf16[8,72,512]{2,1,0:T(8,128)(2,1)S(1)} %all_to_all.30.refs_8_), channel_id=1, source_target_pairs={{0,1},{1,0},{2,3},{3,2},{4,5},{5,4},{6,7},{7,6},{8,9},{9,8},{10,11... | collective-permute-start | bytes 1769480 | tf_op jit(solution)/shard_map/ppermute | solution.py:38
  75.4 169.5 %all-gather.15.cloned.1.call-start = ((), (), s32[]{:S(2)}) async-start(), calls=%async_computation.9 | async-start | bytes 5013504 | tf_op jit(solution)/shard_map/all_gather | solution.py:872
  78.4 14.7 %collective-permute-start.10 = (bf16[8,72,512]{2,1,0:T(8,128)(2,1)}, bf16[8,72,512]{2,1,0:T(8,128)(2,1)S(1)}, u32[]{:S(2)}, u32[]{:S(2)}) collective-permute-start(bf16[8,72,512]{2,1,0:T(8,128)(2,1)} %copy-done.48), channel_id=1, source_target_pairs={{0,1},{1,0},{2,3},{3,2},{4,5},{5,4},{6,7},{7,6},{8,9},{9,8},{10,11... | collective-permute-start | bytes 1769480 | tf_op jit(solution)/shard_map/ppermute | solution.py:38
  93.1 28.1 %collective-permute-start.12 = (bf16[8,64,256]{2,1,0:T(8,128)(2,1)S(1)}, bf16[8,64,256]{2,1,0:T(8,128)(2,1)S(1)}, u32[]{:S(2)}, u32[]{:S(2)}) collective-permute-start(bf16[8,64,256]{2,1,0:T(8,128)(2,1)S(1)} %all_to_all.31.refs_0_), channel_id=1, source_target_pairs={{0,2},{1,3},{2,0},{3,1},{4,6},{5,7},{6,4},{7,5},{8,10},{9,11},{10,... | collective-permute-start | bytes 786440 | tf_op jit(solution)/shard_map/ppermute | solution.py:38
  96.1 25.1 %collective-permute-start.11 = (bf16[8,64,256]{2,1,0:T(8,128)(2,1)S(1)}, bf16[8,64,256]{2,1,0:T(8,128)(2,1)S(1)}, u32[]{:S(2)}, u32[]{:S(2)}) collective-permute-start(bf16[8,64,256]{2,1,0:T(8,128)(2,1)S(1)} %all_to_all.31.refs_0_), channel_id=1, source_target_pairs={{0,1},{1,0},{2,3},{3,2},{4,5},{5,4},{6,7},{7,6},{8,9},{9,8},{10,11... | collective-permute-start | bytes 786440 | tf_op jit(solution)/shard_map/ppermute | solution.py:38
  97.9 25.2 %collective-permute-start.15 = (bf16[64,2048]{1,0:T(8,128)(2,1)S(1)}, bf16[64,2048]{1,0:T(8,128)(2,1)S(1)}, u32[]{:S(2)}, u32[]{:S(2)}) collective-permute-start(bf16[64,2048]{1,0:T(8,128)(2,1)S(1)} %copy-done.43), channel_id=1, source_target_pairs={{0,2},{1,3},{2,0},{3,1},{4,6},{5,7},{6,4},{7,5},{8,10},{9,11},{10,... | collective-permute-start | bytes 786440 | tf_op jit(solution)/shard_map/ppermute | solution.py:38
  97.9 25.1 %collective-permute-start.14 = (bf16[64,2048]{1,0:T(8,128)(2,1)S(1)}, bf16[64,2048]{1,0:T(8,128)(2,1)S(1)}, u32[]{:S(2)}, u32[]{:S(2)}) collective-permute-start(bf16[64,2048]{1,0:T(8,128)(2,1)S(1)} %copy-done.43), channel_id=1, source_target_pairs={{0,1},{1,0},{2,3},{3,2},{4,5},{5,4},{6,7},{7,6},{8,9},{9,8},{10,11... | collective-permute-start | bytes 786440 | tf_op jit(solution)/shard_map/ppermute | solution.py:38
  121.3 8.6 %collective-permute-start.13 = (bf16[8,64,256]{2,1,0:T(8,128)(2,1)S(1)}, bf16[8,64,256]{2,1,0:T(8,128)(2,1)S(1)}, u32[]{:S(2)}, u32[]{:S(2)}) collective-permute-start(bf16[8,64,256]{2,1,0:T(8,128)(2,1)S(1)} %collective-permute-done.12.refs_2_), channel_id=1, source_target_pairs={{0,1},{1,0},{2,3},{3,2},{4,5},{5,4},{6,7},{7,6},{8,9},{9,8},{10,11... | collective-permute-start | bytes 786440 | tf_op jit(solution)/shard_map/ppermute | solution.py:38
  129.9 17.9 %collective-permute-start.16 = (bf16[64,2048]{1,0:T(8,128)(2,1)S(1)}, bf16[64,2048]{1,0:T(8,128)(2,1)S(1)}, u32[]{:S(2)}, u32[]{:S(2)}) collective-permute-start(bf16[64,2048]{1,0:T(8,128)(2,1)S(1)} %collective-permute-done.15), channel_id=1, source_target_pairs={{0,1},{1,0},{2,3},{3,2},{4,5},{5,4},{6,7},{7,6},{8,9},{9,8},{10,11... | collective-permute-start | bytes 786440 | tf_op jit(solution)/shard_map/ppermute | solution.py:38
  149.8 4.2 collective-permute-start.17
  155.8 15.0 %collective-permute-start.18 = (bf16[128,2048]{1,0:T(8,128)(2,1)}, bf16[128,2048]{1,0:T(8,128)(2,1)S(1)}, u32[]{:S(2)}, u32[]{:S(2)}) collective-permute-start(bf16[128,2048]{1,0:T(8,128)(2,1)} %get-tuple-element.180), channel_id=1, source_target_pairs={{0,8},{4,12},{8,0},{12,4},{16,24},{20,28},{24,16},{28,20},{1,9},{5... | collective-permute-start | bytes 1572872 | tf_op jit(solution)/shard_map/ppermute | solution.py:38
  157.2 25.0 %collective-permute-start.20 = (bf16[128,2048]{1,0:T(8,128)(2,1)}, bf16[128,2048]{1,0:T(8,128)(2,1)S(1)}, u32[]{:S(2)}, u32[]{:S(2)}) collective-permute-start(bf16[128,2048]{1,0:T(8,128)(2,1)} %get-tuple-element.181), channel_id=1, source_target_pairs={{0,24},{4,28},{8,16},{12,20},{16,8},{20,12},{24,0},{28,4},{1,25},{... | collective-permute-start | bytes 1572872 | tf_op jit(solution)/shard_map/ppermute | solution.py:38
  158.6 25.0 %collective-permute-start.19 = (bf16[128,2048]{1,0:T(8,128)(2,1)}, bf16[128,2048]{1,0:T(8,128)(2,1)}, u32[]{:S(2)}, u32[]{:S(2)}) collective-permute-start(bf16[128,2048]{1,0:T(8,128)(2,1)} %get-tuple-element.182), channel_id=1, source_target_pairs={{0,16},{4,20},{8,24},{12,28},{16,0},{20,4},{24,8},{28,12},{1,17},{... | collective-permute-start | bytes 1572872 | tf_op jit(solution)/shard_map/ppermute | solution.py:38
  186.1 14.9 %collective-permute-start.21 = (bf16[128,2048]{1,0:T(8,128)(2,1)S(1)}, bf16[128,2048]{1,0:T(8,128)(2,1)S(1)}, u32[]{:S(2)}, u32[]{:S(2)}) collective-permute-start(bf16[128,2048]{1,0:T(8,128)(2,1)S(1)} %multiply_convert_fusion.2.refs_0_), channel_id=1, source_target_pairs={{0,8},{4,12},{8,0},{12,4},{16,24},{20,28},{24,16},{28,20},{1,9},{5... | collective-permute-start | bytes 1572872 | tf_op jit(solution)/shard_map/ppermute | solution.py:38
  186.8 23.2 %collective-permute-start.23 = (bf16[128,2048]{1,0:T(8,128)(2,1)S(1)}, bf16[128,2048]{1,0:T(8,128)(2,1)S(1)}, u32[]{:S(2)}, u32[]{:S(2)}) collective-permute-start(bf16[128,2048]{1,0:T(8,128)(2,1)S(1)} %multiply_convert_fusion.2.refs_0_), channel_id=1, source_target_pairs={{0,24},{4,28},{8,16},{12,20},{16,8},{20,12},{24,0},{28,4},{1,25},{... | collective-permute-start | bytes 1572872 | tf_op jit(solution)/shard_map/ppermute | solution.py:38
  188.3 23.2 %collective-permute-start.22 = (bf16[128,2048]{1,0:T(8,128)(2,1)S(1)}, bf16[128,2048]{1,0:T(8,128)(2,1)}, u32[]{:S(2)}, u32[]{:S(2)}) collective-permute-start(bf16[128,2048]{1,0:T(8,128)(2,1)S(1)} %multiply_convert_fusion.2.refs_0_), channel_id=1, source_target_pairs={{0,16},{4,20},{8,24},{12,28},{16,0},{20,4},{24,8},{28,12},{1,17},{... | collective-permute-start | bytes 1572872 | tf_op jit(solution)/shard_map/ppermute | solution.py:38
  189.7 24.5 %collective-permute-start.28 = (bf16[128,2048]{1,0:T(8,128)(2,1)S(1)}, bf16[128,2048]{1,0:T(8,128)(2,1)S(1)}, u32[]{:S(2)}, u32[]{:S(2)}) collective-permute-start(bf16[128,2048]{1,0:T(8,128)(2,1)S(1)} %multiply_convert_fusion.2.refs_0_), channel_id=1, source_target_pairs={{0,2},{1,3},{2,0},{3,1},{4,6},{5,7},{6,4},{7,5},{8,10},{9,11},{10,... | collective-permute-start | bytes 1572872 | tf_op jit(solution)/shard_map/ppermute | solution.py:38
  210.0 4.1 collective-permute-start.27
  211.5 3.0 collective-permute-start.26
  211.5 3.0 collective-permute-start.24
  212.0 3.0 collective-permute-start.25
  215.0 28.8 %collective-permute-start.31 = (bf16[128,2048]{1,0:T(8,128)(2,1)S(1)}, bf16[128,2048]{1,0:T(8,128)(2,1)S(1)}, u32[]{:S(2)}, u32[]{:S(2)}) collective-permute-start(bf16[128,2048]{1,0:T(8,128)(2,1)S(1)} %collective-permute-done.28.refs_0_), channel_id=1, source_target_pairs={{0,24},{4,28},{8,16},{12,20},{16,8},{20,12},{24,0},{28,4},{1,25},{... | collective-permute-start | bytes 1572872 | tf_op jit(solution)/shard_map/ppermute | solution.py:38
  216.5 27.4 %collective-permute-start.30 = (bf16[128,2048]{1,0:T(8,128)(2,1)S(1)}, bf16[128,2048]{1,0:T(8,128)(2,1)S(1)}, u32[]{:S(2)}, u32[]{:S(2)}) collective-permute-start(bf16[128,2048]{1,0:T(8,128)(2,1)S(1)} %collective-permute-done.28.refs_0_), channel_id=1, source_target_pairs={{0,16},{4,20},{8,24},{12,28},{16,0},{20,4},{24,8},{28,12},{1,17},{... | collective-permute-start | bytes 1572872 | tf_op jit(solution)/shard_map/ppermute | solution.py:38
  217.8 26.1 %collective-permute-start.29 = (bf16[128,2048]{1,0:T(8,128)(2,1)S(1)}, bf16[128,2048]{1,0:T(8,128)(2,1)}, u32[]{:S(2)}, u32[]{:S(2)}) collective-permute-start(bf16[128,2048]{1,0:T(8,128)(2,1)S(1)} %collective-permute-done.28.refs_0_), channel_id=1, source_target_pairs={{0,8},{4,12},{8,0},{12,4},{16,24},{20,28},{24,16},{28,20},{1,9},{5... | collective-permute-start | bytes 1572872 | tf_op jit(solution)/shard_map/ppermute | solution.py:38
  243.8 2.0 collective-permute-start.32
  243.9 3.7 collective-permute-start.33
  244.4 3.1 collective-permute-start.34
  244.5 3.6 collective-permute-start.35
  298.6 9.5 %collective-permute-start.36 = (bf16[4,128,2176]{2,1,0:T(8,128)(2,1)}, bf16[4,128,2176]{2,1,0:T(8,128)(2,1)}, u32[]{:S(2)}, u32[]{:S(2)}) collective-permute-start(bf16[4,128,2176]{2,1,0:T(8,128)(2,1)} %bitcast.220), channel_id=1, source_target_pairs={{0,4},{4,0},{8,12},{12,8},{16,20},{20,16},{24,28},{28,24},{1,5},{5... | collective-permute-start | bytes 6684680 | tf_op jit(solution)/shard_map/ppermute | solution.py:38
  298.7 64.3 %collective-permute-start.37 = (bf16[2,2,512,512]{3,2,1,0:T(8,128)(2,1)}, bf16[2,2,512,512]{3,2,1,0:T(8,128)(2,1)}, u32[]{:S(2)}, u32[]{:S(2)}) collective-permute-start(bf16[2,2,512,512]{3,2,1,0:T(8,128)(2,1)} %bitcast.33), channel_id=1, source_target_pairs={{0,1},{1,0},{2,3},{3,2},{4,5},{5,4},{6,7},{7,6},{8,9},{9,8},{10,11... | collective-permute-start | bytes 6291464 | tf_op jit(solution)/shard_map/ppermute | solution.py:38
  311.6 36.2 %all-to-all-start.2 = ((bf16[4,128,2176]{2,1,0:T(8,128)(2,1)}), bf16[4,128,2176]{2,1,0:T(8,128)(2,1)S(1)}, u32[]{:S(2)}, u32[]{:S(2)}) async-start(bf16[4,128,2176]{2,1,0:T(8,128)(2,1)} %add_convert_fusion.1), calls=%async_computation.2 | async-start | bytes 4456448 | tf_op jit(solution)/shard_map/all_to_all | solution.py:87
  315.2 103.0 %all-gather.17.cloned.1.call-start = ((), (), s32[]{:S(2)}) async-start(), calls=%async_computation.10 | async-start | bytes 6291456 | tf_op jit(solution)/shard_map/all_gather | solution.py:937
  362.9 5.4 collective-permute-start.38
  364.5 31.5 %collective-permute-start.39 = (bf16[128,2176]{1,0:T(8,128)(2,1)}, bf16[128,2176]{1,0:T(8,128)(2,1)}, u32[]{:S(2)}, u32[]{:S(2)}) collective-permute-start(bf16[128,2176]{1,0:T(8,128)(2,1)} %convert_reduce_fusion.1), channel_id=1, source_target_pairs={{0,2},{1,3},{2,0},{3,1},{4,6},{5,7},{6,4},{7,5},{8,10},{9,11},{10,... | collective-permute-start | bytes 1671176 | tf_op jit(solution)/shard_map/ppermute | solution.py:38
  371.9 39.1 %all-to-all-start.3 = ((bf16[4,128,2176]{2,1,0:T(8,128)(2,1)}), bf16[4,128,2176]{2,1,0:T(8,128)(2,1)S(1)}, u32[]{:S(2)}, u32[]{:S(2)}) async-start(bf16[4,128,2176]{2,1,0:T(8,128)(2,1)} %add_convert_fusion), calls=%async_computation.3 | async-start | bytes 4456448 | tf_op jit(solution)/shard_map/all_to_all | solution.py:87
  375.6 188.4 %all-gather.19.cloned.1.call-start = ((), (), s32[]{:S(2)}) async-start(), calls=%async_computation.11 | async-start | bytes 6291456 | tf_op jit(solution)/shard_map/all_gather | solution.py:937
  393.1 197.2 %reduce-scatter.2.cloned.1.call-start = ((), (), s32[]{:S(2)}) async-start(), calls=%async_computation.7 | async-start | bytes 9437184 | tf_op jit(solution)/shard_map/reduce_scatter | solution.py:1003
  399.3 49.2 %collective-permute-start.47 = (bf16[2,512,512]{2,1,0:T(8,128)(2,1)}, bf16[2,512,512]{2,1,0:T(8,128)(2,1)}, u32[]{:S(2)}, u32[]{:S(2)}) collective-permute-start(bf16[2,512,512]{2,1,0:T(8,128)(2,1)} %fusion.8), channel_id=1, source_target_pairs={{0,2},{1,3},{2,0},{3,1},{4,6},{5,7},{6,4},{7,5},{8,10},{9,11},{10,... | collective-permute-start | bytes 3145736 | tf_op jit(solution)/shard_map/ppermute | solution.py:38
  414.7 15.8 %collective-permute-start.42 = (bf16[128,2048]{1,0:T(8,128)(2,1)S(1)}, bf16[128,2048]{1,0:T(8,128)(2,1)S(1)}, u32[]{:S(2)}, u32[]{:S(2)}) collective-permute-start(bf16[128,2048]{1,0:T(8,128)(2,1)S(1)} %get-tuple-element.141.refs_0_), channel_id=1, source_target_pairs={{0,24},{4,28},{8,16},{12,20},{16,8},{20,12},{24,0},{28,4},{1,25},{... | collective-permute-start | bytes 1572872 | tf_op jit(solution)/shard_map/ppermute | solution.py:38
  417.6 23.1 %collective-permute-start.41 = (bf16[128,2048]{1,0:T(8,128)(2,1)S(1)}, bf16[128,2048]{1,0:T(8,128)(2,1)}, u32[]{:S(2)}, u32[]{:S(2)}) collective-permute-start(bf16[128,2048]{1,0:T(8,128)(2,1)S(1)} %get-tuple-element.141.refs_0_), channel_id=1, source_target_pairs={{0,16},{4,20},{8,24},{12,28},{16,0},{20,4},{24,8},{28,12},{1,17},{... | collective-permute-start | bytes 1572872 | tf_op jit(solution)/shard_map/ppermute | solution.py:38
  418.1 22.8 %collective-permute-start.40 = (bf16[128,2048]{1,0:T(8,128)(2,1)S(1)}, bf16[128,2048]{1,0:T(8,128)(2,1)}, u32[]{:S(2)}, u32[]{:S(2)}) collective-permute-start(bf16[128,2048]{1,0:T(8,128)(2,1)S(1)} %get-tuple-element.141.refs_0_), channel_id=1, source_target_pairs={{0,8},{4,12},{8,0},{12,4},{16,24},{20,28},{24,16},{28,20},{1,9},{5... | collective-permute-start | bytes 1572872 | tf_op jit(solution)/shard_map/ppermute | solution.py:38
  440.9 7.6 %collective-permute-start.46 = (bf16[128,2048]{1,0:T(8,128)(2,1)S(1)}, bf16[128,2048]{1,0:T(8,128)(2,1)S(1)}, u32[]{:S(2)}, u32[]{:S(2)}) collective-permute-start(bf16[128,2048]{1,0:T(8,128)(2,1)S(1)} %collective-permute-done.42.refs_3_), channel_id=1, source_target_pairs={{0,4},{4,0},{8,12},{12,8},{16,20},{20,16},{24,28},{28,24},{1,5},{5... | collective-permute-start | bytes 1572872 | tf_op jit(solution)/shard_map/ppermute | solution.py:38
  440.9 7.6 %collective-permute-start.45 = (bf16[128,2048]{1,0:T(8,128)(2,1)}, bf16[128,2048]{1,0:T(8,128)(2,1)S(1)}, u32[]{:S(2)}, u32[]{:S(2)}) collective-permute-start(bf16[128,2048]{1,0:T(8,128)(2,1)} %collective-permute-done.41.refs_2_), channel_id=1, source_target_pairs={{0,4},{4,0},{8,12},{12,8},{16,20},{20,16},{24,28},{28,24},{1,5},{5... | collective-permute-start | bytes 1572872 | tf_op jit(solution)/shard_map/ppermute | solution.py:38
  441.4 7.1 %collective-permute-start.43 = (bf16[128,2048]{1,0:T(8,128)(2,1)S(1)}, bf16[128,2048]{1,0:T(8,128)(2,1)S(1)}, u32[]{:S(2)}, u32[]{:S(2)}) collective-permute-start(bf16[128,2048]{1,0:T(8,128)(2,1)S(1)} %get-tuple-element.141.refs_0_), channel_id=1, source_target_pairs={{0,4},{4,0},{8,12},{12,8},{16,20},{20,16},{24,28},{28,24},{1,5},{5... | collective-permute-start | bytes 1572872 | tf_op jit(solution)/shard_map/ppermute | solution.py:38
  441.4 8.7 %collective-permute-start.44 = (bf16[128,2048]{1,0:T(8,128)(2,1)}, bf16[128,2048]{1,0:T(8,128)(2,1)}, u32[]{:S(2)}, u32[]{:S(2)}) collective-permute-start(bf16[128,2048]{1,0:T(8,128)(2,1)} %collective-permute-done.40.refs_1_), channel_id=1, source_target_pairs={{0,4},{4,0},{8,12},{12,8},{16,20},{20,16},{24,28},{28,24},{1,5},{5... | collective-permute-start | bytes 1572872 | tf_op jit(solution)/shard_map/ppermute | solution.py:38
  468.2 175.5 %collective-permute-start.55 = (bf16[2,512,512]{2,1,0:T(8,128)(2,1)}, bf16[2,512,512]{2,1,0:T(8,128)(2,1)}, u32[]{:S(2)}, u32[]{:S(2)}) collective-permute-start(bf16[2,512,512]{2,1,0:T(8,128)(2,1)} %fusion.9), channel_id=1, source_target_pairs={{0,2},{1,3},{2,0},{3,1},{4,6},{5,7},{6,4},{7,5},{8,10},{9,11},{10,... | collective-permute-start | bytes 3145736 | tf_op jit(solution)/shard_map/ppermute | solution.py:38
  519.5 47.7 %all-to-all-start.5 = ((bf16[32,80,256]{2,1,0:T(8,128)(2,1)}), bf16[32,80,256]{2,1,0:T(8,128)(2,1)}, u32[]{:S(2)}, u32[]{:S(2)}) async-start(bf16[32,80,256]{2,1,0:T(8,128)(2,1)} %pad_maximum_fusion), calls=%async_computation.6 | async-start | bytes 2621440 | tf_op jit(solution)/shard_map/all_to_all | solution.py:1032
  530.2 40.4 %collective-permute-start.49 = (bf16[512,2048]{1,0:T(8,128)(2,1)}, bf16[512,2048]{1,0:T(8,128)(2,1)}, u32[]{:S(2)}, u32[]{:S(2)}) collective-permute-start(bf16[512,2048]{1,0:T(8,128)(2,1)} %add_convert_fusion.2), channel_id=1, source_target_pairs={{0,4},{4,0},{8,12},{12,8},{16,20},{20,16},{24,28},{28,24},{1,5},{5... | collective-permute-start | bytes 6291464 | tf_op jit(solution)/shard_map/ppermute | solution.py:38
  530.7 30.1 %collective-permute-start.53 = (bf16[2,64,2048]{2,1,0:T(8,128)(2,1)S(1)}, bf16[2,64,2048]{2,1,0:T(8,128)(2,1)S(1)}, u32[]{:S(2)}, u32[]{:S(2)}) collective-permute-start(bf16[2,64,2048]{2,1,0:T(8,128)(2,1)S(1)} %pad_maximum_fusion.7), channel_id=1, source_target_pairs={{0,1},{1,0},{2,3},{3,2},{4,5},{5,4},{6,7},{7,6},{8,9},{9,8},{10,11... | collective-permute-start | bytes 1572872 | tf_op jit(solution)/shard_map/ppermute | solution.py:38
  561.7 81.9 %collective-permute-start.54 = (bf16[64,2048]{1,0:T(8,128)(2,1)}, bf16[64,2048]{1,0:T(8,128)(2,1)S(1)}, u32[]{:S(2)}, u32[]{:S(2)}) collective-permute-start(bf16[64,2048]{1,0:T(8,128)(2,1)} %fusion.24), channel_id=1, source_target_pairs={{0,2},{1,3},{2,0},{3,1},{4,6},{5,7},{6,4},{7,5},{8,10},{9,11},{10,... | collective-permute-start | bytes 786440 | tf_op jit(solution)/shard_map/ppermute | solution.py:38
  567.2 82.0 %all-to-all-start.4 = ((bf16[32,64,512]{2,1,0:T(8,128)(2,1)}), bf16[32,64,512]{2,1,0:T(8,128)(2,1)}, u32[]{:S(2)}, u32[]{:S(2)}) async-start(bf16[32,64,512]{2,1,0:T(8,128)(2,1)} %bitcast.188), calls=%async_computation.5 | async-start | bytes 4194304 | tf_op jit(solution)/shard_map/all_to_all | solution.py:1032
  573.6 29.0 %collective-permute-start.50 = (bf16[128,2048]{1,0:T(8,128)(2,1)}, bf16[128,2048]{1,0:T(8,128)(2,1)}, u32[]{:S(2)}, u32[]{:S(2)}) collective-permute-start(bf16[128,2048]{1,0:T(8,128)(2,1)} %get-tuple-element.177), channel_id=1, source_target_pairs={{0,8},{4,12},{8,0},{12,4},{16,24},{20,28},{24,16},{28,20},{1,9},{5... | collective-permute-start | bytes 1572872 | tf_op jit(solution)/shard_map/ppermute | solution.py:38
  575.1 42.1 %collective-permute-start.52 = (bf16[128,2048]{1,0:T(8,128)(2,1)}, bf16[128,2048]{1,0:T(8,128)(2,1)}, u32[]{:S(2)}, u32[]{:S(2)}) collective-permute-start(bf16[128,2048]{1,0:T(8,128)(2,1)} %get-tuple-element.178), channel_id=1, source_target_pairs={{0,24},{4,28},{8,16},{12,20},{16,8},{20,12},{24,0},{28,4},{1,25},{... | collective-permute-start | bytes 1572872 | tf_op jit(solution)/shard_map/ppermute | solution.py:38
  576.6 40.6 %collective-permute-start.51 = (bf16[128,2048]{1,0:T(8,128)(2,1)}, bf16[128,2048]{1,0:T(8,128)(2,1)}, u32[]{:S(2)}, u32[]{:S(2)}) collective-permute-start(bf16[128,2048]{1,0:T(8,128)(2,1)} %get-tuple-element.179), channel_id=1, source_target_pairs={{0,16},{4,20},{8,24},{12,28},{16,0},{20,4},{24,8},{28,12},{1,17},{... | collective-permute-start | bytes 1572872 | tf_op jit(solution)/shard_map/ppermute | solution.py:38
  602.6 41.0 %collective-permute-start.48 = (bf16[128,2048]{1,0:T(8,128)(2,1)S(1)}, bf16[128,2048]{1,0:T(8,128)(2,1)S(1)}, u32[]{:S(2)}, u32[]{:S(2)}) collective-permute-start(bf16[128,2048]{1,0:T(8,128)(2,1)S(1)} %slice_bitcast_fusion.2), channel_id=1, source_target_pairs={{0,2},{1,3},{2,0},{3,1},{4,6},{5,7},{6,4},{7,5},{8,10},{9,11},{10,... | collective-permute-start | bytes 1572872 | tf_op jit(solution)/shard_map/ppermute | solution.py:38
  (67 other events, 776.5 us)
Sparse Core Ops, SparseCore 0:
  75.6 38.7 all-gather.12
  119.6 38.5 all-gather.14
  317.6 87.2 all-gather.16
  406.3 79.2 all-gather.18
  488.9 85.1 reduce-scatter.1
